TPU v7x, 32 devices: a whole 2x2x4 slice. The times are simulated.
32 devices in a mesh: batch: 8 (over z, y), blk: 4 (over x, core).
Axes of the slice: x: 2, y: 2, z: 4, core: 2. Of those that a mesh axis runs over, the one named last changes fastest.
Arguments:
- inputs: bfloat16 [64, 512, 768], P('batch', 'blk'), may hold values from -6 to 6
- w_qkv: bfloat16 [768, 2304], P(('batch', 'blk')), may hold values from -0.21875 to 0.21875
- bias_query: bfloat16 [768], P(('batch', 'blk')), may hold values from -1.75 to 1.75
- bias_value: bfloat16 [768], P(('batch', 'blk')), may hold values from -1.75 to 1.75
- w_out: bfloat16 [768, 768], P(('batch', 'blk')), may hold values from -1.75 to 1.75
- bias_out: bfloat16 [768], P(('batch', 'blk')), may hold values from -1.75 to 1.75
- gain_first: bfloat16 [768], P(('batch', 'blk')), may hold values from 0.5 to 1.5
- shift_first: bfloat16 [768], P(('batch', 'blk')), may hold values from -1.75 to 1.75
- w_up: bfloat16 [768, 3072], P(('batch', 'blk')), may hold values from -0.21875 to 0.21875
- bias_up: bfloat16 [3072], P(('batch', 'blk')), may hold values from -1.75 to 1.75
- w_down: bfloat16 [3072, 768], P(('batch', 'blk')), may hold values from -0.109375 to 0.109375
- bias_down: bfloat16 [768], P(('batch', 'blk')), may hold values from -1.75 to 1.75
- gain_second: bfloat16 [768], P(('batch', 'blk')), may hold values from 0.5 to 1.5
- shift_second: bfloat16 [768], P(('batch', 'blk')), may hold values from -1.75 to 1.75
- dam_mask: int32 [12, 512, 512], P(None, 'blk'), may hold values from 0 to 1, as said below
- positions: int32 [64, 128], P('batch'), may hold values from -1 to 511, as said below
- counts: int32 [64], P('batch'), may hold values from 16 to 128, as said below
- cot_values: bfloat16 [64, 128, 768], P('batch'), may hold values from -6 to 6
Outputs:
- activations: bfloat16 [64, 512, 768], P('batch', 'blk')
- input_grad: float32 [64, 512, 768], P('batch', 'blk')
- grad_w_qkv: float32 [768, 2304], P(('batch', 'blk'))
- grad_bias_query: float32 [768], P(('batch', 'blk'))
- grad_bias_value: float32 [768], P(('batch', 'blk'))
- grad_w_out: float32 [768, 768], P(('batch', 'blk'))
- grad_bias_out: float32 [768], P(('batch', 'blk'))
- grad_gain_first: float32 [768], P(('batch', 'blk'))
- grad_shift_first: float32 [768], P(('batch', 'blk'))
- grad_w_up: float32 [768, 3072], P(('batch', 'blk'))
- grad_bias_up: float32 [3072], P(('batch', 'blk'))
- grad_w_down: float32 [3072, 768], P(('batch', 'blk'))
- grad_bias_down: float32 [768], P(('batch', 'blk'))
- grad_gain_second: float32 [768], P(('batch', 'blk'))
- grad_shift_second: float32 [768], P(('batch', 'blk'))
Inputs may be any that keep to these rules, and one draw needn't show every extreme that they name: `dam_mask`: every head's mask is 1 on its diagonal. The first counts[s] entries of row s are distinct positions of sequence s; the remaining entries are -1. `counts`: some sequence has exactly 128 masked positions in every draw.
All inputs are finite; a program needn't handle non-finite values.
Results may differ from a plain program's by a relative error of at most 0.014.
Values may be sent and summed in bfloat16 or wider, within the bound.
No kernel may reach another device: no remote copies, remote signals or barrier semaphores. Data moves between devices by JAX's collectives and lax.ppermute only.
A program may use at most 192 MiB of HBM per device.

v0:
```python
from functools import partial

import jax
import jax.numpy as jnp
from jax import lax
from jax.sharding import PartitionSpec as P

norm_eps = 1e-06
masked_score = -1e30


def matmul(left, right):
    return jnp.dot(left, right, preferred_element_type=jnp.float32)


def matmul_left_t(left, right):
    return jnp.einsum("ti,tj->ij", left, right, preferred_element_type=jnp.float32)


def matmul_right_t(left, right):
    return jnp.einsum("tj,ij->ti", left, right, preferred_element_type=jnp.float32)


def norm_forward(token_rows, gain, shift):
    center = jnp.mean(token_rows, axis=-1, keepdims=True)
    centered = token_rows - center
    spread = jnp.mean(centered * centered, axis=-1, keepdims=True)
    inverse = lax.rsqrt(spread + norm_eps)
    normed = centered * inverse
    return (normed * gain + shift, normed, inverse)


def norm_backward(upstream, normed, inverse, gain):
    grad_gain = jnp.sum(upstream * normed, axis=0)
    grad_shift = jnp.sum(upstream, axis=0)
    scaled = upstream * gain
    inner = jnp.mean(scaled, axis=-1, keepdims=True)
    projected = jnp.mean(scaled * normed, axis=-1, keepdims=True)
    return (inverse * (scaled - inner - normed * projected), grad_gain, grad_shift)


def split_heads(tensor, head_count):
    return tensor.reshape(tensor.shape[0], head_count, tensor.shape[1] // head_count)


def scores_of(queries, keys_all, allowed, head_count):
    head_dim = queries.shape[1] // head_count
    scores = jnp.einsum(
        "qhd,khd->hqk",
        split_heads(queries, head_count),
        split_heads(keys_all, head_count),
        preferred_element_type=jnp.float32,
    ) * head_dim ** (-0.5)
    return jnp.where(allowed, scores, masked_score)


def attend_forward(triple, allowed, head_count):
    queries, keys_all, values_all = triple
    scores = scores_of(queries, keys_all, allowed, head_count)
    row_top = jnp.max(scores, axis=-1, keepdims=True)
    weights = jnp.exp(scores - row_top)
    totals = jnp.sum(weights, axis=-1, keepdims=True)
    probabilities = (weights / totals).astype(jnp.bfloat16)
    attended = jnp.einsum(
        "hqk,khd->qhd",
        probabilities,
        split_heads(values_all, head_count),
        preferred_element_type=jnp.float32,
    )
    return (attended.reshape(queries.shape[0], queries.shape[1]), row_top + jnp.log(totals))


def score_grads(queries, keys_all, values_all, log_totals, upstream, allowed, head_count):
    scores = scores_of(queries, keys_all, allowed, head_count)
    exact = jnp.exp(scores - log_totals)
    up_heads = split_heads(upstream, head_count)
    grad_probs = jnp.einsum(
        "qhd,khd->hqk",
        up_heads,
        split_heads(values_all, head_count),
        preferred_element_type=jnp.float32,
    )
    inner = jnp.sum(grad_probs * exact, axis=-1, keepdims=True)
    grad_scores = (exact * (grad_probs - inner)).astype(jnp.bfloat16)
    return (exact, grad_scores, inner)


def attend_backward(pieces, allowed, head_count):
    queries, keys_all, values_all, log_totals, upstream = pieces
    head_dim = queries.shape[1] // head_count
    score_scale = head_dim ** (-0.5)
    exact, grad_scores, inner = score_grads(
        queries, keys_all, values_all, log_totals, upstream, allowed, head_count
    )
    up_heads = split_heads(upstream, head_count)
    grad_values = jnp.einsum(
        "hqk,qhd->khd", exact.astype(jnp.bfloat16), up_heads, preferred_element_type=jnp.float32
    )
    grad_queries = (
        jnp.einsum(
            "hqk,khd->qhd",
            grad_scores,
            split_heads(keys_all, head_count),
            preferred_element_type=jnp.float32,
        )
        * score_scale
    )
    grad_keys = (
        jnp.einsum(
            "hqk,qhd->khd",
            grad_scores,
            split_heads(queries, head_count),
            preferred_element_type=jnp.float32,
        )
        * score_scale
    )
    width = queries.shape[1]
    return (
        grad_queries.reshape(queries.shape[0], width),
        grad_keys.reshape(keys_all.shape[0], width),
        grad_values.reshape(keys_all.shape[0], width),
    )


def local(
    inputs,
    w_qkv,
    bias_query,
    bias_value,
    w_out,
    bias_out,
    gain_first,
    shift_first,
    w_up,
    bias_up,
    w_down,
    bias_down,
    gain_second,
    shift_second,
    dam_mask,
    positions,
    counts,
    cot_values,
):
    (
        qkv_full,
        query_bias,
        value_bias,
        out_full,
        out_bias,
        first_gain,
        first_shift,
        up_full,
        up_bias,
        down_full,
        down_bias,
        second_gain,
        second_shift,
    ) = (
        lax.all_gather(w_qkv, ("batch", "blk"), axis=0, tiled=True),
        lax.all_gather(bias_query, ("batch", "blk"), axis=0, tiled=True),
        lax.all_gather(bias_value, ("batch", "blk"), axis=0, tiled=True),
        lax.all_gather(w_out, ("batch", "blk"), axis=0, tiled=True),
        lax.all_gather(bias_out, ("batch", "blk"), axis=0, tiled=True),
        lax.all_gather(gain_first, ("batch", "blk"), axis=0, tiled=True),
        lax.all_gather(shift_first, ("batch", "blk"), axis=0, tiled=True),
        lax.all_gather(w_up, ("batch", "blk"), axis=0, tiled=True),
        lax.all_gather(bias_up, ("batch", "blk"), axis=0, tiled=True),
        lax.all_gather(w_down, ("batch", "blk"), axis=0, tiled=True),
        lax.all_gather(bias_down, ("batch", "blk"), axis=0, tiled=True),
        lax.all_gather(gain_second, ("batch", "blk"), axis=0, tiled=True),
        lax.all_gather(shift_second, ("batch", "blk"), axis=0, tiled=True),
    )
    groups, block_rows, width = inputs.shape
    head_count = dam_mask.shape[0]
    token_count = groups * block_rows
    allowed = dam_mask > 0
    token_rows = inputs.reshape(token_count, width)
    joined = matmul(token_rows, qkv_full)
    queries = (joined[:, :width] + query_bias.astype(jnp.float32)).astype(jnp.bfloat16)
    keys_local = joined[:, width : 2 * width].astype(jnp.bfloat16)
    values_local = (joined[:, 2 * width :] + value_bias.astype(jnp.float32)).astype(jnp.bfloat16)
    query_blocks = queries.reshape(groups, block_rows, width)
    key_blocks = keys_local.reshape(groups, block_rows, width)
    value_blocks = values_local.reshape(groups, block_rows, width)
    keys_whole, values_whole = (
        lax.all_gather(key_blocks, "blk", axis=1, tiled=True),
        lax.all_gather(value_blocks, "blk", axis=1, tiled=True),
    )
    attended, log_totals = lax.map(
        partial(attend_forward, allowed=allowed, head_count=head_count),
        (query_blocks, keys_whole, values_whole),
    )
    attended = attended.reshape(token_count, width).astype(jnp.bfloat16)
    branch = matmul(attended, out_full) + out_bias.astype(jnp.float32)
    first_sum = token_rows.astype(jnp.float32) + branch
    gain_one = first_gain.astype(jnp.float32)
    hidden, normed_first, inverse_first = norm_forward(
        first_sum, gain_one, first_shift.astype(jnp.float32)
    )
    hidden_low = hidden.astype(jnp.bfloat16)
    gate_in = matmul(hidden_low, up_full) + up_bias.astype(jnp.float32)
    active = jax.nn.gelu(gate_in, approximate=False).astype(jnp.bfloat16)
    second = matmul(active, down_full) + down_bias.astype(jnp.float32)
    gain_two = second_gain.astype(jnp.float32)
    result, normed_second, inverse_second = norm_forward(
        hidden + second, gain_two, second_shift.astype(jnp.float32)
    )
    activations = result.astype(jnp.bfloat16).reshape(groups, block_rows, width)
    first_row = lax.axis_index("blk") * block_rows
    local_rows = positions - first_row
    live = jnp.arange(positions.shape[1], dtype=jnp.int32)[None, :] < counts[:, None]
    picks = (
        local_rows[:, :, None] == jnp.arange(block_rows, dtype=jnp.int32)[None, None, :]
    ) & live[:, :, None]
    upstream = jnp.einsum(
        "gpr,gpd->grd", picks.astype(jnp.bfloat16), cot_values, preferred_element_type=jnp.float32
    ).reshape(token_count, width)
    grad_second_sum, grad_gain_second, grad_shift_second = norm_backward(
        upstream, normed_second, inverse_second, gain_two
    )
    grad_down_in = grad_second_sum.astype(jnp.bfloat16)
    grad_bias_down = jnp.sum(grad_down_in.astype(jnp.float32), axis=0)
    grad_w_down = matmul_left_t(active, grad_down_in)
    grad_active = matmul_right_t(grad_down_in, down_full)
    unused, gelu_pull = jax.vjp(partial(jax.nn.gelu, approximate=False), gate_in)
    grad_gate = gelu_pull(grad_active)[0].astype(jnp.bfloat16)
    grad_bias_up = jnp.sum(grad_gate.astype(jnp.float32), axis=0)
    grad_w_up = matmul_left_t(hidden_low, grad_gate)
    grad_hidden = grad_second_sum + matmul_right_t(grad_gate, up_full)
    grad_first_sum, grad_gain_first, grad_shift_first = norm_backward(
        grad_hidden, normed_first, inverse_first, gain_one
    )
    grad_branch = grad_first_sum.astype(jnp.bfloat16)
    grad_bias_out = jnp.sum(grad_branch.astype(jnp.float32), axis=0)
    grad_w_out = matmul_left_t(attended, grad_branch)
    grad_attended = (
        matmul_right_t(grad_branch, out_full)
        .astype(jnp.bfloat16)
        .reshape(groups, block_rows, width)
    )
    keys_back, values_back = (keys_whole, values_whole)
    grad_queries, grad_keys, grad_values = lax.map(
        partial(attend_backward, allowed=allowed, head_count=head_count),
        (query_blocks, keys_back, values_back, log_totals, grad_attended),
    )
    grad_keys_home, grad_values_home = (
        lax.psum_scatter(
            grad_keys.astype(jnp.bfloat16), "blk", scatter_dimension=1, tiled=True
        ).astype(jnp.float32),
        lax.psum_scatter(
            grad_values.astype(jnp.bfloat16), "blk", scatter_dimension=1, tiled=True
        ).astype(jnp.float32),
    )
    grad_joined = jnp.concatenate(
        [
            grad_queries.reshape(token_count, width).astype(jnp.bfloat16),
            grad_keys_home.reshape(token_count, width).astype(jnp.bfloat16),
            grad_values_home.reshape(token_count, width).astype(jnp.bfloat16),
        ],
        axis=1,
    )
    grad_bias_query = jnp.sum(grad_joined[:, :width].astype(jnp.float32), axis=0)
    grad_bias_value = jnp.sum(grad_joined[:, 2 * width :].astype(jnp.float32), axis=0)
    grad_w_qkv = matmul_left_t(token_rows, grad_joined)
    grad_inputs = grad_first_sum + matmul_right_t(grad_joined, qkv_full)
    (
        share_w_qkv,
        share_bias_query,
        share_bias_value,
        share_w_out,
        share_bias_out,
        share_gain_first,
        share_shift_first,
        share_w_up,
        share_bias_up,
        share_w_down,
        share_bias_down,
        share_gain_second,
        share_shift_second,
    ) = (
        lax.psum_scatter(grad_w_qkv, ("batch", "blk"), scatter_dimension=0, tiled=True),
        lax.psum_scatter(grad_bias_query, ("batch", "blk"), scatter_dimension=0, tiled=True),
        lax.psum_scatter(grad_bias_value, ("batch", "blk"), scatter_dimension=0, tiled=True),
        lax.psum_scatter(grad_w_out, ("batch", "blk"), scatter_dimension=0, tiled=True),
        lax.psum_scatter(grad_bias_out, ("batch", "blk"), scatter_dimension=0, tiled=True),
        lax.psum_scatter(grad_gain_first, ("batch", "blk"), scatter_dimension=0, tiled=True),
        lax.psum_scatter(grad_shift_first, ("batch", "blk"), scatter_dimension=0, tiled=True),
        lax.psum_scatter(grad_w_up, ("batch", "blk"), scatter_dimension=0, tiled=True),
        lax.psum_scatter(grad_bias_up, ("batch", "blk"), scatter_dimension=0, tiled=True),
        lax.psum_scatter(grad_w_down, ("batch", "blk"), scatter_dimension=0, tiled=True),
        lax.psum_scatter(grad_bias_down, ("batch", "blk"), scatter_dimension=0, tiled=True),
        lax.psum_scatter(grad_gain_second, ("batch", "blk"), scatter_dimension=0, tiled=True),
        lax.psum_scatter(grad_shift_second, ("batch", "blk"), scatter_dimension=0, tiled=True),
    )
    return (
        activations,
        grad_inputs.reshape(groups, block_rows, width),
        share_w_qkv,
        share_bias_query,
        share_bias_value,
        share_w_out,
        share_bias_out,
        share_gain_first,
        share_shift_first,
        share_w_up,
        share_bias_up,
        share_w_down,
        share_bias_down,
        share_gain_second,
        share_shift_second,
    )


def solution(mesh):
    return jax.shard_map(
        local,
        mesh=mesh,
        in_specs=(
            P("batch", "blk", None),
            P(("batch", "blk"), None),
            P(("batch", "blk")),
            P(("batch", "blk")),
            P(("batch", "blk"), None),
            P(("batch", "blk")),
            P(("batch", "blk")),
            P(("batch", "blk")),
            P(("batch", "blk"), None),
            P(("batch", "blk")),
            P(("batch", "blk"), None),
            P(("batch", "blk")),
            P(("batch", "blk")),
            P(("batch", "blk")),
            P(None, "blk", None),
            P("batch", None),
            P("batch"),
            P("batch", None, None),
        ),
        out_specs=(
            P("batch", "blk", None),
            P("batch", "blk", None),
            P(("batch", "blk"), None),
            P(("batch", "blk")),
            P(("batch", "blk")),
            P(("batch", "blk"), None),
            P(("batch", "blk")),
            P(("batch", "blk")),
            P(("batch", "blk")),
            P(("batch", "blk"), None),
            P(("batch", "blk")),
            P(("batch", "blk"), None),
            P(("batch", "blk")),
            P(("batch", "blk")),
            P(("batch", "blk")),
        ),
        check_vma=False,
    )
```

profile of v0, /device:TPU:0, one launch (start us, length us, event | category | flops | bytes accessed | tf_op | source)
XLA Modules:
  0.0 1234.8 jit_solution(16429673692586914878)
XLA Ops:
  15.5 42.5 %all-reduce.19 = (bf16[768]{0:T(1024)(128)(2,1)S(1)}, bf16[768]{0:T(1024)(128)(2,1)S(1)}, bf16[768]{0:T(1024)(128)(2,1)S(1)}, bf16[768]{0:T(1024)(128)(2,1)S(1)}...) all-reduce(bf16[768]{0:T(1024)(128)(2,1)S(1)} %dynamic-update-slice, ...), channel_id=1, replica_groups=mesh['batch'=8,'blk'=4] {'batch','blk'}, use_global_device_ids=true, to_apply=%add | all-reduce | flops 9216 | bytes 36864
  58.1 15.7 %all-gather.7.cloned.1.call-done = bf16[768,2304]{1,0:T(8,128)(2,1)} async-done(((bf16[24,2304]{1,0:T(8,128)(2,1)}), bf16[768,2304]{1,0:T(8,128)(2,1)}) %all-gather.7.cloned.1.call-update) | async-done | bytes 3538960 | tf_op jit(solution)/shard_map/all_gather | solution.py:160
  73.8 6.3 fusion.38
  80.1 2.2 fusion.10
  82.3 1.9 copy-done.11
  85.9 2.0 slice.23
  91.7 2.8 broadcast_compare_fusion
  94.6 2.8 fusion.33
  97.5 2.7 copy.51
  100.2 31.8 %all-gather.9.cloned.1.call-done = bf16[8,512,768]{1,2,0:T(8,128)(2,1)} async-done(((bf16[8,128,768]{1,2,0:T(8,128)(2,1)}), bf16[8,512,768]{1,2,0:T(8,128)(2,1)}) %all-gather.9.cloned.1.call-update) | async-done | bytes 6291472 | tf_op jit(solution)/shard_map/all_gather | solution.py:188
  132.0 48.8 %all-gather.11.cloned.1.call-done = bf16[8,512,768]{1,2,0:T(8,128)(2,1)} async-done(((bf16[8,128,768]{1,2,0:T(8,128)(2,1)}), bf16[8,512,768]{1,2,0:T(8,128)(2,1)}) %all-gather.11.cloned.1.call-update) | async-done | bytes 6291472 | tf_op jit(solution)/shard_map/all_gather | solution.py:187
  182.1 55.0 %while.26 = (s32[]{:T(128)}, bf16[8,128,768]{2,1,0:T(8,128)(2,1)}, f32[8,12,128,1]{2,1,3,0:T(8,128)}, bf16[8,512,768]{1,2,0:T(8,128)(2,1)}, bf16[8,128,768]{1,2,...) while((s32[]{:T(128)}, bf16[8,128,768]{2,1,0:T(8,128)(2,1)}, ...), condition=%wide.region_3.4_spmd, body=%wide.region_0.3_spmd.sunk | while | flops 207616512 | bytes 16567389 | solution.py:190
  237.7 3.8 fusion.36
  243.6 59.4 %all-gather.15.cloned.1.call-done = bf16[768,3072]{1,0:T(8,128)(2,1)} async-done(((bf16[24,3072]{1,0:T(8,128)(2,1)}), bf16[768,3072]{1,0:T(8,128)(2,1)}) %all-gather.15.cloned.1.call-update) | async-done | bytes 4718608 | tf_op jit(solution)/shard_map/all_gather | solution.py:167
  303.0 38.5 %multiply_convert_fusion.1 = (bf16[1024,3072]{1,0:T(8,128)(2,1)}, f32[1024,3072]{1,0:T(8,128)}, f32[1024,3072]{1,0:T(8,128)}) fusion(f32[3072]{0:T(1024)S(1)} %convert_element_type.126, bf16[768,3072]{1,0:T(8,128)(2,1)} %all-gather.15.cloned.1.call-done, f32[1024,768]{1,0:T(8,128)} %copy-done.7, f32[768]{0:T(1024)S(1)} %convert_element_type.124, ...), kind=kOutput, calls=%fused_computation.29 | convolution fusion | flops 5043388416 | bytes 39348224 | tf_op jit(solution)/shard_map/dot_general | solution.py:13
  341.5 26.8 %all-gather.17.cloned.1.call-done = bf16[3072,768]{1,0:T(8,128)(2,1)} async-done(((bf16[96,768]{1,0:T(8,128)(2,1)}), bf16[3072,768]{1,0:T(8,128)(2,1)}) %all-gather.17.cloned.1.call-update) | async-done | bytes 4718608 | tf_op jit(solution)/shard_map/all_gather | solution.py:169
  368.2 9.3 fusion.37
  381.1 3.8 convert_reduce_fusion.1
  384.9 19.5 %convert_reduce_fusion = (f32[3072]{0:T(1024)}, bf16[1024,3072]{1,0:T(8,128)(2,1)}) fusion(f32[1024,3072]{1,0:T(8,128)} %get-tuple-element.273, bf16[3072,768]{1,0:T(8,128)(2,1)} %all-gather.17.cloned.1.call-done, f32[1024,768]{1,0:T(8,128)} %get-tuple-element.269, f32[1024,3072]{1,0:T(8,128)} %get-tuple-element.287, f32[3072]{0:T(1024)S(1)} %convert_element_type.126), kind=kOutput, calls=%fused_computation.27 | convolution fusion | flops 4886098944 | bytes 39346176 | tf_op jit(solution)/shard_map/tj,ij->ti/dot_general | solution.py:21
  404.4 10.7 multiply_reduce_fusion.1
  415.0 1.7 convert_reduce_fusion.2
  416.8 2.6 convolution_convert_fusion
  420.6 175.5 %while.27 = (s32[]{:T(128)}, bf16[8,128,768]{2,1,0:T(8,128)(2,1)}, bf16[8,512,768]{2,1,0:T(8,128)(2,1)}, bf16[8,512,768]{2,1,0:T(8,128)(2,1)}, bf16[8,512,768]{1...) while((s32[]{:T(128)}, bf16[8,128,768]{2,1,0:T(8,128)(2,1)}, ...), condition=%wide.region_14.15_spmd, body=%wide.region_12.14_spmd.sunk | while | flops 511375872 | bytes 59604208 | solution.py:243
  423.9 2.1 subtract_exponential_fusion.3
  433.7 2.3 copy.96
  438.8 2.4 constant_dynamic-update-slice_fusion.9
  445.9 2.1 subtract_exponential_fusion.3
  448.0 1.6 constant_dynamic-slice_fusion.17
  455.7 2.3 copy.96
  460.8 2.4 constant_dynamic-update-slice_fusion.9
  467.8 2.1 subtract_exponential_fusion.3
  469.9 1.6 constant_dynamic-slice_fusion.17
  477.6 2.3 copy.96
  482.7 2.4 constant_dynamic-update-slice_fusion.9
  489.7 2.1 subtract_exponential_fusion.3
  491.8 1.6 constant_dynamic-slice_fusion.17
  499.5 2.3 copy.96
  504.6 2.4 constant_dynamic-update-slice_fusion.9
  511.6 2.1 subtract_exponential_fusion.3
  521.4 2.3 copy.96
  526.6 2.4 constant_dynamic-update-slice_fusion.9
  533.6 2.1 subtract_exponential_fusion.3
  543.3 2.3 copy.96
  548.5 2.4 constant_dynamic-update-slice_fusion.9
  555.5 2.1 subtract_exponential_fusion.3
  565.3 2.3 copy.96
  570.4 2.4 constant_dynamic-update-slice_fusion.9
  577.4 2.1 subtract_exponential_fusion.3
  587.2 2.3 copy.96
  592.3 2.4 constant_dynamic-update-slice_fusion.9
  597.0 5.3 fusion.23
  602.4 12.2 fusion.29
  614.7 2.3 copy-done.14
  617.0 10.3 fusion.26
  627.6 25.9 %reduce-scatter.11.cloned.1.call-done = bf16[8,128,768]{2,1,0:T(8,128)(2,1)} async-done(((bf16[8,512,768]{2,1,0:T(8,128)(2,1)}), bf16[8,128,768]{2,1,0:T(8,128)(2,1)}) %reduce-scatter.11.cloned.1.call-update) | async-done | bytes 1572880 | tf_op jit(solution)/shard_map/reduce_scatter | solution.py:251
  653.5 61.1 %reduce-scatter.9.cloned.1.call-done = bf16[8,128,768]{2,1,0:T(8,128)(2,1)} async-done(((bf16[8,512,768]{2,1,0:T(8,128)(2,1)}), bf16[8,128,768]{2,1,0:T(8,128)(2,1)}) %reduce-scatter.9.cloned.1.call-update) | async-done | bytes 1572880 | tf_op jit(solution)/shard_map/reduce_scatter | solution.py:248
  714.6 8.7 convolution_bitcast_fusion
  723.3 8.1 copy.59
  733.1 40.2 %all-reduce.18 = (f32[768]{0:T(1024)S(1)}, f32[768]{0:T(1024)S(1)}, f32[768]{0:T(1024)S(1)}, f32[768]{0:T(1024)S(1)}, f32[768]{0:T(1024)S(1)}, /*index=5*/f32[30...) all-reduce(f32[768]{0:T(1024)S(1)} %convert_reduce_fusion.4, ...), channel_id=5, replica_groups=mesh['batch'=8,'blk'=4] {'batch','blk'}, use_global_device_ids=true, to_apply=%region_19.20.clone | all-reduce | flops 9216 | bytes 73728
  778.6 9.6 fusion.15
  788.2 31.4 %reduce-scatter.13.cloned.1.call-done = f32[24,768]{1,0:T(8,128)} async-done(((f32[768,768]{1,0:T(8,128)}), f32[24,768]{1,0:T(8,128)}) %reduce-scatter.13.cloned.1.call-update) | async-done | bytes 73744 | tf_op jit(solution)/shard_map/reduce_scatter | solution.py:285
  819.5 141.8 %reduce-scatter.15.cloned.1.call-done = f32[24,3072]{1,0:T(8,128)} async-done(((f32[768,3072]{1,0:T(8,128)}), f32[24,3072]{1,0:T(8,128)}) %reduce-scatter.15.cloned.1.call-update) | async-done | bytes 294928 | tf_op jit(solution)/shard_map/reduce_scatter | solution.py:289
  961.3 141.0 %reduce-scatter.17.cloned.1.call-done = f32[96,768]{1,0:T(8,128)} async-done(((f32[3072,768]{1,0:T(8,128)}), f32[96,768]{1,0:T(8,128)}) %reduce-scatter.17.cloned.1.call-update) | async-done | bytes 294928 | tf_op jit(solution)/shard_map/reduce_scatter | solution.py:291
  1102.3 125.3 %reduce-scatter.19.cloned.1.call-done = f32[24,2304]{1,0:T(8,128)} async-done(((f32[768,2304]{1,0:T(8,128)}), f32[24,2304]{1,0:T(8,128)}) %reduce-scatter.19.cloned.1.call-update) | async-done | bytes 221200
  (363 shorter events, 200.9 us)
Async XLA Ops:
  7.2 87.5 %copy-start = (bf16[8,128,768]{2,1,0:T(8,128)(2,1)S(1)}, bf16[8,128,768]{2,1,0:T(8,128)(2,1)}, u32[]{:S(2)}) copy-start(bf16[8,128,768]{2,1,0:T(8,128)(2,1)} %param.39) | copy-start | bytes 4718596
  7.2 66.6 %all-gather.7.cloned.1.call-start = ((), (), s32[]{:S(2)}) async-start(), calls=%async_computation.6 | async-start | bytes 3649536 | tf_op jit(solution)/shard_map/all_gather | solution.py:160
  7.9 124.1 %all-gather.9.cloned.1.call-start = ((), (), s32[]{:S(2)}) async-start(), calls=%async_computation.7 | async-start | bytes 7864320 | tf_op jit(solution)/shard_map/all_gather | solution.py:188
  80.1 4.2 copy-start.11
  85.9 95.0 %all-gather.11.cloned.1.call-start = ((), (), s32[]{:S(2)}) async-start(), calls=%async_computation.8 | async-start | bytes 7864320 | tf_op jit(solution)/shard_map/all_gather | solution.py:187
  89.6 5.0 copy-start.26
  89.6 5.1 copy-start.21
  89.6 148.1 %all-gather.13.cloned.1.call-start = ((), (), s32[]{:S(2)}) async-start(), calls=%async_computation.9 | async-start | bytes 1216512 | tf_op jit(solution)/shard_map/all_gather | solution.py:163
  90.2 212.9 %all-gather.15.cloned.1.call-start = ((), (), s32[]{:S(2)}) async-start(), calls=%async_computation.10 | async-start | bytes 4866048 | tf_op jit(solution)/shard_map/all_gather | solution.py:167
  90.8 277.5 %all-gather.17.cloned.1.call-start = ((), (), s32[]{:S(2)}) async-start(), calls=%async_computation.11 | async-start | bytes 4866048 | tf_op jit(solution)/shard_map/all_gather | solution.py:169
  91.3 562.2 %reduce-scatter.11.cloned.1.call-start = ((), (), s32[]{:S(2)}) async-start(), calls=%async_computation.13 | async-start | bytes 7864320 | tf_op jit(solution)/shard_map/reduce_scatter | solution.py:251
  237.1 104.3 %copy-start.6 = (pred[12,128,512]{2,1,0:T(32,128)(4,1)}, pred[12,128,512]{2,1,0:T(32,128)(4,1)S(1)}, u32[]{:S(2)}) copy-start(pred[12,128,512]{2,1,0:T(32,128)(4,1)S(1)} %get-tuple-element.485) | copy-start | bytes 2359300
  241.5 1.6 copy-start.7
  377.6 1.9 copy-start.10
  384.9 19.5 %copy-start.8 = (f32[1024,768]{1,0:T(8,128)S(1)}, f32[1024,768]{1,0:T(8,128)}, u32[]{:S(2)}) copy-start(f32[1024,768]{1,0:T(8,128)} %copy-done.7) | copy-start | bytes 9437188
  415.0 1.7 copy-start.25
  416.8 2.6 copy-start.13
  422.0 1.9 copy-start.4
  431.3 1.2 copy-start.2
  437.3 4.0 copy-start.3
  437.3 4.0 copy-start.5
  444.0 1.9 copy-start.4
  453.2 1.2 copy-start.2
  459.2 4.0 copy-start.3
  459.2 4.0 copy-start.5
  465.9 1.9 copy-start.4
  481.1 4.0 copy-start.3
  481.1 4.0 copy-start.5
  487.8 1.9 copy-start.4
  497.0 1.2 copy-start.2
  503.0 4.0 copy-start.3
  503.0 4.0 copy-start.5
  509.7 1.9 copy-start.4
  519.0 1.2 copy-start.2
  525.0 4.0 copy-start.3
  525.0 4.0 copy-start.5
  531.6 1.9 copy-start.4
  540.9 1.2 copy-start.2
  546.9 4.0 copy-start.3
  546.9 4.0 copy-start.5
  553.6 1.9 copy-start.4
  568.8 4.0 copy-start.3
  568.8 4.0 copy-start.5
  575.5 1.9 copy-start.4
  590.7 3.9 copy-start.3
  590.7 3.9 copy-start.5
  596.2 118.4 %reduce-scatter.9.cloned.1.call-start = ((), (), s32[]{:S(2)}) async-start(), calls=%async_computation.12 | async-start | bytes 7864320 | tf_op jit(solution)/shard_map/reduce_scatter | solution.py:248
  597.0 5.5 copy-start.9
  597.0 222.5 %reduce-scatter.13.cloned.1.call-start = ((), (), s32[]{:S(2)}) async-start(), calls=%async_computation.14 | async-start | bytes 2433024 | tf_op jit(solution)/shard_map/reduce_scatter | solution.py:285
  602.4 359.0 %reduce-scatter.15.cloned.1.call-start = ((), (), s32[]{:S(2)}) async-start(), calls=%async_computation.15 | async-start | bytes 9732096 | tf_op jit(solution)/shard_map/reduce_scatter | solution.py:289
  614.6 2.3 copy-start.14
  614.6 487.7 %reduce-scatter.17.cloned.1.call-start = ((), (), s32[]{:S(2)}) async-start(), calls=%async_computation.16 | async-start | bytes 9732096 | tf_op jit(solution)/shard_map/reduce_scatter | solution.py:291
  627.3 87.3 %copy-start.12 = (bf16[8,128,768]{2,1,0:T(8,128)(2,1)S(1)}, bf16[8,128,768]{2,1,0:T(8,128)(2,1)}, u32[]{:S(2)}) copy-start(bf16[8,128,768]{2,1,0:T(8,128)(2,1)} %get-tuple-element.109) | copy-start | bytes 4718596
  627.3 87.3 %copy-start.24 = (bf16[8,128,768]{2,1,0:T(8,128)(2,1)S(1)}, bf16[8,128,768]{2,1,0:T(8,128)(2,1)}, u32[]{:S(2)}) copy-start(bf16[8,128,768]{2,1,0:T(8,128)(2,1)} %param.22) | copy-start | bytes 4718596
  627.3 600.3 %reduce-scatter.19.cloned.1.call-start = ((), (), s32[]{:S(2)}) async-start(), calls=%async_computation.17 | async-start | bytes 7299072
  731.3 1.4 copy-start.15
  731.4 1.7 copy-start.16
  731.4 1.7 copy-start.17
  731.4 1.7 copy-start.18
  731.4 1.7 copy-start.19
  731.4 1.7 copy-start.20
  731.4 1.7 copy-start.22
  731.4 1.7 copy-start.23
  778.6 449.1 %copy-start.1 = (bf16[8,128,768]{2,1,0:T(8,128)(2,1)S(1)}, bf16[8,128,768]{2,1,0:T(8,128)(2,1)}, u32[]{:S(2)}) copy-start(bf16[8,128,768]{2,1,0:T(8,128)(2,1)} %param.39) | copy-start | bytes 4718596
  (3 other events, 3.5 us)
Sparse Core Ops, SparseCore 0:
  10.9 62.8 all-gather.6
  86.0 45.9 all-gather.8
  133.6 47.2 all-gather.10
  183.6 54.0 all-gather.12
  240.4 62.5 all-gather.14
  305.8 62.4 all-gather.16
  596.3 57.1 reduce-scatter.10
  656.2 58.3 reduce-scatter.8
  720.5 98.9 reduce-scatter.12
  826.8 134.4 reduce-scatter.14
  967.8 134.4 reduce-scatter.16
  1109.4 118.2 reduce-scatter.18
where the time goes:
time: 1240 us; the launch traced here: 1230 us
  waiting for transfers between devices  713 us (58%)
  matrix products  204 us (16%)
  local copies, waits for them, and re-layouts  188 us (15%)
  blocking collectives  82.7 us (7%)
  other arithmetic  30.9 us (2%)
  between operations  14.8 us (1%)
    reduce_scatter x1, waiting for transfers between devices, local(): lax.psum_scatter(grad_w_up, ('batch', 'blk'), scatter_dimension=0, tiled=...  142 us
    reduce_scatter x1, waiting for transfers between devices, local(): lax.psum_scatter(grad_w_down, ('batch', 'blk'), scatter_dimension=0, tile...  141 us
    unnamed x13, waiting for transfers between devices  128 us
    unnamed x2, blocking collectives  82.7 us
    dynamic_slice x56, local copies, waits for them, and re-layouts, local(): lax.map(partial(attend_forward, allowed=allowed, head_count=head_count),...  69.6 us
    reduce_scatter x1, waiting for transfers between devices, local(): lax.psum_scatter(grad_keys.astype(jnp.bfloat16), 'blk', scatter_dimension...  61.1 us
    all_gather x1, waiting for transfers between devices, local(): lax.all_gather(w_up, ('batch', 'blk'), axis=0, tiled=True)  59.4 us
    dot_general x4, matrix products, matmul(): return jnp.dot(left, right, preferred_element_type=jnp.float32)  57.9 us
  transfers between devices with their start and end apart: 12, of which 12 were waited for; matrix products, arithmetic and copies ran while one was open for 14% of the time, Pallas kernels for 0%

commit v1 on v0

v1 whole, which is shorter than its diff:
```python
from functools import partial

import jax
import jax.numpy as jnp
from jax import lax
from jax.sharding import PartitionSpec as P

norm_eps = 1e-06
masked_score = -1e30
f32 = jnp.float32
bf16 = jnp.bfloat16
both = ("batch", "blk")


def matmul(left, right):
    return jnp.dot(left, right, preferred_element_type=f32)


def matmul_left_t(left, right):
    return jnp.einsum("ti,tj->ij", left, right, preferred_element_type=f32)


def matmul_right_t(left, right):
    return jnp.einsum("tj,ij->ti", left, right, preferred_element_type=f32)


def norm_forward(token_rows, gain, shift):
    center = jnp.mean(token_rows, axis=-1, keepdims=True)
    centered = token_rows - center
    spread = jnp.mean(centered * centered, axis=-1, keepdims=True)
    inverse = lax.rsqrt(spread + norm_eps)
    normed = centered * inverse
    return (normed * gain + shift, normed, inverse)


def norm_backward(upstream, normed, inverse, gain):
    grad_gain = jnp.sum(upstream * normed, axis=0)
    grad_shift = jnp.sum(upstream, axis=0)
    scaled = upstream * gain
    inner = jnp.mean(scaled, axis=-1, keepdims=True)
    projected = jnp.mean(scaled * normed, axis=-1, keepdims=True)
    return (inverse * (scaled - inner - normed * projected), grad_gain, grad_shift)


class Grid:
    def __init__(self, mesh):
        batch, blk = mesh.shape["batch"], mesh.shape["blk"]
        self.sizes = {"z": batch // 2, "y": 2, "x": blk // 2, "c": 2}
        self.strides = {"c": 1, "x": 2, "y": blk, "z": 2 * blk}
        self.total = batch * blk
        self.blk = blk

    def digit(self, name):
        index = lax.axis_index("batch") * self.blk + lax.axis_index("blk")
        return (index // self.strides[name]) % self.sizes[name]

    def swap(self, array, name, delta=1):
        size, stride = self.sizes[name], self.strides[name]
        pairs = []
        for index in range(self.total):
            here = (index // stride) % size
            pairs.append((index, index + ((here ^ delta) - here) * stride))
        return lax.ppermute(array, both, pairs)

    def swap_blk(self, array, delta):
        pairs = [(index, index ^ delta) for index in range(self.total)]
        return lax.ppermute(array, both, pairs)


def place(parts, index):
    if len(parts) == 1:
        return parts[0][None]
    rows = []
    for target in range(len(parts)):
        row = parts[0]
        for delta in range(1, len(parts)):
            row = jnp.where(index == target ^ delta, parts[delta], row)
        rows.append(row)
    return jnp.stack(rows)


def pick(array, index):
    return lax.dynamic_index_in_dim(array, index, axis=0, keepdims=False)


def gather_rows(grid, shard):
    rows, cols = shard.shape
    half = cols // 2
    core = grid.digit("c")
    halves = jnp.stack([shard[:, :half], shard[:, half:]])
    mine, other = pick(halves, core), pick(halves, 1 - core)
    held = place([mine, grid.swap(other, "c")], core)
    for name in ("x", "z", "y"):
        parts = [held] + [grid.swap(held, name, d) for d in range(1, grid.sizes[name])]
        held = place(parts, grid.digit(name))
        if name == "y":
            held = jnp.moveaxis(held, 0, 1)
        held = held.reshape((-1,) + held.shape[2:]) if name == "x" else held
    held = held.reshape(grid.total * rows, half)
    back = grid.swap(held, "c")
    return jnp.concatenate(
        [jnp.where(core == 0, held, back), jnp.where(core == 0, back, held)], axis=1
    )


def add_low(*parts):
    total = parts[0].astype(f32)
    for part in parts[1:]:
        total = total + part.astype(f32)
    return total


def scatter_rows(grid, array):
    total_rows, cols = array.shape
    half = cols // 2
    rows = total_rows // grid.total
    core = grid.digit("c")
    low, high = array[:, :half], array[:, half:]
    kept = jnp.where(core == 0, low, high)
    sent = jnp.where(core == 0, high, low)
    held = add_low(kept, grid.swap(sent, "c")).astype(bf16)
    zs, ys, xs = grid.sizes["z"], grid.sizes["y"], grid.sizes["x"]
    held = held.reshape(zs, ys, xs * 2 * rows, half)
    where_y = grid.digit("y")
    kept = lax.dynamic_index_in_dim(held, where_y, axis=1, keepdims=False)
    sent = lax.dynamic_index_in_dim(held, 1 - where_y, axis=1, keepdims=False)
    held = add_low(kept, grid.swap(sent, "y")).astype(bf16)
    where_z = grid.digit("z")
    parts = [pick(held, where_z)]
    for delta in range(1, zs):
        parts.append(grid.swap(pick(held, where_z ^ delta), "z", delta))
    held = add_low(*parts).astype(bf16).reshape(xs, 2, rows, half)
    where_x = grid.digit("x")
    parts = [pick(held, where_x)]
    for delta in range(1, xs):
        parts.append(grid.swap(pick(held, where_x ^ delta), "x", delta))
    held = add_low(*parts).astype(bf16)
    mine = pick(held, core)
    back = grid.swap(pick(held, 1 - core), "c")
    return jnp.concatenate(
        [jnp.where(core == 0, mine, back), jnp.where(core == 0, back, mine)], axis=1
    ).astype(f32)


def split_heads(tensor, head_count):
    return tensor.reshape(tensor.shape[0], head_count, tensor.shape[1] // head_count)


def scores_of(queries, keys_all, addend, head_count):
    head_dim = queries.shape[1] // head_count
    scores = jnp.einsum(
        "qhd,khd->hqk",
        split_heads(queries, head_count),
        split_heads(keys_all, head_count),
        preferred_element_type=f32,
    ) * head_dim ** (-0.5)
    return scores + addend.astype(f32)


def attend_forward(triple, addend, head_count):
    queries, keys_all, values_all = triple
    scores = scores_of(queries, keys_all, addend, head_count)
    row_top = jnp.max(scores, axis=-1, keepdims=True)
    weights = jnp.exp(scores - row_top)
    totals = jnp.sum(weights, axis=-1, keepdims=True)
    probabilities = (weights / totals).astype(bf16)
    attended = jnp.einsum(
        "hqk,khd->qhd",
        probabilities,
        split_heads(values_all, head_count),
        preferred_element_type=f32,
    )
    return (attended.reshape(queries.shape[0], queries.shape[1]), row_top + jnp.log(totals))


def attend_backward(pieces, addend, head_count):
    queries, keys_all, values_all, log_totals, upstream = pieces
    head_dim = queries.shape[1] // head_count
    score_scale = head_dim ** (-0.5)
    scores = scores_of(queries, keys_all, addend, head_count)
    exact = jnp.exp(scores - log_totals)
    up_heads = split_heads(upstream, head_count)
    grad_probs = jnp.einsum(
        "qhd,khd->hqk", up_heads, split_heads(values_all, head_count), preferred_element_type=f32
    )
    inner = jnp.sum(grad_probs * exact, axis=-1, keepdims=True)
    grad_scores = (exact * (grad_probs - inner)).astype(bf16)
    grad_values = jnp.einsum("hqk,qhd->khd", exact.astype(bf16), up_heads, preferred_element_type=f32)
    grad_queries = (
        jnp.einsum(
            "hqk,khd->qhd", grad_scores, split_heads(keys_all, head_count), preferred_element_type=f32
        )
        * score_scale
    )
    grad_keys = (
        jnp.einsum(
            "hqk,qhd->khd", grad_scores, split_heads(queries, head_count), preferred_element_type=f32
        )
        * score_scale
    )
    width = queries.shape[1]
    return jnp.concatenate(
        [g.reshape(g.shape[0], width).astype(bf16) for g in (grad_queries, grad_keys, grad_values)],
        axis=1,
    )


def local(
    grid,
    inputs,
    w_qkv,
    bias_query,
    bias_value,
    w_out,
    bias_out,
    gain_first,
    shift_first,
    w_up,
    bias_up,
    w_down,
    bias_down,
    gain_second,
    shift_second,
    dam_mask,
    positions,
    counts,
    cot_values,
):
    groups, block_rows, width = inputs.shape
    head_count = dam_mask.shape[0]
    blk = grid.blk
    seqs = groups // blk
    length = blk * block_rows
    token_count = seqs * length
    here = lax.axis_index("blk")
    rows = w_qkv.shape[0]
    up_per = bias_up.shape[0] // rows

    by_home = inputs.reshape(blk, seqs, block_rows, width)
    parts = [pick(by_home, here)]
    for delta in range(1, blk):
        parts.append(grid.swap_blk(pick(by_home, here ^ delta), delta))

    pad_cols = 256
    vectors = (
        bias_query,
        bias_value,
        bias_out,
        gain_first,
        shift_first,
        bias_down,
        gain_second,
        shift_second,
    )
    columns = jnp.concatenate([jnp.stack(vectors, axis=1), bias_up.reshape(rows, up_per)], axis=1)
    columns = jnp.pad(columns, ((0, 0), (0, pad_cols - columns.shape[1])))
    first_group = gather_rows(grid, jnp.concatenate([w_qkv, columns], axis=1))

    addend = jnp.where(dam_mask > 0, 0.0, masked_score).astype(bf16)
    mask_parts = [addend, grid.swap(addend, "c")]
    far = grid.swap(addend, "x") if grid.sizes["x"] > 1 else None
    if far is not None:
        mask_parts += [far, grid.swap(far, "c")]
    second_group = gather_rows(grid, jnp.concatenate([w_out, w_up], axis=1))
    down_full = gather_rows(grid, w_down)

    qkv_full = first_group[:, : 3 * width]
    gathered = first_group[:, 3 * width :]
    vector_rows = gathered[:, : len(vectors)].T.astype(f32)
    (
        query_bias,
        value_bias,
        out_bias,
        gain_one,
        shift_one,
        down_bias,
        gain_two,
        shift_two,
    ) = [vector_rows[i] for i in range(len(vectors))]
    up_bias = gathered[:, len(vectors) : len(vectors) + up_per].reshape(-1).astype(f32)
    out_full = second_group[:, :width]
    up_full = second_group[:, width:]

    token_rows = place(parts, here).transpose(1, 0, 2, 3).reshape(token_count, width)
    addend_all = place(mask_parts, here).transpose(1, 0, 2, 3).reshape(head_count, length, length)

    joined = matmul(token_rows, qkv_full)
    queries = (joined[:, :width] + query_bias).astype(bf16).reshape(seqs, length, width)
    keys = joined[:, width : 2 * width].astype(bf16).reshape(seqs, length, width)
    values = (joined[:, 2 * width :] + value_bias).astype(bf16).reshape(seqs, length, width)
    attended, log_totals = lax.map(
        partial(attend_forward, addend=addend_all, head_count=head_count), (queries, keys, values)
    )
    attended = attended.reshape(token_count, width).astype(bf16)
    branch = matmul(attended, out_full) + out_bias
    first_sum = token_rows.astype(f32) + branch
    hidden, normed_first, inverse_first = norm_forward(first_sum, gain_one, shift_one)
    hidden_low = hidden.astype(bf16)
    gate_in = matmul(hidden_low, up_full) + up_bias
    active = jax.nn.gelu(gate_in, approximate=False).astype(bf16)
    second = matmul(active, down_full) + down_bias
    result, normed_second, inverse_second = norm_forward(hidden + second, gain_two, shift_two)

    def home(array):
        by_place = array.astype(bf16).reshape(seqs, blk, block_rows, width)
        got = [lax.dynamic_index_in_dim(by_place, here, axis=1, keepdims=False)]
        for delta in range(1, blk):
            sent = lax.dynamic_index_in_dim(by_place, here ^ delta, axis=1, keepdims=False)
            got.append(grid.swap_blk(sent, delta))
        return place(got, here).reshape(groups, block_rows, width)

    activations = home(result)

    my_positions = pick(positions.reshape(blk, seqs, -1), here)
    my_counts = pick(counts.reshape(blk, seqs), here)
    my_values = pick(cot_values.reshape((blk, seqs) + cot_values.shape[1:]), here)
    live = jnp.arange(positions.shape[1], dtype=jnp.int32)[None, :] < my_counts[:, None]
    picks = (
        my_positions[:, :, None] == jnp.arange(length, dtype=jnp.int32)[None, None, :]
    ) & live[:, :, None]
    upstream = jnp.einsum(
        "gpr,gpd->grd", picks.astype(bf16), my_values, preferred_element_type=f32
    ).reshape(token_count, width)
    grad_second_sum, grad_gain_second, grad_shift_second = norm_backward(
        upstream, normed_second, inverse_second, gain_two
    )
    grad_down_in = grad_second_sum.astype(bf16)
    grad_bias_down = jnp.sum(grad_down_in.astype(f32), axis=0)
    share_w_down = scatter_rows(grid, matmul_left_t(active, grad_down_in).astype(bf16))
    grad_active = matmul_right_t(grad_down_in, down_full)
    unused, gelu_pull = jax.vjp(partial(jax.nn.gelu, approximate=False), gate_in)
    grad_gate = gelu_pull(grad_active)[0].astype(bf16)
    grad_bias_up = jnp.sum(grad_gate.astype(f32), axis=0)
    grad_w_up = matmul_left_t(hidden_low, grad_gate).astype(bf16)
    grad_hidden = grad_second_sum + matmul_right_t(grad_gate, up_full)
    grad_first_sum, grad_gain_first, grad_shift_first = norm_backward(
        grad_hidden, normed_first, inverse_first, gain_one
    )
    grad_branch = grad_first_sum.astype(bf16)
    grad_bias_out = jnp.sum(grad_branch.astype(f32), axis=0)
    grad_w_out = matmul_left_t(attended, grad_branch).astype(bf16)
    share_second = scatter_rows(grid, jnp.concatenate([grad_w_out, grad_w_up], axis=1))
    grad_attended = matmul_right_t(grad_branch, out_full).astype(bf16).reshape(seqs, length, width)
    grad_joined = lax.map(
        partial(attend_backward, addend=addend_all, head_count=head_count),
        (queries, keys, values, log_totals, grad_attended),
    ).reshape(token_count, 3 * width)
    grad_bias_query = jnp.sum(grad_joined[:, :width].astype(f32), axis=0)
    grad_bias_value = jnp.sum(grad_joined[:, 2 * width :].astype(f32), axis=0)
    grad_w_qkv = matmul_left_t(token_rows, grad_joined).astype(bf16)
    vector_grads = (
        grad_bias_query,
        grad_bias_value,
        grad_bias_out,
        grad_gain_first,
        grad_shift_first,
        grad_bias_down,
        grad_gain_second,
        grad_shift_second,
    )
    columns = jnp.concatenate(
        [jnp.stack(vector_grads, axis=1), grad_bias_up.reshape(width, up_per)], axis=1
    )
    columns = jnp.pad(columns, ((0, 0), (0, pad_cols - columns.shape[1]))).astype(bf16)
    share_first = scatter_rows(grid, jnp.concatenate([grad_w_qkv, columns], axis=1))
    grad_inputs = home(grad_first_sum + matmul_right_t(grad_joined, qkv_full)).astype(f32)

    share_vectors = [share_first[:, 3 * width + i] for i in range(len(vectors))]
    share_bias_up = share_first[
        :, 3 * width + len(vectors) : 3 * width + len(vectors) + up_per
    ].reshape(-1)
    (
        share_bias_query,
        share_bias_value,
        share_bias_out,
        share_gain_first,
        share_shift_first,
        share_bias_down,
        share_gain_second,
        share_shift_second,
    ) = share_vectors
    return (
        activations,
        grad_inputs,
        share_first[:, : 3 * width],
        share_bias_query,
        share_bias_value,
        share_second[:, :width],
        share_bias_out,
        share_gain_first,
        share_shift_first,
        share_second[:, width:],
        share_bias_up,
        share_w_down,
        share_bias_down,
        share_gain_second,
        share_shift_second,
    )


def solution(mesh):
    sharded = P(both)
    rows = P(both, None)
    whole = P("batch", "blk", None)
    return jax.shard_map(
        partial(local, Grid(mesh)),
        mesh=mesh,
        in_specs=(
            whole,
            rows,
            sharded,
            sharded,
            rows,
            sharded,
            sharded,
            sharded,
            rows,
            sharded,
            rows,
            sharded,
            sharded,
            sharded,
            P(None, "blk", None),
            P("batch", None),
            P("batch"),
            P("batch", None, None),
        ),
        out_specs=(
            whole,
            whole,
            rows,
            sharded,
            sharded,
            rows,
            sharded,
            sharded,
            sharded,
            rows,
            sharded,
            rows,
            sharded,
            sharded,
            sharded,
        ),
        check_vma=False,
    )
```

time: 1240 us -> 700 us (0.56)
  waiting for transfers between devices: 713 us -> 226 us
  local copies, waits for them, and re-layouts: 188 us -> 81.6 us
  starting transfers between devices: 1.02 us -> 93.7 us
  blocking collectives: 82.7 us -> 0 us
  other arithmetic: 30.9 us -> 90.2 us
    reduce_scatter x5 -> x0, waiting for transfers between devices: 401 us -> none  [the longest x1 142 us: local(): lax.psum_scatter(grad_w_up, ('batch', 'blk'), scatter_dimension=0, tiled=...]
    ppermute x0 -> x54, waiting for transfers between devices: none -> 226 us  [the longest x45 210 us: swap(): return lax.ppermute(array, both, pairs)]
    all_gather x6 -> x0, waiting for transfers between devices: 183 us -> none  [the longest x1 59.4 us: local(): lax.all_gather(w_up, ('batch', 'blk'), axis=0, tiled=True)]
    unnamed x13 -> x0, waiting for transfers between devices: 128 us -> none
    ppermute x0 -> x54, starting transfers between devices: none -> 93.7 us  [the longest x45 84.9 us: swap(): return lax.ppermute(array, both, pairs)]
    unnamed x2 -> x0, blocking collectives: 82.7 us -> none
    dynamic_slice x56 -> x12, local copies, waits for them, and re-layouts: 69.6 us -> 15.3 us  [local(): lax.map(partial(attend_forward, addend=addend_all, head_count=head_count)...]
    dynamic_update_slice x56 -> x8, local copies, waits for them, and re-layouts: 63.4 us -> 17.4 us  [the longest x4 15 us: local(): lax.map(partial(attend_backward, addend=addend_all, head_count=head_count...]
  transfers between devices with their start and end apart: 12 -> 54, of which waited for: 12 -> 24; matrix products, arithmetic and copies ran while one was open for 14% -> 20% of each run, Pallas kernels for 0% -> 0%
where the time goes in v1:
time: 700 us; the launch traced here: 688 us
  waiting for transfers between devices  226 us (32%)
  matrix products  193 us (28%)
  starting transfers between devices  93.7 us (13%)
  other arithmetic  90.2 us (13%)
  local copies, waits for them, and re-layouts  81.6 us (12%)
    ppermute x45, waiting for transfers between devices, swap(): return lax.ppermute(array, both, pairs)  210 us
    ppermute x45, starting transfers between devices, swap(): return lax.ppermute(array, both, pairs)  84.9 us
    dot_general x4, matrix products, matmul(): return jnp.dot(left, right, preferred_element_type=f32)  61.9 us
    dot_general x4, matrix products, matmul_right_t(): return jnp.einsum('tj,ij->ti', left, right, preferred_element_type=f32)  40.3 us
    dot_general x4, matrix products, matmul_left_t(): return jnp.einsum('ti,tj->ij', left, right, preferred_element_type=f32)  26.8 us
    dot_general x4, matrix products, scores_of(): jnp.einsum('qhd,khd->hqk', split_heads(queries, head_count), split_heads(...  25.8 us
    dot_general x2, matrix products, attend_backward(): jnp.einsum('qhd,khd->hqk', up_heads, split_heads(values_all, head_count),...  22.9 us
    ppermute x9, waiting for transfers between devices, swap_blk(): return lax.ppermute(array, both, pairs)  16.5 us
  transfers between devices with their start and end apart: 54, of which 24 were waited for; matrix products, arithmetic and copies ran while one was open for 20% of the time, Pallas kernels for 0%

profile of v1, /device:TPU:0, one launch (start us, length us, event | category | flops | bytes accessed | tf_op | source)
XLA Modules:
  0.0 688.2 jit_solution(6744509862828227558)
XLA Ops:
  6.3 2.6 collective-permute-start
  11.1 3.5 select_convert_fusion
  20.3 43.3 %collective-permute-done.4 = bf16[2,24,1280]{2,1,0:T(8,128)(2,1)S(1)} collective-permute-done((bf16[2,24,1280]{2,1,0:T(8,128)(2,1)S(1)}, bf16[2,24,1280]{2,1,0:T(8,128)(2,1)S(1)}, u32[]{:S(2)}, u32[]{:S(2)}) %collective-permute-start.4) | collective-permute-done | bytes 122912 | tf_op jit(solution)/shard_map/ppermute | solution.py:63
  65.7 3.8 collective-permute-done.21
  71.4 4.1 collective-permute-done.14
  75.5 3.5 collective-permute-start.5
  80.0 3.5 collective-permute-start.22
  86.2 19.5 %collective-permute-start.23 = (bf16[4,96,384]{2,1,0:T(8,128)(2,1)S(1)}, bf16[4,96,384]{2,1,0:T(8,128)(2,1)S(1)}, u32[]{:S(2)}, u32[]{:S(2)}) collective-permute-start(bf16[4,96,384]{2,1,0:T(8,128)(2,1)S(1)} %bitcast.559), channel_id=1, source_target_pairs={{0,16},{1,17},{2,18},{3,19},{4,20},{5,21},{6,22},{7,23},{8,24},{9,... | collective-permute-start | bytes 884744 | tf_op jit(solution)/shard_map/ppermute | solution.py:63
  105.8 4.5 collective-permute-done.6
  110.3 2.5 collective-permute-start.15
  113.1 19.3 %collective-permute-start.16 = (bf16[4,24,1920]{2,1,0:T(8,128)(2,1)S(1)}, bf16[4,24,1920]{2,1,0:T(8,128)(2,1)S(1)}, u32[]{:S(2)}, u32[]{:S(2)}) collective-permute-start(bf16[4,24,1920]{2,1,0:T(8,128)(2,1)S(1)} %bitcast.554), channel_id=1, source_target_pairs={{0,16},{1,17},{2,18},{3,19},{4,20},{5,21},{6,22},{7,23},{8,24},{9,... | collective-permute-start | bytes 1105928 | tf_op jit(solution)/shard_map/ppermute | solution.py:63
  132.4 7.7 %collective-permute-done.23 = bf16[4,96,384]{2,1,0:T(8,128)(2,1)S(1)} collective-permute-done((bf16[4,96,384]{2,1,0:T(8,128)(2,1)S(1)}, bf16[4,96,384]{2,1,0:T(8,128)(2,1)S(1)}, u32[]{:S(2)}, u32[]{:S(2)}) %collective-permute-start.23) | collective-permute-done | bytes 294944 | tf_op jit(solution)/shard_map/ppermute | solution.py:63
  141.8 13.1 %collective-permute-done.16 = bf16[4,24,1920]{2,1,0:T(8,128)(2,1)S(1)} collective-permute-done((bf16[4,24,1920]{2,1,0:T(8,128)(2,1)S(1)}, bf16[4,24,1920]{2,1,0:T(8,128)(2,1)S(1)}, u32[]{:S(2)}, u32[]{:S(2)}) %collective-permute-start.16) | collective-permute-done | bytes 368672 | tf_op jit(solution)/shard_map/ppermute | solution.py:63
  159.9 24.2 %collective-permute-done.25 = bf16[4,4,96,384]{3,2,1,0:T(8,128)(2,1)S(1)} collective-permute-done((bf16[4,4,96,384]{3,2,1,0:T(8,128)(2,1)S(1)}, bf16[4,4,96,384]{3,2,1,0:T(8,128)(2,1)S(1)}, u32[]{:S(2)}, u32[]{:S(2)}) %collective-permute-start.25) | collective-permute-done | bytes 1179680 | tf_op jit(solution)/shard_map/ppermute | solution.py:63
  186.1 28.3 %collective-permute-done.18 = bf16[4,4,24,1920]{3,2,1,0:T(8,128)(2,1)S(1)} collective-permute-done((bf16[4,4,24,1920]{3,2,1,0:T(8,128)(2,1)S(1)}, bf16[4,4,24,1920]{3,2,1,0:T(8,128)(2,1)S(1)}, u32[]{:S(2)}, u32[]{:S(2)}) %collective-permute-start.18) | collective-permute-done | bytes 1474592 | tf_op jit(solution)/shard_map/ppermute | solution.py:63
  218.9 3.2 maximum_bitcast_fusion.1
  222.1 10.6 %copy.144 = bf16[12,4,128,512]{2,1,3,0:T(4,128)(2,1)} copy(bf16[12,4,128,512]{3,2,0,1:T(8,128)(2,1)} %maximum_bitcast_fusion.1) | data formatting | bytes 12582912 | tf_op jit(solution)/shard_map/transpose | solution.py:285
  232.7 10.1 %reshape.300 = bf16[12,512,512]{1,2,0:T(8,128)(2,1)} reshape(bf16[12,4,128,512]{2,1,3,0:T(4,128)(2,1)} %copy.144) | data formatting | bytes 12582912 | tf_op jit(solution)/shard_map/reshape | solution.py:285
  247.3 3.8 fusion.23
  253.6 2.6 copy.145
  256.2 2.6 copy.146
  260.4 27.0 %while.22 = (s32[]{:T(128)}, bf16[2,512,768]{2,1,0:T(8,128)(2,1)}, f32[2,12,512,1]{2,1,3,0:T(8,128)}, bf16[2,512,768]{1,2,0:T(8,128)(2,1)}, bf16[2,512,768]{1,2,...) while((s32[]{:T(128)}, bf16[2,512,768]{2,1,0:T(8,128)(2,1)}, ...), condition=%wide.region_3.4_spmd, body=%wide.region_0.3_spmd.sunk | while | flops 833611776 | bytes 55256156 | solution.py:291
  262.2 4.6 fusion.165
  275.6 4.6 fusion.165
  290.3 2.8 broadcast_select_fusion.5
  293.1 5.0 broadcast_select_fusion.2
  300.7 48.4 %multiply_convert_fusion.3 = (bf16[1024,3072]{1,0:T(8,128)(2,1)}, f32[1024,3072]{1,0:T(8,128)}, f32[1024,3072]{1,0:T(8,128)}) fusion(f32[3072]{0:T(1024)S(1)} %reshape.322, bf16[768,1920]{1,0:T(8,128)(2,1)S(1)} %get-tuple-element.235, bf16[768,1920]{1,0:T(8,128)(2,1)S(1)} %get-tuple-element.234, f32[1024,768]{1,0:T(8,128)S(1)} %get-tuple-element.314, ...), kind=kOutput, calls=%fused_computation.28 | convolution fusion | flops 5052825600 | bytes 40527872 | tf_op jit(solution)/shard_map/dot_general | solution.py:16
  349.1 8.2 %fusion.121 = (f32[1024]{0:T(1024)S(1)}, f32[1024,768]{1,0:T(8,128)S(1)}) fusion(f32[768]{0:T(1024)S(1)} %copy-done.38, bf16[1024,3072]{1,0:T(8,128)(2,1)} %get-tuple-element.218, bf16[3072,384]{1,0:T(8,128)(2,1)S(1)} %get-tuple-element.237, bf16[3072,384]{1,0:T(8,128)(2,1)S(1)} %get-tuple-element.236, f32[768]{0:T(1024)S(1)} %copy-done.36, ...), kind=kOutput, calls=%fused_computation.352 | convolution fusion | flops 4846779392 | bytes 17323008 | tf_op jit(solution)/shard_map/dot_general | solution.py:16
  358.0 3.3 fusion.16
  363.2 7.0 %convolution_convert_fusion = bf16[3072,768]{1,0:T(8,128)(2,1)} fusion(bf16[1024,3072]{1,0:T(8,128)(2,1)S(1)} %bitcast.581, f32[1024,768]{1,0:T(8,128)S(1)} %get-tuple-element.215), kind=kOutput, calls=%fused_computation.44 | convolution fusion | flops 4834983936 | bytes 14155776 | tf_op jit(solution)/shard_map/ti,tj->ij/dot_general | solution.py:20
  370.2 18.0 %fusion.122 = (bf16[3072]{0:T(1024)(128)(2,1)}, bf16[1024,3072]{1,0:T(8,128)(2,1)}) fusion(f32[1024,3072]{1,0:T(8,128)} %get-tuple-element.219, bf16[3072,384]{1,0:T(8,128)(2,1)} %copy-done.16, bf16[3072,384]{1,0:T(8,128)(2,1)} %copy-done.15, f32[1024,768]{1,0:T(8,128)} %copy-done.10, f32[1024,3072]{1,0:T(8,128)} %get-tuple-element.315, f32[3072]{0:T(1024)S(1)} %reshape.322), kind=kOutput, calls=%fused_computation.353 | convolution fusion | flops 4892390400 | bytes 39340032 | tf_op jit(solution)/shard_map/tj,ij->ti/dot_general | solution.py:24
  388.2 12.5 %multiply_reduce_fusion.1 = (bf16[768]{0:T(1024)(128)(2,1)}, f32[1024]{0:T(1024)S(1)}, f32[1024]{0:T(1024)S(1)}, bf16[768]{0:T(1024)(128)(2,1)}, f32[1024,768]{1,0:T(8,128)S(1)}) fusion(f32[1024,768]{1,0:T(8,128)} %copy-done.3, f32[1024]{0:T(1024)S(1)} %add_rsqrt_fusion.1, f32[1024]{0:T(1024)S(1)} %broadcast_multiply_fusion.4, f32[768]{0:T(1024)S(1)} %copy-done.27, ...), kind=kOutput, calls=%fused_computation.62 | convolution fusion | flops 4849135616 | bytes 21649408 | tf_op jit(solution)/shard_map/tj,ij->ti/dot_general | solution.py:24
  402.4 4.8 convolution_convert_fusion.3
  407.3 91.8 %while.23 = (s32[]{:T(128)}, bf16[2,512,2304]{2,1,0:T(8,128)(2,1)}, bf16[2,512,768]{1,2,0:T(8,128)(2,1)}, bf16[2,512,768]{1,2,0:T(8,128)(2,1)}, bf16[12,512,512]...) while((s32[]{:T(128)}, bf16[2,512,2304]{2,1,0:T(8,128)(2,1)}, ...), condition=%wide.region_14.15_spmd, body=%wide.region_12.14_spmd.sunk | while | flops 2053761024 | bytes 174711504 | solution.py:344
  410.1 8.3 %subtract_exponential_fusion.3 = f32[12,512,512]{1,2,0:T(8,128)} fusion(bf16[12,512,512]{1,2,0:T(8,128)(2,1)} %get-tuple-element.480, f32[12,512]{1,0:T(8,128)S(1)} %dynamic-slice_bitcast_fusion.29, bf16[512,12,64]{0,2,1:T(8,128)(2,1)S(1)} %bitcast.513, bf16[512,12,64]{0,2,1:T(8,128)(2,1)S(1)} %bitcast.509), kind=kOutput, calls=%fused_computation.12.clone.1 | convolution fusion | flops 415236096 | bytes 20471808 | tf_op jit(solution)/shard_map/while/body/eval_jaxpr/qhd,khd->hqk/dot_general | solution.py:151
  420.8 11.5 %multiply_reduce_fusion.9 = (f32[12,512]{1,0:T(8,128)S(1)}, f32[12,512,512]{1,2,0:T(8,128)}) fusion(f32[12,512,512]{1,2,0:T(8,128)} %subtract_exponential_fusion.3, bf16[512,12,64]{0,2,1:T(8,128)(2,1)S(1)} %bitcast.511, bf16[512,12,64]{0,2,1:T(8,128)(2,1)S(1)} %bitcast.516), kind=kOutput, calls=%fused_computation.11.clone.1 | convolution fusion | flops 408938496 | bytes 26763264 | tf_op jit(solution)/shard_map/while/body/eval_jaxpr/qhd,khd->hqk/dot_general | solution.py:183
  432.3 6.7 multiply_convert_fusion.7
  445.8 4.3 copy.199
  450.0 3.2 constant_dynamic-update-slice_fusion.5
  455.9 8.3 %subtract_exponential_fusion.3 = f32[12,512,512]{1,2,0:T(8,128)} fusion(bf16[12,512,512]{1,2,0:T(8,128)(2,1)} %get-tuple-element.480, f32[12,512]{1,0:T(8,128)S(1)} %dynamic-slice_bitcast_fusion.29, bf16[512,12,64]{0,2,1:T(8,128)(2,1)S(1)} %bitcast.513, bf16[512,12,64]{0,2,1:T(8,128)(2,1)S(1)} %bitcast.509), kind=kOutput, calls=%fused_computation.12.clone.1 | convolution fusion | flops 415236096 | bytes 20471808 | tf_op jit(solution)/shard_map/while/body/eval_jaxpr/qhd,khd->hqk/dot_general | solution.py:151
  466.6 11.5 %multiply_reduce_fusion.9 = (f32[12,512]{1,0:T(8,128)S(1)}, f32[12,512,512]{1,2,0:T(8,128)}) fusion(f32[12,512,512]{1,2,0:T(8,128)} %subtract_exponential_fusion.3, bf16[512,12,64]{0,2,1:T(8,128)(2,1)S(1)} %bitcast.511, bf16[512,12,64]{0,2,1:T(8,128)(2,1)S(1)} %bitcast.516), kind=kOutput, calls=%fused_computation.11.clone.1 | convolution fusion | flops 408938496 | bytes 26763264 | tf_op jit(solution)/shard_map/while/body/eval_jaxpr/qhd,khd->hqk/dot_general | solution.py:183
  478.1 6.7 multiply_convert_fusion.7
  491.6 4.3 copy.199
  495.9 3.2 constant_dynamic-update-slice_fusion.5
  499.1 2.5 slice_reduce_fusion
  501.7 8.0 %convolution_convert_fusion.2 = bf16[768,2304]{1,0:T(8,128)(2,1)} fusion(bf16[1024,768]{1,0:T(8,128)(2,1)S(1)} %bitcast.549, bf16[1024,2304]{1,0:T(8,128)(2,1)} %bitcast.541), kind=kOutput, calls=%fused_computation.46 | convolution fusion | flops 3625648128 | bytes 9830400 | tf_op jit(solution)/shard_map/ti,tj->ij/dot_general | solution.py:20
  509.7 2.5 convolution_convert_fusion.4
  512.3 5.0 add_convert_fusion.4
  521.6 3.9 broadcast_select_fusion.6
  531.0 9.2 %convolution_convert_fusion.1 = bf16[768,3072]{1,0:T(8,128)(2,1)S(1)} fusion(bf16[1024,3072]{1,0:T(8,128)(2,1)} %get-tuple-element.321, f32[1024,768]{1,0:T(8,128)} %copy-done.3, f32[768]{0:T(1024)S(1)} %copy-done.37, f32[768]{0:T(1024)S(1)} %copy-done.28, f32[1024]{0:T(1024)S(1)} %copy-done.30, f32[1024]{0:T(1024)S(1)} %copy-done.26), kind=kOutput, calls=%fused_computation.45 | convolution fusion | flops 4838129664 | bytes 14170112 | tf_op jit(solution)/shard_map/ti,tj->ij/dot_general | solution.py:20
  542.9 6.3 collective-permute-done.31
  553.9 3.1 collective-permute-done.27
  558.7 7.0 %collective-permute-done.28 = bf16[2,128,768]{2,1,0:T(8,128)(2,1)S(1)} collective-permute-done((bf16[2,128,768]{2,1,0:T(8,128)(2,1)S(1)}, bf16[2,128,768]{2,1,0:T(8,128)(2,1)S(1)}, u32[]{:S(2)}, u32[]{:S(2)}) %collective-permute-start.28) | collective-permute-done | bytes 393248 | tf_op jit(solution)/shard_map/ppermute | solution.py:67
  570.7 10.4 %collective-permute-done.34 = bf16[4,96,1280]{2,1,0:T(8,128)(2,1)S(1)} collective-permute-done((bf16[4,96,1280]{2,1,0:T(8,128)(2,1)S(1)}, bf16[4,96,1280]{2,1,0:T(8,128)(2,1)S(1)}, u32[]{:S(2)}, u32[]{:S(2)}) %collective-permute-start.34) | collective-permute-done | bytes 983072 | tf_op jit(solution)/shard_map/ppermute | solution.py:63
  585.9 2.6 add_convert_fusion.2
  590.4 2.6 collective-permute-done.35
  593.0 10.6 %collective-permute-done.36 = bf16[96,1280]{1,0:T(8,128)(2,1)S(1)} collective-permute-done((bf16[96,1280]{1,0:T(8,128)(2,1)S(1)}, bf16[96,1280]{1,0:T(8,128)(2,1)S(1)}, u32[]{:S(2)}, u32[]{:S(2)}) %collective-permute-start.36) | collective-permute-done | bytes 245792 | tf_op jit(solution)/shard_map/ppermute | solution.py:63
  610.7 6.9 collective-permute-done.48
  623.2 4.8 collective-permute-done.49
  628.0 12.4 %collective-permute-done.50 = bf16[384,384]{1,0:T(8,128)(2,1)S(1)} collective-permute-done((bf16[384,384]{1,0:T(8,128)(2,1)S(1)}, bf16[384,384]{1,0:T(8,128)(2,1)S(1)}, u32[]{:S(2)}, u32[]{:S(2)}) %collective-permute-start.50) | collective-permute-done | bytes 294944 | tf_op jit(solution)/shard_map/ppermute | solution.py:63
  642.9 4.2 collective-permute-done.41
  657.0 7.7 %collective-permute-done.42 = bf16[96,1920]{1,0:T(8,128)(2,1)} collective-permute-done((bf16[96,1920]{1,0:T(8,128)(2,1)}, bf16[96,1920]{1,0:T(8,128)(2,1)}, u32[]{:S(2)}, u32[]{:S(2)}) %collective-permute-start.42) | collective-permute-done | bytes 368672 | tf_op jit(solution)/shard_map/ppermute | solution.py:63
  664.7 13.2 %collective-permute-done.43 = bf16[96,1920]{1,0:T(8,128)(2,1)} collective-permute-done((bf16[96,1920]{1,0:T(8,128)(2,1)}, bf16[96,1920]{1,0:T(8,128)(2,1)}, u32[]{:S(2)}, u32[]{:S(2)}) %collective-permute-start.43) | collective-permute-done | bytes 368672 | tf_op jit(solution)/shard_map/ppermute | solution.py:63
  681.0 3.9 collective-permute-done.45
  (386 shorter events, 154.7 us)
Async XLA Ops:
  0.6 288.1 %copy-start = (bf16[8,128,768]{2,1,0:T(8,128)(2,1)S(1)}, bf16[8,128,768]{2,1,0:T(8,128)(2,1)}, u32[]{:S(2)}) copy-start(bf16[8,128,768]{2,1,0:T(8,128)(2,1)} %param.39) | copy-start | bytes 4718596
  2.6 14.5 %collective-permute-start.20 = (bf16[96,384]{1,0:T(8,128)(2,1)}, bf16[96,384]{1,0:T(8,128)(2,1)}, u32[]{:S(2)}, u32[]{:S(2)}) collective-permute-start(bf16[96,384]{1,0:T(8,128)(2,1)} %fusion.95), channel_id=1, source_target_pairs={{0,1},{1,0},{2,3},{3,2},{4,5},{5,4},{6,7},{7,6},{8,9},{9,8},{10,11... | collective-permute-start | bytes 221192 | tf_op jit(solution)/shard_map/ppermute | solution.py:63
  4.0 15.7 %collective-permute-start.13 = (bf16[24,1920]{1,0:T(8,128)(2,1)S(1)}, bf16[24,1920]{1,0:T(8,128)(2,1)S(1)}, u32[]{:S(2)}, u32[]{:S(2)}) collective-permute-start(bf16[24,1920]{1,0:T(8,128)(2,1)S(1)} %fusion.90), channel_id=1, source_target_pairs={{0,1},{1,0},{2,3},{3,2},{4,5},{5,4},{6,7},{7,6},{8,9},{9,8},{10,11... | collective-permute-start | bytes 276488 | tf_op jit(solution)/shard_map/ppermute | solution.py:63
  6.3 72.8 %collective-permute-start = (bf16[2,128,768]{2,1,0:T(8,128)(2,1)}, bf16[2,128,768]{2,1,0:T(8,128)(2,1)S(1)}, u32[]{:S(2)}, u32[]{:S(2)}) collective-permute-start(bf16[2,128,768]{2,1,0:T(8,128)(2,1)} %get-tuple-element.267), channel_id=1, source_target_pairs={{0,3},{1,2},{2,1},{3,0},{4,7},{5,6},{6,5},{7,4},{8,11},{9,10},{10,... | collective-permute-start | bytes 1179656 | tf_op jit(solution)/shard_map/ppermute | solution.py:67
  8.9 70.3 %collective-permute-start.1 = (bf16[2,128,768]{2,1,0:T(8,128)(2,1)}, bf16[2,128,768]{2,1,0:T(8,128)(2,1)S(1)}, u32[]{:S(2)}, u32[]{:S(2)}) collective-permute-start(bf16[2,128,768]{2,1,0:T(8,128)(2,1)} %get-tuple-element.266), channel_id=1, source_target_pairs={{0,2},{1,3},{2,0},{3,1},{4,6},{5,7},{6,4},{7,5},{8,10},{9,11},{10,... | collective-permute-start | bytes 1179656 | tf_op jit(solution)/shard_map/ppermute | solution.py:67
  11.0 5.5 collective-permute-start.3
  16.6 63.5 %collective-permute-start.2 = (bf16[2,128,768]{2,1,0:T(8,128)(2,1)S(1)}, bf16[2,128,768]{2,1,0:T(8,128)(2,1)S(1)}, u32[]{:S(2)}, u32[]{:S(2)}) collective-permute-start(bf16[2,128,768]{2,1,0:T(8,128)(2,1)S(1)} %get-tuple-element.265), channel_id=1, source_target_pairs={{0,1},{1,0},{2,3},{3,2},{4,5},{5,4},{6,7},{7,6},{8,9},{9,8},{10,11... | collective-permute-start | bytes 1179656 | tf_op jit(solution)/shard_map/ppermute | solution.py:67
  17.1 142.0 %collective-permute-start.10 = (bf16[12,128,512]{2,1,0:T(8,128)(2,1)}, bf16[12,128,512]{2,1,0:T(8,128)(2,1)S(1)}, u32[]{:S(2)}, u32[]{:S(2)}) collective-permute-start(bf16[12,128,512]{2,1,0:T(8,128)(2,1)} %select_convert_fusion), channel_id=1, source_target_pairs={{0,2},{1,3},{2,0},{3,1},{4,6},{5,7},{6,4},{7,5},{8,10},{9,11},{10,... | collective-permute-start | bytes 4718600 | tf_op jit(solution)/shard_map/ppermute | solution.py:63
  19.7 43.8 %collective-permute-start.4 = (bf16[2,24,1280]{2,1,0:T(8,128)(2,1)S(1)}, bf16[2,24,1280]{2,1,0:T(8,128)(2,1)S(1)}, u32[]{:S(2)}, u32[]{:S(2)}) collective-permute-start(bf16[2,24,1280]{2,1,0:T(8,128)(2,1)S(1)} %pad_maximum_fusion.31), channel_id=1, source_target_pairs={{0,2},{1,3},{2,0},{3,1},{4,6},{5,7},{6,4},{7,5},{8,10},{9,11},{10,... | collective-permute-start | bytes 368648 | tf_op jit(solution)/shard_map/ppermute | solution.py:63
  63.6 6.0 collective-permute-start.21
  69.6 5.9 collective-permute-start.14
  75.5 10.8 %collective-permute-start.5 = (bf16[4,24,1280]{2,1,0:T(8,128)(2,1)S(1)}, bf16[4,24,1280]{2,1,0:T(8,128)(2,1)S(1)}, u32[]{:S(2)}, u32[]{:S(2)}) collective-permute-start(bf16[4,24,1280]{2,1,0:T(8,128)(2,1)S(1)} %bitcast.563), channel_id=1, source_target_pairs={{0,24},{1,25},{2,26},{3,27},{4,28},{5,29},{6,30},{7,31},{8,16},{9,... | collective-permute-start | bytes 737288 | tf_op jit(solution)/shard_map/ppermute | solution.py:63
  79.1 31.2 %collective-permute-start.6 = (bf16[4,24,1280]{2,1,0:T(8,128)(2,1)S(1)}, bf16[4,24,1280]{2,1,0:T(8,128)(2,1)S(1)}, u32[]{:S(2)}, u32[]{:S(2)}) collective-permute-start(bf16[4,24,1280]{2,1,0:T(8,128)(2,1)S(1)} %bitcast.564), channel_id=1, source_target_pairs={{0,16},{1,17},{2,18},{3,19},{4,20},{5,21},{6,22},{7,23},{8,24},{9,... | collective-permute-start | bytes 737288 | tf_op jit(solution)/shard_map/ppermute | solution.py:63
  79.2 31.1 %collective-permute-start.7 = (bf16[4,24,1280]{2,1,0:T(8,128)(2,1)S(1)}, bf16[4,24,1280]{2,1,0:T(8,128)(2,1)S(1)}, u32[]{:S(2)}, u32[]{:S(2)}) collective-permute-start(bf16[4,24,1280]{2,1,0:T(8,128)(2,1)S(1)} %bitcast.565), channel_id=1, source_target_pairs={{0,8},{1,9},{2,10},{3,11},{4,12},{5,13},{6,14},{7,15},{8,0},{9,1},... | collective-permute-start | bytes 737288 | tf_op jit(solution)/shard_map/ppermute | solution.py:63
  80.0 33.1 %collective-permute-start.22 = (bf16[4,96,384]{2,1,0:T(8,128)(2,1)S(1)}, bf16[4,96,384]{2,1,0:T(8,128)(2,1)S(1)}, u32[]{:S(2)}, u32[]{:S(2)}) collective-permute-start(bf16[4,96,384]{2,1,0:T(8,128)(2,1)S(1)} %bitcast.558), channel_id=1, source_target_pairs={{0,24},{1,25},{2,26},{3,27},{4,28},{5,29},{6,30},{7,31},{8,16},{9,... | collective-permute-start | bytes 884744 | tf_op jit(solution)/shard_map/ppermute | solution.py:63
  86.2 53.9 %collective-permute-start.23 = (bf16[4,96,384]{2,1,0:T(8,128)(2,1)S(1)}, bf16[4,96,384]{2,1,0:T(8,128)(2,1)S(1)}, u32[]{:S(2)}, u32[]{:S(2)}) collective-permute-start(bf16[4,96,384]{2,1,0:T(8,128)(2,1)S(1)} %bitcast.559), channel_id=1, source_target_pairs={{0,16},{1,17},{2,18},{3,19},{4,20},{5,21},{6,22},{7,23},{8,24},{9,... | collective-permute-start | bytes 884744 | tf_op jit(solution)/shard_map/ppermute | solution.py:63
  110.3 29.8 %collective-permute-start.24 = (bf16[4,96,384]{2,1,0:T(8,128)(2,1)S(1)}, bf16[4,96,384]{2,1,0:T(8,128)(2,1)S(1)}, u32[]{:S(2)}, u32[]{:S(2)}) collective-permute-start(bf16[4,96,384]{2,1,0:T(8,128)(2,1)S(1)} %bitcast.560), channel_id=1, source_target_pairs={{0,8},{1,9},{2,10},{3,11},{4,12},{5,13},{6,14},{7,15},{8,0},{9,1},... | collective-permute-start | bytes 884744 | tf_op jit(solution)/shard_map/ppermute | solution.py:63
  110.3 31.4 %collective-permute-start.15 = (bf16[4,24,1920]{2,1,0:T(8,128)(2,1)S(1)}, bf16[4,24,1920]{2,1,0:T(8,128)(2,1)S(1)}, u32[]{:S(2)}, u32[]{:S(2)}) collective-permute-start(bf16[4,24,1920]{2,1,0:T(8,128)(2,1)S(1)} %bitcast.553), channel_id=1, source_target_pairs={{0,24},{1,25},{2,26},{3,27},{4,28},{5,29},{6,30},{7,31},{8,16},{9,... | collective-permute-start | bytes 1105928 | tf_op jit(solution)/shard_map/ppermute | solution.py:63
  113.1 41.8 %collective-permute-start.16 = (bf16[4,24,1920]{2,1,0:T(8,128)(2,1)S(1)}, bf16[4,24,1920]{2,1,0:T(8,128)(2,1)S(1)}, u32[]{:S(2)}, u32[]{:S(2)}) collective-permute-start(bf16[4,24,1920]{2,1,0:T(8,128)(2,1)S(1)} %bitcast.554), channel_id=1, source_target_pairs={{0,16},{1,17},{2,18},{3,19},{4,20},{5,21},{6,22},{7,23},{8,24},{9,... | collective-permute-start | bytes 1105928 | tf_op jit(solution)/shard_map/ppermute | solution.py:63
  140.1 16.3 %collective-permute-start.17 = (bf16[4,24,1920]{2,1,0:T(8,128)(2,1)S(1)}, bf16[4,24,1920]{2,1,0:T(8,128)(2,1)S(1)}, u32[]{:S(2)}, u32[]{:S(2)}) collective-permute-start(bf16[4,24,1920]{2,1,0:T(8,128)(2,1)S(1)} %bitcast.555), channel_id=1, source_target_pairs={{0,8},{1,9},{2,10},{3,11},{4,12},{5,13},{6,14},{7,15},{8,0},{9,1},... | collective-permute-start | bytes 1105928 | tf_op jit(solution)/shard_map/ppermute | solution.py:63
  140.1 18.8 %collective-permute-start.8 = (bf16[4,4,24,1280]{3,2,1,0:T(8,128)(2,1)S(1)}, bf16[4,4,24,1280]{3,2,1,0:T(8,128)(2,1)S(1)}, u32[]{:S(2)}, u32[]{:S(2)}) collective-permute-start(bf16[4,4,24,1280]{3,2,1,0:T(8,128)(2,1)S(1)} %pad_maximum_fusion.24), channel_id=1, source_target_pairs={{0,4},{1,5},{2,6},{3,7},{4,0},{5,1},{6,2},{7,3},{8,12},{9,13},{10,... | collective-permute-start | bytes 2949128 | tf_op jit(solution)/shard_map/ppermute | solution.py:63
  141.7 75.0 %collective-permute-start.12 = (bf16[12,128,512]{2,1,0:T(8,128)(2,1)}, bf16[12,128,512]{2,1,0:T(8,128)(2,1)S(1)}, u32[]{:S(2)}, u32[]{:S(2)}) collective-permute-start(bf16[12,128,512]{2,1,0:T(8,128)(2,1)} %select_convert_fusion), channel_id=1, source_target_pairs={{0,1},{1,0},{2,3},{3,2},{4,5},{5,4},{6,7},{7,6},{8,9},{9,8},{10,11... | collective-permute-start | bytes 4718600 | tf_op jit(solution)/shard_map/ppermute | solution.py:63
  154.9 29.2 %collective-permute-start.25 = (bf16[4,4,96,384]{3,2,1,0:T(8,128)(2,1)S(1)}, bf16[4,4,96,384]{3,2,1,0:T(8,128)(2,1)S(1)}, u32[]{:S(2)}, u32[]{:S(2)}) collective-permute-start(bf16[4,4,96,384]{3,2,1,0:T(8,128)(2,1)S(1)} %pad_maximum_fusion.23), channel_id=1, source_target_pairs={{0,4},{1,5},{2,6},{3,7},{4,0},{5,1},{6,2},{7,3},{8,12},{9,13},{10,... | collective-permute-start | bytes 3538952 | tf_op jit(solution)/shard_map/ppermute | solution.py:63
  156.9 57.5 %collective-permute-start.18 = (bf16[4,4,24,1920]{3,2,1,0:T(8,128)(2,1)S(1)}, bf16[4,4,24,1920]{3,2,1,0:T(8,128)(2,1)S(1)}, u32[]{:S(2)}, u32[]{:S(2)}) collective-permute-start(bf16[4,4,24,1920]{3,2,1,0:T(8,128)(2,1)S(1)} %pad_maximum_fusion.22), channel_id=1, source_target_pairs={{0,4},{1,5},{2,6},{3,7},{4,0},{5,1},{6,2},{7,3},{8,12},{9,13},{10,... | collective-permute-start | bytes 4423688 | tf_op jit(solution)/shard_map/ppermute | solution.py:63
  159.0 57.7 %collective-permute-start.11 = (bf16[12,128,512]{2,1,0:T(8,128)(2,1)S(1)}, bf16[12,128,512]{2,1,0:T(8,128)(2,1)S(1)}, u32[]{:S(2)}, u32[]{:S(2)}) collective-permute-start(bf16[12,128,512]{2,1,0:T(8,128)(2,1)S(1)} %collective-permute-done.10), channel_id=1, source_target_pairs={{0,1},{1,0},{2,3},{3,2},{4,5},{5,4},{6,7},{7,6},{8,9},{9,8},{10,11... | collective-permute-start | bytes 4718600 | tf_op jit(solution)/shard_map/ppermute | solution.py:63
  159.3 83.6 %collective-permute-start.9 = (bf16[768,1280]{1,0:T(8,128)(2,1)S(1)}, bf16[768,1280]{1,0:T(8,128)(2,1)}, u32[]{:S(2)}, u32[]{:S(2)}) collective-permute-start(bf16[768,1280]{1,0:T(8,128)(2,1)S(1)} %bitcast.534), channel_id=1, source_target_pairs={{0,1},{1,0},{2,3},{3,2},{4,5},{5,4},{6,7},{7,6},{8,9},{9,8},{10,11... | collective-permute-start | bytes 5898248 | tf_op jit(solution)/shard_map/ppermute | solution.py:63
  186.1 104.1 %collective-permute-start.26 = (bf16[3072,384]{1,0:T(8,128)(2,1)}, bf16[3072,384]{1,0:T(8,128)(2,1)}, u32[]{:S(2)}, u32[]{:S(2)}) collective-permute-start(bf16[3072,384]{1,0:T(8,128)(2,1)} %bitcast.106), channel_id=1, source_target_pairs={{0,1},{1,0},{2,3},{3,2},{4,5},{5,4},{6,7},{7,6},{8,9},{9,8},{10,11... | collective-permute-start | bytes 7077896 | tf_op jit(solution)/shard_map/ppermute | solution.py:63
  216.8 76.4 %collective-permute-start.19 = (bf16[768,1920]{1,0:T(8,128)(2,1)}, bf16[768,1920]{1,0:T(8,128)(2,1)}, u32[]{:S(2)}, u32[]{:S(2)}) collective-permute-start(bf16[768,1920]{1,0:T(8,128)(2,1)} %bitcast.87), channel_id=1, source_target_pairs={{0,1},{1,0},{2,3},{3,2},{4,5},{5,4},{6,7},{7,6},{8,9},{9,8},{10,11... | collective-permute-start | bytes 8847368 | tf_op jit(solution)/shard_map/ppermute | solution.py:63
  260.4 28.3 %copy-start.39 = (s32[2,128]{1,0:T(2,128)S(1)}, s32[2,128]{1,0:T(2,128)}, u32[]{:S(2)}) copy-start(s32[2,128]{1,0:T(2,128)} %fusion.103) | copy-start | bytes 3076
  260.4 28.3 %copy-start.42 = (pred[2,128]{1,0:T(4,128)(4,1)S(1)}, pred[2,128]{1,0:T(4,128)(4,1)}, u32[]{:S(2)}) copy-start(pred[2,128]{1,0:T(4,128)(4,1)} %iota_compare_fusion.1) | copy-start | bytes 772
  293.1 56.0 %copy-start.15 = (bf16[3072,384]{1,0:T(8,128)(2,1)}, bf16[3072,384]{1,0:T(8,128)(2,1)S(1)}, u32[]{:S(2)}) copy-start(bf16[3072,384]{1,0:T(8,128)(2,1)S(1)} %get-tuple-element.236) | copy-start | bytes 7077892
  293.1 56.0 %copy-start.16 = (bf16[3072,384]{1,0:T(8,128)(2,1)}, bf16[3072,384]{1,0:T(8,128)(2,1)S(1)}, u32[]{:S(2)}) copy-start(bf16[3072,384]{1,0:T(8,128)(2,1)S(1)} %get-tuple-element.237) | copy-start | bytes 7077892
  300.0 49.1 %copy-start.3 = (f32[1024,768]{1,0:T(8,128)}, f32[1024,768]{1,0:T(8,128)S(1)}, u32[]{:S(2)}) copy-start(f32[1024,768]{1,0:T(8,128)S(1)} %get-tuple-element.314) | copy-start | bytes 9437188
  300.0 100.7 %copy-start.25 = (f32[1024]{0:T(1024)}, f32[1024]{0:T(1024)S(1)}, u32[]{:S(2)}) copy-start(f32[1024]{0:T(1024)S(1)} %broadcast_multiply_fusion.4) | copy-start | bytes 12292
  300.5 100.2 %copy-start.29 = (f32[1024]{0:T(1024)}, f32[1024]{0:T(1024)S(1)}, u32[]{:S(2)}) copy-start(f32[1024]{0:T(1024)S(1)} %add_rsqrt_fusion.1) | copy-start | bytes 12292
  300.7 48.4 %copy-start.38 = (f32[768]{0:T(1024)S(1)}, f32[768]{0:T(1024)}, u32[]{:S(2)}) copy-start(f32[768]{0:T(1024)} %get-tuple-element.170) | copy-start | bytes 9220
  519.1 66.8 %collective-permute-start.47 = (bf16[3072,384]{1,0:T(8,128)(2,1)}, bf16[3072,384]{1,0:T(8,128)(2,1)}, u32[]{:S(2)}, u32[]{:S(2)}) collective-permute-start(bf16[3072,384]{1,0:T(8,128)(2,1)} %broadcast_select_fusion.3), channel_id=1, source_target_pairs={{0,1},{1,0},{2,3},{3,2},{4,5},{5,4},{6,7},{7,6},{8,9},{9,8},{10,11... | collective-permute-start | bytes 7077896 | tf_op jit(solution)/shard_map/ppermute | solution.py:63
  525.5 25.3 %collective-permute-start.33 = (bf16[768,1280]{1,0:T(8,128)(2,1)}, bf16[768,1280]{1,0:T(8,128)(2,1)}, u32[]{:S(2)}, u32[]{:S(2)}) collective-permute-start(bf16[768,1280]{1,0:T(8,128)(2,1)} %broadcast_select_fusion.6), channel_id=1, source_target_pairs={{0,1},{1,0},{2,3},{3,2},{4,5},{5,4},{6,7},{7,6},{8,9},{9,8},{10,11... | collective-permute-start | bytes 5898248 | tf_op jit(solution)/shard_map/ppermute | solution.py:63
  528.9 12.1 %collective-permute-start.30 = (bf16[2,128,768]{2,1,0:T(8,128)(2,1)S(1)}, bf16[2,128,768]{2,1,0:T(8,128)(2,1)S(1)}, u32[]{:S(2)}, u32[]{:S(2)}) collective-permute-start(bf16[2,128,768]{2,1,0:T(8,128)(2,1)S(1)} %get-tuple-element.261), channel_id=1, source_target_pairs={{0,3},{1,2},{2,1},{3,0},{4,7},{5,6},{6,5},{7,4},{8,11},{9,10},{10,... | collective-permute-start | bytes 1179656 | tf_op jit(solution)/shard_map/ppermute | solution.py:67
  530.4 18.7 %collective-permute-start.31 = (bf16[2,128,768]{2,1,0:T(8,128)(2,1)S(1)}, bf16[2,128,768]{2,1,0:T(8,128)(2,1)S(1)}, u32[]{:S(2)}, u32[]{:S(2)}) collective-permute-start(bf16[2,128,768]{2,1,0:T(8,128)(2,1)S(1)} %get-tuple-element.260), channel_id=1, source_target_pairs={{0,2},{1,3},{2,0},{3,1},{4,6},{5,7},{6,4},{7,5},{8,10},{9,11},{10,... | collective-permute-start | bytes 1179656 | tf_op jit(solution)/shard_map/ppermute | solution.py:67
  530.8 22.5 %collective-permute-start.32 = (bf16[2,128,768]{2,1,0:T(8,128)(2,1)S(1)}, bf16[2,128,768]{2,1,0:T(8,128)(2,1)S(1)}, u32[]{:S(2)}, u32[]{:S(2)}) collective-permute-start(bf16[2,128,768]{2,1,0:T(8,128)(2,1)S(1)} %get-tuple-element.259), channel_id=1, source_target_pairs={{0,1},{1,0},{2,3},{3,2},{4,5},{5,4},{6,7},{7,6},{8,9},{9,8},{10,11... | collective-permute-start | bytes 1179656 | tf_op jit(solution)/shard_map/ppermute | solution.py:67
  541.1 15.9 %collective-permute-start.27 = (bf16[2,128,768]{2,1,0:T(8,128)(2,1)S(1)}, bf16[2,128,768]{2,1,0:T(8,128)(2,1)S(1)}, u32[]{:S(2)}, u32[]{:S(2)}) collective-permute-start(bf16[2,128,768]{2,1,0:T(8,128)(2,1)S(1)} %get-tuple-element.264), channel_id=1, source_target_pairs={{0,3},{1,2},{2,1},{3,0},{4,7},{5,6},{6,5},{7,4},{8,11},{9,10},{10,... | collective-permute-start | bytes 1179656 | tf_op jit(solution)/shard_map/ppermute | solution.py:67
  549.2 16.6 %collective-permute-start.28 = (bf16[2,128,768]{2,1,0:T(8,128)(2,1)S(1)}, bf16[2,128,768]{2,1,0:T(8,128)(2,1)S(1)}, u32[]{:S(2)}, u32[]{:S(2)}) collective-permute-start(bf16[2,128,768]{2,1,0:T(8,128)(2,1)S(1)} %get-tuple-element.263), channel_id=1, source_target_pairs={{0,2},{1,3},{2,0},{3,1},{4,6},{5,7},{6,4},{7,5},{8,10},{9,11},{10,... | collective-permute-start | bytes 1179656 | tf_op jit(solution)/shard_map/ppermute | solution.py:67
  550.8 14.9 %collective-permute-start.29 = (bf16[2,128,768]{2,1,0:T(8,128)(2,1)S(1)}, bf16[2,128,768]{2,1,0:T(8,128)(2,1)S(1)}, u32[]{:S(2)}, u32[]{:S(2)}) collective-permute-start(bf16[2,128,768]{2,1,0:T(8,128)(2,1)S(1)} %get-tuple-element.262), channel_id=1, source_target_pairs={{0,1},{1,0},{2,3},{3,2},{4,5},{5,4},{6,7},{7,6},{8,9},{9,8},{10,11... | collective-permute-start | bytes 1179656 | tf_op jit(solution)/shard_map/ppermute | solution.py:67
  553.3 52.2 %collective-permute-start.40 = (bf16[768,1920]{1,0:T(8,128)(2,1)S(1)}, bf16[768,1920]{1,0:T(8,128)(2,1)S(1)}, u32[]{:S(2)}, u32[]{:S(2)}) collective-permute-start(bf16[768,1920]{1,0:T(8,128)(2,1)S(1)} %broadcast_select_fusion), channel_id=1, source_target_pairs={{0,1},{1,0},{2,3},{3,2},{4,5},{5,4},{6,7},{7,6},{8,9},{9,8},{10,11... | collective-permute-start | bytes 8847368 | tf_op jit(solution)/shard_map/ppermute | solution.py:63
  557.0 24.1 %collective-permute-start.34 = (bf16[4,96,1280]{2,1,0:T(8,128)(2,1)S(1)}, bf16[4,96,1280]{2,1,0:T(8,128)(2,1)S(1)}, u32[]{:S(2)}, u32[]{:S(2)}) collective-permute-start(bf16[4,96,1280]{2,1,0:T(8,128)(2,1)S(1)} %dynamic-slice_bitcast_fusion.3), channel_id=1, source_target_pairs={{0,4},{1,5},{2,6},{3,7},{4,0},{5,1},{6,2},{7,3},{8,12},{9,13},{10,... | collective-permute-start | bytes 2949128 | tf_op jit(solution)/shard_map/ppermute | solution.py:63
  581.4 11.5 %collective-permute-start.35 = (bf16[96,1280]{1,0:T(8,128)(2,1)S(1)}, bf16[96,1280]{1,0:T(8,128)(2,1)S(1)}, u32[]{:S(2)}, u32[]{:S(2)}) collective-permute-start(bf16[96,1280]{1,0:T(8,128)(2,1)S(1)} %get-tuple-element.282), channel_id=1, source_target_pairs={{0,8},{1,9},{2,10},{3,11},{4,12},{5,13},{6,14},{7,15},{8,0},{9,1},... | collective-permute-start | bytes 737288 | tf_op jit(solution)/shard_map/ppermute | solution.py:63
  583.2 20.3 %collective-permute-start.36 = (bf16[96,1280]{1,0:T(8,128)(2,1)S(1)}, bf16[96,1280]{1,0:T(8,128)(2,1)S(1)}, u32[]{:S(2)}, u32[]{:S(2)}) collective-permute-start(bf16[96,1280]{1,0:T(8,128)(2,1)S(1)} %get-tuple-element.284), channel_id=1, source_target_pairs={{0,16},{1,17},{2,18},{3,19},{4,20},{5,21},{6,22},{7,23},{8,24},{9,... | collective-permute-start | bytes 737288 | tf_op jit(solution)/shard_map/ppermute | solution.py:63
  583.7 19.9 %collective-permute-start.37 = (bf16[96,1280]{1,0:T(8,128)(2,1)S(1)}, bf16[96,1280]{1,0:T(8,128)(2,1)S(1)}, u32[]{:S(2)}, u32[]{:S(2)}) collective-permute-start(bf16[96,1280]{1,0:T(8,128)(2,1)S(1)} %get-tuple-element.283), channel_id=1, source_target_pairs={{0,24},{1,25},{2,26},{3,27},{4,28},{5,29},{6,30},{7,31},{8,16},{9,... | collective-permute-start | bytes 737288 | tf_op jit(solution)/shard_map/ppermute | solution.py:63
  588.6 29.0 %collective-permute-start.48 = (bf16[4,384,384]{2,1,0:T(8,128)(2,1)S(1)}, bf16[4,384,384]{2,1,0:T(8,128)(2,1)S(1)}, u32[]{:S(2)}, u32[]{:S(2)}) collective-permute-start(bf16[4,384,384]{2,1,0:T(8,128)(2,1)S(1)} %dynamic-slice_bitcast_fusion.2), channel_id=1, source_target_pairs={{0,4},{1,5},{2,6},{3,7},{4,0},{5,1},{6,2},{7,3},{8,12},{9,13},{10,... | collective-permute-start | bytes 3538952 | tf_op jit(solution)/shard_map/ppermute | solution.py:63
  603.7 4.9 collective-permute-start.38
  608.7 2.0 collective-permute-start.39
  608.9 38.2 %collective-permute-start.41 = (bf16[4,96,1920]{2,1,0:T(8,128)(2,1)S(1)}, bf16[4,96,1920]{2,1,0:T(8,128)(2,1)S(1)}, u32[]{:S(2)}, u32[]{:S(2)}) collective-permute-start(bf16[4,96,1920]{2,1,0:T(8,128)(2,1)S(1)} %dynamic-slice_bitcast_fusion.1), channel_id=1, source_target_pairs={{0,4},{1,5},{2,6},{3,7},{4,0},{5,1},{6,2},{7,3},{8,12},{9,13},{10,... | collective-permute-start | bytes 4423688 | tf_op jit(solution)/shard_map/ppermute | solution.py:63
  618.0 9.9 %collective-permute-start.49 = (bf16[384,384]{1,0:T(8,128)(2,1)S(1)}, bf16[384,384]{1,0:T(8,128)(2,1)S(1)}, u32[]{:S(2)}, u32[]{:S(2)}) collective-permute-start(bf16[384,384]{1,0:T(8,128)(2,1)S(1)} %get-tuple-element.275), channel_id=1, source_target_pairs={{0,8},{1,9},{2,10},{3,11},{4,12},{5,13},{6,14},{7,15},{8,0},{9,1},... | collective-permute-start | bytes 884744 | tf_op jit(solution)/shard_map/ppermute | solution.py:63
  618.1 22.3 %collective-permute-start.50 = (bf16[384,384]{1,0:T(8,128)(2,1)S(1)}, bf16[384,384]{1,0:T(8,128)(2,1)S(1)}, u32[]{:S(2)}, u32[]{:S(2)}) collective-permute-start(bf16[384,384]{1,0:T(8,128)(2,1)S(1)} %get-tuple-element.277), channel_id=1, source_target_pairs={{0,16},{1,17},{2,18},{3,19},{4,20},{5,21},{6,22},{7,23},{8,24},{9,... | collective-permute-start | bytes 884744 | tf_op jit(solution)/shard_map/ppermute | solution.py:63
  620.3 20.1 %collective-permute-start.51 = (bf16[384,384]{1,0:T(8,128)(2,1)S(1)}, bf16[384,384]{1,0:T(8,128)(2,1)S(1)}, u32[]{:S(2)}, u32[]{:S(2)}) collective-permute-start(bf16[384,384]{1,0:T(8,128)(2,1)S(1)} %get-tuple-element.276), channel_id=1, source_target_pairs={{0,24},{1,25},{2,26},{3,27},{4,28},{5,29},{6,30},{7,31},{8,16},{9,... | collective-permute-start | bytes 884744 | tf_op jit(solution)/shard_map/ppermute | solution.py:63
  641.3 14.7 %collective-permute-start.52 = (bf16[2,96,384]{2,1,0:T(8,128)(2,1)}, bf16[2,96,384]{2,1,0:T(8,128)(2,1)}, u32[]{:S(2)}, u32[]{:S(2)}) collective-permute-start(bf16[2,96,384]{2,1,0:T(8,128)(2,1)} %dynamic-slice_bitcast_fusion.23), channel_id=1, source_target_pairs={{0,2},{1,3},{2,0},{3,1},{4,6},{5,7},{6,4},{7,5},{8,10},{9,11},{10,... | collective-permute-start | bytes 442376 | tf_op jit(solution)/shard_map/ppermute | solution.py:63
  647.4 40.3 %copy-start.1 = (bf16[8,128,768]{2,1,0:T(8,128)(2,1)S(1)}, bf16[8,128,768]{2,1,0:T(8,128)(2,1)}, u32[]{:S(2)}) copy-start(bf16[8,128,768]{2,1,0:T(8,128)(2,1)} %param.39) | copy-start | bytes 4718596
  648.5 16.2 %collective-permute-start.42 = (bf16[96,1920]{1,0:T(8,128)(2,1)}, bf16[96,1920]{1,0:T(8,128)(2,1)}, u32[]{:S(2)}, u32[]{:S(2)}) collective-permute-start(bf16[96,1920]{1,0:T(8,128)(2,1)} %get-tuple-element.268), channel_id=1, source_target_pairs={{0,8},{1,9},{2,10},{3,11},{4,12},{5,13},{6,14},{7,15},{8,0},{9,1},... | collective-permute-start | bytes 1105928 | tf_op jit(solution)/shard_map/ppermute | solution.py:63
  649.3 28.5 %collective-permute-start.43 = (bf16[96,1920]{1,0:T(8,128)(2,1)}, bf16[96,1920]{1,0:T(8,128)(2,1)}, u32[]{:S(2)}, u32[]{:S(2)}) collective-permute-start(bf16[96,1920]{1,0:T(8,128)(2,1)} %get-tuple-element.270), channel_id=1, source_target_pairs={{0,16},{1,17},{2,18},{3,19},{4,20},{5,21},{6,22},{7,23},{8,24},{9,... | collective-permute-start | bytes 1105928 | tf_op jit(solution)/shard_map/ppermute | solution.py:63
  650.6 27.2 %collective-permute-start.44 = (bf16[96,1920]{1,0:T(8,128)(2,1)}, bf16[96,1920]{1,0:T(8,128)(2,1)}, u32[]{:S(2)}, u32[]{:S(2)}) collective-permute-start(bf16[96,1920]{1,0:T(8,128)(2,1)} %get-tuple-element.269), channel_id=1, source_target_pairs={{0,24},{1,25},{2,26},{3,27},{4,28},{5,29},{6,30},{7,31},{8,16},{9,... | collective-permute-start | bytes 1105928 | tf_op jit(solution)/shard_map/ppermute | solution.py:63
  656.9 24.0 %collective-permute-start.53 = (bf16[96,384]{1,0:T(8,128)(2,1)S(1)}, bf16[96,384]{1,0:T(8,128)(2,1)S(1)}, u32[]{:S(2)}, u32[]{:S(2)}) collective-permute-start(bf16[96,384]{1,0:T(8,128)(2,1)S(1)} %dynamic-slice_bitcast_fusion.26), channel_id=1, source_target_pairs={{0,1},{1,0},{2,3},{3,2},{4,5},{5,4},{6,7},{7,6},{8,9},{9,8},{10,11... | collective-permute-start | bytes 221192 | tf_op jit(solution)/shard_map/ppermute | solution.py:63
  679.3 5.6 collective-permute-start.45
  685.0 1.4 collective-permute-start.46
  (60 other events, 410.2 us)

commit v2 on v1

--- a/solution.py
+++ b/solution.py
@@ -1,8 +1,11 @@
+import math
 from functools import partial
 
 import jax
 import jax.numpy as jnp
 from jax import lax
+from jax.experimental import pallas as pl
+from jax.experimental.pallas import tpu as pltpu
 from jax.sharding import PartitionSpec as P
 
 norm_eps = 1e-06
@@ -10,36 +13,416 @@
 f32 = jnp.float32
 bf16 = jnp.bfloat16
 both = ("batch", "blk")
-
-
-def matmul(left, right):
+log2e = math.log2(math.e)
+roomy = pltpu.CompilerParams(vmem_limit_bytes=48 << 20)
+vector_names = (
+    "bias_query",
+    "bias_value",
+    "bias_out",
+    "gain_first",
+    "shift_first",
+    "bias_down",
+    "gain_second",
+    "shift_second",
+)
+row_of = {name: index for index, name in enumerate(vector_names)}
+
+
+def dot(left, right):
     return jnp.dot(left, right, preferred_element_type=f32)
 
 
-def matmul_left_t(left, right):
-    return jnp.einsum("ti,tj->ij", left, right, preferred_element_type=f32)
-
-
-def matmul_right_t(left, right):
-    return jnp.einsum("tj,ij->ti", left, right, preferred_element_type=f32)
-
-
-def norm_forward(token_rows, gain, shift):
-    center = jnp.mean(token_rows, axis=-1, keepdims=True)
-    centered = token_rows - center
-    spread = jnp.mean(centered * centered, axis=-1, keepdims=True)
-    inverse = lax.rsqrt(spread + norm_eps)
-    normed = centered * inverse
-    return (normed * gain + shift, normed, inverse)
-
-
-def norm_backward(upstream, normed, inverse, gain):
-    grad_gain = jnp.sum(upstream * normed, axis=0)
-    grad_shift = jnp.sum(upstream, axis=0)
+def dot_right_t(left, right):
+    return lax.dot_general(left, right, (((1,), (1,)), ((), ())), preferred_element_type=f32)
+
+
+def dot_left_t(left, right):
+    return lax.dot_general(left, right, (((0,), (0,)), ((), ())), preferred_element_type=f32)
+
+
+def norm_stats(rows):
+    center = jnp.mean(rows, axis=-1, keepdims=True)
+    centered = rows - center
+    inverse = lax.rsqrt(jnp.mean(centered * centered, axis=-1, keepdims=True) + norm_eps)
+    return centered * inverse, inverse
+
+
+def norm_pull(upstream, normed, inverse, gain):
     scaled = upstream * gain
     inner = jnp.mean(scaled, axis=-1, keepdims=True)
     projected = jnp.mean(scaled * normed, axis=-1, keepdims=True)
-    return (inverse * (scaled - inner - normed * projected), grad_gain, grad_shift)
+    return inverse * (scaled - inner - normed * projected)
+
+
+def vector(ref, name):
+    index = row_of[name]
+    return ref[index : index + 1, :]
+
+
+def add_sums(sums_ref, rows):
+    total = jnp.concatenate(
+        [jnp.sum(row, axis=0, keepdims=True) for row in rows]
+        + [jnp.zeros((sums_ref.shape[0] - len(rows), sums_ref.shape[1]), f32)],
+        axis=0,
+    )
+
+    @pl.when(pl.program_id(0) == 0)
+    def _():
+        sums_ref[...] = total
+
+    @pl.when(pl.program_id(0) > 0)
+    def _():
+        sums_ref[...] += total
+
+
+def piece_rows(here, piece, rows):
+    return pl.ds(pl.multiple_of((here ^ piece) * rows, rows), rows)
+
+
+def stack_pieces(ref, places):
+    return jnp.concatenate([ref[place_, :] for place_ in places], axis=0)
+
+
+def attend_kernel(head_dim, here_ref, q_ref, k_ref, v_ref, *rest):
+    pieces, (o_ref, lse_ref) = rest[:-2], rest[-2:]
+    here = here_ref[0]
+    pair, seq = pl.program_id(0), pl.program_id(1)
+    length, wide = q_ref.shape
+    per = wide // head_dim
+    rows = pieces[0].shape[1]
+    lanes = lax.broadcasted_iota(jnp.int32, (1, wide), 1)
+    log_lanes = lax.broadcasted_iota(jnp.int32, (1, lse_ref.shape[1]), 1)
+    keys, values = k_ref[...], v_ref[...]
+    for first in range(0, len(pieces), 2):
+        span = range(first, min(first + 2, len(pieces)))
+        places = [piece_rows(here, piece, rows) for piece in span]
+        queries = stack_pieces(q_ref, places)
+        out, logs = None, []
+        for head in range(per):
+            mine = lanes // head_dim == head
+            scores = dot_right_t(jnp.where(mine, queries, 0), keys) * (head_dim**-0.5 * log2e)
+            addend = jnp.concatenate([pieces[piece][head] for piece in span], axis=0)
+            scores = scores + addend.astype(f32)
+            top = jnp.max(scores, axis=1, keepdims=True)
+            weights = jnp.exp2(scores - top)
+            total = jnp.sum(weights, axis=1, keepdims=True)
+            part = dot(weights.astype(bf16), values) * (1.0 / total)
+            out = part if out is None else jnp.where(mine, part, out)
+            logs.append(top + jnp.log2(total))
+        for index, place_ in enumerate(places):
+            here_rows = slice(index * rows, (index + 1) * rows)
+            o_ref[place_, :] = out[here_rows].astype(bf16)
+            start = seq * length + (here ^ span[index]) * rows
+            log_place = pl.ds(pl.multiple_of(start, rows), rows)
+            kept = lse_ref[log_place, :]
+            for head in range(per):
+                kept = jnp.where(log_lanes == pair * per + head, logs[head][here_rows], kept)
+            lse_ref[log_place, :] = kept
+
+
+def attend_back_kernel(head_dim, here_ref, q_ref, k_ref, v_ref, o_ref, g_ref, lse_ref, *rest):
+    pieces, (dq_ref, dk_ref, dv_ref) = rest[:-3], rest[-3:]
+    here = here_ref[0]
+    pair, seq = pl.program_id(0), pl.program_id(1)
+    length, wide = q_ref.shape
+    per = wide // head_dim
+    rows = pieces[0].shape[1]
+    lanes = lax.broadcasted_iota(jnp.int32, (1, wide), 1)
+    log_lanes = lax.broadcasted_iota(jnp.int32, (1, lse_ref.shape[1]), 1)
+    keys, values = k_ref[...], v_ref[...]
+    back = head_dim**-0.5
+    dk = jnp.zeros(keys.shape, f32)
+    dv = jnp.zeros(keys.shape, f32)
+    for first in range(0, len(pieces), 2):
+        span = range(first, min(first + 2, len(pieces)))
+        places = [piece_rows(here, piece, rows) for piece in span]
+        queries, ups = stack_pieces(q_ref, places), stack_pieces(g_ref, places)
+        products = ups.astype(f32) * stack_pieces(o_ref, places).astype(f32)
+        starts = [seq * length + (here ^ piece) * rows for piece in span]
+        logs = stack_pieces(lse_ref, [pl.ds(pl.multiple_of(at, rows), rows) for at in starts])
+        dq = None
+        for head in range(per):
+            mine = lanes // head_dim == head
+            q_mine, g_mine = jnp.where(mine, queries, 0), jnp.where(mine, ups, 0)
+            inner = jnp.sum(jnp.where(mine, products, 0.0), axis=1, keepdims=True)
+            log = jnp.sum(
+                jnp.where(log_lanes == pair * per + head, logs, 0.0), axis=1, keepdims=True
+            )
+            scores = dot_right_t(q_mine, keys) * (back * log2e)
+            addend = jnp.concatenate([pieces[piece][head] for piece in span], axis=0)
+            exact = jnp.exp2(scores + addend.astype(f32) - log)
+            grads = (exact * (dot_right_t(g_mine, values) - inner)).astype(bf16)
+            dv = dv + dot_left_t(exact.astype(bf16), g_mine)
+            dk = dk + dot_left_t(grads, q_mine)
+            part = dot(grads, keys)
+            dq = part if dq is None else jnp.where(mine, part, dq)
+        for index, place_ in enumerate(places):
+            dq_ref[place_, :] = (dq[index * rows : (index + 1) * rows] * back).astype(bf16)
+    dk_ref[...] = (dk * back).astype(bf16)
+    dv_ref[...] = dv.astype(bf16)
+
+
+def attention_call(kernel, here, per_head, logs, mask_parts, outs, seqs, head_count, cost):
+    tokens = per_head[0][0].shape[0]
+    rows, length = mask_parts[0].shape[1:]
+    width = per_head[-1][0].shape[1] if len(per_head) > 3 else per_head[0][0].shape[1] // 3
+    head_dim = width // head_count
+    wide = 2 * head_dim
+
+    def block(first):
+        return pl.BlockSpec((length, wide), lambda p, s, h: (s, first + p))
+
+    log_block = pl.BlockSpec((tokens, 128), lambda p, s, h: (0, 0))
+    mask_block = pl.BlockSpec((2, rows, length), lambda p, s, h: (p, 0, 0))
+    log_shape = jax.ShapeDtypeStruct((tokens, 128), f32)
+    shapes = [jax.ShapeDtypeStruct((tokens, width), bf16)] * outs
+    out_specs = [block(0)] * outs
+    if logs is None:
+        shapes.append(log_shape)
+        out_specs.append(log_block)
+    return pl.pallas_call(
+        partial(kernel, head_dim),
+        out_shape=shapes,
+        grid_spec=pltpu.PrefetchScalarGridSpec(
+            num_scalar_prefetch=1,
+            grid=(width // wide, seqs),
+            in_specs=[block(first) for unused, first in per_head]
+            + ([] if logs is None else [log_block])
+            + [mask_block] * len(mask_parts),
+            out_specs=out_specs,
+        ),
+        compiler_params=roomy,
+        cost_estimate=cost,
+    )(here, *[array for array, unused in per_head], *([] if logs is None else [logs]), *mask_parts)
+
+
+def attend(here, joined, mask_parts, seqs, head_count):
+    tokens, width = joined.shape[0], joined.shape[1] // 3
+    blocks = head_count // 2
+    cells = tokens * mask_parts[0].shape[2] * head_count
+    return attention_call(
+        attend_kernel,
+        here,
+        [(joined, 0), (joined, blocks), (joined, 2 * blocks)],
+        None,
+        mask_parts,
+        1,
+        seqs,
+        head_count,
+        pl.CostEstimate(flops=cells * 3000, bytes_accessed=tokens * width * 16, transcendentals=cells),
+    )
+
+
+def attend_back(here, joined, attended, upstream, logs, mask_parts, seqs, head_count):
+    tokens, width = attended.shape
+    blocks = head_count // 2
+    cells = tokens * mask_parts[0].shape[2] * head_count
+    return attention_call(
+        attend_back_kernel,
+        here,
+        [(joined, 0), (joined, blocks), (joined, 2 * blocks), (attended, 0), (upstream, 0)],
+        logs,
+        mask_parts,
+        3,
+        seqs,
+        head_count,
+        pl.CostEstimate(flops=cells * 4500, bytes_accessed=tokens * width * 24, transcendentals=cells),
+    )
+
+
+def out_kernel(att_ref, w_ref, x_ref, vec_ref, first_ref, low_ref):
+    first = x_ref[...].astype(f32) + (dot(att_ref[...], w_ref[...]) + vector(vec_ref, "bias_out"))
+    first_ref[...] = first
+    gain, shift = vector(vec_ref, "gain_first"), vector(vec_ref, "shift_first")
+    low_ref[...] = (norm_stats(first)[0] * gain + shift).astype(bf16)
+
+
+def whole_block(array):
+    return pl.BlockSpec(array.shape, lambda *unused: (0,) * array.ndim)
+
+
+def out_projection(attended, w_out, token_rows, vectors, block):
+    tokens, width = attended.shape
+    row = pl.BlockSpec((block, width), lambda i: (i, 0))
+    return pl.pallas_call(
+        out_kernel,
+        out_shape=(
+            jax.ShapeDtypeStruct((tokens, width), f32),
+            jax.ShapeDtypeStruct((tokens, width), bf16),
+        ),
+        grid=(tokens // block,),
+        in_specs=[row, whole_block(w_out), row, whole_block(vectors)],
+        out_specs=(row, row),
+        compiler_params=roomy,
+        cost_estimate=pl.CostEstimate(
+            flops=4 * tokens * width * width, bytes_accessed=tokens * width * 10, transcendentals=0
+        ),
+    )(attended, w_out, token_rows, vectors)
+
+
+def up_kernel(chunk, h_ref, w_ref, b_ref, act_ref, der_ref):
+    weights, bias = w_ref[...], b_ref[...]
+    for first in range(0, h_ref.shape[0], chunk):
+        place_ = slice(first, first + chunk)
+        gate = dot(h_ref[place_, :], weights) + bias
+        share = 0.5 + 0.5 * lax.erf(gate * math.sqrt(0.5))
+        bell = jnp.exp2((-0.5 * log2e) * (gate * gate)) * (1.0 / math.sqrt(2.0 * math.pi))
+        act_ref[place_, :] = (gate * share).astype(bf16)
+        der_ref[place_, :] = (share + gate * bell).astype(bf16)
+
+
+def up_projection(hidden_low, w_up, bias, block):
+    tokens, width = hidden_low.shape
+    cols = w_up.shape[1]
+    out = pl.BlockSpec((tokens, block), lambda j: (0, j))
+    shape = jax.ShapeDtypeStruct((tokens, cols), bf16)
+    return pl.pallas_call(
+        partial(up_kernel, 128),
+        out_shape=(shape, shape),
+        grid=(cols // block,),
+        in_specs=[
+            whole_block(hidden_low),
+            pl.BlockSpec((width, block), lambda j: (0, j)),
+            pl.BlockSpec((1, block), lambda j: (0, j)),
+        ],
+        out_specs=(out, out),
+        compiler_params=roomy,
+        cost_estimate=pl.CostEstimate(
+            flops=5 * tokens * width * cols,
+            bytes_accessed=tokens * cols * 4,
+            transcendentals=2 * tokens * cols,
+        ),
+    )(hidden_low, w_up, bias)
+
+
+def down_kernel(
+    steps_per_seq,
+    here_ref,
+    pos_ref,
+    cot_ref,
+    act_ref,
+    der_ref,
+    first_ref,
+    w_ref,
+    vec_ref,
+    out_ref,
+    gss_ref,
+    gdi_ref,
+    gate_ref,
+    sums_ref,
+    up_sum_ref,
+):
+    step = pl.program_id(0)
+    block = act_ref.shape[0]
+    normed_one = norm_stats(first_ref[...])[0]
+    hidden = normed_one * vector(vec_ref, "gain_first") + vector(vec_ref, "shift_first")
+    second = hidden + (dot(act_ref[...], w_ref[...]) + vector(vec_ref, "bias_down"))
+    normed, inverse = norm_stats(second)
+    gain = vector(vec_ref, "gain_second")
+    out_ref[...] = (normed * gain + vector(vec_ref, "shift_second")).astype(bf16)
+    slots = pos_ref.shape[-1]
+    token = lax.broadcasted_iota(jnp.int32, (block, slots), 0) + (step % steps_per_seq) * block
+    picks = jnp.where(token == pos_ref[0], 1.0, 0.0).astype(bf16)
+    upstream = dot(picks, cot_ref[0])
+    grad = norm_pull(upstream, normed, inverse, gain)
+    gss_ref[...] = grad
+    low = grad.astype(bf16)
+    gdi_ref[...] = low
+    add_sums(sums_ref, [low.astype(f32), upstream * normed, upstream])
+    grad_gate = (dot_right_t(low, w_ref[...]) * der_ref[...].astype(f32)).astype(bf16)
+    gate_ref[...] = grad_gate
+    add_sums(up_sum_ref, [grad_gate.astype(f32)])
+
+
+def down_projection(here, active, slope, first_sum, w_down, vectors, marks, cot_values, seqs, block):
+    tokens, cols = active.shape
+    width = w_down.shape[1]
+    steps = tokens // seqs // block
+    slots = marks.shape[-1]
+    row = pl.BlockSpec((block, width), lambda i, h: (i, 0))
+    wide = pl.BlockSpec((block, cols), lambda i, h: (i, 0))
+    sums = jax.ShapeDtypeStruct((8, width), f32)
+    up_sums = jax.ShapeDtypeStruct((8, cols), f32)
+    return pl.pallas_call(
+        partial(down_kernel, steps),
+        out_shape=(
+            jax.ShapeDtypeStruct((tokens, width), bf16),
+            jax.ShapeDtypeStruct((tokens, width), f32),
+            jax.ShapeDtypeStruct((tokens, width), bf16),
+            jax.ShapeDtypeStruct((tokens, cols), bf16),
+            sums,
+            up_sums,
+        ),
+        grid_spec=pltpu.PrefetchScalarGridSpec(
+            num_scalar_prefetch=1,
+            grid=(tokens // block,),
+            in_specs=[
+                pl.BlockSpec((1, 1, slots), lambda i, h: (i // steps, 0, 0)),
+                pl.BlockSpec((1, slots, width), lambda i, h: (h[0] * seqs + i // steps, 0, 0)),
+                wide,
+                wide,
+                row,
+                whole_block(w_down),
+                whole_block(vectors),
+            ],
+            out_specs=(row, row, row, wide, whole_block(sums), whole_block(up_sums)),
+        ),
+        compiler_params=roomy,
+        cost_estimate=pl.CostEstimate(
+            flops=6 * tokens * width * cols, bytes_accessed=tokens * cols * 8, transcendentals=0
+        ),
+    )(here, marks, cot_values, active, slope, first_sum, w_down, vectors)
+
+
+def first_back_kernel(
+    gate_ref, gss_ref, first_ref, w_up_ref, w_out_ref, vec_ref, gfs_ref, branch_ref, att_ref, sums_ref
+):
+    grad_hidden = gss_ref[...] + dot_right_t(gate_ref[...], w_up_ref[...])
+    normed, inverse = norm_stats(first_ref[...])
+    grad = norm_pull(grad_hidden, normed, inverse, vector(vec_ref, "gain_first"))
+    gfs_ref[...] = grad
+    low = grad.astype(bf16)
+    branch_ref[...] = low
+    att_ref[...] = dot_right_t(low, w_out_ref[...]).astype(bf16)
+    add_sums(sums_ref, [low.astype(f32), grad_hidden * normed, grad_hidden])
+
+
+def first_back(grad_gate, grad_second_sum, first_sum, w_up, w_out, vectors, block):
+    tokens, cols = grad_gate.shape
+    width = w_out.shape[0]
+    row = pl.BlockSpec((block, width), lambda i: (i, 0))
+    sums = jax.ShapeDtypeStruct((8, width), f32)
+    low = jax.ShapeDtypeStruct((tokens, width), bf16)
+    return pl.pallas_call(
+        first_back_kernel,
+        out_shape=(jax.ShapeDtypeStruct((tokens, width), f32), low, low, sums),
+        grid=(tokens // block,),
+        in_specs=[
+            pl.BlockSpec((block, cols), lambda i: (i, 0)),
+            row,
+            row,
+            whole_block(w_up),
+            whole_block(w_out),
+            whole_block(vectors),
+        ],
+        out_specs=(row, row, row, whole_block(sums)),
+        compiler_params=roomy,
+        cost_estimate=pl.CostEstimate(
+            flops=4 * tokens * width * cols, bytes_accessed=tokens * cols * 4, transcendentals=0
+        ),
+    )(grad_gate, grad_second_sum, first_sum, w_up, w_out, vectors)
+
+
+def matmul(left, right):
+    return jnp.dot(left, right, preferred_element_type=f32)
+
+
+def matmul_left_t(left, right):
+    return jnp.einsum("ti,tj->ij", left, right, preferred_element_type=f32)
+
+
+def matmul_right_t(left, right):
+    return jnp.einsum("tj,ij->ti", left, right, preferred_element_type=f32)
 
 
 class Grid:
@@ -142,69 +525,6 @@
     ).astype(f32)
 
 
-def split_heads(tensor, head_count):
-    return tensor.reshape(tensor.shape[0], head_count, tensor.shape[1] // head_count)
-
-
-def scores_of(queries, keys_all, addend, head_count):
-    head_dim = queries.shape[1] // head_count
-    scores = jnp.einsum(
-        "qhd,khd->hqk",
-        split_heads(queries, head_count),
-        split_heads(keys_all, head_count),
-        preferred_element_type=f32,
-    ) * head_dim ** (-0.5)
-    return scores + addend.astype(f32)
-
-
-def attend_forward(triple, addend, head_count):
-    queries, keys_all, values_all = triple
-    scores = scores_of(queries, keys_all, addend, head_count)
-    row_top = jnp.max(scores, axis=-1, keepdims=True)
-    weights = jnp.exp(scores - row_top)
-    totals = jnp.sum(weights, axis=-1, keepdims=True)
-    probabilities = (weights / totals).astype(bf16)
-    attended = jnp.einsum(
-        "hqk,khd->qhd",
-        probabilities,
-        split_heads(values_all, head_count),
-        preferred_element_type=f32,
-    )
-    return (attended.reshape(queries.shape[0], queries.shape[1]), row_top + jnp.log(totals))
-
-
-def attend_backward(pieces, addend, head_count):
-    queries, keys_all, values_all, log_totals, upstream = pieces
-    head_dim = queries.shape[1] // head_count
-    score_scale = head_dim ** (-0.5)
-    scores = scores_of(queries, keys_all, addend, head_count)
-    exact = jnp.exp(scores - log_totals)
-    up_heads = split_heads(upstream, head_count)
-    grad_probs = jnp.einsum(
-        "qhd,khd->hqk", up_heads, split_heads(values_all, head_count), preferred_element_type=f32
-    )
-    inner = jnp.sum(grad_probs * exact, axis=-1, keepdims=True)
-    grad_scores = (exact * (grad_probs - inner)).astype(bf16)
-    grad_values = jnp.einsum("hqk,qhd->khd", exact.astype(bf16), up_heads, preferred_element_type=f32)
-    grad_queries = (
-        jnp.einsum(
-            "hqk,khd->qhd", grad_scores, split_heads(keys_all, head_count), preferred_element_type=f32
-        )
-        * score_scale
-    )
-    grad_keys = (
-        jnp.einsum(
-            "hqk,qhd->khd", grad_scores, split_heads(queries, head_count), preferred_element_type=f32
-        )
-        * score_scale
-    )
-    width = queries.shape[1]
-    return jnp.concatenate(
-        [g.reshape(g.shape[0], width).astype(bf16) for g in (grad_queries, grad_keys, grad_values)],
-        axis=1,
-    )
-
-
 def local(
     grid,
     inputs,
@@ -267,39 +587,30 @@
     qkv_full = first_group[:, : 3 * width]
     gathered = first_group[:, 3 * width :]
     vector_rows = gathered[:, : len(vectors)].T.astype(f32)
-    (
-        query_bias,
-        value_bias,
-        out_bias,
-        gain_one,
-        shift_one,
-        down_bias,
-        gain_two,
-        shift_two,
-    ) = [vector_rows[i] for i in range(len(vectors))]
-    up_bias = gathered[:, len(vectors) : len(vectors) + up_per].reshape(-1).astype(f32)
+    up_bias = gathered[:, len(vectors) : len(vectors) + up_per].reshape(1, -1).astype(f32)
     out_full = second_group[:, :width]
     up_full = second_group[:, width:]
 
     token_rows = place(parts, here).transpose(1, 0, 2, 3).reshape(token_count, width)
-    addend_all = place(mask_parts, here).transpose(1, 0, 2, 3).reshape(head_count, length, length)
-
-    joined = matmul(token_rows, qkv_full)
-    queries = (joined[:, :width] + query_bias).astype(bf16).reshape(seqs, length, width)
-    keys = joined[:, width : 2 * width].astype(bf16).reshape(seqs, length, width)
-    values = (joined[:, 2 * width :] + value_bias).astype(bf16).reshape(seqs, length, width)
-    attended, log_totals = lax.map(
-        partial(attend_forward, addend=addend_all, head_count=head_count), (queries, keys, values)
-    )
-    attended = attended.reshape(token_count, width).astype(bf16)
-    branch = matmul(attended, out_full) + out_bias
-    first_sum = token_rows.astype(f32) + branch
-    hidden, normed_first, inverse_first = norm_forward(first_sum, gain_one, shift_one)
-    hidden_low = hidden.astype(bf16)
-    gate_in = matmul(hidden_low, up_full) + up_bias
-    active = jax.nn.gelu(gate_in, approximate=False).astype(bf16)
-    second = matmul(active, down_full) + down_bias
-    result, normed_second, inverse_second = norm_forward(hidden + second, gain_two, shift_two)
+    joined_bias = jnp.concatenate(
+        [vector_rows[0], jnp.zeros((width,), f32), vector_rows[1]], axis=0
+    )
+    joined = (matmul(token_rows, qkv_full) + joined_bias).astype(bf16)
+    here_1 = here.reshape(1).astype(jnp.int32)
+    attended, logs = attend(here_1, joined, mask_parts, seqs, head_count)
+    block = min(256, length)
+    first_sum, hidden_low = out_projection(attended, out_full, token_rows, vector_rows, block)
+    active, slope = up_projection(hidden_low, up_full, up_bias, min(512, up_full.shape[1]))
+
+    my_positions = pick(positions.reshape(blk, seqs, -1), here)
+    my_counts = pick(counts.reshape(blk, seqs), here)
+    live = jnp.arange(positions.shape[1], dtype=jnp.int32)[None, :] < my_counts[:, None]
+    marks = jnp.where(live, my_positions, -1)[:, None, :]
+    result, grad_second_sum, grad_down_in, grad_gate, second_sums, up_sums = down_projection(
+        here_1, active, slope, first_sum, down_full, vector_rows, marks, cot_values, seqs, block
+    )
+    grad_bias_down, grad_gain_second, grad_shift_second = second_sums[:3]
+    grad_bias_up = up_sums[0]
 
     def home(array):
         by_place = array.astype(bf16).reshape(seqs, blk, block_rows, width)
@@ -311,40 +622,20 @@
 
     activations = home(result)
 
-    my_positions = pick(positions.reshape(blk, seqs, -1), here)
-    my_counts = pick(counts.reshape(blk, seqs), here)
-    my_values = pick(cot_values.reshape((blk, seqs) + cot_values.shape[1:]), here)
-    live = jnp.arange(positions.shape[1], dtype=jnp.int32)[None, :] < my_counts[:, None]
-    picks = (
-        my_positions[:, :, None] == jnp.arange(length, dtype=jnp.int32)[None, None, :]
-    ) & live[:, :, None]
-    upstream = jnp.einsum(
-        "gpr,gpd->grd", picks.astype(bf16), my_values, preferred_element_type=f32
-    ).reshape(token_count, width)
-    grad_second_sum, grad_gain_second, grad_shift_second = norm_backward(
-        upstream, normed_second, inverse_second, gain_two
-    )
-    grad_down_in = grad_second_sum.astype(bf16)
-    grad_bias_down = jnp.sum(grad_down_in.astype(f32), axis=0)
     share_w_down = scatter_rows(grid, matmul_left_t(active, grad_down_in).astype(bf16))
-    grad_active = matmul_right_t(grad_down_in, down_full)
-    unused, gelu_pull = jax.vjp(partial(jax.nn.gelu, approximate=False), gate_in)
-    grad_gate = gelu_pull(grad_active)[0].astype(bf16)
-    grad_bias_up = jnp.sum(grad_gate.astype(f32), axis=0)
     grad_w_up = matmul_left_t(hidden_low, grad_gate).astype(bf16)
-    grad_hidden = grad_second_sum + matmul_right_t(grad_gate, up_full)
-    grad_first_sum, grad_gain_first, grad_shift_first = norm_backward(
-        grad_hidden, normed_first, inverse_first, gain_one
-    )
-    grad_branch = grad_first_sum.astype(bf16)
-    grad_bias_out = jnp.sum(grad_branch.astype(f32), axis=0)
+    grad_first_sum, grad_branch, grad_attended, first_sums = first_back(
+        grad_gate, grad_second_sum, first_sum, up_full, out_full, vector_rows, block
+    )
+    grad_bias_out, grad_gain_first, grad_shift_first = first_sums[:3]
     grad_w_out = matmul_left_t(attended, grad_branch).astype(bf16)
     share_second = scatter_rows(grid, jnp.concatenate([grad_w_out, grad_w_up], axis=1))
-    grad_attended = matmul_right_t(grad_branch, out_full).astype(bf16).reshape(seqs, length, width)
-    grad_joined = lax.map(
-        partial(attend_backward, addend=addend_all, head_count=head_count),
-        (queries, keys, values, log_totals, grad_attended),
-    ).reshape(token_count, 3 * width)
+    grad_joined = jnp.concatenate(
+        attend_back(
+            here_1, joined, attended, grad_attended, logs, mask_parts, seqs, head_count
+        ),
+        axis=1,
+    )
     grad_bias_query = jnp.sum(grad_joined[:, :width].astype(f32), axis=0)
     grad_bias_value = jnp.sum(grad_joined[:, 2 * width :].astype(f32), axis=0)
     grad_w_qkv = matmul_left_t(token_rows, grad_joined).astype(bf16)

time: 700 us -> 502 us (0.72)
  matrix products: 193 us -> 31.4 us
  Pallas kernels: 0 us -> 100 us
  local copies, waits for them, and re-layouts: 81.6 us -> 31.7 us
  waiting for transfers between devices: 226 us -> 180 us
  other arithmetic: 90.2 us -> 63 us
  starting transfers between devices: 93.7 us -> 84.6 us
    pallas_call x0 -> x6, Pallas kernels: none -> 100 us  [the longest x2 47.7 us: attention_call(): pl.pallas_call(partial(kernel, head_dim), out_shape=shapes, grid_spec=plt...]
    dot_general x15 -> x0, matrix products: 64.6 us -> none  [the longest x4 25.8 us: scores_of(): jnp.einsum('qhd,khd->hqk', split_heads(queries, head_count), split_heads(...]
    dot_general x4 -> x1, matrix products: 61.9 us -> 7.66 us  [matmul(): return jnp.dot(left, right, preferred_element_type=f32)]
    ppermute x45, waiting for transfers between devices: 210 us -> 167 us  [swap(): return lax.ppermute(array, both, pairs)]
    dot_general x4 -> x1, matrix products: 40.3 us -> 5.48 us  [matmul_right_t(): return jnp.einsum('tj,ij->ti', left, right, preferred_element_type=f32)]
    dynamic_update_slice x8 -> x0, local copies, waits for them, and re-layouts: 17.4 us -> none  [the longest x4 15 us: local(): lax.map(partial(attend_backward, addend=addend_all, head_count=head_count...]
    convert_element_type x4 -> x2, other arithmetic: 16.8 us -> 0.52 us  [the longest x1 0.52 us: home(): by_place = array.astype(bf16).reshape(seqs, blk, block_rows, width)]
    dynamic_slice x12 -> x1, local copies, waits for them, and re-layouts: 15.3 us -> 0.01 us  [pick(): return lax.dynamic_index_in_dim(array, index, axis=0, keepdims=False)]
  transfers between devices with their start and end apart: 54 -> 54, of which waited for: 24 -> 22; matrix products, arithmetic and copies ran while one was open for 20% -> 18% of each run, Pallas kernels for 0% -> 4%
where the time goes in v2:
time: 502 us; the launch traced here: 492 us
  waiting for transfers between devices  180 us (36%)
  Pallas kernels  100 us (20%)
  starting transfers between devices  84.6 us (17%)
  other arithmetic  63 us (13%)
  local copies, waits for them, and re-layouts  31.7 us (6%)
  matrix products  31.4 us (6%)
    ppermute x45, waiting for transfers between devices, swap(): return lax.ppermute(array, both, pairs)  167 us
    ppermute x45, starting transfers between devices, swap(): return lax.ppermute(array, both, pairs)  75.7 us
    pallas_call x2, Pallas kernels, attention_call(): pl.pallas_call(partial(kernel, head_dim), out_shape=shapes, grid_spec=plt...  47.7 us
    pallas_call x1, Pallas kernels, down_projection(): pl.pallas_call(partial(down_kernel, steps), out_shape=(jax.ShapeDtypeStru...  21.9 us
    another operation x29, other arithmetic, place(): return jnp.stack(rows)  19.1 us
    dot_general x4, matrix products, matmul_left_t(): return jnp.einsum('ti,tj->ij', left, right, preferred_element_type=f32)  18.2 us
    pallas_call x1, Pallas kernels, first_back(): pl.pallas_call(first_back_kernel, out_shape=(jax.ShapeDtypeStruct((tokens...  15.1 us
    ppermute x9, waiting for transfers between devices, swap_blk(): return lax.ppermute(array, both, pairs)  12.8 us
  transfers between devices with their start and end apart: 54, of which 22 were waited for; matrix products, arithmetic and copies ran while one was open for 18% of the time, Pallas kernels for 4%

profile of v2, /device:TPU:0, one launch (start us, length us, event | category | flops | bytes accessed | tf_op | source)
XLA Modules:
  0.0 492.4 jit_solution(4925578960734076618)
XLA Ops:
  15.9 2.3 dynamic-slice_bitcast_fusion.9
  18.2 2.6 collective-permute-start
  20.9 1.6 select_convert_fusion.rest_0_
  24.6 2.1 collective-permute-start.21
  27.8 5.8 %collective-permute-done.4 = bf16[2,24,1280]{2,1,0:T(8,128)(2,1)S(1)} collective-permute-done((bf16[2,24,1280]{2,1,0:T(8,128)(2,1)S(1)}, bf16[2,24,1280]{2,1,0:T(8,128)(2,1)S(1)}, u32[]{:S(2)}, u32[]{:S(2)}) %collective-permute-start.4) | collective-permute-done | bytes 122912 | tf_op jit(solution)/shard_map/ppermute | solution.py:446
  33.6 4.3 collective-permute-start.5
  40.5 3.7 collective-permute-start.22
  44.8 13.5 %collective-permute-start.23 = (bf16[4,96,384]{2,1,0:T(8,128)(2,1)S(1)}, bf16[4,96,384]{2,1,0:T(8,128)(2,1)S(1)}, u32[]{:S(2)}, u32[]{:S(2)}) collective-permute-start(bf16[4,96,384]{2,1,0:T(8,128)(2,1)S(1)} %bitcast.418), channel_id=1, source_target_pairs={{0,16},{1,17},{2,18},{3,19},{4,20},{5,21},{6,22},{7,23},{8,24},{9,... | collective-permute-start | bytes 884744 | tf_op jit(solution)/shard_map/ppermute | solution.py:446
  58.3 13.3 %collective-permute-done.6 = bf16[4,24,1280]{2,1,0:T(8,128)(2,1)S(1)} collective-permute-done((bf16[4,24,1280]{2,1,0:T(8,128)(2,1)S(1)}, bf16[4,24,1280]{2,1,0:T(8,128)(2,1)S(1)}, u32[]{:S(2)}, u32[]{:S(2)}) %collective-permute-start.6) | collective-permute-done | bytes 245792 | tf_op jit(solution)/shard_map/ppermute | solution.py:446
  72.2 2.8 collective-permute-start.15
  75.3 16.9 %collective-permute-start.16 = (bf16[4,24,1920]{2,1,0:T(8,128)(2,1)S(1)}, bf16[4,24,1920]{2,1,0:T(8,128)(2,1)S(1)}, u32[]{:S(2)}, u32[]{:S(2)}) collective-permute-start(bf16[4,24,1920]{2,1,0:T(8,128)(2,1)S(1)} %bitcast.413), channel_id=1, source_target_pairs={{0,16},{1,17},{2,18},{3,19},{4,20},{5,21},{6,22},{7,23},{8,24},{9,... | collective-permute-start | bytes 1105928 | tf_op jit(solution)/shard_map/ppermute | solution.py:446
  92.2 7.9 %collective-permute-done.23 = bf16[4,96,384]{2,1,0:T(8,128)(2,1)S(1)} collective-permute-done((bf16[4,96,384]{2,1,0:T(8,128)(2,1)S(1)}, bf16[4,96,384]{2,1,0:T(8,128)(2,1)S(1)}, u32[]{:S(2)}, u32[]{:S(2)}) %collective-permute-start.23) | collective-permute-done | bytes 294944 | tf_op jit(solution)/shard_map/ppermute | solution.py:446
  104.4 10.3 %collective-permute-done.16 = bf16[4,24,1920]{2,1,0:T(8,128)(2,1)S(1)} collective-permute-done((bf16[4,24,1920]{2,1,0:T(8,128)(2,1)S(1)}, bf16[4,24,1920]{2,1,0:T(8,128)(2,1)S(1)}, u32[]{:S(2)}, u32[]{:S(2)}) %collective-permute-start.16) | collective-permute-done | bytes 368672 | tf_op jit(solution)/shard_map/ppermute | solution.py:446
  120.7 2.7 copy.74
  125.8 24.4 %collective-permute-done.11.rest_2_ = bf16[12,128,512]{2,1,0:T(8,128)(2,1)} collective-permute-done((bf16[12,128,512]{2,1,0:T(8,128)(2,1)}, bf16[12,128,512]{2,1,0:T(8,128)(2,1)}, u32[]{:S(2)}, u32[]{:S(2)}) %collective-permute-start.11) | collective-permute-done | bytes 1572896 | tf_op jit(solution)/shard_map/ppermute | solution.py:446
  150.2 1.6 select_bitcast_fusion.3
  151.8 1.6 pad_maximum_fusion.5
  154.0 20.8 %collective-permute-done.18 = bf16[4,4,24,1920]{3,2,1,0:T(8,128)(2,1)} collective-permute-done((bf16[4,4,24,1920]{3,2,1,0:T(8,128)(2,1)}, bf16[4,4,24,1920]{3,2,1,0:T(8,128)(2,1)}, u32[]{:S(2)}, u32[]{:S(2)}) %collective-permute-start.18) | collective-permute-done | bytes 1474592 | tf_op jit(solution)/shard_map/ppermute | solution.py:446
  174.8 1.8 select_bitcast_fusion.1
  176.6 1.9 pad_maximum_fusion.4
  182.8 7.7 %add_convert_fusion.q_ref.k_ref.v_ref = bf16[1024,2304]{1,0:T(8,128)(2,1)} fusion(bf16[1024,768]{1,0:T(8,128)(2,1)S(1)} %bitcast.393, f32[2304]{0:T(1024)S(1)} %pad_maximum_fusion.23, bf16[768,1280]{0,1:T(8,128)(2,1)} %copy-done.32, bf16[768,1280]{0,1:T(8,128)(2,1)} %get-tuple-element.67), kind=kOutput, calls=%fused_computation | convolution fusion | flops 3635675136 | bytes 10232832 | tf_op jit(solution)/shard_map/dot_general | solution.py:417
  190.5 19.3 %shard_map.289 = (bf16[1024,768]{1,0:T(8,128)(2,1)S(1)}, f32[1024,128]{1,0:T(8,128)S(1)}) custom-call(s32[1]{0:T(128)} %bitcast.here_ref, bf16[1024,2304]{1,0:T(8,128)(2,1)} %add_convert_fusion.q_ref.k_ref.v_ref, bf16[1024,2304]{1,0:T(8,128)(2,1)} %add_convert_fusion.q_ref.k_ref.v_ref, bf16[1024,2304]{1,0:T(8,128)(2,1)} %add_convert_fusion.q_ref.k_ref.v_ref, ...), custom_call_target="tpu_custom_call" | custom-call | flops 18874368000 | bytes 12582912 | tf_op jit(solution)/shard_map/pallas_call | solution.py:183
  209.8 3.4 broadcast_select_fusion.5
  213.2 2.5 pad_maximum_fusion.1.w_ref
  215.7 3.3 broadcast_select_fusion.1
  219.1 2.9 pad_maximum_fusion.w_ref.w_up_ref
  221.9 3.7 shard_map.290
  225.6 11.7 %shard_map.291 = (bf16[1024,3072]{1,0:T(8,128)(2,1)}, bf16[1024,3072]{1,0:T(8,128)(2,1)}) custom-call(bf16[1024,768]{1,0:T(8,128)(2,1)S(1)} %get-tuple-element.35.h_ref, bf16[768,3072]{1,0:T(8,128)(2,1)} %pad_maximum_fusion.w_ref.w_up_ref, f32[1,3072]{1,0:T(1,128)S(1)} %reshape.204.b_ref), custom_call_target="tpu_custom_call" | custom-call | flops 12079595520 | bytes 12582912 | tf_op jit(solution)/shard_map/pallas_call | solution.py:279
  237.3 21.9 %shard_map.292 = (bf16[1024,768]{1,0:T(8,128)(2,1)S(1)}, f32[1024,768]{1,0:T(8,128)}, bf16[1024,768]{1,0:T(8,128)(2,1)S(1)}, bf16[1024,3072]{1,0:T(8,128)(2,1)},...) custom-call(s32[1]{0:T(128)} %bitcast.here_ref, s32[2,1,128]{2,1,0:T(1,128)S(1)} %compare_select_fusion.pos_ref, ...), custom_call_target="tpu_custom_call" | custom-call | flops 14495514624 | bytes 25165824 | tf_op jit(solution)/shard_map/pallas_call | solution.py:346
  259.3 15.1 %shard_map.293 = (f32[1024,768]{1,0:T(8,128)}, bf16[1024,768]{1,0:T(8,128)(2,1)S(1)}, bf16[1024,768]{1,0:T(8,128)(2,1)S(1)}, f32[8,768]{1,0:T(8,128)S(1)}) custom-call(bf16[1024,3072]{1,0:T(8,128)(2,1)} %get-tuple-element.40.gate_ref, f32[1024,768]{1,0:T(8,128)} %get-tuple-element.41.gss_ref, f32[1024,768]{1,0:T(8,128)} %get-tuple-element.38.first_ref, ...), custom_call_target="tpu_custom_call" | custom-call | flops 9663676416 | bytes 12582912 | tf_op jit(solution)/shard_map/pallas_call | solution.py:396
  276.7 28.4 %shard_map.294 = (bf16[1024,768]{1,0:T(8,128)(2,1)S(1)}, bf16[1024,768]{1,0:T(8,128)(2,1)S(1)}, bf16[1024,768]{1,0:T(8,128)(2,1)S(1)}) custom-call(s32[1]{0:T(128)} %bitcast.here_ref, bf16[1024,2304]{1,0:T(8,128)(2,1)} %add_convert_fusion.q_ref.k_ref.v_ref, bf16[1024,2304]{1,0:T(8,128)(2,1)} %add_convert_fusion.q_ref.k_ref.v_ref, ...), custom_call_target="tpu_custom_call" | custom-call | flops 28311552000 | bytes 18874368 | tf_op jit(solution)/shard_map/pallas_call | solution.py:183
  306.1 5.6 %convolution_convert_fusion.2 = bf16[768,2304]{0,1:T(8,128)(2,1)} fusion(bf16[1024,768]{1,0:T(8,128)(2,1)S(1)} %bitcast.395, bf16[1024,2304]{1,0:T(8,128)(2,1)S(1)} %get-tuple-element.88), kind=kOutput, calls=%fused_computation.4 | convolution fusion | flops 3625648128 | bytes 9830400 | tf_op jit(solution)/shard_map/ti,tj->ij/dot_general | solution.py:421
  311.8 5.5 %fusion.3 = f32[1024,768]{1,0:T(8,128)} fusion(bf16[1024,2304]{1,0:T(8,128)(2,1)S(1)} %get-tuple-element.88, bf16[768,1280]{0,1:T(8,128)(2,1)S(1)} %copy-done.33, bf16[768,1280]{0,1:T(8,128)(2,1)S(1)} %copy-done.34), kind=kOutput, calls=%fused_computation.27 | convolution fusion | flops 3630956544 | bytes 11796480 | tf_op jit(solution)/shard_map/tj,ij->ti/dot_general | solution.py:425
  317.3 5.5 %convolution_convert_fusion = bf16[3072,768]{1,0:T(8,128)(2,1)S(1)} fusion(bf16[1024,3072]{1,0:T(8,128)(2,1)S(1)} %bitcast.439, bf16[1024,768]{1,0:T(8,128)(2,1)S(1)} %get-tuple-element.52), kind=kOutput, calls=%fused_computation.2 | convolution fusion | flops 4834197504 | bytes 12582912 | tf_op jit(solution)/shard_map/ti,tj->ij/dot_general | solution.py:421
  322.8 2.0 broadcast_select_fusion.3
  326.7 2.6 broadcast_select_fusion.6
  337.3 5.6 %convolution_convert_fusion.1 = bf16[768,3072]{1,0:T(8,128)(2,1)S(1)} fusion(bf16[1024,768]{1,0:T(8,128)(2,1)S(1)} %copy-done.8, bf16[1024,3072]{1,0:T(8,128)(2,1)S(1)} %bitcast.437), kind=kOutput, calls=%fused_computation.3 | convolution fusion | flops 4834197504 | bytes 12582912 | tf_op jit(solution)/shard_map/ti,tj->ij/dot_general | solution.py:421
  343.0 2.4 broadcast_select_fusion
  348.2 6.3 %collective-permute-done.31 = bf16[2,128,768]{2,1,0:T(8,128)(2,1)S(1)} collective-permute-done((bf16[2,128,768]{2,1,0:T(8,128)(2,1)S(1)}, bf16[2,128,768]{2,1,0:T(8,128)(2,1)S(1)}, u32[]{:S(2)}, u32[]{:S(2)}) %collective-permute-start.31) | collective-permute-done | bytes 393248 | tf_op jit(solution)/shard_map/ppermute | solution.py:450
  356.0 3.8 add_convert_fusion.3
  359.8 2.7 copy.81
  364.6 6.5 %collective-permute-done.28 = bf16[2,128,768]{2,1,0:T(8,128)(2,1)} collective-permute-done((bf16[2,128,768]{2,1,0:T(8,128)(2,1)}, bf16[2,128,768]{2,1,0:T(8,128)(2,1)}, u32[]{:S(2)}, u32[]{:S(2)}) %collective-permute-start.28) | collective-permute-done | bytes 393248 | tf_op jit(solution)/shard_map/ppermute | solution.py:450
  371.2 1.9 fusion.17
  374.6 2.0 bitcast_convert_fusion
  376.7 10.2 %collective-permute-done.34 = bf16[4,96,1280]{2,1,0:T(8,128)(2,1)S(1)} collective-permute-done((bf16[4,96,1280]{2,1,0:T(8,128)(2,1)S(1)}, bf16[4,96,1280]{2,1,0:T(8,128)(2,1)S(1)}, u32[]{:S(2)}, u32[]{:S(2)}) %collective-permute-start.34) | collective-permute-done | bytes 983072 | tf_op jit(solution)/shard_map/ppermute | solution.py:446
  387.2 1.8 collective-permute-start.35
  389.2 2.5 collective-permute-start.37
  391.7 2.7 add_convert_fusion.2
  396.1 2.0 collective-permute-done.35
  398.0 11.2 %collective-permute-done.36 = bf16[96,1280]{1,0:T(8,128)(2,1)S(1)} collective-permute-done((bf16[96,1280]{1,0:T(8,128)(2,1)S(1)}, bf16[96,1280]{1,0:T(8,128)(2,1)S(1)}, u32[]{:S(2)}, u32[]{:S(2)}) %collective-permute-start.36) | collective-permute-done | bytes 245792 | tf_op jit(solution)/shard_map/ppermute | solution.py:446
  411.9 2.5 collective-permute-done.38
  414.6 1.6 collective-permute-start.41
  416.3 7.2 %collective-permute-done.48 = bf16[4,384,384]{2,1,0:T(8,128)(2,1)S(1)} collective-permute-done((bf16[4,384,384]{2,1,0:T(8,128)(2,1)S(1)}, bf16[4,384,384]{2,1,0:T(8,128)(2,1)S(1)}, u32[]{:S(2)}, u32[]{:S(2)}) %collective-permute-start.48) | collective-permute-done | bytes 1179680 | tf_op jit(solution)/shard_map/ppermute | solution.py:446
  424.0 1.9 collective-permute-start.50
  425.9 2.4 collective-permute-start.51
  428.4 6.0 %collective-permute-done.49 = bf16[384,384]{1,0:T(8,128)(2,1)S(1)} collective-permute-done((bf16[384,384]{1,0:T(8,128)(2,1)S(1)}, bf16[384,384]{1,0:T(8,128)(2,1)S(1)}, u32[]{:S(2)}, u32[]{:S(2)}) %collective-permute-start.49) | collective-permute-done | bytes 294944 | tf_op jit(solution)/shard_map/ppermute | solution.py:446
  434.4 11.4 %collective-permute-done.50 = bf16[384,384]{1,0:T(8,128)(2,1)S(1)} collective-permute-done((bf16[384,384]{1,0:T(8,128)(2,1)S(1)}, bf16[384,384]{1,0:T(8,128)(2,1)S(1)}, u32[]{:S(2)}, u32[]{:S(2)}) %collective-permute-start.50) | collective-permute-done | bytes 294944 | tf_op jit(solution)/shard_map/ppermute | solution.py:446
  446.0 1.7 collective-permute-start.52
  447.6 4.8 collective-permute-done.41
  455.3 2.2 collective-permute-start.44
  459.7 9.6 %collective-permute-done.42 = bf16[96,1920]{1,0:T(8,128)(2,1)} collective-permute-done((bf16[96,1920]{1,0:T(8,128)(2,1)S(1)}, bf16[96,1920]{1,0:T(8,128)(2,1)}, u32[]{:S(2)}, u32[]{:S(2)}) %collective-permute-start.42) | collective-permute-done | bytes 368672 | tf_op jit(solution)/shard_map/ppermute | solution.py:446
  469.4 13.0 %collective-permute-done.43 = bf16[96,1920]{1,0:T(8,128)(2,1)} collective-permute-done((bf16[96,1920]{1,0:T(8,128)(2,1)S(1)}, bf16[96,1920]{1,0:T(8,128)(2,1)}, u32[]{:S(2)}, u32[]{:S(2)}) %collective-permute-start.43) | collective-permute-done | bytes 368672 | tf_op jit(solution)/shard_map/ppermute | solution.py:446
  483.8 1.7 collective-permute-start.45
  485.5 3.9 collective-permute-done.45
  (282 shorter events, 76.2 us)
Async XLA Ops:
  0.6 21.9 %copy-start = (s32[8,128]{1,0:T(8,128)S(1)}, s32[8,128]{1,0:T(8,128)}, u32[]{:S(2)}) copy-start(s32[8,128]{1,0:T(8,128)} %param.33) | copy-start | bytes 12292
  2.3 21.4 %collective-permute-start.20 = (bf16[96,384]{1,0:T(8,128)(2,1)}, bf16[96,384]{1,0:T(8,128)(2,1)}, u32[]{:S(2)}, u32[]{:S(2)}) collective-permute-start(bf16[96,384]{1,0:T(8,128)(2,1)} %fusion.64), channel_id=1, source_target_pairs={{0,1},{1,0},{2,3},{3,2},{4,5},{5,4},{6,7},{7,6},{8,9},{9,8},{10,11... | collective-permute-start | bytes 221192 | tf_op jit(solution)/shard_map/ppermute | solution.py:446
  4.6 22.1 %collective-permute-start.13 = (bf16[24,1920]{1,0:T(8,128)(2,1)}, bf16[24,1920]{1,0:T(8,128)(2,1)}, u32[]{:S(2)}, u32[]{:S(2)}) collective-permute-start(bf16[24,1920]{1,0:T(8,128)(2,1)} %fusion.59), channel_id=1, source_target_pairs={{0,1},{1,0},{2,3},{3,2},{4,5},{5,4},{6,7},{7,6},{8,9},{9,8},{10,11... | collective-permute-start | bytes 276488 | tf_op jit(solution)/shard_map/ppermute | solution.py:446
  15.4 7.2 %collective-permute-start.3 = (bf16[24,1280]{1,0:T(8,128)(2,1)}, bf16[24,1280]{1,0:T(8,128)(2,1)}, u32[]{:S(2)}, u32[]{:S(2)}) collective-permute-start(bf16[24,1280]{1,0:T(8,128)(2,1)} %fusion.70), channel_id=1, source_target_pairs={{0,1},{1,0},{2,3},{3,2},{4,5},{5,4},{6,7},{7,6},{8,9},{9,8},{10,11... | collective-permute-start | bytes 184328 | tf_op jit(solution)/shard_map/ppermute | solution.py:446
  18.2 102.1 %collective-permute-start = (bf16[2,128,768]{2,1,0:T(8,128)(2,1)}, bf16[2,128,768]{2,1,0:T(8,128)(2,1)}, u32[]{:S(2)}, u32[]{:S(2)}) collective-permute-start(bf16[2,128,768]{2,1,0:T(8,128)(2,1)} %get-tuple-element.99), channel_id=1, source_target_pairs={{0,3},{1,2},{2,1},{3,0},{4,7},{5,6},{6,5},{7,4},{8,11},{9,10},{10,... | collective-permute-start | bytes 1179656 | tf_op jit(solution)/shard_map/ppermute | solution.py:450
  23.6 10.0 %collective-permute-start.4 = (bf16[2,24,1280]{2,1,0:T(8,128)(2,1)S(1)}, bf16[2,24,1280]{2,1,0:T(8,128)(2,1)S(1)}, u32[]{:S(2)}, u32[]{:S(2)}) collective-permute-start(bf16[2,24,1280]{2,1,0:T(8,128)(2,1)S(1)} %pad_maximum_fusion.21), channel_id=1, source_target_pairs={{0,2},{1,3},{2,0},{3,1},{4,6},{5,7},{6,4},{7,5},{8,10},{9,11},{10,... | collective-permute-start | bytes 368648 | tf_op jit(solution)/shard_map/ppermute | solution.py:446
  24.6 13.2 %collective-permute-start.21 = (bf16[2,96,384]{2,1,0:T(8,128)(2,1)S(1)}, bf16[2,96,384]{2,1,0:T(8,128)(2,1)S(1)}, u32[]{:S(2)}, u32[]{:S(2)}) collective-permute-start(bf16[2,96,384]{2,1,0:T(8,128)(2,1)S(1)} %pad_maximum_fusion.20), channel_id=1, source_target_pairs={{0,2},{1,3},{2,0},{3,1},{4,6},{5,7},{6,4},{7,5},{8,10},{9,11},{10,... | collective-permute-start | bytes 442376 | tf_op jit(solution)/shard_map/ppermute | solution.py:446
  27.7 12.8 %collective-permute-start.14 = (bf16[2,24,1920]{2,1,0:T(8,128)(2,1)S(1)}, bf16[2,24,1920]{2,1,0:T(8,128)(2,1)S(1)}, u32[]{:S(2)}, u32[]{:S(2)}) collective-permute-start(bf16[2,24,1920]{2,1,0:T(8,128)(2,1)S(1)} %pad_maximum_fusion.18), channel_id=1, source_target_pairs={{0,2},{1,3},{2,0},{3,1},{4,6},{5,7},{6,4},{7,5},{8,10},{9,11},{10,... | collective-permute-start | bytes 552968 | tf_op jit(solution)/shard_map/ppermute | solution.py:446
  33.6 11.2 %collective-permute-start.5 = (bf16[4,24,1280]{2,1,0:T(8,128)(2,1)S(1)}, bf16[4,24,1280]{2,1,0:T(8,128)(2,1)S(1)}, u32[]{:S(2)}, u32[]{:S(2)}) collective-permute-start(bf16[4,24,1280]{2,1,0:T(8,128)(2,1)S(1)} %bitcast.422), channel_id=1, source_target_pairs={{0,24},{1,25},{2,26},{3,27},{4,28},{5,29},{6,30},{7,31},{8,16},{9,... | collective-permute-start | bytes 737288 | tf_op jit(solution)/shard_map/ppermute | solution.py:446
  37.9 33.8 %collective-permute-start.6 = (bf16[4,24,1280]{2,1,0:T(8,128)(2,1)S(1)}, bf16[4,24,1280]{2,1,0:T(8,128)(2,1)S(1)}, u32[]{:S(2)}, u32[]{:S(2)}) collective-permute-start(bf16[4,24,1280]{2,1,0:T(8,128)(2,1)S(1)} %bitcast.423), channel_id=1, source_target_pairs={{0,16},{1,17},{2,18},{3,19},{4,20},{5,21},{6,22},{7,23},{8,24},{9,... | collective-permute-start | bytes 737288 | tf_op jit(solution)/shard_map/ppermute | solution.py:446
  37.9 34.3 %collective-permute-start.7 = (bf16[4,24,1280]{2,1,0:T(8,128)(2,1)S(1)}, bf16[4,24,1280]{2,1,0:T(8,128)(2,1)S(1)}, u32[]{:S(2)}, u32[]{:S(2)}) collective-permute-start(bf16[4,24,1280]{2,1,0:T(8,128)(2,1)S(1)} %bitcast.424), channel_id=1, source_target_pairs={{0,8},{1,9},{2,10},{3,11},{4,12},{5,13},{6,14},{7,15},{8,0},{9,1},... | collective-permute-start | bytes 737288 | tf_op jit(solution)/shard_map/ppermute | solution.py:446
  40.5 34.8 %collective-permute-start.22 = (bf16[4,96,384]{2,1,0:T(8,128)(2,1)S(1)}, bf16[4,96,384]{2,1,0:T(8,128)(2,1)S(1)}, u32[]{:S(2)}, u32[]{:S(2)}) collective-permute-start(bf16[4,96,384]{2,1,0:T(8,128)(2,1)S(1)} %bitcast.417), channel_id=1, source_target_pairs={{0,24},{1,25},{2,26},{3,27},{4,28},{5,29},{6,30},{7,31},{8,16},{9,... | collective-permute-start | bytes 884744 | tf_op jit(solution)/shard_map/ppermute | solution.py:446
  44.8 55.3 %collective-permute-start.23 = (bf16[4,96,384]{2,1,0:T(8,128)(2,1)S(1)}, bf16[4,96,384]{2,1,0:T(8,128)(2,1)S(1)}, u32[]{:S(2)}, u32[]{:S(2)}) collective-permute-start(bf16[4,96,384]{2,1,0:T(8,128)(2,1)S(1)} %bitcast.418), channel_id=1, source_target_pairs={{0,16},{1,17},{2,18},{3,19},{4,20},{5,21},{6,22},{7,23},{8,24},{9,... | collective-permute-start | bytes 884744 | tf_op jit(solution)/shard_map/ppermute | solution.py:446
  71.7 28.4 %collective-permute-start.24 = (bf16[4,96,384]{2,1,0:T(8,128)(2,1)S(1)}, bf16[4,96,384]{2,1,0:T(8,128)(2,1)S(1)}, u32[]{:S(2)}, u32[]{:S(2)}) collective-permute-start(bf16[4,96,384]{2,1,0:T(8,128)(2,1)S(1)} %bitcast.419), channel_id=1, source_target_pairs={{0,8},{1,9},{2,10},{3,11},{4,12},{5,13},{6,14},{7,15},{8,0},{9,1},... | collective-permute-start | bytes 884744 | tf_op jit(solution)/shard_map/ppermute | solution.py:446
  72.2 30.8 %collective-permute-start.15 = (bf16[4,24,1920]{2,1,0:T(8,128)(2,1)S(1)}, bf16[4,24,1920]{2,1,0:T(8,128)(2,1)S(1)}, u32[]{:S(2)}, u32[]{:S(2)}) collective-permute-start(bf16[4,24,1920]{2,1,0:T(8,128)(2,1)S(1)} %bitcast.412), channel_id=1, source_target_pairs={{0,24},{1,25},{2,26},{3,27},{4,28},{5,29},{6,30},{7,31},{8,16},{9,... | collective-permute-start | bytes 1105928 | tf_op jit(solution)/shard_map/ppermute | solution.py:446
  75.3 27.7 %copy-start.37 = (bf16[2,128,768]{2,1,0:T(8,128)(2,1)S(1)}, bf16[2,128,768]{2,1,0:T(8,128)(2,1)}, u32[]{:S(2)}) copy-start(bf16[2,128,768]{2,1,0:T(8,128)(2,1)} %get-tuple-element.98) | copy-start | bytes 1179652
  75.3 39.5 %collective-permute-start.16 = (bf16[4,24,1920]{2,1,0:T(8,128)(2,1)S(1)}, bf16[4,24,1920]{2,1,0:T(8,128)(2,1)S(1)}, u32[]{:S(2)}, u32[]{:S(2)}) collective-permute-start(bf16[4,24,1920]{2,1,0:T(8,128)(2,1)S(1)} %bitcast.413), channel_id=1, source_target_pairs={{0,16},{1,17},{2,18},{3,19},{4,20},{5,21},{6,22},{7,23},{8,24},{9,... | collective-permute-start | bytes 1105928 | tf_op jit(solution)/shard_map/ppermute | solution.py:446
  100.1 16.1 %collective-permute-start.17 = (bf16[4,24,1920]{2,1,0:T(8,128)(2,1)S(1)}, bf16[4,24,1920]{2,1,0:T(8,128)(2,1)S(1)}, u32[]{:S(2)}, u32[]{:S(2)}) collective-permute-start(bf16[4,24,1920]{2,1,0:T(8,128)(2,1)S(1)} %bitcast.414), channel_id=1, source_target_pairs={{0,8},{1,9},{2,10},{3,11},{4,12},{5,13},{6,14},{7,15},{8,0},{9,1},... | collective-permute-start | bytes 1105928 | tf_op jit(solution)/shard_map/ppermute | solution.py:446
  100.1 19.4 %collective-permute-start.8 = (bf16[4,4,24,1280]{3,2,1,0:T(8,128)(2,1)S(1)}, bf16[4,4,24,1280]{3,2,1,0:T(8,128)(2,1)S(1)}, u32[]{:S(2)}, u32[]{:S(2)}) collective-permute-start(bf16[4,4,24,1280]{3,2,1,0:T(8,128)(2,1)S(1)} %pad_maximum_fusion.14), channel_id=1, source_target_pairs={{0,4},{1,5},{2,6},{3,7},{4,0},{5,1},{6,2},{7,3},{8,12},{9,13},{10,... | collective-permute-start | bytes 2949128 | tf_op jit(solution)/shard_map/ppermute | solution.py:446
  103.0 20.5 %collective-permute-start.1 = (bf16[2,128,768]{2,1,0:T(8,128)(2,1)S(1)}, bf16[2,128,768]{2,1,0:T(8,128)(2,1)}, u32[]{:S(2)}, u32[]{:S(2)}) collective-permute-start(bf16[2,128,768]{2,1,0:T(8,128)(2,1)S(1)} %copy-done.37), channel_id=1, source_target_pairs={{0,2},{1,3},{2,0},{3,1},{4,6},{5,7},{6,4},{7,5},{8,10},{9,11},{10,... | collective-permute-start | bytes 1179656 | tf_op jit(solution)/shard_map/ppermute | solution.py:450
  114.8 35.4 %collective-permute-start.11 = (bf16[12,128,512]{2,1,0:T(8,128)(2,1)}, bf16[12,128,512]{2,1,0:T(8,128)(2,1)}, u32[]{:S(2)}, u32[]{:S(2)}) collective-permute-start(bf16[12,128,512]{2,1,0:T(8,128)(2,1)} %select_convert_fusion.rest_0_), channel_id=1, source_target_pairs={{0,2},{1,3},{2,0},{3,1},{4,6},{5,7},{6,4},{7,5},{8,10},{9,11},{10,... | collective-permute-start | bytes 4718600 | tf_op jit(solution)/shard_map/ppermute | solution.py:446
  116.3 33.9 %collective-permute-start.25 = (bf16[4,4,96,384]{3,2,1,0:T(8,128)(2,1)}, bf16[4,4,96,384]{3,2,1,0:T(8,128)(2,1)}, u32[]{:S(2)}, u32[]{:S(2)}) collective-permute-start(bf16[4,4,96,384]{3,2,1,0:T(8,128)(2,1)} %pad_maximum_fusion.13), channel_id=1, source_target_pairs={{0,4},{1,5},{2,6},{3,7},{4,0},{5,1},{6,2},{7,3},{8,12},{9,13},{10,... | collective-permute-start | bytes 3538952 | tf_op jit(solution)/shard_map/ppermute | solution.py:446
  119.6 55.2 %collective-permute-start.18 = (bf16[4,4,24,1920]{3,2,1,0:T(8,128)(2,1)}, bf16[4,4,24,1920]{3,2,1,0:T(8,128)(2,1)}, u32[]{:S(2)}, u32[]{:S(2)}) collective-permute-start(bf16[4,4,24,1920]{3,2,1,0:T(8,128)(2,1)} %pad_maximum_fusion.12), channel_id=1, source_target_pairs={{0,4},{1,5},{2,6},{3,7},{4,0},{5,1},{6,2},{7,3},{8,12},{9,13},{10,... | collective-permute-start | bytes 4423688 | tf_op jit(solution)/shard_map/ppermute | solution.py:446
  120.5 3.5 collective-permute-start.2
  123.4 55.1 %collective-permute-start.9 = (bf16[768,1280]{0,1:T(8,128)(2,1)}, bf16[768,1280]{0,1:T(8,128)(2,1)S(1)}, u32[]{:S(2)}, u32[]{:S(2)}) collective-permute-start(bf16[768,1280]{0,1:T(8,128)(2,1)} %copy.74), channel_id=1, source_target_pairs={{0,1},{1,0},{2,3},{3,2},{4,5},{5,4},{6,7},{7,6},{8,9},{9,8},{10,11... | collective-permute-start | bytes 5898248 | tf_op jit(solution)/shard_map/ppermute | solution.py:446
  124.0 66.5 %collective-permute-start.10 = (bf16[12,128,512]{2,1,0:T(8,128)(2,1)}, bf16[12,128,512]{2,1,0:T(8,128)(2,1)}, u32[]{:S(2)}, u32[]{:S(2)}) collective-permute-start(bf16[12,128,512]{2,1,0:T(8,128)(2,1)} %select_convert_fusion.rest_0_), channel_id=1, source_target_pairs={{0,1},{1,0},{2,3},{3,2},{4,5},{5,4},{6,7},{7,6},{8,9},{9,8},{10,11... | collective-permute-start | bytes 4718600 | tf_op jit(solution)/shard_map/ppermute | solution.py:446
  125.6 24.6 %copy-start.27 = (bf16[1,4,96,384]{3,2,1,0:T(8,128)(2,1)S(1)}, bf16[1,4,96,384]{3,2,1,0:T(8,128)(2,1)}, u32[]{:S(2)}) copy-start(bf16[1,4,96,384]{3,2,1,0:T(8,128)(2,1)} %copy-done.26) | copy-start | bytes 884740
  125.6 24.6 %copy-start.29 = (bf16[1,4,96,384]{3,2,1,0:T(8,128)(2,1)S(1)}, bf16[1,4,96,384]{3,2,1,0:T(8,128)(2,1)}, u32[]{:S(2)}) copy-start(bf16[1,4,96,384]{3,2,1,0:T(8,128)(2,1)} %copy-done.28) | copy-start | bytes 884740
  125.6 24.6 %copy-start.31 = (bf16[1,4,96,384]{3,2,1,0:T(8,128)(2,1)S(1)}, bf16[1,4,96,384]{3,2,1,0:T(8,128)(2,1)}, u32[]{:S(2)}) copy-start(bf16[1,4,96,384]{3,2,1,0:T(8,128)(2,1)} %copy-done.30) | copy-start | bytes 884740
  150.2 40.3 %collective-permute-start.12 = (bf16[12,128,512]{2,1,0:T(8,128)(2,1)}, bf16[12,128,512]{2,1,0:T(8,128)(2,1)}, u32[]{:S(2)}, u32[]{:S(2)}) collective-permute-start(bf16[12,128,512]{2,1,0:T(8,128)(2,1)} %collective-permute-done.11.rest_2_), channel_id=1, source_target_pairs={{0,1},{1,0},{2,3},{3,2},{4,5},{5,4},{6,7},{7,6},{8,9},{9,8},{10,11... | collective-permute-start | bytes 4718600 | tf_op jit(solution)/shard_map/ppermute | solution.py:446
  151.8 23.0 %copy-start.18 = (bf16[1,4,24,1920]{3,2,1,0:T(8,128)(2,1)S(1)}, bf16[1,4,24,1920]{3,2,1,0:T(8,128)(2,1)}, u32[]{:S(2)}) copy-start(bf16[1,4,24,1920]{3,2,1,0:T(8,128)(2,1)} %copy-done.17) | copy-start | bytes 1105924
  151.8 23.0 %copy-start.20 = (bf16[1,4,24,1920]{3,2,1,0:T(8,128)(2,1)S(1)}, bf16[1,4,24,1920]{3,2,1,0:T(8,128)(2,1)}, u32[]{:S(2)}) copy-start(bf16[1,4,24,1920]{3,2,1,0:T(8,128)(2,1)} %copy-done.19) | copy-start | bytes 1105924
  151.8 23.0 %copy-start.22 = (bf16[1,4,24,1920]{3,2,1,0:T(8,128)(2,1)S(1)}, bf16[1,4,24,1920]{3,2,1,0:T(8,128)(2,1)}, u32[]{:S(2)}) copy-start(bf16[1,4,24,1920]{3,2,1,0:T(8,128)(2,1)} %copy-done.21) | copy-start | bytes 1105924
  153.5 56.3 %collective-permute-start.26 = (bf16[3072,384]{1,0:T(8,128)(2,1)}, bf16[3072,384]{1,0:T(8,128)(2,1)}, u32[]{:S(2)}, u32[]{:S(2)}) collective-permute-start(bf16[3072,384]{1,0:T(8,128)(2,1)} %bitcast.82), channel_id=1, source_target_pairs={{0,1},{1,0},{2,3},{3,2},{4,5},{5,4},{6,7},{7,6},{8,9},{9,8},{10,11... | collective-permute-start | bytes 7077896 | tf_op jit(solution)/shard_map/ppermute | solution.py:446
  178.5 37.2 %collective-permute-start.19 = (bf16[768,1920]{1,0:T(8,128)(2,1)}, bf16[768,1920]{1,0:T(8,128)(2,1)}, u32[]{:S(2)}, u32[]{:S(2)}) collective-permute-start(bf16[768,1920]{1,0:T(8,128)(2,1)} %bitcast.63), channel_id=1, source_target_pairs={{0,1},{1,0},{2,3},{3,2},{4,5},{5,4},{6,7},{7,6},{8,9},{9,8},{10,11... | collective-permute-start | bytes 8847368 | tf_op jit(solution)/shard_map/ppermute | solution.py:446
  325.7 66.0 %collective-permute-start.47 = (bf16[3072,384]{1,0:T(8,128)(2,1)}, bf16[3072,384]{1,0:T(8,128)(2,1)}, u32[]{:S(2)}, u32[]{:S(2)}) collective-permute-start(bf16[3072,384]{1,0:T(8,128)(2,1)} %broadcast_select_fusion.3), channel_id=1, source_target_pairs={{0,1},{1,0},{2,3},{3,2},{4,5},{5,4},{6,7},{7,6},{8,9},{9,8},{10,11... | collective-permute-start | bytes 7077896 | tf_op jit(solution)/shard_map/ppermute | solution.py:446
  329.3 26.7 %collective-permute-start.33 = (bf16[768,1280]{0,1:T(8,128)(2,1)S(1)}, bf16[768,1280]{0,1:T(8,128)(2,1)S(1)}, u32[]{:S(2)}, u32[]{:S(2)}) collective-permute-start(bf16[768,1280]{0,1:T(8,128)(2,1)S(1)} %broadcast_select_fusion.6), channel_id=1, source_target_pairs={{0,1},{1,0},{2,3},{3,2},{4,5},{5,4},{6,7},{7,6},{8,9},{9,8},{10,11... | collective-permute-start | bytes 5898248 | tf_op jit(solution)/shard_map/ppermute | solution.py:446
  334.3 12.4 %collective-permute-start.30 = (bf16[2,128,768]{2,1,0:T(8,128)(2,1)S(1)}, bf16[2,128,768]{2,1,0:T(8,128)(2,1)S(1)}, u32[]{:S(2)}, u32[]{:S(2)}) collective-permute-start(bf16[2,128,768]{2,1,0:T(8,128)(2,1)S(1)} %get-tuple-element.93), channel_id=1, source_target_pairs={{0,3},{1,2},{2,1},{3,0},{4,7},{5,6},{6,5},{7,4},{8,11},{9,10},{10,... | collective-permute-start | bytes 1179656 | tf_op jit(solution)/shard_map/ppermute | solution.py:450
  335.6 18.9 %collective-permute-start.31 = (bf16[2,128,768]{2,1,0:T(8,128)(2,1)S(1)}, bf16[2,128,768]{2,1,0:T(8,128)(2,1)S(1)}, u32[]{:S(2)}, u32[]{:S(2)}) collective-permute-start(bf16[2,128,768]{2,1,0:T(8,128)(2,1)S(1)} %get-tuple-element.92), channel_id=1, source_target_pairs={{0,2},{1,3},{2,0},{3,1},{4,6},{5,7},{6,4},{7,5},{8,10},{9,11},{10,... | collective-permute-start | bytes 1179656 | tf_op jit(solution)/shard_map/ppermute | solution.py:450
  336.2 26.3 %collective-permute-start.32 = (bf16[2,128,768]{2,1,0:T(8,128)(2,1)}, bf16[2,128,768]{2,1,0:T(8,128)(2,1)}, u32[]{:S(2)}, u32[]{:S(2)}) collective-permute-start(bf16[2,128,768]{2,1,0:T(8,128)(2,1)} %get-tuple-element.91), channel_id=1, source_target_pairs={{0,1},{1,0},{2,3},{3,2},{4,5},{5,4},{6,7},{7,6},{8,9},{9,8},{10,11... | collective-permute-start | bytes 1179656 | tf_op jit(solution)/shard_map/ppermute | solution.py:450
  346.7 16.4 %collective-permute-start.27 = (bf16[2,128,768]{2,1,0:T(8,128)(2,1)}, bf16[2,128,768]{2,1,0:T(8,128)(2,1)}, u32[]{:S(2)}, u32[]{:S(2)}) collective-permute-start(bf16[2,128,768]{2,1,0:T(8,128)(2,1)} %get-tuple-element.96), channel_id=1, source_target_pairs={{0,3},{1,2},{2,1},{3,0},{4,7},{5,6},{6,5},{7,4},{8,11},{9,10},{10,... | collective-permute-start | bytes 1179656 | tf_op jit(solution)/shard_map/ppermute | solution.py:450
  354.5 16.6 %collective-permute-start.28 = (bf16[2,128,768]{2,1,0:T(8,128)(2,1)}, bf16[2,128,768]{2,1,0:T(8,128)(2,1)}, u32[]{:S(2)}, u32[]{:S(2)}) collective-permute-start(bf16[2,128,768]{2,1,0:T(8,128)(2,1)} %get-tuple-element.95), channel_id=1, source_target_pairs={{0,2},{1,3},{2,0},{3,1},{4,6},{5,7},{6,4},{7,5},{8,10},{9,11},{10,... | collective-permute-start | bytes 1179656 | tf_op jit(solution)/shard_map/ppermute | solution.py:450
  355.9 15.2 %collective-permute-start.29 = (bf16[2,128,768]{2,1,0:T(8,128)(2,1)}, bf16[2,128,768]{2,1,0:T(8,128)(2,1)}, u32[]{:S(2)}, u32[]{:S(2)}) collective-permute-start(bf16[2,128,768]{2,1,0:T(8,128)(2,1)} %get-tuple-element.94), channel_id=1, source_target_pairs={{0,1},{1,0},{2,3},{3,2},{4,5},{5,4},{6,7},{7,6},{8,9},{9,8},{10,11... | collective-permute-start | bytes 1179656 | tf_op jit(solution)/shard_map/ppermute | solution.py:450
  362.5 48.0 %collective-permute-start.40 = (bf16[768,1920]{1,0:T(8,128)(2,1)}, bf16[768,1920]{1,0:T(8,128)(2,1)S(1)}, u32[]{:S(2)}, u32[]{:S(2)}) collective-permute-start(bf16[768,1920]{1,0:T(8,128)(2,1)} %broadcast_select_fusion), channel_id=1, source_target_pairs={{0,1},{1,0},{2,3},{3,2},{4,5},{5,4},{6,7},{7,6},{8,9},{9,8},{10,11... | collective-permute-start | bytes 8847368 | tf_op jit(solution)/shard_map/ppermute | solution.py:446
  363.1 23.7 %collective-permute-start.34 = (bf16[4,96,1280]{2,1,0:T(8,128)(2,1)S(1)}, bf16[4,96,1280]{2,1,0:T(8,128)(2,1)S(1)}, u32[]{:S(2)}, u32[]{:S(2)}) collective-permute-start(bf16[4,96,1280]{2,1,0:T(8,128)(2,1)S(1)} %dynamic-slice_bitcast_fusion.2), channel_id=1, source_target_pairs={{0,4},{1,5},{2,6},{3,7},{4,0},{5,1},{6,2},{7,3},{8,12},{9,13},{10,... | collective-permute-start | bytes 2949128 | tf_op jit(solution)/shard_map/ppermute | solution.py:446
  387.2 10.9 %collective-permute-start.35 = (bf16[96,1280]{1,0:T(8,128)(2,1)S(1)}, bf16[96,1280]{1,0:T(8,128)(2,1)S(1)}, u32[]{:S(2)}, u32[]{:S(2)}) collective-permute-start(bf16[96,1280]{1,0:T(8,128)(2,1)S(1)} %get-tuple-element.114), channel_id=1, source_target_pairs={{0,8},{1,9},{2,10},{3,11},{4,12},{5,13},{6,14},{7,15},{8,0},{9,1},... | collective-permute-start | bytes 737288 | tf_op jit(solution)/shard_map/ppermute | solution.py:446
  388.9 20.3 %collective-permute-start.36 = (bf16[96,1280]{1,0:T(8,128)(2,1)S(1)}, bf16[96,1280]{1,0:T(8,128)(2,1)S(1)}, u32[]{:S(2)}, u32[]{:S(2)}) collective-permute-start(bf16[96,1280]{1,0:T(8,128)(2,1)S(1)} %get-tuple-element.116), channel_id=1, source_target_pairs={{0,16},{1,17},{2,18},{3,19},{4,20},{5,21},{6,22},{7,23},{8,24},{9,... | collective-permute-start | bytes 737288 | tf_op jit(solution)/shard_map/ppermute | solution.py:446
  389.2 21.4 %slice-start.1 = ((s8[4718592]{0:T(1024)(128)(4,1)}), s8[524288]{0:T(1024)(128)(4,1)S(1)}, s32[]{:S(2)}) async-start(s8[4718592]{0:T(1024)(128)(4,1)} %bitcast.396), calls=%async_computation.1 | async-start | bytes 1048576
  389.2 20.1 %collective-permute-start.37 = (bf16[96,1280]{1,0:T(8,128)(2,1)S(1)}, bf16[96,1280]{1,0:T(8,128)(2,1)S(1)}, u32[]{:S(2)}, u32[]{:S(2)}) collective-permute-start(bf16[96,1280]{1,0:T(8,128)(2,1)S(1)} %get-tuple-element.115), channel_id=1, source_target_pairs={{0,24},{1,25},{2,26},{3,27},{4,28},{5,29},{6,30},{7,31},{8,16},{9,... | collective-permute-start | bytes 737288 | tf_op jit(solution)/shard_map/ppermute | solution.py:446
  394.5 29.0 %collective-permute-start.48 = (bf16[4,384,384]{2,1,0:T(8,128)(2,1)S(1)}, bf16[4,384,384]{2,1,0:T(8,128)(2,1)S(1)}, u32[]{:S(2)}, u32[]{:S(2)}) collective-permute-start(bf16[4,384,384]{2,1,0:T(8,128)(2,1)S(1)} %dynamic-slice_bitcast_fusion.1), channel_id=1, source_target_pairs={{0,4},{1,5},{2,6},{3,7},{4,0},{5,1},{6,2},{7,3},{8,12},{9,13},{10,... | collective-permute-start | bytes 3538952 | tf_op jit(solution)/shard_map/ppermute | solution.py:446
  409.4 4.9 %collective-permute-start.38 = (bf16[2,24,1280]{2,1,0:T(8,128)(2,1)S(1)}, bf16[2,24,1280]{2,1,0:T(8,128)(2,1)S(1)}, u32[]{:S(2)}, u32[]{:S(2)}) collective-permute-start(bf16[2,24,1280]{2,1,0:T(8,128)(2,1)S(1)} %dynamic-slice_bitcast_fusion.23), channel_id=1, source_target_pairs={{0,2},{1,3},{2,0},{3,1},{4,6},{5,7},{6,4},{7,5},{8,10},{9,11},{10,... | collective-permute-start | bytes 368648 | tf_op jit(solution)/shard_map/ppermute | solution.py:446
  414.4 1.8 collective-permute-start.39
  414.6 37.8 %collective-permute-start.41 = (bf16[4,96,1920]{2,1,0:T(8,128)(2,1)S(1)}, bf16[4,96,1920]{2,1,0:T(8,128)(2,1)S(1)}, u32[]{:S(2)}, u32[]{:S(2)}) collective-permute-start(bf16[4,96,1920]{2,1,0:T(8,128)(2,1)S(1)} %dynamic-slice_bitcast_fusion), channel_id=1, source_target_pairs={{0,4},{1,5},{2,6},{3,7},{4,0},{5,1},{6,2},{7,3},{8,12},{9,13},{10,... | collective-permute-start | bytes 4423688 | tf_op jit(solution)/shard_map/ppermute | solution.py:446
  423.9 10.4 %collective-permute-start.49 = (bf16[384,384]{1,0:T(8,128)(2,1)S(1)}, bf16[384,384]{1,0:T(8,128)(2,1)S(1)}, u32[]{:S(2)}, u32[]{:S(2)}) collective-permute-start(bf16[384,384]{1,0:T(8,128)(2,1)S(1)} %get-tuple-element.107), channel_id=1, source_target_pairs={{0,8},{1,9},{2,10},{3,11},{4,12},{5,13},{6,14},{7,15},{8,0},{9,1},... | collective-permute-start | bytes 884744 | tf_op jit(solution)/shard_map/ppermute | solution.py:446
  424.0 21.8 %collective-permute-start.50 = (bf16[384,384]{1,0:T(8,128)(2,1)S(1)}, bf16[384,384]{1,0:T(8,128)(2,1)S(1)}, u32[]{:S(2)}, u32[]{:S(2)}) collective-permute-start(bf16[384,384]{1,0:T(8,128)(2,1)S(1)} %get-tuple-element.109), channel_id=1, source_target_pairs={{0,16},{1,17},{2,18},{3,19},{4,20},{5,21},{6,22},{7,23},{8,24},{9,... | collective-permute-start | bytes 884744 | tf_op jit(solution)/shard_map/ppermute | solution.py:446
  425.9 19.8 %collective-permute-start.51 = (bf16[384,384]{1,0:T(8,128)(2,1)S(1)}, bf16[384,384]{1,0:T(8,128)(2,1)S(1)}, u32[]{:S(2)}, u32[]{:S(2)}) collective-permute-start(bf16[384,384]{1,0:T(8,128)(2,1)S(1)} %get-tuple-element.108), channel_id=1, source_target_pairs={{0,24},{1,25},{2,26},{3,27},{4,28},{5,29},{6,30},{7,31},{8,16},{9,... | collective-permute-start | bytes 884744 | tf_op jit(solution)/shard_map/ppermute | solution.py:446
  446.0 13.6 %collective-permute-start.52 = (bf16[2,96,384]{2,1,0:T(8,128)(2,1)S(1)}, bf16[2,96,384]{2,1,0:T(8,128)(2,1)S(1)}, u32[]{:S(2)}, u32[]{:S(2)}) collective-permute-start(bf16[2,96,384]{2,1,0:T(8,128)(2,1)S(1)} %dynamic-slice_bitcast_fusion.22), channel_id=1, source_target_pairs={{0,2},{1,3},{2,0},{3,1},{4,6},{5,7},{6,4},{7,5},{8,10},{9,11},{10,... | collective-permute-start | bytes 442376 | tf_op jit(solution)/shard_map/ppermute | solution.py:446
  453.0 16.4 %collective-permute-start.42 = (bf16[96,1920]{1,0:T(8,128)(2,1)S(1)}, bf16[96,1920]{1,0:T(8,128)(2,1)}, u32[]{:S(2)}, u32[]{:S(2)}) collective-permute-start(bf16[96,1920]{1,0:T(8,128)(2,1)S(1)} %get-tuple-element.100), channel_id=1, source_target_pairs={{0,8},{1,9},{2,10},{3,11},{4,12},{5,13},{6,14},{7,15},{8,0},{9,1},... | collective-permute-start | bytes 1105928 | tf_op jit(solution)/shard_map/ppermute | solution.py:446
  454.0 28.3 %collective-permute-start.43 = (bf16[96,1920]{1,0:T(8,128)(2,1)S(1)}, bf16[96,1920]{1,0:T(8,128)(2,1)}, u32[]{:S(2)}, u32[]{:S(2)}) collective-permute-start(bf16[96,1920]{1,0:T(8,128)(2,1)S(1)} %get-tuple-element.102), channel_id=1, source_target_pairs={{0,16},{1,17},{2,18},{3,19},{4,20},{5,21},{6,22},{7,23},{8,24},{9,... | collective-permute-start | bytes 1105928 | tf_op jit(solution)/shard_map/ppermute | solution.py:446
  455.3 27.1 %collective-permute-start.44 = (bf16[96,1920]{1,0:T(8,128)(2,1)S(1)}, bf16[96,1920]{1,0:T(8,128)(2,1)}, u32[]{:S(2)}, u32[]{:S(2)}) collective-permute-start(bf16[96,1920]{1,0:T(8,128)(2,1)S(1)} %get-tuple-element.101), channel_id=1, source_target_pairs={{0,24},{1,25},{2,26},{3,27},{4,28},{5,29},{6,30},{7,31},{8,16},{9,... | collective-permute-start | bytes 1105928 | tf_op jit(solution)/shard_map/ppermute | solution.py:446
  459.6 32.6 %copy-start.1 = (s32[8,128]{1,0:T(8,128)S(1)}, s32[8,128]{1,0:T(8,128)}, u32[]{:S(2)}) copy-start(s32[8,128]{1,0:T(8,128)} %param.33) | copy-start | bytes 12292
  459.6 25.8 %collective-permute-start.53 = (bf16[96,384]{1,0:T(8,128)(2,1)S(1)}, bf16[96,384]{1,0:T(8,128)(2,1)S(1)}, u32[]{:S(2)}, u32[]{:S(2)}) collective-permute-start(bf16[96,384]{1,0:T(8,128)(2,1)S(1)} %dynamic-slice_bitcast_fusion.25), channel_id=1, source_target_pairs={{0,1},{1,0},{2,3},{3,2},{4,5},{5,4},{6,7},{7,6},{8,9},{9,8},{10,11... | collective-permute-start | bytes 221192 | tf_op jit(solution)/shard_map/ppermute | solution.py:446
  483.8 5.6 %collective-permute-start.45 = (bf16[2,24,1920]{2,1,0:T(8,128)(2,1)S(1)}, bf16[2,24,1920]{2,1,0:T(8,128)(2,1)S(1)}, u32[]{:S(2)}, u32[]{:S(2)}) collective-permute-start(bf16[2,24,1920]{2,1,0:T(8,128)(2,1)S(1)} %dynamic-slice_bitcast_fusion.21), channel_id=1, source_target_pairs={{0,2},{1,3},{2,0},{3,1},{4,6},{5,7},{6,4},{7,5},{8,10},{9,11},{10,... | collective-permute-start | bytes 552968 | tf_op jit(solution)/shard_map/ppermute | solution.py:446
  489.5 1.4 collective-permute-start.46
  (41 other events, 308.4 us)

commit v3 on v1

v3 whole, which is shorter than its diff:
```python
import math
from functools import partial

import jax
import jax.numpy as jnp
from jax import lax
from jax.experimental import pallas as pl
from jax.experimental.pallas import tpu as pltpu
from jax.sharding import PartitionSpec as P

norm_eps = 1e-06
masked_score = -1e30
f32 = jnp.float32
bf16 = jnp.bfloat16
both = ("batch", "blk")
log2e = math.log2(math.e)
long, brief, least = 10**11, 100000000000, 100000000000
roomy = pltpu.CompilerParams(vmem_limit_bytes=48 << 20)
vector_names = (
    "bias_query",
    "bias_value",
    "bias_out",
    "gain_first",
    "shift_first",
    "bias_down",
    "gain_second",
    "shift_second",
)
row_of = {name: index for index, name in enumerate(vector_names)}


def dot(left, right):
    return jnp.dot(left, right, preferred_element_type=f32)


def dot_right_t(left, right):
    return lax.dot_general(left, right, (((1,), (1,)), ((), ())), preferred_element_type=f32)


def dot_left_t(left, right):
    return lax.dot_general(left, right, (((0,), (0,)), ((), ())), preferred_element_type=f32)


def norm_stats(rows):
    center = jnp.mean(rows, axis=-1, keepdims=True)
    centered = rows - center
    inverse = lax.rsqrt(jnp.mean(centered * centered, axis=-1, keepdims=True) + norm_eps)
    return centered * inverse, inverse


def norm_pull(upstream, normed, inverse, gain):
    scaled = upstream * gain
    inner = jnp.mean(scaled, axis=-1, keepdims=True)
    projected = jnp.mean(scaled * normed, axis=-1, keepdims=True)
    return inverse * (scaled - inner - normed * projected)


def vector(ref, name):
    index = row_of[name]
    return ref[index : index + 1, :]


def add_sums(sums_ref, rows):
    total = jnp.concatenate(
        [jnp.sum(row, axis=0, keepdims=True) for row in rows]
        + [jnp.zeros((sums_ref.shape[0] - len(rows), sums_ref.shape[1]), f32)],
        axis=0,
    )

    @pl.when(pl.program_id(0) == 0)
    def _():
        sums_ref[...] = total

    @pl.when(pl.program_id(0) > 0)
    def _():
        sums_ref[...] += total


def piece_rows(here, piece, rows):
    return pl.ds(pl.multiple_of((here ^ piece) * rows, rows), rows)


def stack_pieces(ref, places, cols):
    return jnp.concatenate([ref[0, place_, cols] for place_ in places], axis=0)


def any_block():
    return pl.BlockSpec(memory_space=pl.ANY)


def whole_block(array):
    return pl.BlockSpec(array.shape, lambda *unused: (0,) * len(array.shape))


def pair_order(core, first, second, wide):
    blocks = []
    for start in range(0, first.shape[-1], wide):
        left, right = first[:, start : start + wide], second[:, start : start + wide]
        blocks += [jnp.where(core == 0, left, right), jnp.where(core == 0, right, left)]
    return jnp.concatenate(blocks, axis=1)


def pair_split(core, array, wide):
    outs = []
    for turn in range(2):
        outs.append(
            jnp.concatenate(
                [
                    jnp.where(
                        core == turn,
                        array[:, start : start + wide],
                        array[:, start + wide : start + 2 * wide],
                    )
                    for start in range(0, array.shape[1], 2 * wide)
                ],
                axis=1,
            )
        )
    return outs


def half_split(core, array):
    half = array.shape[1] // 2
    left, right = array[:, :half], array[:, half:]
    return jnp.where(core == 0, left, right), jnp.where(core == 0, right, left)


class Run:
    def __init__(self, ids):
        self.ids, self.token = ids, None


id_of = {"here": 0, "c": 1, "y": 2, "z": 3, "x": 4}
token_shape = jax.ShapeDtypeStruct((8, 128), f32)


def after(run, arrays, *ties):
    shapes = [jax.ShapeDtypeStruct(array.shape, array.dtype) for array in arrays]

    def body(*refs):
        refs[-1][...] = jnp.zeros(token_shape.shape, f32)

    *arrays, run.token = pl.pallas_call(
        body,
        out_shape=shapes + [token_shape],
        in_specs=[any_block()] * (len(arrays) + len(ties)),
        out_specs=[any_block()] * len(arrays) + [pl.BlockSpec(memory_space=pltpu.VMEM)],
        input_output_aliases={index: index for index in range(len(arrays))},
    )(*arrays, *ties)
    return arrays


def kernel_call(
    kernel, run, arrays, ties, grid, in_specs, out_specs, out_shape, scratch=(), cost=long
):
    several = isinstance(out_shape, (list, tuple))
    out_specs, out_shape = [
        list(value) if several else [value] for value in (out_specs, out_shape)
    ]
    count, outs = 1 + len(arrays), len(out_shape)

    def body(*refs):
        inputs, refs = refs[:count], refs[count + len(ties) :]
        refs[outs][...] = jnp.zeros(token_shape.shape, f32)
        kernel(*inputs, *refs[:outs], *refs[outs + 1 :])

    *results, run.token = pl.pallas_call(
        body,
        out_shape=out_shape + [token_shape],
        grid_spec=pltpu.PrefetchScalarGridSpec(
            num_scalar_prefetch=1,
            grid=grid,
            in_specs=list(in_specs) + [any_block()] * len(ties),
            out_specs=out_specs + [whole_block(token_shape)],
            scratch_shapes=scratch,
        ),
        compiler_params=roomy,
        cost_estimate=pl.CostEstimate(flops=cost, bytes_accessed=1024, transcendentals=0),
    )(run.ids, *arrays, *ties)
    return results if several else results[0]


def place_kernel(digit, count, ids, *refs):
    parts, (out, sems) = refs[:count], refs[count:]
    copies = [
        pltpu.make_async_copy(part, out.at[ids[digit] ^ delta], sems.at[delta])
        for delta, part in enumerate(parts)
    ]
    for copy in copies:
        copy.start()
    for copy in copies:
        copy.wait()


def place_parts(run, parts, digit, ties=()):
    count = len(parts)
    return kernel_call(
        partial(place_kernel, id_of[digit], count),
        run,
        parts,
        ties,
        (1,),
        [whole_block(part) for part in parts],
        any_block(),
        jax.ShapeDtypeStruct((count, *parts[0].shape), parts[0].dtype),
        [pltpu.SemaphoreType.DMA((count,))],
        cost=least,
    )


def widen_kernel(digit, count, ids, *refs):
    for delta in range(count):
        refs[count][ids[digit] ^ delta] = refs[delta][...].astype(f32)


def widen_parts(run, parts, digit, ties=()):
    count = len(parts)
    shape = jax.ShapeDtypeStruct((count, *parts[0].shape), f32)
    return kernel_call(
        partial(widen_kernel, id_of[digit], count),
        run,
        parts,
        ties,
        (1,),
        [whole_block(part) for part in parts],
        whole_block(shape),
        shape,
    )


class Loader:
    def __init__(self, ids, sems, digit="y"):
        self.core, self.digit = ids[id_of["c"]], ids[id_of[digit]]
        self.sems, self.copies = sems, []

    def put(self, source, target):
        copy = pltpu.make_async_copy(source, target, self.sems.at[len(self.copies)])
        copy.start()
        self.copies.append(copy)

    def rows(self, pieces, start, size, target):
        for turn, piece in enumerate(pieces):
            self.put(piece.at[:, :, pl.ds(start, size)], target.at[:, self.digit ^ turn])

    def columns(self, both_cores, start, size, target):
        for other, pieces in enumerate(both_cores):
            lanes = pl.ds(pl.multiple_of((self.core ^ other) * size, 128), size)
            for turn, piece in enumerate(pieces):
                self.put(
                    piece.at[:, :, pl.ds(start, size)], target.at[:, self.digit ^ turn, :, lanes]
                )

    def wait(self):
        for copy in self.copies:
            copy.wait()


def flat(ref, first=None, count=None):
    value = ref[...] if first is None else ref[pl.ds(first, count)]
    return value.reshape(-1, value.shape[-1])


def place_shape(piece, cols):
    return pltpu.VMEM((piece.shape[0], 2, piece.shape[1], cols), bf16)


def split_kernel(ids, qkv_ref, vec_ref, out_ref, up_ref, down_ref, *outs):
    core = ids[1]
    width = down_ref.shape[1]
    lanes = lax.broadcasted_iota(jnp.int32, (vec_ref.shape[0], 128), 1)
    eye = lanes == lax.broadcasted_iota(jnp.int32, lanes.shape, 0)
    columns = dot_left_t(vec_ref[...], jnp.where(eye, 1.0, 0.0).astype(bf16)).astype(bf16)
    for turn in range(2):
        first, second, down = outs[3 * turn : 3 * turn + 3]
        pairs = []
        for start in range(0, width, 256):
            for part in range(3):
                left = qkv_ref[:, part * width + start : part * width + start + 128]
                right = qkv_ref[:, part * width + start + 128 : part * width + start + 256]
                pairs.append(jnp.where(core == turn, left, right))
        first[...] = jnp.concatenate(pairs + [columns], axis=1)
        second[...] = jnp.concatenate(
            [half_split(core, ref[...])[turn] for ref in (out_ref, up_ref)], axis=1
        )
        down[...] = half_split(core, down_ref[...])[turn]


def split_weights(ids, w_qkv, vectors, w_out, w_up, w_down, ties=()):
    rows, cols = w_qkv.shape
    arrays = [w_qkv, vectors, w_out, w_up, w_down]
    shapes = [
        jax.ShapeDtypeStruct((rows, cols // 2 + 128), bf16),
        jax.ShapeDtypeStruct((rows, (w_out.shape[1] + w_up.shape[1]) // 2), bf16),
        jax.ShapeDtypeStruct((w_down.shape[0], w_down.shape[1] // 2), bf16),
    ] * 2
    outs = kernel_call(
        split_kernel,
        ids,
        arrays,
        ties,
        (1,),
        [whole_block(array) for array in arrays],
        [whole_block(shape) for shape in shapes],
        shapes,
        cost=least,
    )
    return list(zip(outs[:3], outs[3:]))


def load_qkv(load, chunks, targets):
    for turn, target in enumerate(targets):
        cols, split = target.shape[-1], chunks[0][0].shape[-1]
        for start, size, chunk in ((0, split, chunks[0]), (split, cols - split, chunks[1])):
            load.rows(
                chunk[2 * turn : 2 * turn + 2], 0, size, target.at[:, :, :, pl.ds(start, size)]
            )


def qkv_kernel(blk, ids, *refs):
    parts, refs = refs[:blk], refs[blk:]
    chunks, refs = (refs[:4], refs[4:8]), refs[8:]
    x_ref, vec_ref, out_ref, w_ref, w_far_ref, v_ref, sems = refs
    here, core = ids[0], ids[1]
    step = pl.program_id(0)
    cols = out_ref.shape[2]

    @pl.when(step == 0)
    def _():
        load = Loader(ids, sems)
        for piece, part in enumerate(parts):
            load.put(part, x_ref.at[:, here ^ piece])
        load_qkv(load, chunks, (w_ref, w_far_ref))
        used = cols - chunks[0][0].shape[-1]
        load.rows(chunks[1][:2], used, 128, v_ref)
        load.wait()
        vec_ref[...] = flat(v_ref).astype(f32).T[: vec_ref.shape[0]]

    per_seq = x_ref.shape[1] // 2
    rows = x_ref[step // per_seq, pl.ds(2 * (step % per_seq), 2)].reshape(-1, x_ref.shape[-1])
    for turn, weights in enumerate((w_ref, w_far_ref)):
        bias = []
        for start in range(0, vec_ref.shape[1], 256):
            for name in ("bias_query", None, "bias_value"):
                if name is None:
                    bias.append(jnp.zeros((1, 128), f32))
                    continue
                row = vector(vec_ref, name)
                bias.append(
                    jnp.where(
                        core == turn, row[:, start : start + 128], row[:, start + 128 : start + 256]
                    )
                )
        total = dot(rows, flat(weights)) + jnp.concatenate(bias, axis=1)
        out_ref[turn] = total.astype(bf16)


def qkv_projection(ids, parts, pieces, cols, ties=()):
    blk = len(parts)
    seqs, block_rows, width = parts[0].shape
    tokens = seqs * blk * block_rows
    block = 2 * block_rows
    piece = pieces[0][0][0]
    shape = place_shape(piece, cols)
    x_shape = jax.ShapeDtypeStruct((seqs, blk, block_rows, width), bf16)
    v_shape = jax.ShapeDtypeStruct((16, width), f32)
    return kernel_call(
        partial(qkv_kernel, blk),
        ids,
        [*parts, *[piece for chunk in pieces for pair in chunk for piece in pair]],
        ties,
        (tokens // block,),
        [any_block()] * (blk + 8),
        (
            whole_block(x_shape),
            whole_block(v_shape),
            pl.BlockSpec((2, block, cols), lambda i, ids: (0, i, 0)),
        ),
        (x_shape, v_shape, jax.ShapeDtypeStruct((2, tokens, cols), bf16)),
        [shape, shape, place_shape(piece, 128), pltpu.SemaphoreType.DMA((blk + 10,))],
        cost=brief,
    )


def attend_kernel(head_dim, ids, qkv_ref, *rest):
    pieces, (o_ref, lse_ref) = rest[:-2], rest[-2:]
    here = ids[0]
    pair, seq = pl.program_id(1), pl.program_id(2)
    length, wide = o_ref.shape[1:]
    per = wide // head_dim
    rows = pieces[0].shape[1]
    lanes = lax.broadcasted_iota(jnp.int32, (1, wide), 1)
    log_lanes = lax.broadcasted_iota(jnp.int32, (1, lse_ref.shape[2]), 1)
    keys, values = qkv_ref[0, :, wide : 2 * wide], qkv_ref[0, :, 2 * wide :]
    for first in range(0, len(pieces), 2):
        span = range(first, min(first + 2, len(pieces)))
        places = [piece_rows(here, piece, rows) for piece in span]
        queries = stack_pieces(qkv_ref, places, slice(0, wide))
        out, logs = None, []
        for head in range(per):
            mine = lanes // head_dim == head
            scores = dot_right_t(jnp.where(mine, queries, 0), keys) * (head_dim**-0.5 * log2e)
            addend = jnp.concatenate([pieces[piece][head] for piece in span], axis=0)
            scores = scores + addend.astype(f32)
            top = jnp.max(scores, axis=1, keepdims=True)
            weights = jnp.exp2(scores - top)
            total = jnp.sum(weights, axis=1, keepdims=True)
            part = dot(weights.astype(bf16), values) * (1.0 / total)
            out = part if out is None else jnp.where(mine, part, out)
            logs.append(top + jnp.log2(total))
        for index, place_ in enumerate(places):
            here_rows = slice(index * rows, (index + 1) * rows)
            o_ref[0, place_, :] = out[here_rows].astype(bf16)
            start = seq * length + (here ^ span[index]) * rows
            log_place = pl.ds(pl.multiple_of(start, rows), rows)
            kept = lse_ref[0, log_place, :]
            for head in range(per):
                kept = jnp.where(log_lanes == pair * per + head, logs[head][here_rows], kept)
            lse_ref[0, log_place, :] = kept


def attend_back_kernel(head_dim, ids, qkv_ref, o_ref, g_ref, lse_ref, *rest):
    pieces, (out_ref, sums_ref) = rest[:-2], rest[-2:]
    here = ids[0]
    pair, seq = pl.program_id(1), pl.program_id(2)
    length, wide = o_ref.shape[1:]
    per = wide // head_dim
    rows = pieces[0].shape[1]
    lanes = lax.broadcasted_iota(jnp.int32, (1, wide), 1)
    log_lanes = lax.broadcasted_iota(jnp.int32, (1, lse_ref.shape[2]), 1)
    keys, values = qkv_ref[0, :, wide : 2 * wide], qkv_ref[0, :, 2 * wide :]
    everything = slice(None)
    back = head_dim**-0.5
    dk = jnp.zeros(keys.shape, f32)
    dv = jnp.zeros(keys.shape, f32)
    for first in range(0, len(pieces), 2):
        span = range(first, min(first + 2, len(pieces)))
        places = [piece_rows(here, piece, rows) for piece in span]
        queries = stack_pieces(qkv_ref, places, slice(0, wide))
        ups = stack_pieces(g_ref, places, everything)
        products = ups.astype(f32) * stack_pieces(o_ref, places, everything).astype(f32)
        starts = [seq * length + (here ^ piece) * rows for piece in span]
        log_places = [pl.ds(pl.multiple_of(at, rows), rows) for at in starts]
        logs = stack_pieces(lse_ref, log_places, everything)
        dq = None
        for head in range(per):
            mine = lanes // head_dim == head
            q_mine, g_mine = jnp.where(mine, queries, 0), jnp.where(mine, ups, 0)
            inner = jnp.sum(jnp.where(mine, products, 0.0), axis=1, keepdims=True)
            log = jnp.sum(
                jnp.where(log_lanes == pair * per + head, logs, 0.0), axis=1, keepdims=True
            )
            scores = dot_right_t(q_mine, keys) * (back * log2e)
            addend = jnp.concatenate([pieces[piece][head] for piece in span], axis=0)
            exact = jnp.exp2(scores + addend.astype(f32) - log)
            grads = (exact * (dot_right_t(g_mine, values) - inner)).astype(bf16)
            dv = dv + dot_left_t(exact.astype(bf16), g_mine)
            dk = dk + dot_left_t(grads, q_mine)
            part = dot(grads, keys)
            dq = part if dq is None else jnp.where(mine, part, dq)
        for index, place_ in enumerate(places):
            out_ref[0, place_, :wide] = (dq[index * rows : (index + 1) * rows] * back).astype(bf16)
    out_ref[0, :, wide : 2 * wide] = (dk * back).astype(bf16)
    out_ref[0, :, 2 * wide :] = dv.astype(bf16)
    sums = dot(jnp.ones((sums_ref.shape[2], length), bf16), out_ref[0])

    @pl.when(seq == 0)
    def _():
        sums_ref[0, 0] = sums

    @pl.when(seq > 0)
    def _():
        sums_ref[0, 0] += sums


def attention_specs(joined, mask_parts):
    rows, length = mask_parts[0].shape[1:]

    def block(cols):
        return pl.BlockSpec((1, length, cols), lambda r, p, s, ids: (r, s, p))

    logs = pl.BlockSpec((1, joined.shape[1], 128), lambda r, p, s, ids: (r, 0, 0))
    mask = pl.BlockSpec((2, rows, length), lambda r, p, s, ids: (2 * p + (ids[1] ^ r), 0, 0))
    return block, logs, [mask] * len(mask_parts)


def attend(ids, joined, mask_parts, seqs, head_dim, ties=()):
    tokens, cols = joined.shape[1:]
    block, logs, masks = attention_specs(joined, mask_parts)
    width = cols // 3
    return kernel_call(
        partial(attend_kernel, head_dim),
        ids,
        [joined, *mask_parts],
        ties,
        (2, width // 128, seqs),
        [block(384)] + masks,
        (block(128), logs),
        (
            jax.ShapeDtypeStruct((2, tokens, width), bf16),
            jax.ShapeDtypeStruct((2, tokens, 128), f32),
        ),
        cost=brief,
    )


def attend_back(
    ids, joined, attended, upstream, logs, mask_parts, seqs, head_dim, ties=()
):
    tokens, cols = joined.shape[1:]
    count = cols // 384
    block, log_block, masks = attention_specs(joined, mask_parts)
    return kernel_call(
        partial(attend_back_kernel, head_dim),
        ids,
        [joined, attended, upstream, logs, *mask_parts],
        ties,
        (2, count, seqs),
        [block(384), block(128), block(128), log_block] + masks,
        (
            block(384),
            pl.BlockSpec((1, 1, 8, 384), lambda r, p, s, ids: (r, p, 0, 0)),
        ),
        (
            jax.ShapeDtypeStruct((2, tokens, cols), bf16),
            jax.ShapeDtypeStruct((2, count, 8, 384), f32),
        ),
    )


def out_kernel(ids, att_ref, x_ref, vec_ref, *refs):
    pieces, (first_ref, low_ref, w_ref, sems) = (refs[:2], refs[2:4]), refs[4:]

    @pl.when(pl.program_id(0) == 0)
    def _():
        load = Loader(ids, sems)
        load.columns(pieces, 0, w_ref.shape[-1] // 2, w_ref)
        load.wait()

    attended = pair_order(ids[1], att_ref[0], att_ref[1], 128)
    first = x_ref[...].astype(f32) + (dot(attended, flat(w_ref)) + vector(vec_ref, "bias_out"))
    first_ref[...] = first
    gain, shift = vector(vec_ref, "gain_first"), vector(vec_ref, "shift_first")
    low_ref[...] = (norm_stats(first)[0] * gain + shift).astype(bf16)


def out_projection(ids, attended, pieces, token_rows, vectors, block, ties=()):
    tokens, width = token_rows.shape
    row = pl.BlockSpec((block, width), lambda i, ids: (i, 0))
    return kernel_call(
        out_kernel,
        ids,
        [attended, token_rows, vectors, *pieces[0], *pieces[1]],
        ties,
        (tokens // block,),
        [
            pl.BlockSpec((2, block, width // 2), lambda i, ids: (0, i, 0)),
            row,
            whole_block(vectors),
        ]
        + [any_block()] * 4,
        (row, row),
        (jax.ShapeDtypeStruct((tokens, width), f32), jax.ShapeDtypeStruct((tokens, width), bf16)),
        [place_shape(pieces[0][0], width), pltpu.SemaphoreType.DMA((4,))],
        cost=brief,
    )


def up_kernel(chunk, steps, ids, h_ref, b_ref, *refs):
    pieces, (act_ref, der_ref, w_ref, w_far_ref, sems) = (refs[:2], refs[2:4]), refs[4:]
    step = pl.program_id(0)
    block = act_ref.shape[1]
    cols = w_ref.shape[-1]

    @pl.when(step == 0)
    def _():
        load = Loader(ids, sems)
        start = pieces[0][0].shape[-1] - cols
        load.rows(pieces[0], start, cols, w_ref)
        load.rows(pieces[1], start, cols, w_far_ref)
        load.wait()

    def run(ref):
        lanes = pl.ds(pl.multiple_of((step % steps) * block, block), block)
        weights = ref[:, :, :, lanes].reshape(-1, block)
        bias = b_ref[0]
        for first in range(0, h_ref.shape[0], chunk):
            place_ = slice(first, first + chunk)
            gate = dot(h_ref[place_, :], weights) + bias
            share = 0.5 + 0.5 * lax.erf(gate * math.sqrt(0.5))
            bell = jnp.exp2((-0.5 * log2e) * (gate * gate)) * (1.0 / math.sqrt(2.0 * math.pi))
            act_ref[place_, :] = (gate * share).astype(bf16)
            der_ref[place_, :] = (share + gate * bell).astype(bf16)

    pl.when(step < steps)(lambda: run(w_ref))
    pl.when(step >= steps)(lambda: run(w_far_ref))


def up_projection(ids, hidden_low, pieces, bias, ties=()):
    tokens, width = hidden_low.shape
    half = bias.shape[2]
    block = width
    steps = half // block
    out = pl.BlockSpec((tokens, block), lambda j, ids: (0, (ids[1] ^ (j // steps)) * steps + j % steps))
    shape = jax.ShapeDtypeStruct((tokens, 2 * half), bf16)
    scratch = place_shape(pieces[0][0], half)
    return kernel_call(
        partial(up_kernel, 128, steps),
        ids,
        [hidden_low, bias, *pieces[0], *pieces[1]],
        ties,
        (2 * steps,),
        [
            whole_block(hidden_low),
            pl.BlockSpec((1, 1, block), lambda j, ids: (ids[1] ^ (j // steps), 0, j % steps)),
        ]
        + [any_block()] * 4,
        (out, out),
        (shape, shape),
        [scratch, scratch, pltpu.SemaphoreType.DMA((4,))],
        cost=brief,
    )


def down_kernel(blk, ids, *refs):
    pos_ref, cot_ref, act_ref, der_ref, first_ref, vec_ref = refs[:6]
    mine, other = refs[6:8], refs[8:10]
    outs, refs = refs[10 : 10 + blk], refs[10 + blk :]
    gss_ref, gdi_ref, gate_ref, sums_ref, up_ref, w_ref, sems = refs
    step = pl.program_id(0)
    here = ids[0]
    seqs, rows, width = first_ref.shape

    @pl.when(step == 0)
    def _():
        load = Loader(ids, sems)
        load.columns((mine, other), 0, width // 2, w_ref)
        load.wait()

    weights = flat(w_ref)
    cols = act_ref.shape[-1]
    normed_one = norm_stats(first_ref[...].reshape(-1, width))[0]
    hidden = normed_one * vector(vec_ref, "gain_first") + vector(vec_ref, "shift_first")
    product = dot(act_ref[...].reshape(-1, cols), weights)
    second = hidden + (product + vector(vec_ref, "bias_down"))
    normed, inverse = norm_stats(second)
    gain = vector(vec_ref, "gain_second")
    result = (normed * gain + vector(vec_ref, "shift_second")).astype(bf16)
    for piece, out in enumerate(outs):

        @pl.when(step == piece)
        def _():
            out[...] = result.reshape(out.shape)

    slots = pos_ref.shape[-1]
    token = lax.broadcasted_iota(jnp.int32, (rows, slots), 0) + (here ^ step) * rows
    upstream = jnp.concatenate(
        [
            dot(jnp.where(token == pos_ref[seq], 1.0, 0.0).astype(bf16), cot_ref[seq])
            for seq in range(seqs)
        ],
        axis=0,
    )
    grad = norm_pull(upstream, normed, inverse, gain)
    gss_ref[...] = grad.reshape(gss_ref.shape)
    low = grad.astype(bf16)
    gdi_ref[...] = low.reshape(gdi_ref.shape)
    add_sums(sums_ref, [low.astype(f32), upstream * normed, upstream])
    grad_gate = dot_right_t(low, weights) * der_ref[...].reshape(-1, cols).astype(f32)
    grad_gate = grad_gate.astype(bf16)
    gate_ref[...] = grad_gate.reshape(gate_ref.shape)
    add_sums(up_ref, [grad_gate.astype(f32)])


def down_projection(
    ids, active, slope, first_sum, pieces, vectors, marks, cot_values, seqs, blk, ties=()
):
    tokens, cols = active.shape
    width = first_sum.shape[1]
    length = tokens // seqs
    rows = length // blk

    def block(size):
        return pl.BlockSpec((seqs, rows, size), lambda d, ids: (0, ids[0] ^ d, 0))

    def shape(size, dtype):
        return jax.ShapeDtypeStruct((seqs, length, size), dtype)

    piece = jax.ShapeDtypeStruct((seqs, rows, width), bf16)
    sums = jax.ShapeDtypeStruct((8, width), f32)
    up_sums = jax.ShapeDtypeStruct((8, cols), f32)
    slots = marks.shape[-1]
    by_seq = [array.reshape(seqs, length, -1) for array in (active, slope, first_sum)]
    outs = kernel_call(
        partial(down_kernel, blk),
        ids,
        [marks, cot_values, *by_seq, vectors, *pieces[0], *pieces[1]],
        ties,
        (blk,),
        [
            whole_block(marks),
            pl.BlockSpec((seqs, slots, width), lambda d, ids: (ids[0], 0, 0)),
            block(cols),
            block(cols),
            block(width),
            whole_block(vectors),
        ]
        + [any_block()] * 4,
        [whole_block(piece)] * blk
        + [block(width), block(width), block(cols), whole_block(sums), whole_block(up_sums)],
        [piece] * blk + [shape(width, f32), shape(width, bf16), shape(cols, bf16), sums, up_sums],
        [place_shape(pieces[0][0], width), pltpu.SemaphoreType.DMA((4,))],
    )
    rest = outs[blk:]
    return outs[:blk], [array.reshape(tokens, -1) for array in rest[:3]], rest[3:]


def first_back_kernel(ids, gate_ref, gss_ref, first_ref, vec_ref, *refs):
    pieces, refs = (refs[:2], refs[2:4]), refs[4:]
    gfs_ref, branch_ref, att_ref, sums_ref, w_ref, w_out_ref, sems = refs
    width = gss_ref.shape[1]

    @pl.when(pl.program_id(0) == 0)
    def _():
        load = Loader(ids, sems)
        load.columns(pieces, width // 2, w_ref.shape[-1] // 2, w_ref)
        load.columns(pieces, 0, width // 2, w_out_ref)
        load.wait()

    grad_hidden = gss_ref[...] + dot_right_t(gate_ref[...], flat(w_ref))
    normed, inverse = norm_stats(first_ref[...])
    grad = norm_pull(grad_hidden, normed, inverse, vector(vec_ref, "gain_first"))
    gfs_ref[...] = grad
    low = grad.astype(bf16)
    branch_ref[...] = low
    grad_att = dot_right_t(low, flat(w_out_ref)).astype(bf16)
    att_ref[0], att_ref[1] = pair_split(ids[1], grad_att, 128)
    add_sums(sums_ref, [low.astype(f32), grad_hidden * normed, grad_hidden])


def first_back(ids, grad_gate, grad_second_sum, first_sum, pieces, vectors, block, ties=()):
    tokens, cols = grad_gate.shape
    width = first_sum.shape[1]

    def row(size):
        return pl.BlockSpec((block, size), lambda i, ids: (i, 0))

    def shape(size, dtype):
        return jax.ShapeDtypeStruct((tokens, size), dtype)

    sums = jax.ShapeDtypeStruct((8, width), f32)
    piece = pieces[0][0]
    return kernel_call(
        first_back_kernel,
        ids,
        [grad_gate, grad_second_sum, first_sum, vectors, *pieces[0], *pieces[1]],
        ties,
        (tokens // block,),
        [row(cols), row(width), row(width), whole_block(vectors)] + [any_block()] * 4,
        (
            row(width),
            row(width),
            pl.BlockSpec((2, block, width // 2), lambda i, ids: (0, i, 0)),
            whole_block(sums),
        ),
        (
            shape(width, f32),
            shape(width, bf16),
            jax.ShapeDtypeStruct((2, tokens, width // 2), bf16),
            sums,
        ),
        [place_shape(piece, cols), place_shape(piece, width), pltpu.SemaphoreType.DMA((8,))],
    )


def beside(array, devices, per):
    groups = array.reshape(devices, per, -1, array.shape[-1])
    return jnp.concatenate(
        [groups[:, index].reshape(-1, array.shape[-1]) for index in range(per)], axis=1
    )


def down_grad_kernel(devices, per, ids, act_ref, g_ref, keep_ref, send_ref):
    halves = half_split(ids[1], dot_left_t(act_ref[...], g_ref[...]))
    for half, out in zip(halves, (keep_ref, send_ref)):
        out[...] = (beside(half, devices, per) if per > 1 else half).astype(bf16)


def down_grad(ids, active, grad_down_in, devices, ties=()):
    tokens, cols = active.shape
    width = grad_down_in.shape[1]
    per, block = cols // width, width
    inside = (width // devices) % 8 == 0
    groups = per if inside else 1
    out = pl.BlockSpec((block // groups, groups * width // 2), lambda i, ids: (i, 0))
    shape = jax.ShapeDtypeStruct((cols // groups, groups * width // 2), bf16)
    halves = kernel_call(
        partial(down_grad_kernel, devices // per, groups),
        ids,
        [active, grad_down_in],
        ties,
        (cols // block,),
        [pl.BlockSpec((tokens, block), lambda i, ids: (0, i)), whole_block(grad_down_in)],
        (out, out),
        (shape, shape),
    )
    return halves if inside else [beside(half, devices, per) for half in halves]


def up_grad_kernel(ids, h_ref, g_ref, g_far_ref, keep_ref, send_ref):
    keep_ref[...] = dot_left_t(h_ref[...], g_ref[...]).astype(bf16)
    send_ref[...] = dot_left_t(h_ref[...], g_far_ref[...]).astype(bf16)


def up_grad(ids, hidden_low, grad_gate, block, ties=()):
    tokens, width = hidden_low.shape
    cols = grad_gate.shape[1] // 2
    steps = cols // block
    shape = jax.ShapeDtypeStruct((width, cols), bf16)
    out = pl.BlockSpec((width, block), lambda j, ids: (0, j))
    return kernel_call(
        up_grad_kernel,
        ids,
        [hidden_low, grad_gate, grad_gate],
        ties,
        (steps,),
        [
            whole_block(hidden_low),
            pl.BlockSpec((tokens, block), lambda j, ids: (0, ids[1] * steps + j)),
            pl.BlockSpec((tokens, block), lambda j, ids: (0, (1 - ids[1]) * steps + j)),
        ],
        (out, out),
        (shape, shape),
    )


def left_grad_kernel(
    ids,
    x_ref,
    g_ref,
    att_ref,
    branch_ref,
    sums_ref,
    first_ref,
    second_ref,
    up_ref,
    keep_ref,
    send_ref,
):
    core, step = ids[1], pl.program_id(0)
    attended = pair_order(core, att_ref[0], att_ref[1], 128)
    out_grads = half_split(core, dot_left_t(attended, branch_ref[...]))
    sums = [sums_ref[turn, step][:1] for turn in range(2)]
    rows = [
        pair_order(core, sums[0][:, at : at + 128], sums[1][:, at : at + 128], 128)
        for at in (0, 256)
    ]
    rows += [first_ref[:3], second_ref[:3], up_ref[...]]
    used = sum(row.shape[0] for row in rows)
    rows = jnp.concatenate(rows + [jnp.zeros((16 - used, rows[0].shape[1]), f32)], axis=0)
    lanes = lax.broadcasted_iota(jnp.int32, (16, 128), 1)
    eye = lanes == lax.broadcasted_iota(jnp.int32, lanes.shape, 0)
    columns = dot_left_t(rows.astype(bf16), jnp.where(eye, 1.0, 0.0).astype(bf16))
    for turn, out in enumerate((keep_ref, send_ref)):
        grad = dot_left_t(x_ref[...], g_ref[turn])
        out[...] = jnp.concatenate([grad, out_grads[turn], columns], axis=1).astype(bf16)


def left_grad(ids, left, grads, attended, grad_branch, sums, totals, ties=()):
    tokens, width = left.shape
    cols = grads.shape[2] + width // 2 + 128
    shape = jax.ShapeDtypeStruct((width, cols), bf16)
    out = pl.BlockSpec((256, cols), lambda i, ids: (i, 0))
    return kernel_call(
        left_grad_kernel,
        ids,
        [left, grads, attended, grad_branch, sums, *totals],
        ties,
        (width // 256,),
        [
            pl.BlockSpec((tokens, 256), lambda i, ids: (0, i)),
            whole_block(grads),
            pl.BlockSpec((2, tokens, 128), lambda i, ids: (0, 0, i)),
            whole_block(grad_branch),
            whole_block(sums),
        ]
        + [pl.BlockSpec((array.shape[0], 256), lambda i, ids: (0, i)) for array in totals],
        (out, out),
        (shape, shape),
    )


def input_grad_kernel(blk, ids, g_ref, gfs_ref, *refs):
    chunks, refs = (refs[:4], refs[4:8]), refs[8:]
    outs, (w_ref, w_far_ref, sems) = refs[:blk], refs[blk:]
    step = pl.program_id(0)

    @pl.when(step == 0)
    def _():
        load = Loader(ids, sems)
        load_qkv(load, chunks, (w_ref, w_far_ref))
        load.wait()

    width = gfs_ref.shape[-1]
    total = gfs_ref[...].reshape(-1, width)
    for turn, weights in enumerate((w_ref, w_far_ref)):
        total = total + dot_right_t(g_ref[turn].reshape(-1, g_ref.shape[-1]), flat(weights))
    for piece, out in enumerate(outs):

        @pl.when(step == piece)
        def _():
            out[...] = total.astype(bf16).reshape(out.shape)


def input_grad(ids, grads, grad_first_sum, pieces, seqs, blk, ties=()):
    tokens, width = grad_first_sum.shape
    length = tokens // seqs
    rows = length // blk
    cols = grads.shape[2]
    piece = jax.ShapeDtypeStruct((seqs, rows, width), bf16)
    shape = place_shape(pieces[0][0][0], cols)
    pieces = [piece for chunk in pieces for pair in chunk for piece in pair]
    return kernel_call(
        partial(input_grad_kernel, blk),
        ids,
        [
            grads.reshape(2, seqs, length, cols),
            grad_first_sum.reshape(seqs, length, width),
            *pieces,
        ],
        ties,
        (blk,),
        [
            pl.BlockSpec((2, seqs, rows, cols), lambda d, ids: (0, 0, ids[0] ^ d, 0)),
            pl.BlockSpec((seqs, rows, width), lambda d, ids: (0, ids[0] ^ d, 0)),
        ]
        + [any_block()] * len(pieces),
        [whole_block(piece)] * blk,
        [piece] * blk,
        [shape, shape, pltpu.SemaphoreType.DMA((len(pieces),))],
    )


class Grid:
    def __init__(self, mesh):
        batch, blk = mesh.shape["batch"], mesh.shape["blk"]
        self.sizes = {"z": batch // 2, "y": 2, "x": blk // 2, "c": 2}
        self.strides = {"c": 1, "x": 2, "y": blk, "z": 2 * blk}
        self.total = batch * blk
        self.blk = blk

    def digit(self, name):
        index = lax.axis_index("batch") * self.blk + lax.axis_index("blk")
        return (index // self.strides[name]) % self.sizes[name]

    def swap(self, array, name, delta=1):
        size, stride = self.sizes[name], self.strides[name]
        pairs = []
        for index in range(self.total):
            here = (index // stride) % size
            pairs.append((index, index + ((here ^ delta) - here) * stride))
        return lax.ppermute(array, both, pairs)

    def swap_blk(self, array, delta):
        pairs = [(index, index ^ delta) for index in range(self.total)]
        return lax.ppermute(array, both, pairs)


def place(parts, index):
    if len(parts) == 1:
        return parts[0][None]
    rows = []
    for target in range(len(parts)):
        row = parts[0]
        for delta in range(1, len(parts)):
            row = jnp.where(index == target ^ delta, parts[delta], row)
        rows.append(row)
    return jnp.stack(rows)


def pick(array, index):
    return lax.dynamic_index_in_dim(array, index, axis=0, keepdims=False)


def gather_core(grid, mine, other):
    cols = mine.shape[1]
    return place([mine, grid.swap(other, "c")], grid.digit("c")).reshape(-1, cols)


def gather_step(grid, run, held, name, *ties):
    parts = [grid.swap(held, name, d) for d in range(1, grid.sizes[name])]
    return place_parts(run, [held, *parts], name, ties)


def gather_last(grid, held, name):
    far = grid.swap(held, name)
    if held.shape[1] % 16 == 0:
        return [held, far]
    where = grid.digit(name)
    whole = jnp.moveaxis(place([held, far], where), 0, 1).reshape(4, 2, -1, held.shape[2])
    return [lax.dynamic_index_in_dim(whole, where ^ d, 1, keepdims=False) for d in range(2)]


def gather_pieces(grid, run, held, *ties):
    near, far = held
    if ties:
        (far,) = after(run, [far], *ties)
    return [[near, far], [grid.swap(near, "c"), grid.swap(far, "c")]]


def add_low(*parts):
    total = parts[0].astype(f32)
    for part in parts[1:]:
        total = total + part.astype(f32)
    return total


def fold_kernel(count, groups, ids, *refs):
    outs = refs[len(refs) - count :]
    refs = list(refs[: len(refs) - count])
    for out in outs:
        sums = []
        for terms in groups:
            picked, refs = refs[:terms], refs[terms:]
            total = picked[0][...].astype(f32)
            for ref in picked[1:]:
                total = total + ref[...].astype(f32)
            sums.append(total.astype(out.dtype))
        out[...] = jnp.concatenate(sums, axis=-1).reshape(out.shape)


def fold(ids, which, groups, ties):
    outer, count, rows, unused = groups[0][0].shape
    steps = 2 if outer % 2 == 0 else 1
    part = outer // steps

    def term_block(cols, delta):
        return pl.BlockSpec((part, 1, rows, cols), lambda i, ids: (i, ids[which] ^ delta, 0, 0))

    terms = [term for group in groups for term in group]
    cols = sum(group[0].shape[3] for group in groups)
    shape = jax.ShapeDtypeStruct((outer, rows, cols), bf16)
    return kernel_call(
        partial(fold_kernel, count, [len(group) for group in groups]),
        ids,
        [term for delta in range(count) for term in terms],
        ties,
        (steps,),
        [term_block(term.shape[3], delta) for delta in range(count) for term in terms],
        [pl.BlockSpec((part, rows, cols), lambda i, ids: (i, 0, 0))] * count,
        [shape] * count,
    )


class Scatter:
    def __init__(self, grid, ids, pairs, order):
        self.grid, self.ids, self.order = grid, ids, list(order)
        sizes = grid.sizes
        self.left = [("z", sizes["z"]), ("y", sizes["y"]), ("x", sizes["x"])]
        self.last = 2 * (pairs[0][0].shape[0] // grid.total)
        self.groups = [[keep, grid.swap(send, "c")] for keep, send in pairs]

    def shaped(self, *shape):
        return [[term.reshape(*shape, term.shape[-1]) for term in group] for group in self.groups]

    def step(self, ties=()):
        name = self.order.pop(0)
        index = [left for left, unused in self.left].index(name)
        count = self.left[index][1]
        outer = math.prod(size for unused, size in self.left[:index])
        inner = math.prod(size for unused, size in self.left[index + 1 :]) * self.last
        sums = fold(self.ids, id_of[name], self.shaped(outer, count, inner), ties)
        self.left.pop(index)
        sent = [self.grid.swap(sums[delta], name, delta) for delta in range(1, count)]
        self.groups = [[sums[0], *sent]]

    def end(self, ties=()):
        mine, other = fold(self.ids, id_of["c"], self.shaped(1, 2, self.last // 2), ties)
        mine, other = [array.reshape(array.shape[1:]) for array in (mine, other)]
        return mine.astype(f32), self.grid.swap(other, "c").astype(f32)


def in_order(core, mine, other):
    return jnp.where(core == 0, mine, other), jnp.where(core == 0, other, mine)


def local(
    grid,
    inputs,
    w_qkv,
    bias_query,
    bias_value,
    w_out,
    bias_out,
    gain_first,
    shift_first,
    w_up,
    bias_up,
    w_down,
    bias_down,
    gain_second,
    shift_second,
    dam_mask,
    positions,
    counts,
    cot_values,
):
    groups, block_rows, width = inputs.shape
    head_count = dam_mask.shape[0]
    head_dim = width // head_count
    blk = grid.blk
    seqs = groups // blk
    length = blk * block_rows
    tokens = seqs * length
    here, core = lax.axis_index("blk"), grid.digit("c")
    ids = Run(jnp.stack([here, core] + [grid.digit(name) for name in "yzx"]).astype(jnp.int32))
    rows = w_qkv.shape[0]
    up_per = bias_up.shape[0] // rows
    half = width // 2
    pairs = width // 256

    vectors = (
        bias_query,
        bias_value,
        bias_out,
        gain_first,
        shift_first,
        bias_down,
        gain_second,
        shift_second,
    )
    stacked = jnp.concatenate(
        [
            jnp.stack(vectors),
            bias_up.reshape(rows, up_per).T,
            jnp.zeros((16 - len(vectors) - up_per, rows), bf16),
        ]
    )
    halves = split_weights(ids, w_qkv, stacked, w_out, w_up, w_down)
    first_near, second_near, down_near = [gather_core(grid, *pair) for pair in halves]

    def over_x(held):
        return gather_step(grid, ids, held, "x").reshape(-1, held.shape[1])

    first_near = over_x(first_near)
    event = ids.token
    split = first_near.shape[1] // 2

    by_home = inputs.reshape(blk, seqs, block_rows, width)
    parts = [pick(by_home, here ^ delta) for delta in range(blk)]
    parts[2:] = after(ids, parts[2:], event)
    parts[1:] = [grid.swap_blk(parts[delta], delta) for delta in range(1, blk)]
    second_near = over_x(second_near)
    ties = [ids.token, *parts[2:]]
    down_near = over_x(down_near)
    ties.append(ids.token)
    addend = jnp.where(dam_mask > 0, 0.0, masked_score).astype(bf16)
    (addend,) = after(ids, [addend], event)
    mask_parts = [addend, grid.swap(addend, "c")]
    first_z = gather_step(grid, ids, first_near[:, :split], "z")
    (rest,) = after(ids, [first_near[:, split:]], ids.token)
    first_y = gather_last(grid, first_z, "y")
    rest_z = gather_step(grid, ids, rest, "z", *ties)
    (second_near,) = after(ids, [second_near], ids.token)
    rest_y = gather_last(grid, rest_z, "y")
    first_pieces = [gather_pieces(grid, ids, held) for held in (first_y, rest_y)]
    event = [ids.token]
    if grid.sizes["x"] > 1:
        (far,) = after(ids, [grid.swap(addend, "x")], *event)
        mask_parts += [far, grid.swap(far, "c")]
        event.append(ids.token)
    second_z = gather_step(grid, ids, second_near, "z", *event)
    (down_near,) = after(ids, [down_near], ids.token)
    second_y = gather_last(grid, second_z, "y")
    token_rows, vector_rows, joined = qkv_projection(ids, parts, first_pieces, 3 * half, ties=[ids.token])
    token_rows = token_rows.reshape(tokens, width)
    first_row = len(vectors)
    up_bias = vector_rows[first_row : first_row + up_per].T.reshape(2, 1, -1)

    attended, logs = attend(ids, joined, mask_parts, seqs, head_dim, ties=[ids.token])
    down_z = gather_step(grid, ids, down_near, "z", ids.token)
    down_y = gather_last(grid, down_z, "y")
    second_pieces = gather_pieces(grid, ids, second_y, ids.token)
    first_sum, hidden_low = out_projection(
        ids, attended, second_pieces, token_rows, vector_rows, 2 * block_rows
    )
    active, slope = up_projection(ids, hidden_low, second_pieces, up_bias)
    down_pieces = gather_pieces(grid, ids, down_y, ids.token)

    my_positions = pick(positions.reshape(blk, seqs, -1), here)
    my_counts = pick(counts.reshape(blk, seqs), here)
    live = jnp.arange(positions.shape[1], dtype=jnp.int32)[None, :] < my_counts[:, None]
    marks = jnp.where(live, my_positions, -1)[:, None, :]
    result, (grad_second_sum, grad_down_in, grad_gate), (second_sums, up_sums) = down_projection(
        ids, active, slope, first_sum, down_pieces, vector_rows, marks, cot_values, seqs, blk
    )

    def home(pieces):
        return [pieces[0]] + [grid.swap_blk(pieces[delta], delta) for delta in range(1, blk)]

    result = home(result)
    down_halves = down_grad(ids, active, grad_down_in, grid.total)
    up_halves = up_grad(ids, hidden_low, grad_gate, width, ties=[ids.token])
    ffn_sum = Scatter(grid, ids, [up_halves, down_halves], "yzx")
    ffn_sum.step([ids.token])
    grad_first_sum, grad_branch, grad_attended, first_sums = first_back(
        ids,
        grad_gate,
        grad_second_sum,
        first_sum,
        second_pieces,
        vector_rows,
        2 * block_rows,
        ties=[ids.token],
    )
    result = after(ids, result, ids.token)
    grads, grad_sums = attend_back(
        ids,
        joined,
        attended,
        grad_attended,
        logs,
        mask_parts,
        seqs,
        head_dim,
        ties=[ids.token],
    )
    ffn_sum.step([ids.token])
    up_rows = up_sums[0].reshape(width, up_per).T
    totals = [first_sums, second_sums, up_rows]
    halves = left_grad(
        ids, token_rows, grads, attended, grad_branch, grad_sums, totals, ties=[ids.token]
    )
    att_sum = Scatter(grid, ids, [halves], "xyz")
    att_sum.step([ids.token])
    sent = input_grad(ids, grads, grad_first_sum, first_pieces, seqs, blk, ties=[ids.token])
    grad_inputs = home(sent)
    att_sum.step([ids.token])
    ffn_sum.step([ids.token])
    activations = place_parts(ids, result, "here", [ids.token])
    activations = activations.reshape(groups, block_rows, width)
    att_sum.step([ids.token])
    share_ffn = ffn_sum.end([ids.token])
    grad_inputs = widen_parts(ids, grad_inputs, "here", [ids.token])
    grad_inputs = grad_inputs.reshape(groups, block_rows, width)
    share_att = att_sum.end([ids.token])

    cols = grads.shape[2]
    by_core = jnp.stack(in_order(core, *[share[:, :cols] for share in share_att]), axis=0)
    by_core = by_core.reshape(2, rows, pairs, 3, 128)
    share_qkv = by_core.transpose(1, 3, 2, 0, 4).reshape(rows, 3 * width)
    share_out = jnp.concatenate(
        in_order(core, *[share[:, cols : cols + half] for share in share_att]), axis=1
    )
    up_cols = up_halves[0].shape[1]
    share_up = [share[:, :up_cols] for share in share_ffn]
    share_down = [
        share[:, up_cols:].reshape(rows, up_per, half).transpose(1, 0, 2).reshape(-1, half)
        for share in share_ffn
    ]
    shares = share_att[0][:, cols + half :]
    share_vectors = [shares[:, index] for index in range(len(vectors))]
    share_bias_up = shares[:, len(vectors) : len(vectors) + up_per].reshape(-1)
    (
        share_bias_query,
        share_bias_value,
        share_bias_out,
        share_gain_first,
        share_shift_first,
        share_bias_down,
        share_gain_second,
        share_shift_second,
    ) = share_vectors
    return (
        activations,
        grad_inputs,
        share_qkv,
        share_bias_query,
        share_bias_value,
        share_out,
        share_bias_out,
        share_gain_first,
        share_shift_first,
        jnp.concatenate(in_order(core, *share_up), axis=1),
        share_bias_up,
        jnp.concatenate(in_order(core, *share_down), axis=1),
        share_bias_down,
        share_gain_second,
        share_shift_second,
    )


def solution(mesh):
    sharded = P(both)
    rows = P(both, None)
    whole = P("batch", "blk", None)
    return jax.shard_map(
        partial(local, Grid(mesh)),
        mesh=mesh,
        in_specs=(
            whole,
            rows,
            sharded,
            sharded,
            rows,
            sharded,
            sharded,
            sharded,
            rows,
            sharded,
            rows,
            sharded,
            sharded,
            sharded,
            P(None, "blk", None),
            P("batch", None),
            P("batch"),
            P("batch", None, None),
        ),
        out_specs=(
            whole,
            whole,
            rows,
            sharded,
            sharded,
            rows,
            sharded,
            sharded,
            sharded,
            rows,
            sharded,
            rows,
            sharded,
            sharded,
            sharded,
        ),
        check_vma=False,
    )
```

time: 700 us -> 415 us (0.59); the launches traced: 688 us -> 414 us
  Pallas kernels: 0 us -> 206 us
  matrix products: 193 us -> 0 us
  waiting for transfers between devices: 226 us -> 104 us
  other arithmetic: 90.2 us -> 6.78 us
  local copies, waits for them, and re-layouts: 81.6 us -> 34.6 us
  starting transfers between devices: 93.7 us -> 60.3 us
    pallas_call x0 -> x38, Pallas kernels: none -> 206 us  [the longest x29 201 us: kernel_call(): pl.pallas_call(body, out_shape=out_shape + [token_shape], grid_spec=pltpu...]
    dot_general x27 -> x0, matrix products: 193 us -> none  [the longest x4 61.9 us: matmul(): return jnp.dot(left, right, preferred_element_type=f32)]
    ppermute x45 -> x48, waiting for transfers between devices: 210 us -> 104 us  [swap(): return lax.ppermute(array, both, pairs)]
    convert_element_type x21 -> x4, other arithmetic: 30.9 us -> 0.07 us  [end(): return (mine.astype(f32), self.grid.swap(other, 'c').astype(f32))]
    ppermute x45 -> x48, starting transfers between devices: 84.9 us -> 55.8 us  [swap(): return lax.ppermute(array, both, pairs)]
    unnamed x125 -> x94, local copies, waits for them, and re-layouts: 2.52 us -> 27.2 us
    dynamic_update_slice x8 -> x0, local copies, waits for them, and re-layouts: 17.4 us -> none  [the longest x4 15 us: local(): lax.map(partial(attend_backward, addend=addend_all, head_count=head_count...]
    ppermute x9, waiting for transfers between devices: 16.5 us -> 0.02 us  [swap_blk(): return lax.ppermute(array, both, pairs)]
  transfers between devices with their start and end apart: 54 -> 57, of which waited for: 24 -> 18; matrix products, arithmetic and copies ran while one was open for 20% -> 2% of each run, Pallas kernels for 0% -> 38%
where the time goes in v3:
time: 415 us; the launch traced here: 414 us
  Pallas kernels  206 us (50%)
  waiting for transfers between devices  104 us (25%)
  starting transfers between devices  60.3 us (15%)
  local copies, waits for them, and re-layouts  34.6 us (8%)
  other arithmetic  6.78 us (2%)
    pallas_call x29, Pallas kernels, kernel_call(): pl.pallas_call(body, out_shape=out_shape + [token_shape], grid_spec=pltpu...  201 us
    ppermute x48, waiting for transfers between devices, swap(): return lax.ppermute(array, both, pairs)  104 us
    ppermute x48, starting transfers between devices, swap(): return lax.ppermute(array, both, pairs)  55.8 us
    unnamed x94, local copies, waits for them, and re-layouts  27.2 us
  transfers between devices with their start and end apart: 57, of which 18 were waited for; matrix products, arithmetic and copies ran while one was open for 2% of the time, Pallas kernels for 38%

profile of v3, /device:TPU:0, one launch (start us, length us, event | category | flops | bytes accessed | tf_op | source)
XLA Modules:
  0.0 413.7 jit_solution(503272513076441779)
XLA Ops:
  8.1 3.6 select_convert_fusion.refs_0_
  12.8 2.6 collective-permute-start.2
  16.2 2.0 collective-permute-start.15
  18.2 1.3 collective-permute-done.2.refs_2_
  21.1 4.1 collective-permute-start.7
  26.9 1.7 collective-permute-start.3
  30.3 4.7 %collective-permute-done.6.refs_3_ = bf16[96,640]{1,0:T(8,128)(2,1)S(1)} collective-permute-done((bf16[96,640]{1,0:T(8,128)(2,1)S(1)}, bf16[96,640]{1,0:T(8,128)(2,1)S(1)}, u32[]{:S(2)}, u32[]{:S(2)}) %collective-permute-start.6) | collective-permute-done | bytes 122912 | tf_op jit(solution)/shard_map/ppermute | solution.py:961
  37.5 2.5 collective-permute-start.13
  39.9 1.9 collective-permute-start.11
  41.8 2.0 shard_map.294
  45.7 1.6 collective-permute-start.24
  47.2 3.7 collective-permute-done.12.refs_3_
  51.0 1.5 collective-permute-start.8
  52.5 1.3 shard_map.296
  55.6 1.7 collective-permute-start.23
  57.2 22.0 %collective-permute-done.24.refs_0_ = bf16[12,128,512]{2,1,0:T(8,128)(2,1)} collective-permute-done((bf16[12,128,512]{2,1,0:T(8,128)(2,1)S(1)}, bf16[12,128,512]{2,1,0:T(8,128)(2,1)}, u32[]{:S(2)}, u32[]{:S(2)}) %collective-permute-start.24) | collective-permute-done | bytes 1572896 | tf_op jit(solution)/shard_map/ppermute | solution.py:961
  79.3 5.9 %collective-permute-start.21 = (bf16[96,1920]{1,0:T(8,128)(2,1)}, bf16[96,1920]{1,0:T(8,128)(2,1)S(1)}, u32[]{:S(2)}, u32[]{:S(2)}) collective-permute-start(bf16[96,1920]{1,0:T(8,128)(2,1)} %get-tuple-element.145.refs_1_), channel_id=1, source_target_pairs={{0,8},{1,9},{2,10},{3,11},{4,12},{5,13},{6,14},{7,15},{8,0},{9,1},... | collective-permute-start | bytes 1105928 | tf_op jit(solution)/shard_map/ppermute | solution.py:961
  86.3 2.2 collective-permute-done.22.refs_3_
  88.4 7.7 %collective-permute-done.21.refs_2_ = bf16[96,1920]{1,0:T(8,128)(2,1)S(1)} collective-permute-done((bf16[96,1920]{1,0:T(8,128)(2,1)}, bf16[96,1920]{1,0:T(8,128)(2,1)S(1)}, u32[]{:S(2)}, u32[]{:S(2)}) %collective-permute-start.21) | collective-permute-done | bytes 368672 | tf_op jit(solution)/shard_map/ppermute | solution.py:961
  99.1 2.8 shard_map.300
  103.1 1.6 collective-permute-start.30
  104.7 2.8 collective-permute-start.28
  108.2 9.5 %shard_map.302 = (bf16[2,4,128,768]{3,2,1,0:T(8,128)(2,1)}, f32[16,768]{1,0:T(8,128)S(1)}, bf16[2,1024,1152]{2,1,0:T(8,128)(2,1)}, f32[8,128]{1,0:T(8,128)S(1)}) custom-call(s32[5]{0:T(128)S(1)} %stack.83.refs_0_, bf16[2,128,768]{2,1,0:T(8,128)(2,1)S(1)} %get-tuple-element.248.refs_1_, bf16[2,128,768]{2,1,0:T(8,128)(2,1)} %collective-permute-done.refs_2_, ...), custom_call_target="tpu_custom_call" | custom-call | flops 99999997952 | bytes 1024 | tf_op jit(solution)/shard_map/pallas_call | solution.py:167
  118.3 1.5 collective-permute-start.27
  119.8 19.5 %shard_map.303 = (bf16[2,1024,384]{2,1,0:T(8,128)(2,1)S(1)}, f32[2,1024,128]{2,1,0:T(8,128)S(1)}, f32[8,128]{1,0:T(8,128)S(1)}) custom-call(s32[5]{0:T(128)S(1)} %stack.83.refs_0_, bf16[2,1024,1152]{2,1,0:T(8,128)(2,1)} %get-tuple-element.151.refs_1_, bf16[12,128,512]{2,1,0:T(8,128)(2,1)S(1)} %copy-done.3, ...), custom_call_target="tpu_custom_call" | custom-call | flops 99999997952 | bytes 1024 | tf_op jit(solution)/shard_map/pallas_call | solution.py:167
  140.5 2.7 shard_map.304
  143.9 9.0 %collective-permute-done.27.refs_0_ = bf16[4,96,1920]{2,1,0:T(8,128)(2,1)} collective-permute-done((bf16[4,96,1920]{2,1,0:T(8,128)(2,1)}, bf16[4,96,1920]{2,1,0:T(8,128)(2,1)}, u32[]{:S(2)}, u32[]{:S(2)}) %collective-permute-start.27) | collective-permute-done | bytes 1474592 | tf_op jit(solution)/shard_map/ppermute | solution.py:961
  154.5 1.5 collective-permute-start.33
  157.1 7.6 %shard_map.306 = (f32[1024,768]{1,0:T(8,128)}, bf16[1024,768]{1,0:T(8,128)(2,1)}, f32[8,128]{1,0:T(8,128)}) custom-call(s32[5]{0:T(128)S(1)} %stack.83.refs_0_, bf16[2,1024,384]{2,1,0:T(8,128)(2,1)} %copy-done.38, bf16[1024,768]{1,0:T(8,128)(2,1)} %bitcast.128, f32[16,768]{1,0:T(8,128)S(1)} %get-tuple-element.156.refs_3_.refs_6_.refs_4_, ...), custom_call_target="tpu_custom_call" | custom-call | flops 99999997952 | bytes 1024 | tf_op jit(solution)/shard_map/pallas_call | solution.py:167
  164.7 13.3 %shard_map.307 = (bf16[1024,3072]{1,0:T(8,128)(2,1)}, bf16[1024,3072]{1,0:T(8,128)(2,1)}, f32[8,128]{1,0:T(8,128)S(1)}) custom-call(s32[5]{0:T(128)S(1)} %stack.83.refs_0_, bf16[1024,768]{1,0:T(8,128)(2,1)} %get-tuple-element.162.refs_1_, f32[2,1,1536]{2,1,0:T(1,128)S(1)} %reshape.296.refs_2_, ...), custom_call_target="tpu_custom_call" | custom-call | flops 99999997952 | bytes 1024 | tf_op jit(solution)/shard_map/pallas_call | solution.py:167
  178.7 4.1 collective-permute-done.33.refs_0_
  183.6 3.0 collective-permute-done.35.refs_10_
  186.6 25.1 %shard_map.309 = (bf16[2,128,768]{2,1,0:T(8,128)(2,1)S(1)}, bf16[2,128,768]{2,1,0:T(8,128)(2,1)}, bf16[2,128,768]{2,1,0:T(8,128)(2,1)}, bf16[2,128,768]{2,1,0:T(...) custom-call(s32[5]{0:T(128)S(1)} %stack.83.refs_0_, ...), custom_call_target="tpu_custom_call" | custom-call | flops 99999997952 | bytes 1024 | tf_op jit(solution)/shard_map/pallas_call | solution.py:167
  212.5 1.4 copy-done.35
  213.9 8.8 %shard_map.310 = (bf16[768,1536]{1,0:T(8,128)(2,1)S(1)}, bf16[768,1536]{1,0:T(8,128)(2,1)}, f32[8,128]{1,0:T(8,128)S(1)}) custom-call(s32[5]{0:T(128)S(1)} %stack.83.refs_0_, bf16[1024,3072]{1,0:T(8,128)(2,1)} %get-tuple-element.163.refs_1_, bf16[1024,768]{1,0:T(8,128)(2,1)S(1)} %bitcast.130), custom_call_target="tpu_custom_call" | custom-call | flops 99999997952 | bytes 1024 | tf_op jit(solution)/shard_map/pallas_call | solution.py:167
  222.7 1.5 copy-done.32
  224.4 9.0 %shard_map.311 = (bf16[768,1536]{1,0:T(8,128)(2,1)S(1)}, bf16[768,1536]{1,0:T(8,128)(2,1)}, f32[8,128]{1,0:T(8,128)S(1)}) custom-call(s32[5]{0:T(128)S(1)} %stack.83.refs_0_, bf16[1024,768]{1,0:T(8,128)(2,1)S(1)} %copy-done.40, bf16[1024,3072]{1,0:T(8,128)(2,1)} %bitcast.160, bf16[1024,3072]{1,0:T(8,128)(2,1)} %bitcast.161, ...), custom_call_target="tpu_custom_call" | custom-call | flops 99999997952 | bytes 1024 | tf_op jit(solution)/shard_map/pallas_call | solution.py:167
  233.4 1.4 copy-done.33
  237.5 2.1 collective-permute-done.39
  239.6 5.9 %shard_map.312 = (bf16[4,96,3072]{2,1,0:T(8,128)(2,1)S(1)}, bf16[4,96,3072]{2,1,0:T(8,128)(2,1)}, f32[8,128]{1,0:T(8,128)S(1)}) custom-call(s32[5]{0:T(128)S(1)} %stack.83.refs_0_, bf16[4,2,96,1536]{3,2,1,0:T(8,128)(2,1)} %bitcast.126, bf16[4,2,96,1536]{3,2,1,0:T(8,128)(2,1)} %bitcast.43.refs_2_.refs_6_, bf16[4,2,96,1536]{3,2,1,0:T(8,128)(2,1)} %bitcast.124, ...), custom_call_target="tpu_custom_call" | custom-call | flops 99999997952 | bytes 1024 | tf_op jit(solution)/shard_map/pallas_call | solution.py:167
  245.6 1.4 copy-done.30
  247.0 1.5 collective-permute-start.41
  248.5 17.1 %shard_map.313 = (f32[1024,768]{1,0:T(8,128)}, bf16[1024,768]{1,0:T(8,128)(2,1)}, bf16[2,1024,384]{2,1,0:T(8,128)(2,1)}, f32[8,768]{1,0:T(8,128)S(1)}, f32[8,128]{1,0:T(8,128)S(1)}) custom-call(s32[5]{0:T(128)S(1)} %stack.83.refs_0_, bf16[1024,3072]{1,0:T(8,128)(2,1)} %bitcast.162, f32[1024,768]{1,0:T(8,128)} %bitcast.169, ...), custom_call_target="tpu_custom_call" | custom-call | flops 99999997952 | bytes 1024 | tf_op jit(solution)/shard_map/pallas_call | solution.py:167
  267.5 1.4 copy-done.37
  268.9 1.4 copy-done.39
  271.6 31.1 %shard_map.315 = (bf16[2,1024,1152]{2,1,0:T(8,128)(2,1)}, f32[2,3,8,384]{3,2,1,0:T(8,128)S(1)}, f32[8,128]{1,0:T(8,128)S(1)}) custom-call(s32[5]{0:T(128)S(1)} %stack.83.refs_0_, bf16[2,1024,1152]{2,1,0:T(8,128)(2,1)} %get-tuple-element.151.refs_1_, bf16[2,1024,384]{2,1,0:T(8,128)(2,1)S(1)} %copy-done.39, bf16[2,1024,384]{2,1,0:T(8,128)(2,1)S(1)} %copy-done.37, ...), custom_call_target="tpu_custom_call" | custom-call | flops 99999997952 | bytes 1024 | tf_op jit(solution)/shard_map/pallas_call | solution.py:167
  302.7 3.8 shard_map.316
  306.5 10.2 %shard_map.317 = (bf16[768,1664]{1,0:T(8,128)(2,1)}, bf16[768,1664]{1,0:T(8,128)(2,1)}, f32[8,128]{1,0:T(8,128)S(1)}) custom-call(s32[5]{0:T(128)S(1)} %stack.83.refs_0_, bf16[1024,768]{1,0:T(8,128)(2,1)S(1)} %bitcast.129, bf16[2,1024,1152]{2,1,0:T(8,128)(2,1)} %get-tuple-element.198.refs_2_, bf16[2,1024,384]{2,1,0:T(8,128)(2,1)S(1)} %copy-done.39, ...), custom_call_target="tpu_custom_call" | custom-call | flops 99999997952 | bytes 1024 | tf_op jit(solution)/shard_map/pallas_call | solution.py:167
  316.8 2.1 collective-permute-start.43
  318.9 2.2 collective-permute-start.44
  321.8 1.6 copy-done.45
  323.4 1.7 copy-done.29
  325.1 2.6 shard_map.318
  328.6 10.3 %shard_map.319 = (bf16[2,128,768]{2,1,0:T(8,128)(2,1)S(1)}, bf16[2,128,768]{2,1,0:T(8,128)(2,1)}, bf16[2,128,768]{2,1,0:T(8,128)(2,1)}, bf16[2,128,768]{2,1,0:T(8,128)(2,1)}, f32[8,128]{1,0:T(8,128)S(1)}) custom-call(s32[5]{0:T(128)S(1)} %stack.83.refs_0_, bf16[2,2,512,1152]{3,2,1,0:T(8,128)(2,1)} %bitcast.165, f32[2,512,768]{2,1,0:T(8,128)} %bitcast.168, ...), custom_call_target="tpu_custom_call" | custom-call | flops 99999997952 | bytes 1024 | tf_op jit(solution)/shard_map/pallas_call | solution.py:167
  339.0 18.9 %collective-permute-done.46 = bf16[8,48,1664]{2,1,0:T(8,128)(2,1)S(1)} collective-permute-done((bf16[8,48,1664]{2,1,0:T(8,128)(2,1)S(1)}, bf16[8,48,1664]{2,1,0:T(8,128)(2,1)S(1)}, u32[]{:S(2)}, u32[]{:S(2)}) %collective-permute-start.46) | collective-permute-done | bytes 1277984 | tf_op jit(solution)/shard_map/ppermute | solution.py:961
  360.0 2.8 shard_map.321
  364.6 2.9 shard_map.322
  367.5 13.4 %collective-permute-done.51 = bf16[4,48,1664]{2,1,0:T(8,128)(2,1)S(1)} collective-permute-done((bf16[4,48,1664]{2,1,0:T(8,128)(2,1)S(1)}, bf16[4,48,1664]{2,1,0:T(8,128)(2,1)S(1)}, u32[]{:S(2)}, u32[]{:S(2)}) %collective-permute-start.51) | collective-permute-done | bytes 639008 | tf_op jit(solution)/shard_map/ppermute | solution.py:961
  381.6 1.8 collective-permute-done.50
  383.4 1.6 shard_map.324
  385.1 8.8 %collective-permute-start.52 = (bf16[1,48,1664]{2,1,0:T(8,128)(2,1)S(1)}, bf16[1,48,1664]{2,1,0:T(8,128)(2,1)S(1)}, u32[]{:S(2)}, u32[]{:S(2)}) collective-permute-start(bf16[1,48,1664]{2,1,0:T(8,128)(2,1)S(1)} %get-tuple-element.229), channel_id=1, source_target_pairs={{0,8},{1,9},{2,10},{3,11},{4,12},{5,13},{6,14},{7,15},{8,0},{9,1},... | collective-permute-start | bytes 479240 | tf_op jit(solution)/shard_map/ppermute | solution.py:961
  394.4 2.0 collective-permute-start.54
  396.4 3.6 shard_map.325
  401.7 6.9 %collective-permute-done.53 = bf16[1,48,1664]{2,1,0:T(8,128)(2,1)S(1)} collective-permute-done((bf16[1,48,1664]{2,1,0:T(8,128)(2,1)S(1)}, bf16[1,48,1664]{2,1,0:T(8,128)(2,1)S(1)}, u32[]{:S(2)}, u32[]{:S(2)}) %collective-permute-start.53) | collective-permute-done | bytes 159776 | tf_op jit(solution)/shard_map/ppermute | solution.py:961
  (228 shorter events, 52.7 us)
Async XLA Ops:
  0.6 182.8 %copy-start = (s32[8,128]{1,0:T(8,128)S(1)}, s32[8,128]{1,0:T(8,128)}, u32[]{:S(2)}) copy-start(s32[8,128]{1,0:T(8,128)} %param.33) | copy-start | bytes 12292
  7.1 5.6 %collective-permute-start.1 = (bf16[24,1280]{1,0:T(8,128)(2,1)S(1)}, bf16[24,1280]{1,0:T(8,128)(2,1)S(1)}, u32[]{:S(2)}, u32[]{:S(2)}) collective-permute-start(bf16[24,1280]{1,0:T(8,128)(2,1)S(1)} %get-tuple-element.126), channel_id=1, source_target_pairs={{0,1},{1,0},{2,3},{3,2},{4,5},{5,4},{6,7},{7,6},{8,9},{9,8},{10,11... | collective-permute-start | bytes 184328 | tf_op jit(solution)/shard_map/ppermute | solution.py:961
  7.6 7.8 %collective-permute-start.16 = (bf16[96,384]{1,0:T(8,128)(2,1)S(1)}, bf16[96,384]{1,0:T(8,128)(2,1)S(1)}, u32[]{:S(2)}, u32[]{:S(2)}) collective-permute-start(bf16[96,384]{1,0:T(8,128)(2,1)S(1)} %get-tuple-element.138), channel_id=1, source_target_pairs={{0,1},{1,0},{2,3},{3,2},{4,5},{5,4},{6,7},{7,6},{8,9},{9,8},{10,11... | collective-permute-start | bytes 221192 | tf_op jit(solution)/shard_map/ppermute | solution.py:961
  7.7 7.9 %collective-permute-start.14 = (bf16[24,1920]{1,0:T(8,128)(2,1)S(1)}, bf16[24,1920]{1,0:T(8,128)(2,1)S(1)}, u32[]{:S(2)}, u32[]{:S(2)}) collective-permute-start(bf16[24,1920]{1,0:T(8,128)(2,1)S(1)} %get-tuple-element.135), channel_id=1, source_target_pairs={{0,1},{1,0},{2,3},{3,2},{4,5},{5,4},{6,7},{7,6},{8,9},{9,8},{10,11... | collective-permute-start | bytes 276488 | tf_op jit(solution)/shard_map/ppermute | solution.py:961
  12.8 6.7 %collective-permute-start.2 = (bf16[48,1280]{1,0:T(8,128)(2,1)S(1)}, bf16[48,1280]{1,0:T(8,128)(2,1)S(1)}, u32[]{:S(2)}, u32[]{:S(2)}) collective-permute-start(bf16[48,1280]{1,0:T(8,128)(2,1)S(1)} %bitcast.101), channel_id=1, source_target_pairs={{0,2},{1,3},{2,0},{3,1},{4,6},{5,7},{6,4},{7,5},{8,10},{9,11},{10,... | collective-permute-start | bytes 368648 | tf_op jit(solution)/shard_map/ppermute | solution.py:961
  15.4 11.5 %collective-permute-start.17 = (bf16[192,384]{1,0:T(8,128)(2,1)S(1)}, bf16[192,384]{1,0:T(8,128)(2,1)S(1)}, u32[]{:S(2)}, u32[]{:S(2)}) collective-permute-start(bf16[192,384]{1,0:T(8,128)(2,1)S(1)} %bitcast.99), channel_id=1, source_target_pairs={{0,2},{1,3},{2,0},{3,1},{4,6},{5,7},{6,4},{7,5},{8,10},{9,11},{10,... | collective-permute-start | bytes 442376 | tf_op jit(solution)/shard_map/ppermute | solution.py:961
  16.2 23.7 %collective-permute-start.15 = (bf16[48,1920]{1,0:T(8,128)(2,1)}, bf16[48,1920]{1,0:T(8,128)(2,1)}, u32[]{:S(2)}, u32[]{:S(2)}) collective-permute-start(bf16[48,1920]{1,0:T(8,128)(2,1)} %bitcast.28.refs_1_), channel_id=1, source_target_pairs={{0,2},{1,3},{2,0},{3,1},{4,6},{5,7},{6,4},{7,5},{8,10},{9,11},{10,... | collective-permute-start | bytes 552968 | tf_op jit(solution)/shard_map/ppermute | solution.py:961
  21.1 9.2 %collective-permute-start.7 = (bf16[96,640]{1,0:T(8,128)(2,1)S(1)}, bf16[96,640]{1,0:T(8,128)(2,1)S(1)}, u32[]{:S(2)}, u32[]{:S(2)}) collective-permute-start(bf16[96,640]{1,0:T(8,128)(2,1)S(1)} %get-tuple-element.258.refs_1_), channel_id=1, source_target_pairs={{0,24},{1,25},{2,26},{3,27},{4,28},{5,29},{6,30},{7,31},{8,16},{9,... | collective-permute-start | bytes 368648 | tf_op jit(solution)/shard_map/ppermute | solution.py:961
  25.2 9.9 %collective-permute-start.6 = (bf16[96,640]{1,0:T(8,128)(2,1)S(1)}, bf16[96,640]{1,0:T(8,128)(2,1)S(1)}, u32[]{:S(2)}, u32[]{:S(2)}) collective-permute-start(bf16[96,640]{1,0:T(8,128)(2,1)S(1)} %get-tuple-element.258.refs_1_), channel_id=1, source_target_pairs={{0,16},{1,17},{2,18},{3,19},{4,20},{5,21},{6,22},{7,23},{8,24},{9,... | collective-permute-start | bytes 368648 | tf_op jit(solution)/shard_map/ppermute | solution.py:961
  25.2 9.9 %collective-permute-start.5 = (bf16[96,640]{1,0:T(8,128)(2,1)S(1)}, bf16[96,640]{1,0:T(8,128)(2,1)S(1)}, u32[]{:S(2)}, u32[]{:S(2)}) collective-permute-start(bf16[96,640]{1,0:T(8,128)(2,1)S(1)} %get-tuple-element.258.refs_1_), channel_id=1, source_target_pairs={{0,8},{1,9},{2,10},{3,11},{4,12},{5,13},{6,14},{7,15},{8,0},{9,1},... | collective-permute-start | bytes 368648 | tf_op jit(solution)/shard_map/ppermute | solution.py:961
  26.9 25.6 %collective-permute-start.3 = (bf16[2,128,768]{2,1,0:T(8,128)(2,1)}, bf16[2,128,768]{2,1,0:T(8,128)(2,1)}, u32[]{:S(2)}, u32[]{:S(2)}) collective-permute-start(bf16[2,128,768]{2,1,0:T(8,128)(2,1)} %get-tuple-element.129), channel_id=1, source_target_pairs={{0,2},{1,3},{2,0},{3,1},{4,6},{5,7},{6,4},{7,5},{8,10},{9,11},{10,... | collective-permute-start | bytes 1179656 | tf_op jit(solution)/shard_map/ppermute | solution.py:965
  30.3 22.2 %collective-permute-start.4 = (bf16[2,128,768]{2,1,0:T(8,128)(2,1)}, bf16[2,128,768]{2,1,0:T(8,128)(2,1)}, u32[]{:S(2)}, u32[]{:S(2)}) collective-permute-start(bf16[2,128,768]{2,1,0:T(8,128)(2,1)} %get-tuple-element.130), channel_id=1, source_target_pairs={{0,3},{1,2},{2,1},{3,0},{4,7},{5,6},{6,5},{7,4},{8,11},{9,10},{10,... | collective-permute-start | bytes 1179656 | tf_op jit(solution)/shard_map/ppermute | solution.py:965
  37.5 8.2 %collective-permute-start.13 = (bf16[96,640]{1,0:T(8,128)(2,1)}, bf16[96,640]{1,0:T(8,128)(2,1)S(1)}, u32[]{:S(2)}, u32[]{:S(2)}) collective-permute-start(bf16[96,640]{1,0:T(8,128)(2,1)} %get-tuple-element.134.refs_1_), channel_id=1, source_target_pairs={{0,24},{1,25},{2,26},{3,27},{4,28},{5,29},{6,30},{7,31},{8,16},{9,... | collective-permute-start | bytes 368648 | tf_op jit(solution)/shard_map/ppermute | solution.py:961
  39.9 11.0 %collective-permute-start.12 = (bf16[96,640]{1,0:T(8,128)(2,1)}, bf16[96,640]{1,0:T(8,128)(2,1)S(1)}, u32[]{:S(2)}, u32[]{:S(2)}) collective-permute-start(bf16[96,640]{1,0:T(8,128)(2,1)} %get-tuple-element.134.refs_1_), channel_id=1, source_target_pairs={{0,16},{1,17},{2,18},{3,19},{4,20},{5,21},{6,22},{7,23},{8,24},{9,... | collective-permute-start | bytes 368648 | tf_op jit(solution)/shard_map/ppermute | solution.py:961
  39.9 12.5 %collective-permute-start.11 = (bf16[96,640]{1,0:T(8,128)(2,1)}, bf16[96,640]{1,0:T(8,128)(2,1)S(1)}, u32[]{:S(2)}, u32[]{:S(2)}) collective-permute-start(bf16[96,640]{1,0:T(8,128)(2,1)} %get-tuple-element.134.refs_1_), channel_id=1, source_target_pairs={{0,8},{1,9},{2,10},{3,11},{4,12},{5,13},{6,14},{7,15},{8,0},{9,1},... | collective-permute-start | bytes 368648 | tf_op jit(solution)/shard_map/ppermute | solution.py:961
  45.7 33.6 %collective-permute-start.24 = (bf16[12,128,512]{2,1,0:T(8,128)(2,1)S(1)}, bf16[12,128,512]{2,1,0:T(8,128)(2,1)}, u32[]{:S(2)}, u32[]{:S(2)}) collective-permute-start(bf16[12,128,512]{2,1,0:T(8,128)(2,1)S(1)} %copy-done.2), channel_id=1, source_target_pairs={{0,2},{1,3},{2,0},{3,1},{4,6},{5,7},{6,4},{7,5},{8,10},{9,11},{10,... | collective-permute-start | bytes 4718600 | tf_op jit(solution)/shard_map/ppermute | solution.py:961
  51.0 34.8 %collective-permute-start.8 = (bf16[4,96,640]{2,1,0:T(8,128)(2,1)S(1)}, bf16[4,96,640]{2,1,0:T(8,128)(2,1)S(1)}, u32[]{:S(2)}, u32[]{:S(2)}) collective-permute-start(bf16[4,96,640]{2,1,0:T(8,128)(2,1)S(1)} %get-tuple-element.132.refs_5_.refs_3_), channel_id=1, source_target_pairs={{0,4},{1,5},{2,6},{3,7},{4,0},{5,1},{6,2},{7,3},{8,12},{9,13},{10,... | collective-permute-start | bytes 1474568 | tf_op jit(solution)/shard_map/ppermute | solution.py:961
  54.4 42.4 %collective-permute-start.18 = (bf16[4,96,640]{2,1,0:T(8,128)(2,1)}, bf16[4,96,640]{2,1,0:T(8,128)(2,1)}, u32[]{:S(2)}, u32[]{:S(2)}) collective-permute-start(bf16[4,96,640]{2,1,0:T(8,128)(2,1)} %get-tuple-element.141.refs_9_.refs_7_), channel_id=1, source_target_pairs={{0,4},{1,5},{2,6},{3,7},{4,0},{5,1},{6,2},{7,3},{8,12},{9,13},{10,... | collective-permute-start | bytes 1474568 | tf_op jit(solution)/shard_map/ppermute | solution.py:961
  55.5 41.8 %copy-start.8 = (bf16[96,1920]{1,0:T(8,128)(2,1)S(1)}, bf16[96,1920]{1,0:T(8,128)(2,1)}, u32[]{:S(2)}) copy-start(bf16[96,1920]{1,0:T(8,128)(2,1)} %get-tuple-element.145.refs_1_) | copy-start | bytes 1105924
  55.6 41.8 %copy-start.12 = (f32[8,128]{1,0:T(8,128)S(1)}, f32[8,128]{1,0:T(8,128)}, u32[]{:S(2)}) copy-start(f32[8,128]{1,0:T(8,128)} %get-tuple-element.146.refs_1_.refs_5_) | copy-start | bytes 12292
  55.6 30.2 %collective-permute-start.23 = (bf16[96,1920]{1,0:T(8,128)(2,1)}, bf16[96,1920]{1,0:T(8,128)(2,1)}, u32[]{:S(2)}, u32[]{:S(2)}) collective-permute-start(bf16[96,1920]{1,0:T(8,128)(2,1)} %get-tuple-element.145.refs_1_), channel_id=1, source_target_pairs={{0,24},{1,25},{2,26},{3,27},{4,28},{5,29},{6,30},{7,31},{8,16},{9,... | collective-permute-start | bytes 1105928 | tf_op jit(solution)/shard_map/ppermute | solution.py:961
  57.2 31.2 %collective-permute-start.22 = (bf16[96,1920]{1,0:T(8,128)(2,1)}, bf16[96,1920]{1,0:T(8,128)(2,1)}, u32[]{:S(2)}, u32[]{:S(2)}) collective-permute-start(bf16[96,1920]{1,0:T(8,128)(2,1)} %get-tuple-element.145.refs_1_), channel_id=1, source_target_pairs={{0,16},{1,17},{2,18},{3,19},{4,20},{5,21},{6,22},{7,23},{8,24},{9,... | collective-permute-start | bytes 1105928 | tf_op jit(solution)/shard_map/ppermute | solution.py:961
  79.3 16.8 %collective-permute-start.21 = (bf16[96,1920]{1,0:T(8,128)(2,1)}, bf16[96,1920]{1,0:T(8,128)(2,1)S(1)}, u32[]{:S(2)}, u32[]{:S(2)}) collective-permute-start(bf16[96,1920]{1,0:T(8,128)(2,1)} %get-tuple-element.145.refs_1_), channel_id=1, source_target_pairs={{0,8},{1,9},{2,10},{3,11},{4,12},{5,13},{6,14},{7,15},{8,0},{9,1},... | collective-permute-start | bytes 1105928 | tf_op jit(solution)/shard_map/ppermute | solution.py:961
  85.8 17.3 %collective-permute-start = (bf16[2,128,768]{2,1,0:T(8,128)(2,1)}, bf16[2,128,768]{2,1,0:T(8,128)(2,1)}, u32[]{:S(2)}, u32[]{:S(2)}) collective-permute-start(bf16[2,128,768]{2,1,0:T(8,128)(2,1)} %get-tuple-element.247), channel_id=1, source_target_pairs={{0,1},{1,0},{2,3},{3,2},{4,5},{5,4},{6,7},{7,6},{8,9},{9,8},{10,11... | collective-permute-start | bytes 1179656 | tf_op jit(solution)/shard_map/ppermute | solution.py:965
  85.8 17.3 %collective-permute-start.9 = (bf16[4,96,640]{2,1,0:T(8,128)(2,1)S(1)}, bf16[4,96,640]{2,1,0:T(8,128)(2,1)}, u32[]{:S(2)}, u32[]{:S(2)}) collective-permute-start(bf16[4,96,640]{2,1,0:T(8,128)(2,1)S(1)} %get-tuple-element.132.refs_5_.refs_3_), channel_id=1, source_target_pairs={{0,1},{1,0},{2,3},{3,2},{4,5},{5,4},{6,7},{7,6},{8,9},{9,8},{10,11... | collective-permute-start | bytes 1474568 | tf_op jit(solution)/shard_map/ppermute | solution.py:961
  88.4 16.3 %collective-permute-start.19 = (bf16[4,96,640]{2,1,0:T(8,128)(2,1)}, bf16[4,96,640]{2,1,0:T(8,128)(2,1)}, u32[]{:S(2)}, u32[]{:S(2)}) collective-permute-start(bf16[4,96,640]{2,1,0:T(8,128)(2,1)} %get-tuple-element.141.refs_9_.refs_7_), channel_id=1, source_target_pairs={{0,1},{1,0},{2,3},{3,2},{4,5},{5,4},{6,7},{7,6},{8,9},{9,8},{10,11... | collective-permute-start | bytes 1474568 | tf_op jit(solution)/shard_map/ppermute | solution.py:961
  96.9 7.8 %collective-permute-start.10 = (bf16[4,96,640]{2,1,0:T(8,128)(2,1)S(1)}, bf16[4,96,640]{2,1,0:T(8,128)(2,1)}, u32[]{:S(2)}, u32[]{:S(2)}) collective-permute-start(bf16[4,96,640]{2,1,0:T(8,128)(2,1)S(1)} %collective-permute-done.8.refs_6_.refs_4_), channel_id=1, source_target_pairs={{0,1},{1,0},{2,3},{3,2},{4,5},{5,4},{6,7},{7,6},{8,9},{9,8},{10,11... | collective-permute-start | bytes 1474568 | tf_op jit(solution)/shard_map/ppermute | solution.py:961
  96.9 10.6 %collective-permute-start.20 = (bf16[4,96,640]{2,1,0:T(8,128)(2,1)}, bf16[4,96,640]{2,1,0:T(8,128)(2,1)}, u32[]{:S(2)}, u32[]{:S(2)}) collective-permute-start(bf16[4,96,640]{2,1,0:T(8,128)(2,1)} %collective-permute-done.18.refs_10_.refs_8_), channel_id=1, source_target_pairs={{0,1},{1,0},{2,3},{3,2},{4,5},{5,4},{6,7},{7,6},{8,9},{9,8},{10,11... | collective-permute-start | bytes 1474568 | tf_op jit(solution)/shard_map/ppermute | solution.py:961
  103.0 14.7 %collective-permute-start.25 = (bf16[12,128,512]{2,1,0:T(8,128)(2,1)S(1)}, bf16[12,128,512]{2,1,0:T(8,128)(2,1)S(1)}, u32[]{:S(2)}, u32[]{:S(2)}) collective-permute-start(bf16[12,128,512]{2,1,0:T(8,128)(2,1)S(1)} %copy-done.3), channel_id=1, source_target_pairs={{0,1},{1,0},{2,3},{3,2},{4,5},{5,4},{6,7},{7,6},{8,9},{9,8},{10,11... | collective-permute-start | bytes 4718600 | tf_op jit(solution)/shard_map/ppermute | solution.py:961
  103.1 37.4 %collective-permute-start.30 = (bf16[384,384]{1,0:T(8,128)(2,1)}, bf16[384,384]{1,0:T(8,128)(2,1)}, u32[]{:S(2)}, u32[]{:S(2)}) collective-permute-start(bf16[384,384]{1,0:T(8,128)(2,1)} %get-tuple-element.158.refs_1_), channel_id=1, source_target_pairs={{0,24},{1,25},{2,26},{3,27},{4,28},{5,29},{6,30},{7,31},{8,16},{9,... | collective-permute-start | bytes 884744 | tf_op jit(solution)/shard_map/ppermute | solution.py:961
  104.7 35.8 %collective-permute-start.29 = (bf16[384,384]{1,0:T(8,128)(2,1)}, bf16[384,384]{1,0:T(8,128)(2,1)}, u32[]{:S(2)}, u32[]{:S(2)}) collective-permute-start(bf16[384,384]{1,0:T(8,128)(2,1)} %get-tuple-element.158.refs_1_), channel_id=1, source_target_pairs={{0,16},{1,17},{2,18},{3,19},{4,20},{5,21},{6,22},{7,23},{8,24},{9,... | collective-permute-start | bytes 884744 | tf_op jit(solution)/shard_map/ppermute | solution.py:961
  104.7 35.8 %collective-permute-start.28 = (bf16[384,384]{1,0:T(8,128)(2,1)}, bf16[384,384]{1,0:T(8,128)(2,1)}, u32[]{:S(2)}, u32[]{:S(2)}) collective-permute-start(bf16[384,384]{1,0:T(8,128)(2,1)} %get-tuple-element.158.refs_1_), channel_id=1, source_target_pairs={{0,8},{1,9},{2,10},{3,11},{4,12},{5,13},{6,14},{7,15},{8,0},{9,1},... | collective-permute-start | bytes 884744 | tf_op jit(solution)/shard_map/ppermute | solution.py:961
  107.5 10.8 %collective-permute-start.26 = (bf16[12,128,512]{2,1,0:T(8,128)(2,1)}, bf16[12,128,512]{2,1,0:T(8,128)(2,1)S(1)}, u32[]{:S(2)}, u32[]{:S(2)}) collective-permute-start(bf16[12,128,512]{2,1,0:T(8,128)(2,1)} %get-tuple-element.152.refs_4_.refs_7_), channel_id=1, source_target_pairs={{0,1},{1,0},{2,3},{3,2},{4,5},{5,4},{6,7},{7,6},{8,9},{9,8},{10,11... | collective-permute-start | bytes 4718600 | tf_op jit(solution)/shard_map/ppermute | solution.py:961
  117.7 21.6 %copy-start.19 = (bf16[12,128,512]{2,1,0:T(8,128)(2,1)}, bf16[12,128,512]{2,1,0:T(8,128)(2,1)S(1)}, u32[]{:S(2)}) copy-start(bf16[12,128,512]{2,1,0:T(8,128)(2,1)S(1)} %collective-permute-done.25.refs_3_.refs_6_) | copy-start | bytes 4718596
  117.7 38.3 %collective-permute-start.31 = (bf16[4,96,1920]{2,1,0:T(8,128)(2,1)}, bf16[4,96,1920]{2,1,0:T(8,128)(2,1)}, u32[]{:S(2)}, u32[]{:S(2)}) collective-permute-start(bf16[4,96,1920]{2,1,0:T(8,128)(2,1)} %get-tuple-element.157.refs_4_.refs_3_.refs_5_), channel_id=1, source_target_pairs={{0,1},{1,0},{2,3},{3,2},{4,5},{5,4},{6,7},{7,6},{8,9},{9,8},{10,11... | collective-permute-start | bytes 4423688 | tf_op jit(solution)/shard_map/ppermute | solution.py:961
  118.3 34.6 %collective-permute-start.27 = (bf16[4,96,1920]{2,1,0:T(8,128)(2,1)}, bf16[4,96,1920]{2,1,0:T(8,128)(2,1)}, u32[]{:S(2)}, u32[]{:S(2)}) collective-permute-start(bf16[4,96,1920]{2,1,0:T(8,128)(2,1)} %get-tuple-element.157.refs_4_.refs_3_.refs_5_), channel_id=1, source_target_pairs={{0,4},{1,5},{2,6},{3,7},{4,0},{5,1},{6,2},{7,3},{8,12},{9,13},{10,... | collective-permute-start | bytes 4423688 | tf_op jit(solution)/shard_map/ppermute | solution.py:961
  119.8 20.7 %copy-start.10 = (bf16[384,384]{1,0:T(8,128)(2,1)S(1)}, bf16[384,384]{1,0:T(8,128)(2,1)}, u32[]{:S(2)}) copy-start(bf16[384,384]{1,0:T(8,128)(2,1)} %get-tuple-element.158.refs_1_) | copy-start | bytes 884740
  153.5 3.6 collective-permute-start.32
  153.9 29.6 %collective-permute-start.34 = (bf16[4,384,384]{2,1,0:T(8,128)(2,1)}, bf16[4,384,384]{2,1,0:T(8,128)(2,1)}, u32[]{:S(2)}, u32[]{:S(2)}) collective-permute-start(bf16[4,384,384]{2,1,0:T(8,128)(2,1)} %get-tuple-element.166.refs_7_), channel_id=1, source_target_pairs={{0,1},{1,0},{2,3},{3,2},{4,5},{5,4},{6,7},{7,6},{8,9},{9,8},{10,11... | collective-permute-start | bytes 3538952 | tf_op jit(solution)/shard_map/ppermute | solution.py:961
  154.5 28.3 %collective-permute-start.33 = (bf16[4,384,384]{2,1,0:T(8,128)(2,1)}, bf16[4,384,384]{2,1,0:T(8,128)(2,1)}, u32[]{:S(2)}, u32[]{:S(2)}) collective-permute-start(bf16[4,384,384]{2,1,0:T(8,128)(2,1)} %get-tuple-element.166.refs_7_), channel_id=1, source_target_pairs={{0,4},{1,5},{2,6},{3,7},{4,0},{5,1},{6,2},{7,3},{8,12},{9,13},{10,... | collective-permute-start | bytes 3538952 | tf_op jit(solution)/shard_map/ppermute | solution.py:961
  164.7 18.7 %copy-start.44 = (s32[8]{0:T(128)S(1)}, s32[8]{0:T(128)}, u32[]{:S(2)}) copy-start(s32[8]{0:T(128)} %param.34) | copy-start | bytes 100
  183.4 3.2 collective-permute-start.35
  224.2 13.4 %collective-permute-start.40 = (bf16[768,1536]{1,0:T(8,128)(2,1)}, bf16[768,1536]{1,0:T(8,128)(2,1)}, u32[]{:S(2)}, u32[]{:S(2)}) collective-permute-start(bf16[768,1536]{1,0:T(8,128)(2,1)} %get-tuple-element.180), channel_id=1, source_target_pairs={{0,1},{1,0},{2,3},{3,2},{4,5},{5,4},{6,7},{7,6},{8,9},{9,8},{10,11... | collective-permute-start | bytes 7077896 | tf_op jit(solution)/shard_map/ppermute | solution.py:961
  234.8 4.9 %collective-permute-start.39 = (bf16[768,1536]{1,0:T(8,128)(2,1)}, bf16[768,1536]{1,0:T(8,128)(2,1)}, u32[]{:S(2)}, u32[]{:S(2)}) collective-permute-start(bf16[768,1536]{1,0:T(8,128)(2,1)} %get-tuple-element.178), channel_id=1, source_target_pairs={{0,1},{1,0},{2,3},{3,2},{4,5},{5,4},{6,7},{7,6},{8,9},{9,8},{10,11... | collective-permute-start | bytes 7077896 | tf_op jit(solution)/shard_map/ppermute | solution.py:961
  235.6 30.6 %collective-permute-start.36 = (bf16[2,128,768]{2,1,0:T(8,128)(2,1)}, bf16[2,128,768]{2,1,0:T(8,128)(2,1)}, u32[]{:S(2)}, u32[]{:S(2)}) collective-permute-start(bf16[2,128,768]{2,1,0:T(8,128)(2,1)} %get-tuple-element.170), channel_id=1, source_target_pairs={{0,1},{1,0},{2,3},{3,2},{4,5},{5,4},{6,7},{7,6},{8,9},{9,8},{10,11... | collective-permute-start | bytes 1179656 | tf_op jit(solution)/shard_map/ppermute | solution.py:965
  235.9 30.3 %collective-permute-start.37 = (bf16[2,128,768]{2,1,0:T(8,128)(2,1)}, bf16[2,128,768]{2,1,0:T(8,128)(2,1)}, u32[]{:S(2)}, u32[]{:S(2)}) collective-permute-start(bf16[2,128,768]{2,1,0:T(8,128)(2,1)} %get-tuple-element.171), channel_id=1, source_target_pairs={{0,2},{1,3},{2,0},{3,1},{4,6},{5,7},{6,4},{7,5},{8,10},{9,11},{10,... | collective-permute-start | bytes 1179656 | tf_op jit(solution)/shard_map/ppermute | solution.py:965
  236.7 29.5 %collective-permute-start.38 = (bf16[2,128,768]{2,1,0:T(8,128)(2,1)}, bf16[2,128,768]{2,1,0:T(8,128)(2,1)}, u32[]{:S(2)}, u32[]{:S(2)}) collective-permute-start(bf16[2,128,768]{2,1,0:T(8,128)(2,1)} %get-tuple-element.172), channel_id=1, source_target_pairs={{0,3},{1,2},{2,1},{3,0},{4,7},{5,6},{6,5},{7,4},{8,11},{9,10},{10,... | collective-permute-start | bytes 1179656 | tf_op jit(solution)/shard_map/ppermute | solution.py:965
  247.0 55.7 %collective-permute-start.41 = (bf16[4,96,3072]{2,1,0:T(8,128)(2,1)}, bf16[4,96,3072]{2,1,0:T(8,128)(2,1)}, u32[]{:S(2)}, u32[]{:S(2)}) collective-permute-start(bf16[4,96,3072]{2,1,0:T(8,128)(2,1)} %get-tuple-element.189), channel_id=1, source_target_pairs={{0,4},{1,5},{2,6},{3,7},{4,0},{5,1},{6,2},{7,3},{8,12},{9,13},{10,... | collective-permute-start | bytes 7077896 | tf_op jit(solution)/shard_map/ppermute | solution.py:961
  271.6 31.1 %copy-start.31 = (bf16[4,96,3072]{2,1,0:T(8,128)(2,1)S(1)}, bf16[4,96,3072]{2,1,0:T(8,128)(2,1)}, u32[]{:S(2)}) copy-start(bf16[4,96,3072]{2,1,0:T(8,128)(2,1)} %copy-done.30) | copy-start | bytes 7077892
  316.7 5.0 %collective-permute-start.45 = (bf16[768,1664]{1,0:T(8,128)(2,1)}, bf16[768,1664]{1,0:T(8,128)(2,1)S(1)}, u32[]{:S(2)}, u32[]{:S(2)}) collective-permute-start(bf16[768,1664]{1,0:T(8,128)(2,1)} %get-tuple-element.206), channel_id=1, source_target_pairs={{0,1},{1,0},{2,3},{3,2},{4,5},{5,4},{6,7},{7,6},{8,9},{9,8},{10,11... | collective-permute-start | bytes 7667720 | tf_op jit(solution)/shard_map/ppermute | solution.py:961
  316.7 43.2 %collective-permute-start.42 = (bf16[1,96,3072]{2,1,0:T(8,128)(2,1)}, bf16[1,96,3072]{2,1,0:T(8,128)(2,1)}, u32[]{:S(2)}, u32[]{:S(2)}) collective-permute-start(bf16[1,96,3072]{2,1,0:T(8,128)(2,1)} %get-tuple-element.195), channel_id=1, source_target_pairs={{0,8},{1,9},{2,10},{3,11},{4,12},{5,13},{6,14},{7,15},{8,0},{9,1},... | collective-permute-start | bytes 1769480 | tf_op jit(solution)/shard_map/ppermute | solution.py:961
  316.8 43.2 %collective-permute-start.43 = (bf16[1,96,3072]{2,1,0:T(8,128)(2,1)}, bf16[1,96,3072]{2,1,0:T(8,128)(2,1)}, u32[]{:S(2)}, u32[]{:S(2)}) collective-permute-start(bf16[1,96,3072]{2,1,0:T(8,128)(2,1)} %get-tuple-element.196), channel_id=1, source_target_pairs={{0,16},{1,17},{2,18},{3,19},{4,20},{5,21},{6,22},{7,23},{8,24},{9,... | collective-permute-start | bytes 1769480 | tf_op jit(solution)/shard_map/ppermute | solution.py:961
  318.9 41.1 %collective-permute-start.44 = (bf16[1,96,3072]{2,1,0:T(8,128)(2,1)}, bf16[1,96,3072]{2,1,0:T(8,128)(2,1)}, u32[]{:S(2)}, u32[]{:S(2)}) collective-permute-start(bf16[1,96,3072]{2,1,0:T(8,128)(2,1)} %get-tuple-element.197), channel_id=1, source_target_pairs={{0,24},{1,25},{2,26},{3,27},{4,28},{5,29},{6,30},{7,31},{8,16},{9,... | collective-permute-start | bytes 1769480 | tf_op jit(solution)/shard_map/ppermute | solution.py:961
  327.7 30.2 %collective-permute-start.46 = (bf16[8,48,1664]{2,1,0:T(8,128)(2,1)S(1)}, bf16[8,48,1664]{2,1,0:T(8,128)(2,1)S(1)}, u32[]{:S(2)}, u32[]{:S(2)}) collective-permute-start(bf16[8,48,1664]{2,1,0:T(8,128)(2,1)S(1)} %get-tuple-element.209), channel_id=1, source_target_pairs={{0,2},{1,3},{2,0},{3,1},{4,6},{5,7},{6,4},{7,5},{8,10},{9,11},{10,... | collective-permute-start | bytes 3833864 | tf_op jit(solution)/shard_map/ppermute | solution.py:961
  338.9 55.0 %collective-permute-start.47 = (bf16[2,128,768]{2,1,0:T(8,128)(2,1)}, bf16[2,128,768]{2,1,0:T(8,128)(2,1)}, u32[]{:S(2)}, u32[]{:S(2)}) collective-permute-start(bf16[2,128,768]{2,1,0:T(8,128)(2,1)} %get-tuple-element.217), channel_id=1, source_target_pairs={{0,1},{1,0},{2,3},{3,2},{4,5},{5,4},{6,7},{7,6},{8,9},{9,8},{10,11... | collective-permute-start | bytes 1179656 | tf_op jit(solution)/shard_map/ppermute | solution.py:965
  357.9 36.5 %collective-permute-start.48 = (bf16[2,128,768]{2,1,0:T(8,128)(2,1)}, bf16[2,128,768]{2,1,0:T(8,128)(2,1)}, u32[]{:S(2)}, u32[]{:S(2)}) collective-permute-start(bf16[2,128,768]{2,1,0:T(8,128)(2,1)} %get-tuple-element.218), channel_id=1, source_target_pairs={{0,2},{1,3},{2,0},{3,1},{4,6},{5,7},{6,4},{7,5},{8,10},{9,11},{10,... | collective-permute-start | bytes 1179656 | tf_op jit(solution)/shard_map/ppermute | solution.py:965
  359.9 36.5 %collective-permute-start.49 = (bf16[2,128,768]{2,1,0:T(8,128)(2,1)}, bf16[2,128,768]{2,1,0:T(8,128)(2,1)}, u32[]{:S(2)}, u32[]{:S(2)}) collective-permute-start(bf16[2,128,768]{2,1,0:T(8,128)(2,1)} %get-tuple-element.219), channel_id=1, source_target_pairs={{0,3},{1,2},{2,1},{3,0},{4,7},{5,6},{6,5},{7,4},{8,11},{9,10},{10,... | collective-permute-start | bytes 1179656 | tf_op jit(solution)/shard_map/ppermute | solution.py:965
  362.8 20.6 %collective-permute-start.50 = (bf16[1,48,3072]{2,1,0:T(8,128)(2,1)}, bf16[1,48,3072]{2,1,0:T(8,128)(2,1)}, u32[]{:S(2)}, u32[]{:S(2)}) collective-permute-start(bf16[1,48,3072]{2,1,0:T(8,128)(2,1)} %get-tuple-element.221), channel_id=1, source_target_pairs={{0,2},{1,3},{2,0},{3,1},{4,6},{5,7},{6,4},{7,5},{8,10},{9,11},{10,... | collective-permute-start | bytes 884744 | tf_op jit(solution)/shard_map/ppermute | solution.py:961
  364.1 16.9 %collective-permute-start.51 = (bf16[4,48,1664]{2,1,0:T(8,128)(2,1)S(1)}, bf16[4,48,1664]{2,1,0:T(8,128)(2,1)S(1)}, u32[]{:S(2)}, u32[]{:S(2)}) collective-permute-start(bf16[4,48,1664]{2,1,0:T(8,128)(2,1)S(1)} %get-tuple-element.223), channel_id=1, source_target_pairs={{0,4},{1,5},{2,6},{3,7},{4,0},{5,1},{6,2},{7,3},{8,12},{9,13},{10,... | collective-permute-start | bytes 1916936 | tf_op jit(solution)/shard_map/ppermute | solution.py:961
  385.0 15.0 %collective-permute-start.56 = (bf16[24,3072]{1,0:T(8,128)(2,1)S(1)}, bf16[24,3072]{1,0:T(8,128)(2,1)S(1)}, u32[]{:S(2)}, u32[]{:S(2)}) collective-permute-start(bf16[24,3072]{1,0:T(8,128)(2,1)S(1)} %bitcast.116), channel_id=1, source_target_pairs={{0,1},{1,0},{2,3},{3,2},{4,5},{5,4},{6,7},{7,6},{8,9},{9,8},{10,11... | collective-permute-start | bytes 442376 | tf_op jit(solution)/shard_map/ppermute | solution.py:961
  385.1 16.6 %collective-permute-start.52 = (bf16[1,48,1664]{2,1,0:T(8,128)(2,1)S(1)}, bf16[1,48,1664]{2,1,0:T(8,128)(2,1)S(1)}, u32[]{:S(2)}, u32[]{:S(2)}) collective-permute-start(bf16[1,48,1664]{2,1,0:T(8,128)(2,1)S(1)} %get-tuple-element.229), channel_id=1, source_target_pairs={{0,8},{1,9},{2,10},{3,11},{4,12},{5,13},{6,14},{7,15},{8,0},{9,1},... | collective-permute-start | bytes 479240 | tf_op jit(solution)/shard_map/ppermute | solution.py:961
  393.9 14.7 %collective-permute-start.53 = (bf16[1,48,1664]{2,1,0:T(8,128)(2,1)S(1)}, bf16[1,48,1664]{2,1,0:T(8,128)(2,1)S(1)}, u32[]{:S(2)}, u32[]{:S(2)}) collective-permute-start(bf16[1,48,1664]{2,1,0:T(8,128)(2,1)S(1)} %get-tuple-element.230), channel_id=1, source_target_pairs={{0,16},{1,17},{2,18},{3,19},{4,20},{5,21},{6,22},{7,23},{8,24},{9,... | collective-permute-start | bytes 479240 | tf_op jit(solution)/shard_map/ppermute | solution.py:961
  394.4 14.3 %collective-permute-start.54 = (bf16[1,48,1664]{2,1,0:T(8,128)(2,1)S(1)}, bf16[1,48,1664]{2,1,0:T(8,128)(2,1)S(1)}, u32[]{:S(2)}, u32[]{:S(2)}) collective-permute-start(bf16[1,48,1664]{2,1,0:T(8,128)(2,1)S(1)} %get-tuple-element.231), channel_id=1, source_target_pairs={{0,24},{1,25},{2,26},{3,27},{4,28},{5,29},{6,30},{7,31},{8,16},{9,... | collective-permute-start | bytes 479240 | tf_op jit(solution)/shard_map/ppermute | solution.py:961
  410.5 1.3 collective-permute-start.55
  (40 other events, 93.0 us)

commit v4 on v3

--- a/solution.py
+++ b/solution.py
@@ -307,18 +307,9 @@
     return list(zip(outs[:3], outs[3:]))
 
 
-def load_qkv(load, chunks, targets):
-    for turn, target in enumerate(targets):
-        cols, split = target.shape[-1], chunks[0][0].shape[-1]
-        for start, size, chunk in ((0, split, chunks[0]), (split, cols - split, chunks[1])):
-            load.rows(
-                chunk[2 * turn : 2 * turn + 2], 0, size, target.at[:, :, :, pl.ds(start, size)]
-            )
-
-
 def qkv_kernel(blk, ids, *refs):
     parts, refs = refs[:blk], refs[blk:]
-    chunks, refs = (refs[:4], refs[4:8]), refs[8:]
+    pieces, refs = (refs[:2], refs[2:4]), refs[4:]
     x_ref, vec_ref, out_ref, w_ref, w_far_ref, v_ref, sems = refs
     here, core = ids[0], ids[1]
     step = pl.program_id(0)
@@ -329,9 +320,9 @@
         load = Loader(ids, sems)
         for piece, part in enumerate(parts):
             load.put(part, x_ref.at[:, here ^ piece])
-        load_qkv(load, chunks, (w_ref, w_far_ref))
-        used = cols - chunks[0][0].shape[-1]
-        load.rows(chunks[1][:2], used, 128, v_ref)
+        load.rows(pieces[0], 0, cols, w_ref)
+        load.rows(pieces[1], 0, cols, w_far_ref)
+        load.rows(pieces[0], cols, 128, v_ref)
         load.wait()
         vec_ref[...] = flat(v_ref).astype(f32).T[: vec_ref.shape[0]]
 
@@ -359,24 +350,24 @@
     seqs, block_rows, width = parts[0].shape
     tokens = seqs * blk * block_rows
     block = 2 * block_rows
-    piece = pieces[0][0][0]
+    piece = pieces[0][0]
     shape = place_shape(piece, cols)
     x_shape = jax.ShapeDtypeStruct((seqs, blk, block_rows, width), bf16)
     v_shape = jax.ShapeDtypeStruct((16, width), f32)
     return kernel_call(
         partial(qkv_kernel, blk),
         ids,
-        [*parts, *[piece for chunk in pieces for pair in chunk for piece in pair]],
+        [*parts, *pieces[0], *pieces[1]],
         ties,
         (tokens // block,),
-        [any_block()] * (blk + 8),
+        [any_block()] * (blk + 4),
         (
             whole_block(x_shape),
             whole_block(v_shape),
             pl.BlockSpec((2, block, cols), lambda i, ids: (0, i, 0)),
         ),
         (x_shape, v_shape, jax.ShapeDtypeStruct((2, tokens, cols), bf16)),
-        [shape, shape, place_shape(piece, 128), pltpu.SemaphoreType.DMA((blk + 10,))],
+        [shape, shape, place_shape(piece, 128), pltpu.SemaphoreType.DMA((blk + 6,))],
         cost=brief,
     )
 
@@ -472,14 +463,14 @@
         sums_ref[0, 0] += sums
 
 
-def attention_specs(joined, mask_parts):
+def attention_specs(joined, mask_parts, turn=0):
     rows, length = mask_parts[0].shape[1:]
 
     def block(cols):
-        return pl.BlockSpec((1, length, cols), lambda r, p, s, ids: (r, s, p))
-
-    logs = pl.BlockSpec((1, joined.shape[1], 128), lambda r, p, s, ids: (r, 0, 0))
-    mask = pl.BlockSpec((2, rows, length), lambda r, p, s, ids: (2 * p + (ids[1] ^ r), 0, 0))
+        return pl.BlockSpec((1, length, cols), lambda r, p, s, ids: (turn + r, s, p))
+
+    logs = pl.BlockSpec((1, joined.shape[1], 128), lambda r, p, s, ids: (turn + r, 0, 0))
+    mask = pl.BlockSpec((2, rows, length), lambda r, p, s, ids: (2 * p + (ids[1] ^ (turn + r)), 0, 0))
     return block, logs, [mask] * len(mask_parts)
 
 
@@ -504,25 +495,26 @@
 
 
 def attend_back(
-    ids, joined, attended, upstream, logs, mask_parts, seqs, head_dim, ties=()
+    ids, joined, attended, upstream, logs, mask_parts, turn, seqs, head_dim, ties=()
 ):
     tokens, cols = joined.shape[1:]
     count = cols // 384
-    block, log_block, masks = attention_specs(joined, mask_parts)
+    length = tokens // seqs
+    block, log_block, masks = attention_specs(joined, mask_parts, turn)
     return kernel_call(
         partial(attend_back_kernel, head_dim),
         ids,
         [joined, attended, upstream, logs, *mask_parts],
         ties,
-        (2, count, seqs),
+        (1, count, seqs),
         [block(384), block(128), block(128), log_block] + masks,
         (
-            block(384),
+            pl.BlockSpec((1, length, 384), lambda r, p, s, ids: (0, s, p)),
             pl.BlockSpec((1, 1, 8, 384), lambda r, p, s, ids: (r, p, 0, 0)),
         ),
         (
-            jax.ShapeDtypeStruct((2, tokens, cols), bf16),
-            jax.ShapeDtypeStruct((2, count, 8, 384), f32),
+            jax.ShapeDtypeStruct((1, tokens, cols), bf16),
+            jax.ShapeDtypeStruct((1, count, 8, 384), f32),
         ),
     )
 
@@ -837,19 +829,20 @@
     ids,
     x_ref,
     g_ref,
+    g_far_ref,
     att_ref,
     branch_ref,
     sums_ref,
+    sums_far_ref,
     first_ref,
     second_ref,
     up_ref,
-    keep_ref,
-    send_ref,
+    *outs,
 ):
     core, step = ids[1], pl.program_id(0)
     attended = pair_order(core, att_ref[0], att_ref[1], 128)
     out_grads = half_split(core, dot_left_t(attended, branch_ref[...]))
-    sums = [sums_ref[turn, step][:1] for turn in range(2)]
+    sums = [ref[0, step][:1] for ref in (sums_ref, sums_far_ref)]
     rows = [
         pair_order(core, sums[0][:, at : at + 128], sums[1][:, at : at + 128], 128)
         for at in (0, 256)
@@ -860,50 +853,54 @@
     lanes = lax.broadcasted_iota(jnp.int32, (16, 128), 1)
     eye = lanes == lax.broadcasted_iota(jnp.int32, lanes.shape, 0)
     columns = dot_left_t(rows.astype(bf16), jnp.where(eye, 1.0, 0.0).astype(bf16))
-    for turn, out in enumerate((keep_ref, send_ref)):
-        grad = dot_left_t(x_ref[...], g_ref[turn])
-        out[...] = jnp.concatenate([grad, out_grads[turn], columns], axis=1).astype(bf16)
+    cut = outs[0].shape[1] - 128
+    for turn, ref in enumerate((g_ref, g_far_ref)):
+        grad = dot_left_t(x_ref[...], ref[0])
+        first = jnp.concatenate([grad[:, :cut], columns], axis=1)
+        second = jnp.concatenate([grad[:, cut:], out_grads[turn]], axis=1)
+        outs[turn][...] = first.astype(bf16)
+        outs[2 + turn][...] = second.astype(bf16)
 
 
 def left_grad(ids, left, grads, attended, grad_branch, sums, totals, ties=()):
     tokens, width = left.shape
-    cols = grads.shape[2] + width // 2 + 128
-    shape = jax.ShapeDtypeStruct((width, cols), bf16)
-    out = pl.BlockSpec((256, cols), lambda i, ids: (i, 0))
+    cut = grads[0].shape[2] - 384
+    sizes = [cut + 128] * 2 + [384 + width // 2] * 2
     return kernel_call(
         left_grad_kernel,
         ids,
-        [left, grads, attended, grad_branch, sums, *totals],
+        [left, *grads, attended, grad_branch, *sums, *totals],
         ties,
         (width // 256,),
         [
             pl.BlockSpec((tokens, 256), lambda i, ids: (0, i)),
-            whole_block(grads),
+            *[whole_block(grad) for grad in grads],
             pl.BlockSpec((2, tokens, 128), lambda i, ids: (0, 0, i)),
             whole_block(grad_branch),
-            whole_block(sums),
+            *[whole_block(array) for array in sums],
         ]
         + [pl.BlockSpec((array.shape[0], 256), lambda i, ids: (0, i)) for array in totals],
-        (out, out),
-        (shape, shape),
-    )
-
-
-def input_grad_kernel(blk, ids, g_ref, gfs_ref, *refs):
-    chunks, refs = (refs[:4], refs[4:8]), refs[8:]
+        [pl.BlockSpec((256, size), lambda i, ids: (i, 0)) for size in sizes],
+        [jax.ShapeDtypeStruct((width, size), bf16) for size in sizes],
+    )
+
+
+def input_grad_kernel(blk, ids, g_ref, g_far_ref, gfs_ref, *refs):
+    pieces, refs = (refs[:2], refs[2:4]), refs[4:]
     outs, (w_ref, w_far_ref, sems) = refs[:blk], refs[blk:]
     step = pl.program_id(0)
 
     @pl.when(step == 0)
     def _():
         load = Loader(ids, sems)
-        load_qkv(load, chunks, (w_ref, w_far_ref))
+        load.rows(pieces[0], 0, w_ref.shape[-1], w_ref)
+        load.rows(pieces[1], 0, w_ref.shape[-1], w_far_ref)
         load.wait()
 
     width = gfs_ref.shape[-1]
     total = gfs_ref[...].reshape(-1, width)
-    for turn, weights in enumerate((w_ref, w_far_ref)):
-        total = total + dot_right_t(g_ref[turn].reshape(-1, g_ref.shape[-1]), flat(weights))
+    for ref, weights in ((g_ref, w_ref), (g_far_ref, w_far_ref)):
+        total = total + dot_right_t(ref[...].reshape(-1, ref.shape[-1]), flat(weights))
     for piece, out in enumerate(outs):
 
         @pl.when(step == piece)
@@ -915,22 +912,22 @@
     tokens, width = grad_first_sum.shape
     length = tokens // seqs
     rows = length // blk
-    cols = grads.shape[2]
+    cols = grads[0].shape[2]
     piece = jax.ShapeDtypeStruct((seqs, rows, width), bf16)
-    shape = place_shape(pieces[0][0][0], cols)
-    pieces = [piece for chunk in pieces for pair in chunk for piece in pair]
+    shape = place_shape(pieces[0][0], cols)
+    pieces = [*pieces[0], *pieces[1]]
     return kernel_call(
         partial(input_grad_kernel, blk),
         ids,
         [
-            grads.reshape(2, seqs, length, cols),
+            *[grad.reshape(seqs, length, cols) for grad in grads],
             grad_first_sum.reshape(seqs, length, width),
             *pieces,
         ],
         ties,
         (blk,),
         [
-            pl.BlockSpec((2, seqs, rows, cols), lambda d, ids: (0, 0, ids[0] ^ d, 0)),
+            *[pl.BlockSpec((seqs, rows, cols), lambda d, ids: (0, ids[0] ^ d, 0))] * 2,
             pl.BlockSpec((seqs, rows, width), lambda d, ids: (0, ids[0] ^ d, 0)),
         ]
         + [any_block()] * len(pieces),
@@ -1058,6 +1055,10 @@
         self.left = [("z", sizes["z"]), ("y", sizes["y"]), ("x", sizes["x"])]
         self.last = 2 * (pairs[0][0].shape[0] // grid.total)
         self.groups = [[keep, grid.swap(send, "c")] for keep, send in pairs]
+
+    def join(self, other):
+        self.groups = self.groups + other.groups
+        return self
 
     def shaped(self, *shape):
         return [[term.reshape(*shape, term.shape[-1]) for term in group] for group in self.groups]
@@ -1135,6 +1136,7 @@
             jnp.zeros((16 - len(vectors) - up_per, rows), bf16),
         ]
     )
+    addend = jnp.where(dam_mask > 0, 0.0, masked_score).astype(bf16)
     halves = split_weights(ids, w_qkv, stacked, w_out, w_up, w_down)
     first_near, second_near, down_near = [gather_core(grid, *pair) for pair in halves]
 
@@ -1143,40 +1145,40 @@
 
     first_near = over_x(first_near)
     event = ids.token
-    split = first_near.shape[1] // 2
 
     by_home = inputs.reshape(blk, seqs, block_rows, width)
     parts = [pick(by_home, here ^ delta) for delta in range(blk)]
     parts[2:] = after(ids, parts[2:], event)
     parts[1:] = [grid.swap_blk(parts[delta], delta) for delta in range(1, blk)]
+    (addend,) = after(ids, [addend], event)
+    mask_parts = [addend, grid.swap(addend, "c")]
     second_near = over_x(second_near)
-    ties = [ids.token, *parts[2:]]
+    ties = [ids.token]
     down_near = over_x(down_near)
     ties.append(ids.token)
-    addend = jnp.where(dam_mask > 0, 0.0, masked_score).astype(bf16)
-    (addend,) = after(ids, [addend], event)
-    mask_parts = [addend, grid.swap(addend, "c")]
-    first_z = gather_step(grid, ids, first_near[:, :split], "z")
-    (rest,) = after(ids, [first_near[:, split:]], ids.token)
+
+    first_z = gather_step(grid, ids, first_near, "z", *ties, *parts[2:])
+    (second_near,) = after(ids, [second_near], ids.token)
     first_y = gather_last(grid, first_z, "y")
-    rest_z = gather_step(grid, ids, rest, "z", *ties)
-    (second_near,) = after(ids, [second_near], ids.token)
-    rest_y = gather_last(grid, rest_z, "y")
-    first_pieces = [gather_pieces(grid, ids, held) for held in (first_y, rest_y)]
-    event = [ids.token]
+    first_pieces = gather_pieces(grid, ids, first_y)
+    ties = []
     if grid.sizes["x"] > 1:
-        (far,) = after(ids, [grid.swap(addend, "x")], *event)
+        far = grid.swap(addend, "x")
         mask_parts += [far, grid.swap(far, "c")]
-        event.append(ids.token)
-    second_z = gather_step(grid, ids, second_near, "z", *event)
+        ties = [far]
+    second_z = gather_step(grid, ids, second_near, "z", *ties)
     (down_near,) = after(ids, [down_near], ids.token)
     second_y = gather_last(grid, second_z, "y")
-    token_rows, vector_rows, joined = qkv_projection(ids, parts, first_pieces, 3 * half, ties=[ids.token])
+    token_rows, vector_rows, joined = qkv_projection(
+        ids, parts, first_pieces, 3 * half, ties=[ids.token]
+    )
     token_rows = token_rows.reshape(tokens, width)
     first_row = len(vectors)
     up_bias = vector_rows[first_row : first_row + up_per].T.reshape(2, 1, -1)
 
-    attended, logs = attend(ids, joined, mask_parts, seqs, head_dim, ties=[ids.token])
+    attended, logs = attend(
+        ids, joined, mask_parts, seqs, head_dim, ties=[ids.token]
+    )
     down_z = gather_step(grid, ids, down_near, "z", ids.token)
     down_y = gather_last(grid, down_z, "y")
     second_pieces = gather_pieces(grid, ids, second_y, ids.token)
@@ -1200,8 +1202,10 @@
     result = home(result)
     down_halves = down_grad(ids, active, grad_down_in, grid.total)
     up_halves = up_grad(ids, hidden_low, grad_gate, width, ties=[ids.token])
-    ffn_sum = Scatter(grid, ids, [up_halves, down_halves], "yzx")
+    up_sum = Scatter(grid, ids, [up_halves], "yxz")
+    ffn_sum = Scatter(grid, ids, [down_halves], "xyz")
     ffn_sum.step([ids.token])
+    up_sum.step([ids.token])
     grad_first_sum, grad_branch, grad_attended, first_sums = first_back(
         ids,
         grad_gate,
@@ -1213,51 +1217,64 @@
         ties=[ids.token],
     )
     result = after(ids, result, ids.token)
-    grads, grad_sums = attend_back(
-        ids,
-        joined,
-        attended,
-        grad_attended,
-        logs,
-        mask_parts,
-        seqs,
-        head_dim,
-        ties=[ids.token],
-    )
+    def back(turn):
+        return attend_back(
+            ids,
+            joined,
+            attended,
+            grad_attended,
+            logs,
+            mask_parts,
+            turn,
+            seqs,
+            head_dim,
+            ties=[ids.token],
+        )
+
+    far_grads, far_sums = back(1)
+    ffn_sum.step([ids.token])
+    up_sum.step([ids.token])
+    near_grads, near_sums = back(0)
+    grads, grad_sums = (near_grads, far_grads), (near_sums, far_sums)
+    ffn_sum = up_sum.join(ffn_sum)
     ffn_sum.step([ids.token])
     up_rows = up_sums[0].reshape(width, up_per).T
     totals = [first_sums, second_sums, up_rows]
     halves = left_grad(
         ids, token_rows, grads, attended, grad_branch, grad_sums, totals, ties=[ids.token]
     )
-    att_sum = Scatter(grid, ids, [halves], "xyz")
-    att_sum.step([ids.token])
+    one_sum = Scatter(grid, ids, [halves[:2]], "xyz")
+    two_sum = Scatter(grid, ids, [halves[2:]], "yxz")
+    one_sum.step([ids.token])
+    two_sum.step([ids.token])
     sent = input_grad(ids, grads, grad_first_sum, first_pieces, seqs, blk, ties=[ids.token])
-    grad_inputs = home(sent)
-    att_sum.step([ids.token])
-    ffn_sum.step([ids.token])
+    one_sum.step([ids.token])
+    two_sum.step([ids.token])
+    grad_inputs = home([sent[0], *after(ids, sent[1:], ids.token)])
     activations = place_parts(ids, result, "here", [ids.token])
     activations = activations.reshape(groups, block_rows, width)
+    att_sum = one_sum.join(two_sum)
     att_sum.step([ids.token])
     share_ffn = ffn_sum.end([ids.token])
     grad_inputs = widen_parts(ids, grad_inputs, "here", [ids.token])
     grad_inputs = grad_inputs.reshape(groups, block_rows, width)
     share_att = att_sum.end([ids.token])
 
-    cols = grads.shape[2]
-    by_core = jnp.stack(in_order(core, *[share[:, :cols] for share in share_att]), axis=0)
-    by_core = by_core.reshape(2, rows, pairs, 3, 128)
+    cut = near_grads.shape[2] - 384
+    share_qkv = [
+        jnp.concatenate([share[:, :cut], share[:, cut + 128 : cut + 512]], axis=1)
+        for share in share_att
+    ]
+    by_core = jnp.stack(in_order(core, *share_qkv), axis=0).reshape(2, rows, pairs, 3, 128)
     share_qkv = by_core.transpose(1, 3, 2, 0, 4).reshape(rows, 3 * width)
-    share_out = jnp.concatenate(
-        in_order(core, *[share[:, cols : cols + half] for share in share_att]), axis=1
-    )
+    share_out = jnp.concatenate(in_order(core, *[share[:, cut + 512 :] for share in share_att]), axis=1)
     up_cols = up_halves[0].shape[1]
     share_up = [share[:, :up_cols] for share in share_ffn]
     share_down = [
         share[:, up_cols:].reshape(rows, up_per, half).transpose(1, 0, 2).reshape(-1, half)
         for share in share_ffn
     ]
-    shares = share_att[0][:, cols + half :]
+    shares = share_att[0][:, cut : cut + 128]
     share_vectors = [shares[:, index] for index in range(len(vectors))]
     share_bias_up = shares[:, len(vectors) : len(vectors) + up_per].reshape(-1)
     (

time: 415 us -> 386 us (0.930)
  waiting for transfers between devices: 104 us -> 81.4 us
  starting transfers between devices: 60.3 us -> 50.1 us
    ppermute x48 -> x47, waiting for transfers between devices: 104 us -> 74.1 us  [swap(): return lax.ppermute(array, both, pairs)]
    ppermute x48 -> x47, starting transfers between devices: 55.8 us -> 45.3 us  [swap(): return lax.ppermute(array, both, pairs)]
    ppermute x9, waiting for transfers between devices: 0.02 us -> 7.28 us  [swap_blk(): return lax.ppermute(array, both, pairs)]
    pallas_call x29 -> x33, Pallas kernels: 201 us -> 205 us  [kernel_call(): pl.pallas_call(body, out_shape=out_shape + [token_shape], grid_spec=pltpu...]
    unnamed x94 -> x96, local copies, waits for them, and re-layouts: 27.2 us -> 28.7 us
  transfers between devices with their start and end apart: 57 -> 56, of which waited for: 18 -> 16; matrix products, arithmetic and copies ran while one was open for 2% -> 2% of each run, Pallas kernels for 38% -> 41%
where the time goes in v4:
time: 386 us; the launch traced here: 384 us
  Pallas kernels  209 us (54%)
  waiting for transfers between devices  81.4 us (21%)
  starting transfers between devices  50.1 us (13%)
  local copies, waits for them, and re-layouts  35.3 us (9%)
  other arithmetic  6.78 us (2%)
    pallas_call x33, Pallas kernels, kernel_call(): pl.pallas_call(body, out_shape=out_shape + [token_shape], grid_spec=pltpu...  205 us
    ppermute x47, waiting for transfers between devices, swap(): return lax.ppermute(array, both, pairs)  74.1 us
    ppermute x47, starting transfers between devices, swap(): return lax.ppermute(array, both, pairs)  45.3 us
    unnamed x96, local copies, waits for them, and re-layouts  28.7 us
  transfers between devices with their start and end apart: 56, of which 16 were waited for; matrix products, arithmetic and copies ran while one was open for 2% of the time, Pallas kernels for 41%

profile of v4, /device:TPU:0, one launch (start us, length us, event | category | flops | bytes accessed | tf_op | source)
XLA Modules:
  0.0 384.3 jit_solution(8082910929665491605)
XLA Ops:
  8.1 3.6 select_convert_fusion.refs_0_
  12.8 2.6 collective-permute-start.2
  16.2 2.0 collective-permute-start.9
  18.2 1.3 collective-permute-done.2.refs_2_
  19.5 1.2 shard_map.290
  21.4 4.1 %collective-permute-start.7 = (bf16[96,1280]{1,0:T(8,128)(2,1)}, bf16[96,1280]{1,0:T(8,128)(2,1)}, u32[]{:S(2)}, u32[]{:S(2)}) collective-permute-start(bf16[96,1280]{1,0:T(8,128)(2,1)} %bitcast.25.refs_1_), channel_id=1, source_target_pairs={{0,24},{1,25},{2,26},{3,27},{4,28},{5,29},{6,30},{7,31},{8,16},{9,... | collective-permute-start | bytes 737288 | tf_op jit(solution)/shard_map/ppermute | solution.py:958
  27.2 1.7 collective-permute-start.3
  30.6 2.0 shard_map.292
  34.4 11.7 %collective-permute-done.6.refs_3_ = bf16[96,1280]{1,0:T(8,128)(2,1)} collective-permute-done((bf16[96,1280]{1,0:T(8,128)(2,1)}, bf16[96,1280]{1,0:T(8,128)(2,1)}, u32[]{:S(2)}, u32[]{:S(2)}) %collective-permute-start.6) | collective-permute-done | bytes 245792 | tf_op jit(solution)/shard_map/ppermute | solution.py:958
  47.1 3.1 shard_map.294
  50.9 1.5 collective-permute-start.12
  53.0 3.6 collective-permute-start.17
  57.4 9.1 %collective-permute-done.17.refs_4_ = bf16[96,1920]{1,0:T(8,128)(2,1)S(1)} collective-permute-done((bf16[96,1920]{1,0:T(8,128)(2,1)}, bf16[96,1920]{1,0:T(8,128)(2,1)S(1)}, u32[]{:S(2)}, u32[]{:S(2)}) %collective-permute-start.17) | collective-permute-done | bytes 368672 | tf_op jit(solution)/shard_map/ppermute | solution.py:958
  66.5 22.1 %collective-permute-done.16.refs_3_ = bf16[96,1920]{1,0:T(8,128)(2,1)S(1)} collective-permute-done((bf16[96,1920]{1,0:T(8,128)(2,1)}, bf16[96,1920]{1,0:T(8,128)(2,1)S(1)}, u32[]{:S(2)}, u32[]{:S(2)}) %collective-permute-start.16) | collective-permute-done | bytes 368672 | tf_op jit(solution)/shard_map/ppermute | solution.py:958
  90.2 1.7 shard_map.297
  93.0 2.4 collective-permute-start.24
  95.4 2.0 collective-permute-start.22
  99.1 9.3 %shard_map.299 = (bf16[2,4,128,768]{3,2,1,0:T(8,128)(2,1)}, f32[16,768]{1,0:T(8,128)S(1)}, bf16[2,1024,1152]{2,1,0:T(8,128)(2,1)}, f32[8,128]{1,0:T(8,128)S(1)}) custom-call(s32[5]{0:T(128)S(1)} %stack.79.refs_0_, bf16[2,128,768]{2,1,0:T(8,128)(2,1)S(1)} %get-tuple-element.278.refs_1_, bf16[2,128,768]{2,1,0:T(8,128)(2,1)S(1)} %collective-permute-done.refs_2_, ...), custom_call_target="tpu_custom_call" | custom-call | flops 99999997952 | bytes 1024 | tf_op jit(solution)/shard_map/pallas_call | solution.py:167
  110.2 19.9 %shard_map.300 = (bf16[2,1024,384]{2,1,0:T(8,128)(2,1)S(1)}, f32[2,1024,128]{2,1,0:T(8,128)S(1)}, f32[8,128]{1,0:T(8,128)S(1)}) custom-call(s32[5]{0:T(128)S(1)} %stack.79.refs_0_, bf16[2,1024,1152]{2,1,0:T(8,128)(2,1)} %get-tuple-element.161.refs_1_, bf16[12,128,512]{2,1,0:T(8,128)(2,1)} %get-tuple-element.158.refs_2_.refs_5_, ...), custom_call_target="tpu_custom_call" | custom-call | flops 99999997952 | bytes 1024 | tf_op jit(solution)/shard_map/pallas_call | solution.py:167
  131.3 2.7 shard_map.301
  134.6 9.1 %collective-permute-done.21.refs_0_ = bf16[4,96,1920]{2,1,0:T(8,128)(2,1)} collective-permute-done((bf16[4,96,1920]{2,1,0:T(8,128)(2,1)}, bf16[4,96,1920]{2,1,0:T(8,128)(2,1)}, u32[]{:S(2)}, u32[]{:S(2)}) %collective-permute-start.21) | collective-permute-done | bytes 1474592 | tf_op jit(solution)/shard_map/ppermute | solution.py:958
  145.8 1.9 collective-permute-done.26.refs_7_.refs_6_.refs_8_
  147.7 7.5 %shard_map.303 = (f32[1024,768]{1,0:T(8,128)}, bf16[1024,768]{1,0:T(8,128)(2,1)}, f32[8,128]{1,0:T(8,128)}) custom-call(s32[5]{0:T(128)S(1)} %stack.79.refs_0_, bf16[2,1024,384]{2,1,0:T(8,128)(2,1)} %copy-done.35, bf16[1024,768]{1,0:T(8,128)(2,1)} %bitcast.219, f32[16,768]{1,0:T(8,128)S(1)} %get-tuple-element.165.refs_3_.refs_6_.refs_4_, ...), custom_call_target="tpu_custom_call" | custom-call | flops 99999997952 | bytes 1024 | tf_op jit(solution)/shard_map/pallas_call | solution.py:167
  155.2 12.7 %shard_map.304 = (bf16[1024,3072]{1,0:T(8,128)(2,1)}, bf16[1024,3072]{1,0:T(8,128)(2,1)}, f32[8,128]{1,0:T(8,128)S(1)}) custom-call(s32[5]{0:T(128)S(1)} %stack.79.refs_0_, bf16[1024,768]{1,0:T(8,128)(2,1)} %get-tuple-element.171.refs_1_, f32[2,1,1536]{2,1,0:T(1,128)S(1)} %reshape.384.refs_2_, ...), custom_call_target="tpu_custom_call" | custom-call | flops 99999997952 | bytes 1024 | tf_op jit(solution)/shard_map/pallas_call | solution.py:167
  168.6 5.0 %collective-permute-done.27.refs_0_ = bf16[4,384,384]{2,1,0:T(8,128)(2,1)} collective-permute-done((bf16[4,384,384]{2,1,0:T(8,128)(2,1)}, bf16[4,384,384]{2,1,0:T(8,128)(2,1)}, u32[]{:S(2)}, u32[]{:S(2)}) %collective-permute-start.27) | collective-permute-done | bytes 1179680 | tf_op jit(solution)/shard_map/ppermute | solution.py:958
  174.3 3.0 collective-permute-done.29.refs_10_
  177.4 25.1 %shard_map.306 = (bf16[2,128,768]{2,1,0:T(8,128)(2,1)S(1)}, bf16[2,128,768]{2,1,0:T(8,128)(2,1)}, bf16[2,128,768]{2,1,0:T(8,128)(2,1)}, bf16[2,128,768]{2,1,0:T(...) custom-call(s32[5]{0:T(128)S(1)} %stack.79.refs_0_, ...), custom_call_target="tpu_custom_call" | custom-call | flops 99999997952 | bytes 1024 | tf_op jit(solution)/shard_map/pallas_call | solution.py:167
  203.3 1.4 copy-done.29
  204.7 8.8 %shard_map.307 = (bf16[768,1536]{1,0:T(8,128)(2,1)S(1)}, bf16[768,1536]{1,0:T(8,128)(2,1)}, f32[8,128]{1,0:T(8,128)S(1)}) custom-call(s32[5]{0:T(128)S(1)} %stack.79.refs_0_, bf16[1024,3072]{1,0:T(8,128)(2,1)} %get-tuple-element.172.refs_1_, bf16[1024,768]{1,0:T(8,128)(2,1)S(1)} %bitcast.156), custom_call_target="tpu_custom_call" | custom-call | flops 99999997952 | bytes 1024 | tf_op jit(solution)/shard_map/pallas_call | solution.py:167
  213.5 1.5 copy-done.27
  217.9 1.4 copy-done.38
  219.4 9.2 %shard_map.308 = (bf16[768,1536]{1,0:T(8,128)(2,1)S(1)}, bf16[768,1536]{1,0:T(8,128)(2,1)}, f32[8,128]{1,0:T(8,128)S(1)}) custom-call(s32[5]{0:T(128)S(1)} %stack.79.refs_0_, bf16[1024,768]{1,0:T(8,128)(2,1)S(1)} %copy-done.38, bf16[1024,3072]{1,0:T(8,128)(2,1)} %bitcast.208, bf16[1024,3072]{1,0:T(8,128)(2,1)} %bitcast.209, ...), custom_call_target="tpu_custom_call" | custom-call | flops 99999997952 | bytes 1024 | tf_op jit(solution)/shard_map/pallas_call | solution.py:167
  228.6 1.4 copy-done.46
  230.0 3.3 shard_map.309
  235.1 1.5 copy-done.45
  236.6 3.3 shard_map.310
  241.4 16.7 %shard_map.311 = (f32[1024,768]{1,0:T(8,128)}, bf16[1024,768]{1,0:T(8,128)(2,1)}, bf16[2,1024,384]{2,1,0:T(8,128)(2,1)}, f32[8,768]{1,0:T(8,128)S(1)}, f32[8,128]{1,0:T(8,128)S(1)}) custom-call(s32[5]{0:T(128)S(1)} %stack.79.refs_0_, bf16[1024,3072]{1,0:T(8,128)(2,1)} %bitcast.210, f32[1024,768]{1,0:T(8,128)} %bitcast.216, ...), custom_call_target="tpu_custom_call" | custom-call | flops 99999997952 | bytes 1024 | tf_op jit(solution)/shard_map/pallas_call | solution.py:167
  260.8 1.4 copy-done.36
  263.5 16.9 %shard_map.313 = (bf16[1,1024,1152]{2,1,0:T(8,128)(2,1)}, f32[1,3,8,384]{3,2,1,0:T(8,128)S(1)}, f32[8,128]{1,0:T(8,128)S(1)}) custom-call(s32[5]{0:T(128)S(1)} %stack.79.refs_0_, bf16[2,1024,1152]{2,1,0:T(8,128)(2,1)} %get-tuple-element.161.refs_1_, bf16[2,1024,384]{2,1,0:T(8,128)(2,1)S(1)} %copy-done.36, bf16[2,1024,384]{2,1,0:T(8,128)(2,1)S(1)} %copy-done.34, ...), custom_call_target="tpu_custom_call" | custom-call | flops 99999997952 | bytes 1024 | tf_op jit(solution)/shard_map/pallas_call | solution.py:167
  280.4 2.0 shard_map.314
  282.5 2.2 shard_map.315
  284.7 1.3 collective-permute-start.37
  286.0 1.5 collective-permute-start.38
  287.5 16.7 %shard_map.316 = (bf16[1,1024,1152]{2,1,0:T(8,128)(2,1)}, f32[1,3,8,384]{3,2,1,0:T(8,128)S(1)}, f32[8,128]{1,0:T(8,128)S(1)}) custom-call(s32[5]{0:T(128)S(1)} %stack.79.refs_0_, bf16[2,1024,1152]{2,1,0:T(8,128)(2,1)} %get-tuple-element.161.refs_1_, bf16[2,1024,384]{2,1,0:T(8,128)(2,1)S(1)} %copy-done.37, bf16[2,1024,384]{2,1,0:T(8,128)(2,1)S(1)} %copy-done.34, ...), custom_call_target="tpu_custom_call" | custom-call | flops 99999997952 | bytes 1024 | tf_op jit(solution)/shard_map/pallas_call | solution.py:167
  304.2 1.6 shard_map.317
  305.8 9.8 %shard_map.318 = (bf16[768,896]{1,0:T(8,128)(2,1)S(1)}, bf16[768,896]{1,0:T(8,128)(2,1)S(1)}, bf16[768,768]{1,0:T(8,128)(2,1)S(1)}, bf16[768,768]{1,0:T(8,128)(2,1)S(1)}, f32[8,128]{1,0:T(8,128)S(1)}) custom-call(s32[5]{0:T(128)S(1)} %stack.79.refs_0_, bf16[1024,768]{1,0:T(8,128)(2,1)} %bitcast.220, bf16[1,1024,1152]{2,1,0:T(8,128)(2,1)} %get-tuple-element.208.refs_2_, ...), custom_call_target="tpu_custom_call" | custom-call | flops 99999997952 | bytes 1024 | tf_op jit(solution)/shard_map/pallas_call | solution.py:167
  315.9 2.9 collective-permute-start.47
  318.7 1.4 collective-permute-start.48
  321.4 1.6 collective-permute-done.39
  323.0 1.8 shard_map.320
  326.1 10.2 %shard_map.321 = (bf16[2,128,768]{2,1,0:T(8,128)(2,1)S(1)}, bf16[2,128,768]{2,1,0:T(8,128)(2,1)}, bf16[2,128,768]{2,1,0:T(8,128)(2,1)}, bf16[2,128,768]{2,1,0:T(8,128)(2,1)S(1)}, f32[8,128]{1,0:T(8,128)S(1)}) custom-call(s32[5]{0:T(128)S(1)} %stack.79.refs_0_, bf16[2,512,1152]{2,1,0:T(8,128)(2,1)} %bitcast.218, bf16[2,512,1152]{2,1,0:T(8,128)(2,1)} %bitcast.217, ...), custom_call_target="tpu_custom_call" | custom-call | flops 99999997952 | bytes 1024 | tf_op jit(solution)/shard_map/pallas_call | solution.py:167
  336.4 6.1 %collective-permute-done.42 = bf16[8,48,896]{2,1,0:T(8,128)(2,1)S(1)} collective-permute-done((bf16[8,48,896]{2,1,0:T(8,128)(2,1)S(1)}, bf16[8,48,896]{2,1,0:T(8,128)(2,1)S(1)}, u32[]{:S(2)}, u32[]{:S(2)}) %collective-permute-start.42) | collective-permute-done | bytes 688160 | tf_op jit(solution)/shard_map/ppermute | solution.py:958
  343.5 2.1 shard_map.323
  347.0 1.5 collective-permute-start.49
  349.8 2.9 shard_map.325
  352.7 1.3 collective-permute-done.50
  354.1 1.6 collective-permute-done.49
  357.9 2.0 shard_map.327
  360.8 3.0 collective-permute-start.52
  363.8 4.2 %collective-permute-done.44.refs_3_ = bf16[2,128,768]{2,1,0:T(8,128)(2,1)} collective-permute-done((bf16[2,128,768]{2,1,0:T(8,128)(2,1)}, bf16[2,128,768]{2,1,0:T(8,128)(2,1)}, u32[]{:S(2)}, u32[]{:S(2)}) %collective-permute-start.44) | collective-permute-done | bytes 393248 | tf_op jit(solution)/shard_map/ppermute | solution.py:962
  368.0 2.4 collective-permute-start.53
  370.4 2.2 collective-permute-done.45.refs_4_
  372.6 3.5 shard_map.328
  379.6 1.8 collective-permute-start.54
  (232 shorter events, 56.4 us)
Async XLA Ops:
  0.6 173.6 %copy-start = (s32[8,128]{1,0:T(8,128)S(1)}, s32[8,128]{1,0:T(8,128)}, u32[]{:S(2)}) copy-start(s32[8,128]{1,0:T(8,128)} %param.33) | copy-start | bytes 12292
  7.1 5.6 %collective-permute-start.1 = (bf16[24,1280]{1,0:T(8,128)(2,1)S(1)}, bf16[24,1280]{1,0:T(8,128)(2,1)S(1)}, u32[]{:S(2)}, u32[]{:S(2)}) collective-permute-start(bf16[24,1280]{1,0:T(8,128)(2,1)S(1)} %get-tuple-element.141), channel_id=1, source_target_pairs={{0,1},{1,0},{2,3},{3,2},{4,5},{5,4},{6,7},{7,6},{8,9},{9,8},{10,11... | collective-permute-start | bytes 184328 | tf_op jit(solution)/shard_map/ppermute | solution.py:958
  7.6 7.8 %collective-permute-start.10 = (bf16[96,384]{1,0:T(8,128)(2,1)S(1)}, bf16[96,384]{1,0:T(8,128)(2,1)S(1)}, u32[]{:S(2)}, u32[]{:S(2)}) collective-permute-start(bf16[96,384]{1,0:T(8,128)(2,1)S(1)} %get-tuple-element.150), channel_id=1, source_target_pairs={{0,1},{1,0},{2,3},{3,2},{4,5},{5,4},{6,7},{7,6},{8,9},{9,8},{10,11... | collective-permute-start | bytes 221192 | tf_op jit(solution)/shard_map/ppermute | solution.py:958
  7.7 7.9 %collective-permute-start.8 = (bf16[24,1920]{1,0:T(8,128)(2,1)S(1)}, bf16[24,1920]{1,0:T(8,128)(2,1)S(1)}, u32[]{:S(2)}, u32[]{:S(2)}) collective-permute-start(bf16[24,1920]{1,0:T(8,128)(2,1)S(1)} %get-tuple-element.147), channel_id=1, source_target_pairs={{0,1},{1,0},{2,3},{3,2},{4,5},{5,4},{6,7},{7,6},{8,9},{9,8},{10,11... | collective-permute-start | bytes 276488 | tf_op jit(solution)/shard_map/ppermute | solution.py:958
  12.8 6.7 %collective-permute-start.2 = (bf16[48,1280]{1,0:T(8,128)(2,1)S(1)}, bf16[48,1280]{1,0:T(8,128)(2,1)S(1)}, u32[]{:S(2)}, u32[]{:S(2)}) collective-permute-start(bf16[48,1280]{1,0:T(8,128)(2,1)S(1)} %bitcast.119), channel_id=1, source_target_pairs={{0,2},{1,3},{2,0},{3,1},{4,6},{5,7},{6,4},{7,5},{8,10},{9,11},{10,... | collective-permute-start | bytes 368648 | tf_op jit(solution)/shard_map/ppermute | solution.py:958
  15.4 11.8 %collective-permute-start.11 = (bf16[192,384]{1,0:T(8,128)(2,1)S(1)}, bf16[192,384]{1,0:T(8,128)(2,1)S(1)}, u32[]{:S(2)}, u32[]{:S(2)}) collective-permute-start(bf16[192,384]{1,0:T(8,128)(2,1)S(1)} %bitcast.117), channel_id=1, source_target_pairs={{0,2},{1,3},{2,0},{3,1},{4,6},{5,7},{6,4},{7,5},{8,10},{9,11},{10,... | collective-permute-start | bytes 442376 | tf_op jit(solution)/shard_map/ppermute | solution.py:958
  16.2 14.3 %collective-permute-start.9 = (bf16[48,1920]{1,0:T(8,128)(2,1)}, bf16[48,1920]{1,0:T(8,128)(2,1)}, u32[]{:S(2)}, u32[]{:S(2)}) collective-permute-start(bf16[48,1920]{1,0:T(8,128)(2,1)} %bitcast.28.refs_1_), channel_id=1, source_target_pairs={{0,2},{1,3},{2,0},{3,1},{4,6},{5,7},{6,4},{7,5},{8,10},{9,11},{10,... | collective-permute-start | bytes 552968 | tf_op jit(solution)/shard_map/ppermute | solution.py:958
  21.4 12.0 %collective-permute-start.7 = (bf16[96,1280]{1,0:T(8,128)(2,1)}, bf16[96,1280]{1,0:T(8,128)(2,1)}, u32[]{:S(2)}, u32[]{:S(2)}) collective-permute-start(bf16[96,1280]{1,0:T(8,128)(2,1)} %bitcast.25.refs_1_), channel_id=1, source_target_pairs={{0,24},{1,25},{2,26},{3,27},{4,28},{5,29},{6,30},{7,31},{8,16},{9,... | collective-permute-start | bytes 737288 | tf_op jit(solution)/shard_map/ppermute | solution.py:958
  25.4 20.7 %collective-permute-start.6 = (bf16[96,1280]{1,0:T(8,128)(2,1)}, bf16[96,1280]{1,0:T(8,128)(2,1)}, u32[]{:S(2)}, u32[]{:S(2)}) collective-permute-start(bf16[96,1280]{1,0:T(8,128)(2,1)} %bitcast.25.refs_1_), channel_id=1, source_target_pairs={{0,16},{1,17},{2,18},{3,19},{4,20},{5,21},{6,22},{7,23},{8,24},{9,... | collective-permute-start | bytes 737288 | tf_op jit(solution)/shard_map/ppermute | solution.py:958
  25.4 20.7 %collective-permute-start.5 = (bf16[96,1280]{1,0:T(8,128)(2,1)}, bf16[96,1280]{1,0:T(8,128)(2,1)}, u32[]{:S(2)}, u32[]{:S(2)}) collective-permute-start(bf16[96,1280]{1,0:T(8,128)(2,1)} %bitcast.25.refs_1_), channel_id=1, source_target_pairs={{0,8},{1,9},{2,10},{3,11},{4,12},{5,13},{6,14},{7,15},{8,0},{9,1},... | collective-permute-start | bytes 737288 | tf_op jit(solution)/shard_map/ppermute | solution.py:958
  27.2 19.0 %collective-permute-start.3 = (bf16[2,128,768]{2,1,0:T(8,128)(2,1)}, bf16[2,128,768]{2,1,0:T(8,128)(2,1)}, u32[]{:S(2)}, u32[]{:S(2)}) collective-permute-start(bf16[2,128,768]{2,1,0:T(8,128)(2,1)} %get-tuple-element.144), channel_id=1, source_target_pairs={{0,2},{1,3},{2,0},{3,1},{4,6},{5,7},{6,4},{7,5},{8,10},{9,11},{10,... | collective-permute-start | bytes 1179656 | tf_op jit(solution)/shard_map/ppermute | solution.py:962
  30.6 16.5 %collective-permute-start.4 = (bf16[2,128,768]{2,1,0:T(8,128)(2,1)S(1)}, bf16[2,128,768]{2,1,0:T(8,128)(2,1)S(1)}, u32[]{:S(2)}, u32[]{:S(2)}) collective-permute-start(bf16[2,128,768]{2,1,0:T(8,128)(2,1)S(1)} %copy-done.43), channel_id=1, source_target_pairs={{0,3},{1,2},{2,1},{3,0},{4,7},{5,6},{6,5},{7,4},{8,11},{9,10},{10,... | collective-permute-start | bytes 1179656 | tf_op jit(solution)/shard_map/ppermute | solution.py:962
  33.4 55.8 %collective-permute-start.18 = (bf16[12,128,512]{2,1,0:T(8,128)(2,1)}, bf16[12,128,512]{2,1,0:T(8,128)(2,1)S(1)}, u32[]{:S(2)}, u32[]{:S(2)}) collective-permute-start(bf16[12,128,512]{2,1,0:T(8,128)(2,1)} %get-tuple-element.158.refs_2_.refs_5_), channel_id=1, source_target_pairs={{0,2},{1,3},{2,0},{3,1},{4,6},{5,7},{6,4},{7,5},{8,10},{9,11},{10,... | collective-permute-start | bytes 4718600 | tf_op jit(solution)/shard_map/ppermute | solution.py:958
  50.9 38.2 %collective-permute-start.12 = (bf16[4,96,1280]{2,1,0:T(8,128)(2,1)S(1)}, bf16[4,96,1280]{2,1,0:T(8,128)(2,1)}, u32[]{:S(2)}, u32[]{:S(2)}) collective-permute-start(bf16[4,96,1280]{2,1,0:T(8,128)(2,1)S(1)} %get-tuple-element.153.refs_5_.refs_4_), channel_id=1, source_target_pairs={{0,4},{1,5},{2,6},{3,7},{4,0},{5,1},{6,2},{7,3},{8,12},{9,13},{10,... | collective-permute-start | bytes 2949128 | tf_op jit(solution)/shard_map/ppermute | solution.py:958
  53.0 13.5 %collective-permute-start.17 = (bf16[96,1920]{1,0:T(8,128)(2,1)}, bf16[96,1920]{1,0:T(8,128)(2,1)S(1)}, u32[]{:S(2)}, u32[]{:S(2)}) collective-permute-start(bf16[96,1920]{1,0:T(8,128)(2,1)} %get-tuple-element.157.refs_1_), channel_id=1, source_target_pairs={{0,24},{1,25},{2,26},{3,27},{4,28},{5,29},{6,30},{7,31},{8,16},{9,... | collective-permute-start | bytes 1105928 | tf_op jit(solution)/shard_map/ppermute | solution.py:958
  56.6 32.0 %collective-permute-start.16 = (bf16[96,1920]{1,0:T(8,128)(2,1)}, bf16[96,1920]{1,0:T(8,128)(2,1)S(1)}, u32[]{:S(2)}, u32[]{:S(2)}) collective-permute-start(bf16[96,1920]{1,0:T(8,128)(2,1)} %get-tuple-element.157.refs_1_), channel_id=1, source_target_pairs={{0,16},{1,17},{2,18},{3,19},{4,20},{5,21},{6,22},{7,23},{8,24},{9,... | collective-permute-start | bytes 1105928 | tf_op jit(solution)/shard_map/ppermute | solution.py:958
  56.6 32.0 %collective-permute-start.15 = (bf16[96,1920]{1,0:T(8,128)(2,1)}, bf16[96,1920]{1,0:T(8,128)(2,1)S(1)}, u32[]{:S(2)}, u32[]{:S(2)}) collective-permute-start(bf16[96,1920]{1,0:T(8,128)(2,1)} %get-tuple-element.157.refs_1_), channel_id=1, source_target_pairs={{0,8},{1,9},{2,10},{3,11},{4,12},{5,13},{6,14},{7,15},{8,0},{9,1},... | collective-permute-start | bytes 1105928 | tf_op jit(solution)/shard_map/ppermute | solution.py:958
  66.5 28.9 %collective-permute-start = (bf16[2,128,768]{2,1,0:T(8,128)(2,1)}, bf16[2,128,768]{2,1,0:T(8,128)(2,1)S(1)}, u32[]{:S(2)}, u32[]{:S(2)}) collective-permute-start(bf16[2,128,768]{2,1,0:T(8,128)(2,1)} %get-tuple-element.277), channel_id=1, source_target_pairs={{0,1},{1,0},{2,3},{3,2},{4,5},{5,4},{6,7},{7,6},{8,9},{9,8},{10,11... | collective-permute-start | bytes 1179656 | tf_op jit(solution)/shard_map/ppermute | solution.py:962
  88.6 19.9 %collective-permute-start.19 = (bf16[12,128,512]{2,1,0:T(8,128)(2,1)}, bf16[12,128,512]{2,1,0:T(8,128)(2,1)}, u32[]{:S(2)}, u32[]{:S(2)}) collective-permute-start(bf16[12,128,512]{2,1,0:T(8,128)(2,1)} %get-tuple-element.158.refs_2_.refs_5_), channel_id=1, source_target_pairs={{0,1},{1,0},{2,3},{3,2},{4,5},{5,4},{6,7},{7,6},{8,9},{9,8},{10,11... | collective-permute-start | bytes 4718600 | tf_op jit(solution)/shard_map/ppermute | solution.py:958
  88.6 6.9 %collective-permute-start.13 = (bf16[4,96,1280]{2,1,0:T(8,128)(2,1)S(1)}, bf16[4,96,1280]{2,1,0:T(8,128)(2,1)}, u32[]{:S(2)}, u32[]{:S(2)}) collective-permute-start(bf16[4,96,1280]{2,1,0:T(8,128)(2,1)S(1)} %get-tuple-element.153.refs_5_.refs_4_), channel_id=1, source_target_pairs={{0,1},{1,0},{2,3},{3,2},{4,5},{5,4},{6,7},{7,6},{8,9},{9,8},{10,11... | collective-permute-start | bytes 2949128 | tf_op jit(solution)/shard_map/ppermute | solution.py:958
  89.1 8.3 %collective-permute-start.14 = (bf16[4,96,1280]{2,1,0:T(8,128)(2,1)}, bf16[4,96,1280]{2,1,0:T(8,128)(2,1)}, u32[]{:S(2)}, u32[]{:S(2)}) collective-permute-start(bf16[4,96,1280]{2,1,0:T(8,128)(2,1)} %collective-permute-done.12.refs_6_.refs_5_), channel_id=1, source_target_pairs={{0,1},{1,0},{2,3},{3,2},{4,5},{5,4},{6,7},{7,6},{8,9},{9,8},{10,11... | collective-permute-start | bytes 2949128 | tf_op jit(solution)/shard_map/ppermute | solution.py:958
  90.2 7.3 %copy-start.17 = (bf16[12,128,512]{2,1,0:T(8,128)(2,1)}, bf16[12,128,512]{2,1,0:T(8,128)(2,1)S(1)}, u32[]{:S(2)}) copy-start(bf16[12,128,512]{2,1,0:T(8,128)(2,1)S(1)} %collective-permute-done.18.refs_5_.refs_4_.refs_7_) | copy-start | bytes 4718596
  93.0 38.2 %collective-permute-start.24 = (bf16[384,384]{1,0:T(8,128)(2,1)}, bf16[384,384]{1,0:T(8,128)(2,1)}, u32[]{:S(2)}, u32[]{:S(2)}) collective-permute-start(bf16[384,384]{1,0:T(8,128)(2,1)} %get-tuple-element.167.refs_1_), channel_id=1, source_target_pairs={{0,24},{1,25},{2,26},{3,27},{4,28},{5,29},{6,30},{7,31},{8,16},{9,... | collective-permute-start | bytes 884744 | tf_op jit(solution)/shard_map/ppermute | solution.py:958
  95.4 35.8 %collective-permute-start.23 = (bf16[384,384]{1,0:T(8,128)(2,1)}, bf16[384,384]{1,0:T(8,128)(2,1)}, u32[]{:S(2)}, u32[]{:S(2)}) collective-permute-start(bf16[384,384]{1,0:T(8,128)(2,1)} %get-tuple-element.167.refs_1_), channel_id=1, source_target_pairs={{0,16},{1,17},{2,18},{3,19},{4,20},{5,21},{6,22},{7,23},{8,24},{9,... | collective-permute-start | bytes 884744 | tf_op jit(solution)/shard_map/ppermute | solution.py:958
  95.4 35.8 %collective-permute-start.22 = (bf16[384,384]{1,0:T(8,128)(2,1)}, bf16[384,384]{1,0:T(8,128)(2,1)}, u32[]{:S(2)}, u32[]{:S(2)}) collective-permute-start(bf16[384,384]{1,0:T(8,128)(2,1)} %get-tuple-element.167.refs_1_), channel_id=1, source_target_pairs={{0,8},{1,9},{2,10},{3,11},{4,12},{5,13},{6,14},{7,15},{8,0},{9,1},... | collective-permute-start | bytes 884744 | tf_op jit(solution)/shard_map/ppermute | solution.py:958
  97.4 11.6 %collective-permute-start.20 = (bf16[12,128,512]{2,1,0:T(8,128)(2,1)S(1)}, bf16[12,128,512]{2,1,0:T(8,128)(2,1)S(1)}, u32[]{:S(2)}, u32[]{:S(2)}) collective-permute-start(bf16[12,128,512]{2,1,0:T(8,128)(2,1)S(1)} %collective-permute-done.18.refs_5_.refs_4_.refs_7_), channel_id=1, source_target_pairs={{0,1},{1,0},{2,3},{3,2},{4,5},{5,4},{6,7},{7,6},{8,9},{9,8},{10,11... | collective-permute-start | bytes 4718600 | tf_op jit(solution)/shard_map/ppermute | solution.py:958
  108.5 37.3 %collective-permute-start.25 = (bf16[4,96,1920]{2,1,0:T(8,128)(2,1)}, bf16[4,96,1920]{2,1,0:T(8,128)(2,1)}, u32[]{:S(2)}, u32[]{:S(2)}) collective-permute-start(bf16[4,96,1920]{2,1,0:T(8,128)(2,1)} %get-tuple-element.166.refs_4_.refs_3_.refs_5_), channel_id=1, source_target_pairs={{0,1},{1,0},{2,3},{3,2},{4,5},{5,4},{6,7},{7,6},{8,9},{9,8},{10,11... | collective-permute-start | bytes 4423688 | tf_op jit(solution)/shard_map/ppermute | solution.py:958
  109.1 34.6 %collective-permute-start.21 = (bf16[4,96,1920]{2,1,0:T(8,128)(2,1)}, bf16[4,96,1920]{2,1,0:T(8,128)(2,1)}, u32[]{:S(2)}, u32[]{:S(2)}) collective-permute-start(bf16[4,96,1920]{2,1,0:T(8,128)(2,1)} %get-tuple-element.166.refs_4_.refs_3_.refs_5_), channel_id=1, source_target_pairs={{0,4},{1,5},{2,6},{3,7},{4,0},{5,1},{6,2},{7,3},{8,12},{9,13},{10,... | collective-permute-start | bytes 4423688 | tf_op jit(solution)/shard_map/ppermute | solution.py:958
  110.2 21.1 %copy-start.9 = (bf16[384,384]{1,0:T(8,128)(2,1)S(1)}, bf16[384,384]{1,0:T(8,128)(2,1)}, u32[]{:S(2)}) copy-start(bf16[384,384]{1,0:T(8,128)(2,1)} %get-tuple-element.167.refs_1_) | copy-start | bytes 884740
  144.3 3.5 collective-permute-start.26
  144.7 29.6 %collective-permute-start.28 = (bf16[4,384,384]{2,1,0:T(8,128)(2,1)}, bf16[4,384,384]{2,1,0:T(8,128)(2,1)}, u32[]{:S(2)}, u32[]{:S(2)}) collective-permute-start(bf16[4,384,384]{2,1,0:T(8,128)(2,1)} %get-tuple-element.175.refs_7_), channel_id=1, source_target_pairs={{0,1},{1,0},{2,3},{3,2},{4,5},{5,4},{6,7},{7,6},{8,9},{9,8},{10,11... | collective-permute-start | bytes 3538952 | tf_op jit(solution)/shard_map/ppermute | solution.py:958
  145.3 28.3 %collective-permute-start.27 = (bf16[4,384,384]{2,1,0:T(8,128)(2,1)}, bf16[4,384,384]{2,1,0:T(8,128)(2,1)}, u32[]{:S(2)}, u32[]{:S(2)}) collective-permute-start(bf16[4,384,384]{2,1,0:T(8,128)(2,1)} %get-tuple-element.175.refs_7_), channel_id=1, source_target_pairs={{0,4},{1,5},{2,6},{3,7},{4,0},{5,1},{6,2},{7,3},{8,12},{9,13},{10,... | collective-permute-start | bytes 3538952 | tf_op jit(solution)/shard_map/ppermute | solution.py:958
  155.2 18.9 %copy-start.44 = (s32[8]{0:T(128)S(1)}, s32[8]{0:T(128)}, u32[]{:S(2)}) copy-start(s32[8]{0:T(128)} %param.34) | copy-start | bytes 100
  174.2 3.2 collective-permute-start.29
  215.6 43.2 %collective-permute-start.30 = (bf16[2,128,768]{2,1,0:T(8,128)(2,1)}, bf16[2,128,768]{2,1,0:T(8,128)(2,1)}, u32[]{:S(2)}, u32[]{:S(2)}) collective-permute-start(bf16[2,128,768]{2,1,0:T(8,128)(2,1)} %get-tuple-element.179), channel_id=1, source_target_pairs={{0,1},{1,0},{2,3},{3,2},{4,5},{5,4},{6,7},{7,6},{8,9},{9,8},{10,11... | collective-permute-start | bytes 1179656 | tf_op jit(solution)/shard_map/ppermute | solution.py:962
  215.8 42.9 %collective-permute-start.31 = (bf16[2,128,768]{2,1,0:T(8,128)(2,1)}, bf16[2,128,768]{2,1,0:T(8,128)(2,1)}, u32[]{:S(2)}, u32[]{:S(2)}) collective-permute-start(bf16[2,128,768]{2,1,0:T(8,128)(2,1)} %get-tuple-element.180), channel_id=1, source_target_pairs={{0,2},{1,3},{2,0},{3,1},{4,6},{5,7},{6,4},{7,5},{8,10},{9,11},{10,... | collective-permute-start | bytes 1179656 | tf_op jit(solution)/shard_map/ppermute | solution.py:962
  216.5 42.2 %collective-permute-start.32 = (bf16[2,128,768]{2,1,0:T(8,128)(2,1)}, bf16[2,128,768]{2,1,0:T(8,128)(2,1)}, u32[]{:S(2)}, u32[]{:S(2)}) collective-permute-start(bf16[2,128,768]{2,1,0:T(8,128)(2,1)} %get-tuple-element.181), channel_id=1, source_target_pairs={{0,3},{1,2},{2,1},{3,0},{4,7},{5,6},{6,5},{7,4},{8,11},{9,10},{10,... | collective-permute-start | bytes 1179656 | tf_op jit(solution)/shard_map/ppermute | solution.py:962
  217.5 11.1 %collective-permute-start.34 = (bf16[768,1536]{1,0:T(8,128)(2,1)}, bf16[768,1536]{1,0:T(8,128)(2,1)S(1)}, u32[]{:S(2)}, u32[]{:S(2)}) collective-permute-start(bf16[768,1536]{1,0:T(8,128)(2,1)} %get-tuple-element.189), channel_id=1, source_target_pairs={{0,1},{1,0},{2,3},{3,2},{4,5},{5,4},{6,7},{7,6},{8,9},{9,8},{10,11... | collective-permute-start | bytes 7077896 | tf_op jit(solution)/shard_map/ppermute | solution.py:958
  219.4 10.6 %copy-start.28 = (bf16[768,1536]{1,0:T(8,128)(2,1)S(1)}, bf16[768,1536]{1,0:T(8,128)(2,1)}, u32[]{:S(2)}) copy-start(bf16[768,1536]{1,0:T(8,128)(2,1)} %copy-done.27) | copy-start | bytes 7077892
  228.5 6.6 %collective-permute-start.33 = (bf16[768,1536]{1,0:T(8,128)(2,1)}, bf16[768,1536]{1,0:T(8,128)(2,1)S(1)}, u32[]{:S(2)}, u32[]{:S(2)}) collective-permute-start(bf16[768,1536]{1,0:T(8,128)(2,1)} %get-tuple-element.187), channel_id=1, source_target_pairs={{0,1},{1,0},{2,3},{3,2},{4,5},{5,4},{6,7},{7,6},{8,9},{9,8},{10,11... | collective-permute-start | bytes 7077896 | tf_op jit(solution)/shard_map/ppermute | solution.py:958
  234.3 46.1 %collective-permute-start.36 = (bf16[8,48,1536]{2,1,0:T(8,128)(2,1)}, bf16[8,48,1536]{2,1,0:T(8,128)(2,1)}, u32[]{:S(2)}, u32[]{:S(2)}) collective-permute-start(bf16[8,48,1536]{2,1,0:T(8,128)(2,1)} %get-tuple-element.203), channel_id=1, source_target_pairs={{0,2},{1,3},{2,0},{3,1},{4,6},{5,7},{6,4},{7,5},{8,10},{9,11},{10,... | collective-permute-start | bytes 3538952 | tf_op jit(solution)/shard_map/ppermute | solution.py:958
  240.9 41.6 %collective-permute-start.35 = (bf16[4,96,1536]{2,1,0:T(8,128)(2,1)}, bf16[4,96,1536]{2,1,0:T(8,128)(2,1)}, u32[]{:S(2)}, u32[]{:S(2)}) collective-permute-start(bf16[4,96,1536]{2,1,0:T(8,128)(2,1)} %get-tuple-element.201), channel_id=1, source_target_pairs={{0,4},{1,5},{2,6},{3,7},{4,0},{5,1},{6,2},{7,3},{8,12},{9,13},{10,... | collective-permute-start | bytes 3538952 | tf_op jit(solution)/shard_map/ppermute | solution.py:958
  263.5 17.0 %copy-start.31 = (bf16[8,48,1536]{2,1,0:T(8,128)(2,1)S(1)}, bf16[8,48,1536]{2,1,0:T(8,128)(2,1)}, u32[]{:S(2)}) copy-start(bf16[8,48,1536]{2,1,0:T(8,128)(2,1)} %copy-done.30) | copy-start | bytes 3538948
  284.7 19.6 %collective-permute-start.37 = (bf16[4,48,1536]{2,1,0:T(8,128)(2,1)S(1)}, bf16[4,48,1536]{2,1,0:T(8,128)(2,1)S(1)}, u32[]{:S(2)}, u32[]{:S(2)}) collective-permute-start(bf16[4,48,1536]{2,1,0:T(8,128)(2,1)S(1)} %get-tuple-element.218), channel_id=1, source_target_pairs={{0,2},{1,3},{2,0},{3,1},{4,6},{5,7},{6,4},{7,5},{8,10},{9,11},{10,... | collective-permute-start | bytes 1769480 | tf_op jit(solution)/shard_map/ppermute | solution.py:958
  286.0 18.3 %collective-permute-start.38 = (bf16[4,48,1536]{2,1,0:T(8,128)(2,1)S(1)}, bf16[4,48,1536]{2,1,0:T(8,128)(2,1)S(1)}, u32[]{:S(2)}, u32[]{:S(2)}) collective-permute-start(bf16[4,48,1536]{2,1,0:T(8,128)(2,1)S(1)} %get-tuple-element.220), channel_id=1, source_target_pairs={{0,4},{1,5},{2,6},{3,7},{4,0},{5,1},{6,2},{7,3},{8,12},{9,13},{10,... | collective-permute-start | bytes 1769480 | tf_op jit(solution)/shard_map/ppermute | solution.py:958
  315.6 4.5 %collective-permute-start.40 = (bf16[768,896]{1,0:T(8,128)(2,1)S(1)}, bf16[768,896]{1,0:T(8,128)(2,1)S(1)}, u32[]{:S(2)}, u32[]{:S(2)}) collective-permute-start(bf16[768,896]{1,0:T(8,128)(2,1)S(1)} %get-tuple-element.226), channel_id=1, source_target_pairs={{0,1},{1,0},{2,3},{3,2},{4,5},{5,4},{6,7},{7,6},{8,9},{9,8},{10,11... | collective-permute-start | bytes 4128776 | tf_op jit(solution)/shard_map/ppermute | solution.py:958
  315.7 41.9 %collective-permute-start.46 = (bf16[1,48,3072]{2,1,0:T(8,128)(2,1)}, bf16[1,48,3072]{2,1,0:T(8,128)(2,1)}, u32[]{:S(2)}, u32[]{:S(2)}) collective-permute-start(bf16[1,48,3072]{2,1,0:T(8,128)(2,1)} %get-tuple-element.247), channel_id=1, source_target_pairs={{0,8},{1,9},{2,10},{3,11},{4,12},{5,13},{6,14},{7,15},{8,0},{9,1},... | collective-permute-start | bytes 884744 | tf_op jit(solution)/shard_map/ppermute | solution.py:958
  315.9 42.0 %collective-permute-start.47 = (bf16[1,48,3072]{2,1,0:T(8,128)(2,1)}, bf16[1,48,3072]{2,1,0:T(8,128)(2,1)}, u32[]{:S(2)}, u32[]{:S(2)}) collective-permute-start(bf16[1,48,3072]{2,1,0:T(8,128)(2,1)} %get-tuple-element.248), channel_id=1, source_target_pairs={{0,16},{1,17},{2,18},{3,19},{4,20},{5,21},{6,22},{7,23},{8,24},{9,... | collective-permute-start | bytes 884744 | tf_op jit(solution)/shard_map/ppermute | solution.py:958
  318.7 39.1 %collective-permute-start.48 = (bf16[1,48,3072]{2,1,0:T(8,128)(2,1)}, bf16[1,48,3072]{2,1,0:T(8,128)(2,1)}, u32[]{:S(2)}, u32[]{:S(2)}) collective-permute-start(bf16[1,48,3072]{2,1,0:T(8,128)(2,1)} %get-tuple-element.249), channel_id=1, source_target_pairs={{0,24},{1,25},{2,26},{3,27},{4,28},{5,29},{6,30},{7,31},{8,16},{9,... | collective-permute-start | bytes 884744 | tf_op jit(solution)/shard_map/ppermute | solution.py:958
  320.2 2.8 collective-permute-start.39
  324.8 18.7 %collective-permute-start.41 = (bf16[4,96,768]{2,1,0:T(8,128)(2,1)}, bf16[4,96,768]{2,1,0:T(8,128)(2,1)}, u32[]{:S(2)}, u32[]{:S(2)}) collective-permute-start(bf16[4,96,768]{2,1,0:T(8,128)(2,1)} %get-tuple-element.234), channel_id=1, source_target_pairs={{0,4},{1,5},{2,6},{3,7},{4,0},{5,1},{6,2},{7,3},{8,12},{9,13},{10,... | collective-permute-start | bytes 1769480 | tf_op jit(solution)/shard_map/ppermute | solution.py:958
  325.3 17.2 %collective-permute-start.42 = (bf16[8,48,896]{2,1,0:T(8,128)(2,1)S(1)}, bf16[8,48,896]{2,1,0:T(8,128)(2,1)S(1)}, u32[]{:S(2)}, u32[]{:S(2)}) collective-permute-start(bf16[8,48,896]{2,1,0:T(8,128)(2,1)S(1)} %get-tuple-element.236), channel_id=1, source_target_pairs={{0,2},{1,3},{2,0},{3,1},{4,6},{5,7},{6,4},{7,5},{8,10},{9,11},{10,... | collective-permute-start | bytes 2064392 | tf_op jit(solution)/shard_map/ppermute | solution.py:958
  336.3 7.1 %copy-start.4 = (bf16[2,128,768]{2,1,0:T(8,128)(2,1)}, bf16[2,128,768]{2,1,0:T(8,128)(2,1)S(1)}, u32[]{:S(2)}) copy-start(bf16[2,128,768]{2,1,0:T(8,128)(2,1)S(1)} %get-tuple-element.232.refs_2_) | copy-start | bytes 1179652
  343.5 5.6 %copy-start.3 = (bf16[2,128,768]{2,1,0:T(8,128)(2,1)S(1)}, bf16[2,128,768]{2,1,0:T(8,128)(2,1)}, u32[]{:S(2)}) copy-start(bf16[2,128,768]{2,1,0:T(8,128)(2,1)} %get-tuple-element.194.refs_1_) | copy-start | bytes 1179652
  346.2 7.9 %collective-permute-start.50 = (bf16[4,48,768]{2,1,0:T(8,128)(2,1)S(1)}, bf16[4,48,768]{2,1,0:T(8,128)(2,1)S(1)}, u32[]{:S(2)}, u32[]{:S(2)}) collective-permute-start(bf16[4,48,768]{2,1,0:T(8,128)(2,1)S(1)} %get-tuple-element.253), channel_id=1, source_target_pairs={{0,2},{1,3},{2,0},{3,1},{4,6},{5,7},{6,4},{7,5},{8,10},{9,11},{10,... | collective-permute-start | bytes 884744 | tf_op jit(solution)/shard_map/ppermute | solution.py:958
  347.0 8.7 %collective-permute-start.49 = (bf16[4,48,896]{2,1,0:T(8,128)(2,1)S(1)}, bf16[4,48,896]{2,1,0:T(8,128)(2,1)S(1)}, u32[]{:S(2)}, u32[]{:S(2)}) collective-permute-start(bf16[4,48,896]{2,1,0:T(8,128)(2,1)S(1)} %get-tuple-element.251), channel_id=1, source_target_pairs={{0,4},{1,5},{2,6},{3,7},{4,0},{5,1},{6,2},{7,3},{8,12},{9,13},{10,... | collective-permute-start | bytes 1032200 | tf_op jit(solution)/shard_map/ppermute | solution.py:958
  354.1 6.8 %collective-permute-start.43 = (bf16[2,128,768]{2,1,0:T(8,128)(2,1)}, bf16[2,128,768]{2,1,0:T(8,128)(2,1)}, u32[]{:S(2)}, u32[]{:S(2)}) collective-permute-start(bf16[2,128,768]{2,1,0:T(8,128)(2,1)} %get-tuple-element.243), channel_id=1, source_target_pairs={{0,1},{1,0},{2,3},{3,2},{4,5},{5,4},{6,7},{7,6},{8,9},{9,8},{10,11... | collective-permute-start | bytes 1179656 | tf_op jit(solution)/shard_map/ppermute | solution.py:962
  355.6 12.4 %collective-permute-start.44 = (bf16[2,128,768]{2,1,0:T(8,128)(2,1)}, bf16[2,128,768]{2,1,0:T(8,128)(2,1)}, u32[]{:S(2)}, u32[]{:S(2)}) collective-permute-start(bf16[2,128,768]{2,1,0:T(8,128)(2,1)} %get-tuple-element.244), channel_id=1, source_target_pairs={{0,2},{1,3},{2,0},{3,1},{4,6},{5,7},{6,4},{7,5},{8,10},{9,11},{10,... | collective-permute-start | bytes 1179656 | tf_op jit(solution)/shard_map/ppermute | solution.py:962
  357.9 14.7 %collective-permute-start.45 = (bf16[2,128,768]{2,1,0:T(8,128)(2,1)S(1)}, bf16[2,128,768]{2,1,0:T(8,128)(2,1)S(1)}, u32[]{:S(2)}, u32[]{:S(2)}) collective-permute-start(bf16[2,128,768]{2,1,0:T(8,128)(2,1)S(1)} %copy-done.5), channel_id=1, source_target_pairs={{0,3},{1,2},{2,1},{3,0},{4,7},{5,6},{6,5},{7,4},{8,11},{9,10},{10,... | collective-permute-start | bytes 1179656 | tf_op jit(solution)/shard_map/ppermute | solution.py:962
  359.8 16.3 %collective-permute-start.55 = (bf16[24,3072]{1,0:T(8,128)(2,1)S(1)}, bf16[24,3072]{1,0:T(8,128)(2,1)S(1)}, u32[]{:S(2)}, u32[]{:S(2)}) collective-permute-start(bf16[24,3072]{1,0:T(8,128)(2,1)S(1)} %bitcast.150), channel_id=1, source_target_pairs={{0,1},{1,0},{2,3},{3,2},{4,5},{5,4},{6,7},{7,6},{8,9},{9,8},{10,11... | collective-permute-start | bytes 442376 | tf_op jit(solution)/shard_map/ppermute | solution.py:958
  360.8 17.0 %collective-permute-start.51 = (bf16[1,48,1664]{2,1,0:T(8,128)(2,1)S(1)}, bf16[1,48,1664]{2,1,0:T(8,128)(2,1)S(1)}, u32[]{:S(2)}, u32[]{:S(2)}) collective-permute-start(bf16[1,48,1664]{2,1,0:T(8,128)(2,1)S(1)} %get-tuple-element.259), channel_id=1, source_target_pairs={{0,8},{1,9},{2,10},{3,11},{4,12},{5,13},{6,14},{7,15},{8,0},{9,1},... | collective-permute-start | bytes 479240 | tf_op jit(solution)/shard_map/ppermute | solution.py:958
  360.8 17.0 %collective-permute-start.52 = (bf16[1,48,1664]{2,1,0:T(8,128)(2,1)S(1)}, bf16[1,48,1664]{2,1,0:T(8,128)(2,1)S(1)}, u32[]{:S(2)}, u32[]{:S(2)}) collective-permute-start(bf16[1,48,1664]{2,1,0:T(8,128)(2,1)S(1)} %get-tuple-element.260), channel_id=1, source_target_pairs={{0,16},{1,17},{2,18},{3,19},{4,20},{5,21},{6,22},{7,23},{8,24},{9,... | collective-permute-start | bytes 479240 | tf_op jit(solution)/shard_map/ppermute | solution.py:958
  368.0 9.8 %collective-permute-start.53 = (bf16[1,48,1664]{2,1,0:T(8,128)(2,1)S(1)}, bf16[1,48,1664]{2,1,0:T(8,128)(2,1)S(1)}, u32[]{:S(2)}, u32[]{:S(2)}) collective-permute-start(bf16[1,48,1664]{2,1,0:T(8,128)(2,1)S(1)} %get-tuple-element.261), channel_id=1, source_target_pairs={{0,24},{1,25},{2,26},{3,27},{4,28},{5,29},{6,30},{7,31},{8,16},{9,... | collective-permute-start | bytes 479240 | tf_op jit(solution)/shard_map/ppermute | solution.py:958
  379.6 2.7 collective-permute-start.54
  (40 other events, 57.4 us)

commit v5 on v4

--- a/solution.py
+++ b/solution.py
@@ -228,6 +228,17 @@
     )
 
 
+def addend_kernel(ids, mask_ref, out_ref):
+    out_ref[...] = jnp.where(mask_ref[...] > 0, 0.0, masked_score).astype(bf16)
+
+
+def mask_addend(run, mask, ties):
+    heads, rows, cols = mask.shape
+    block = pl.BlockSpec((heads // 4, rows, cols), lambda i, ids: (i, 0, 0))
+    shape = jax.ShapeDtypeStruct(mask.shape, bf16)
+    return kernel_call(addend_kernel, run, [mask], ties, (4,), [block], block, shape)
+
+
 class Loader:
     def __init__(self, ids, sems, digit="y"):
         self.core, self.digit = ids[id_of["c"]], ids[id_of[digit]]
@@ -278,10 +289,8 @@
                 left = qkv_ref[:, part * width + start : part * width + start + 128]
                 right = qkv_ref[:, part * width + start + 128 : part * width + start + 256]
                 pairs.append(jnp.where(core == turn, left, right))
-        first[...] = jnp.concatenate(pairs + [columns], axis=1)
-        second[...] = jnp.concatenate(
-            [half_split(core, ref[...])[turn] for ref in (out_ref, up_ref)], axis=1
-        )
+        out_half, second[...] = [half_split(core, ref[...])[turn] for ref in (out_ref, up_ref)]
+        first[...] = jnp.concatenate(pairs + [columns, out_half], axis=1)
         down[...] = half_split(core, down_ref[...])[turn]
 
 
@@ -289,8 +298,8 @@
     rows, cols = w_qkv.shape
     arrays = [w_qkv, vectors, w_out, w_up, w_down]
     shapes = [
-        jax.ShapeDtypeStruct((rows, cols // 2 + 128), bf16),
-        jax.ShapeDtypeStruct((rows, (w_out.shape[1] + w_up.shape[1]) // 2), bf16),
+        jax.ShapeDtypeStruct((rows, cols // 2 + 128 + w_out.shape[1] // 2), bf16),
+        jax.ShapeDtypeStruct((rows, w_up.shape[1] // 2), bf16),
         jax.ShapeDtypeStruct((w_down.shape[0], w_down.shape[1] // 2), bf16),
     ] * 2
     outs = kernel_call(
@@ -307,13 +316,14 @@
     return list(zip(outs[:3], outs[3:]))
 
 
-def qkv_kernel(blk, ids, *refs):
+def qkv_kernel(blk, ids, joined_ref, *refs):
     parts, refs = refs[:blk], refs[blk:]
     pieces, refs = (refs[:2], refs[2:4]), refs[4:]
     x_ref, vec_ref, out_ref, w_ref, w_far_ref, v_ref, sems = refs
     here, core = ids[0], ids[1]
     step = pl.program_id(0)
     cols = out_ref.shape[2]
+    block = out_ref.shape[1]
 
     @pl.when(step == 0)
     def _():
@@ -342,48 +352,22 @@
                     )
                 )
         total = dot(rows, flat(weights)) + jnp.concatenate(bias, axis=1)
-        out_ref[turn] = total.astype(bf16)
-
-
-def qkv_projection(ids, parts, pieces, cols, ties=()):
-    blk = len(parts)
-    seqs, block_rows, width = parts[0].shape
-    tokens = seqs * blk * block_rows
-    block = 2 * block_rows
-    piece = pieces[0][0]
-    shape = place_shape(piece, cols)
-    x_shape = jax.ShapeDtypeStruct((seqs, blk, block_rows, width), bf16)
-    v_shape = jax.ShapeDtypeStruct((16, width), f32)
-    return kernel_call(
-        partial(qkv_kernel, blk),
-        ids,
-        [*parts, *pieces[0], *pieces[1]],
-        ties,
-        (tokens // block,),
-        [any_block()] * (blk + 4),
-        (
-            whole_block(x_shape),
-            whole_block(v_shape),
-            pl.BlockSpec((2, block, cols), lambda i, ids: (0, i, 0)),
-        ),
-        (x_shape, v_shape, jax.ShapeDtypeStruct((2, tokens, cols), bf16)),
-        [shape, shape, place_shape(piece, 128), pltpu.SemaphoreType.DMA((blk + 6,))],
-        cost=brief,
-    )
-
-
-def attend_kernel(head_dim, ids, qkv_ref, *rest):
+        low = total.astype(bf16)
+        out_ref[turn] = low
+        joined_ref[turn, pl.ds(pl.multiple_of(step * block, block), block), :] = low
+
+
+def attend_kernel(head_dim, pair, seq, ids, qkv_ref, *rest):
     pieces, (o_ref, lse_ref) = rest[:-2], rest[-2:]
     here = ids[0]
-    pair, seq = pl.program_id(1), pl.program_id(2)
     length, wide = o_ref.shape[1:]
     per = wide // head_dim
     rows = pieces[0].shape[1]
     lanes = lax.broadcasted_iota(jnp.int32, (1, wide), 1)
     log_lanes = lax.broadcasted_iota(jnp.int32, (1, lse_ref.shape[2]), 1)
     keys, values = qkv_ref[0, :, wide : 2 * wide], qkv_ref[0, :, 2 * wide :]
-    for first in range(0, len(pieces), 2):
-        span = range(first, min(first + 2, len(pieces)))
+    for first in range(0, len(pieces), 4):
+        span = range(first, min(first + 4, len(pieces)))
         places = [piece_rows(here, piece, rows) for piece in span]
         queries = stack_pieces(qkv_ref, places, slice(0, wide))
         out, logs = None, []
@@ -423,8 +407,8 @@
     back = head_dim**-0.5
     dk = jnp.zeros(keys.shape, f32)
     dv = jnp.zeros(keys.shape, f32)
-    for first in range(0, len(pieces), 2):
-        span = range(first, min(first + 2, len(pieces)))
+    for first in range(0, len(pieces), 4):
+        span = range(first, min(first + 4, len(pieces)))
         places = [piece_rows(here, piece, rows) for piece in span]
         queries = stack_pieces(qkv_ref, places, slice(0, wide))
         ups = stack_pieces(g_ref, places, everything)
@@ -474,23 +458,84 @@
     return block, logs, [mask] * len(mask_parts)
 
 
-def attend(ids, joined, mask_parts, seqs, head_dim, ties=()):
-    tokens, cols = joined.shape[1:]
-    block, logs, masks = attention_specs(joined, mask_parts)
-    width = cols // 3
+def qkv_attend_kernel(blk, head_dim, steps, seqs, ids, *refs):
+    mask_refs, inputs, refs = refs[:blk], refs[blk : 2 * blk + 4], refs[2 * blk + 4 :]
+    x_ref, vec_ref, out_ref, o_ref, lse_ref, w_ref, w_far_ref, v_ref, joined_ref, sems = refs
+    step = pl.program_id(0)
+
+    @pl.when(step < steps)
+    def _():
+        qkv_kernel(
+            blk, ids, joined_ref, *inputs, x_ref, vec_ref, out_ref, w_ref, w_far_ref, v_ref, sems
+        )
+
+    @pl.when(step >= steps)
+    def _():
+        turn, pair, seq = attend_step(step - steps, out_ref.shape[2] // 384, seqs)
+        length = o_ref.shape[1]
+        view = joined_ref.at[
+            pl.ds(turn, 1),
+            pl.ds(pl.multiple_of(seq * length, length), length),
+            pl.ds(pl.multiple_of(pair * 384, 128), 384),
+        ]
+        attend_kernel(head_dim, pair, seq, ids, view, *mask_refs, o_ref, lse_ref)
+
+
+def attend_step(step, pairs, seqs):
+    step = jnp.maximum(step, 0)
+    return step // (pairs * seqs), step // seqs % pairs, step % seqs
+
+
+def qkv_attend(ids, parts, pieces, cols, mask_parts, head_dim, ties=()):
+    blk = len(parts)
+    seqs, block_rows, width = parts[0].shape
+    length = blk * block_rows
+    tokens = seqs * length
+    block = 2 * block_rows
+    steps = tokens // block
+    pairs = cols // 384
+    piece = pieces[0][0]
+    shape = place_shape(piece, cols)
+    x_shape = jax.ShapeDtypeStruct((seqs, blk, block_rows, width), bf16)
+    v_shape = jax.ShapeDtypeStruct((16, width), f32)
+
+    def at(index):
+        def found(i, ids):
+            return index(ids, *attend_step(i - steps, pairs, seqs))
+
+        return found
+
+    mask = pl.BlockSpec(
+        (2, block_rows, length), at(lambda ids, r, p, s: (2 * p + (ids[1] ^ r), 0, 0))
+    )
     return kernel_call(
-        partial(attend_kernel, head_dim),
+        partial(qkv_attend_kernel, blk, head_dim, steps, seqs),
         ids,
-        [joined, *mask_parts],
+        [*mask_parts, *parts, *pieces[0], *pieces[1]],
         ties,
-        (2, width // 128, seqs),
-        [block(384)] + masks,
-        (block(128), logs),
+        (steps + 2 * pairs * seqs,),
+        [mask] * blk + [any_block()] * (blk + 4),
         (
-            jax.ShapeDtypeStruct((2, tokens, width), bf16),
+            whole_block(x_shape),
+            whole_block(v_shape),
+            pl.BlockSpec((2, block, cols), lambda i, ids: (0, jnp.minimum(i, steps - 1), 0)),
+            pl.BlockSpec((1, length, 128), at(lambda ids, r, p, s: (r, s, p))),
+            pl.BlockSpec((1, tokens, 128), at(lambda ids, r, p, s: (r, 0, 0))),
+        ),
+        (
+            x_shape,
+            v_shape,
+            jax.ShapeDtypeStruct((2, tokens, cols), bf16),
+            jax.ShapeDtypeStruct((2, tokens, cols // 3), bf16),
             jax.ShapeDtypeStruct((2, tokens, 128), f32),
         ),
-        cost=brief,
+        [
+            shape,
+            shape,
+            place_shape(piece, 128),
+            pltpu.VMEM((2, tokens, cols), bf16),
+            pltpu.SemaphoreType.DMA((blk + 6,)),
+        ],
     )
 
 
@@ -525,7 +570,8 @@
     @pl.when(pl.program_id(0) == 0)
     def _():
         load = Loader(ids, sems)
-        load.columns(pieces, 0, w_ref.shape[-1] // 2, w_ref)
+        half = w_ref.shape[-1] // 2
+        load.columns(pieces, pieces[0][0].shape[-1] - half, half, w_ref)
         load.wait()
 
     attended = pair_order(ids[1], att_ref[0], att_ref[1], 128)
@@ -707,15 +753,16 @@
 
 
 def first_back_kernel(ids, gate_ref, gss_ref, first_ref, vec_ref, *refs):
-    pieces, refs = (refs[:2], refs[2:4]), refs[4:]
+    pieces, out_pieces, refs = (refs[:2], refs[2:4]), (refs[4:6], refs[6:8]), refs[8:]
     gfs_ref, branch_ref, att_ref, sums_ref, w_ref, w_out_ref, sems = refs
     width = gss_ref.shape[1]
 
     @pl.when(pl.program_id(0) == 0)
     def _():
         load = Loader(ids, sems)
-        load.columns(pieces, width // 2, w_ref.shape[-1] // 2, w_ref)
-        load.columns(pieces, 0, width // 2, w_out_ref)
+        load.columns(pieces, 0, w_ref.shape[-1] // 2, w_ref)
+        start = out_pieces[0][0].shape[-1] - width // 2
+        load.columns(out_pieces, start, width // 2, w_out_ref)
         load.wait()
 
     grad_hidden = gss_ref[...] + dot_right_t(gate_ref[...], flat(w_ref))
@@ -729,7 +776,9 @@
     add_sums(sums_ref, [low.astype(f32), grad_hidden * normed, grad_hidden])
 
 
-def first_back(ids, grad_gate, grad_second_sum, first_sum, pieces, vectors, block, ties=()):
+def first_back(
+    ids, grad_gate, grad_second_sum, first_sum, pieces, out_pieces, vectors, block, ties=()
+):
     tokens, cols = grad_gate.shape
     width = first_sum.shape[1]
 
@@ -744,10 +793,19 @@
     return kernel_call(
         first_back_kernel,
         ids,
-        [grad_gate, grad_second_sum, first_sum, vectors, *pieces[0], *pieces[1]],
+        [
+            grad_gate,
+            grad_second_sum,
+            first_sum,
+            vectors,
+            *pieces[0],
+            *pieces[1],
+            *out_pieces[0],
+            *out_pieces[1],
+        ],
         ties,
         (tokens // block,),
-        [row(cols), row(width), row(width), whole_block(vectors)] + [any_block()] * 4,
+        [row(cols), row(width), row(width), whole_block(vectors)] + [any_block()] * 8,
         (
             row(width),
             row(width),
@@ -1136,7 +1194,6 @@
             jnp.zeros((16 - len(vectors) - up_per, rows), bf16),
         ]
     )
-    addend = jnp.where(dam_mask > 0, 0.0, masked_score).astype(bf16)
     halves = split_weights(ids, w_qkv, stacked, w_out, w_up, w_down)
     first_near, second_near, down_near = [gather_core(grid, *pair) for pair in halves]
 
@@ -1150,8 +1207,9 @@
     parts = [pick(by_home, here ^ delta) for delta in range(blk)]
     parts[2:] = after(ids, parts[2:], event)
     parts[1:] = [grid.swap_blk(parts[delta], delta) for delta in range(1, blk)]
-    (addend,) = after(ids, [addend], event)
+    addend = mask_addend(ids, dam_mask, [event])
     mask_parts = [addend, grid.swap(addend, "c")]
+    second_near, down_near = after(ids, [second_near, down_near], event)
     second_near = over_x(second_near)
     ties = [ids.token]
     down_near = over_x(down_near)
@@ -1169,21 +1227,17 @@
     second_z = gather_step(grid, ids, second_near, "z", *ties)
     (down_near,) = after(ids, [down_near], ids.token)
     second_y = gather_last(grid, second_z, "y")
-    token_rows, vector_rows, joined = qkv_projection(
-        ids, parts, first_pieces, 3 * half, ties=[ids.token]
+    token_rows, vector_rows, joined, attended, logs = qkv_attend(
+        ids, parts, first_pieces, 3 * half, mask_parts, head_dim, ties=[ids.token]
     )
     token_rows = token_rows.reshape(tokens, width)
     first_row = len(vectors)
     up_bias = vector_rows[first_row : first_row + up_per].T.reshape(2, 1, -1)
-
-    attended, logs = attend(
-        ids, joined, mask_parts, seqs, head_dim, ties=[ids.token]
-    )
     down_z = gather_step(grid, ids, down_near, "z", ids.token)
     down_y = gather_last(grid, down_z, "y")
     second_pieces = gather_pieces(grid, ids, second_y, ids.token)
     first_sum, hidden_low = out_projection(
-        ids, attended, second_pieces, token_rows, vector_rows, 2 * block_rows
+        ids, attended, first_pieces, token_rows, vector_rows, 2 * block_rows
     )
     active, slope = up_projection(ids, hidden_low, second_pieces, up_bias)
     down_pieces = gather_pieces(grid, ids, down_y, ids.token)
@@ -1212,6 +1266,7 @@
         grad_second_sum,
         first_sum,
         second_pieces,
+        first_pieces,
         vector_rows,
         2 * block_rows,
         ties=[ids.token],
@@ -1250,15 +1305,15 @@
     sent = input_grad(ids, grads, grad_first_sum, first_pieces, seqs, blk, ties=[ids.token])
     one_sum.step([ids.token])
     two_sum.step([ids.token])
-    grad_inputs = home([sent[0], *after(ids, sent[1:], ids.token)])
+    grad_inputs = home(sent)
     activations = place_parts(ids, result, "here", [ids.token])
     activations = activations.reshape(groups, block_rows, width)
     att_sum = one_sum.join(two_sum)
     att_sum.step([ids.token])
     share_ffn = ffn_sum.end([ids.token])
+    share_att = att_sum.end([ids.token])
     grad_inputs = widen_parts(ids, grad_inputs, "here", [ids.token])
     grad_inputs = grad_inputs.reshape(groups, block_rows, width)
-    share_att = att_sum.end([ids.token])
 
     cut = near_grads.shape[2] - 384
     share_qkv = [

time: 386 us -> 366 us (0.948)
  Pallas kernels: 209 us -> 200 us
  waiting for transfers between devices: 81.4 us -> 76.4 us
  starting transfers between devices: 50.1 us -> 46.2 us
    pallas_call x33, Pallas kernels: 205 us -> 196 us  [kernel_call(): pl.pallas_call(body, out_shape=out_shape + [token_shape], grid_spec=pltpu...]
    ppermute x47, starting transfers between devices: 45.3 us -> 41.1 us  [swap(): return lax.ppermute(array, both, pairs)]
    unnamed x96 -> x100, local copies, waits for them, and re-layouts: 28.7 us -> 29.7 us
  transfers between devices with their start and end apart: 56 -> 56, of which waited for: 16 -> 15; matrix products, arithmetic and copies ran while one was open for 2% -> 2% of each run, Pallas kernels for 41% -> 41%
where the time goes in v5:
time: 366 us; the launch traced here: 365 us
  Pallas kernels  200 us (55%)
  waiting for transfers between devices  76.4 us (21%)
  starting transfers between devices  46.2 us (13%)
  local copies, waits for them, and re-layouts  36.3 us (10%)
  other arithmetic  3.83 us (1%)
    pallas_call x33, Pallas kernels, kernel_call(): pl.pallas_call(body, out_shape=out_shape + [token_shape], grid_spec=pltpu...  196 us
    ppermute x47, waiting for transfers between devices, swap(): return lax.ppermute(array, both, pairs)  71.4 us
    ppermute x47, starting transfers between devices, swap(): return lax.ppermute(array, both, pairs)  41.1 us
    unnamed x100, local copies, waits for them, and re-layouts  29.7 us
  transfers between devices with their start and end apart: 56, of which 15 were waited for; matrix products, arithmetic and copies ran while one was open for 2% of the time, Pallas kernels for 41%

profile of v5, /device:TPU:0, one launch (start us, length us, event | category | flops | bytes accessed | tf_op | source)
XLA Modules:
  0.0 364.6 jit_solution(18351103224297820904)
XLA Ops:
  9.3 2.7 collective-permute-start.1
  13.4 3.3 collective-permute-done.1.refs_2_
  16.7 1.3 shard_map.290
  18.5 3.9 %collective-permute-start.10 = (bf16[96,1664]{1,0:T(8,128)(2,1)}, bf16[96,1664]{1,0:T(8,128)(2,1)}, u32[]{:S(2)}, u32[]{:S(2)}) collective-permute-start(bf16[96,1664]{1,0:T(8,128)(2,1)} %bitcast.25.refs_1_), channel_id=1, source_target_pairs={{0,24},{1,25},{2,26},{3,27},{4,28},{5,29},{6,30},{7,31},{8,16},{9,... | collective-permute-start | bytes 958472 | tf_op jit(solution)/shard_map/ppermute | solution.py:1016
  23.5 1.7 collective-permute-start.13
  26.3 1.9 copy-done.17
  28.1 1.4 shard_map.291
  30.2 1.7 collective-permute-start.6
  33.6 1.8 shard_map.295
  36.4 13.2 %collective-permute-done.9.refs_3_ = bf16[96,1664]{1,0:T(8,128)(2,1)} collective-permute-done((bf16[96,1664]{1,0:T(8,128)(2,1)}, bf16[96,1664]{1,0:T(8,128)(2,1)}, u32[]{:S(2)}, u32[]{:S(2)}) %collective-permute-start.9) | collective-permute-done | bytes 319520 | tf_op jit(solution)/shard_map/ppermute | solution.py:1016
  50.1 2.2 shard_map.296
  52.3 1.6 collective-permute-start.15
  54.5 3.6 collective-permute-start.20
  58.9 7.6 %collective-permute-done.20.refs_4_ = bf16[96,1536]{1,0:T(8,128)(2,1)S(1)} collective-permute-done((bf16[96,1536]{1,0:T(8,128)(2,1)}, bf16[96,1536]{1,0:T(8,128)(2,1)S(1)}, u32[]{:S(2)}, u32[]{:S(2)}) %collective-permute-start.20) | collective-permute-done | bytes 294944 | tf_op jit(solution)/shard_map/ppermute | solution.py:1016
  66.5 17.3 %collective-permute-done.19.refs_3_ = bf16[96,1536]{1,0:T(8,128)(2,1)S(1)} collective-permute-done((bf16[96,1536]{1,0:T(8,128)(2,1)}, bf16[96,1536]{1,0:T(8,128)(2,1)S(1)}, u32[]{:S(2)}, u32[]{:S(2)}) %collective-permute-start.19) | collective-permute-done | bytes 294944 | tf_op jit(solution)/shard_map/ppermute | solution.py:1016
  88.8 2.4 collective-permute-start.24
  91.2 2.0 collective-permute-start.22
  96.1 26.5 %shard_map.300 = (bf16[2,4,128,768]{3,2,1,0:T(8,128)(2,1)}, f32[16,768]{1,0:T(8,128)S(1)}, bf16[2,1024,1152]{2,1,0:T(8,128)(2,1)}, bf16[2,1024,384]{2,1,0:T(8,12...) custom-call(s32[5]{0:T(128)S(1)} %stack.79.refs_0_, bf16[12,128,512]{2,1,0:T(8,128)(2,1)} %copy-done.18, ...), custom_call_target="tpu_custom_call" | custom-call | flops 99999997952 | bytes 1024 | tf_op jit(solution)/shard_map/pallas_call | solution.py:167
  122.7 1.6 shard_map.302
  127.0 7.5 %shard_map.301 = (f32[1024,768]{1,0:T(8,128)}, bf16[1024,768]{1,0:T(8,128)(2,1)}, f32[8,128]{1,0:T(8,128)}) custom-call(s32[5]{0:T(128)S(1)} %stack.79.refs_0_, bf16[2,1024,384]{2,1,0:T(8,128)(2,1)} %get-tuple-element.160.refs_1_.refs_2_.refs_4_, bf16[1024,768]{1,0:T(8,128)(2,1)} %bitcast.219, f32[16,768]{1,0:T(8,128)S(1)} %get-tuple-element.162.refs_3_.refs_6_.refs_4_, ...), custom_call_target="tpu_custom_call" | custom-call | flops 99999997952 | bytes 1024 | tf_op jit(solution)/shard_map/pallas_call | solution.py:167
  135.0 13.1 %shard_map.304 = (bf16[1024,3072]{1,0:T(8,128)(2,1)}, bf16[1024,3072]{1,0:T(8,128)(2,1)}, f32[8,128]{1,0:T(8,128)S(1)}) custom-call(s32[5]{0:T(128)S(1)} %stack.79.refs_0_, bf16[1024,768]{1,0:T(8,128)(2,1)} %get-tuple-element.163.refs_1_, f32[2,1,1536]{2,1,0:T(1,128)S(1)} %reshape.384.refs_2_, bf16[4,96,1536]{2,1,0:T(8,128)(2,1)S(1)} %copy-done.21, ...), custom_call_target="tpu_custom_call" | custom-call | flops 99999997952 | bytes 1024 | tf_op jit(solution)/shard_map/pallas_call | solution.py:167
  148.6 5.0 %collective-permute-done.27.refs_0_ = bf16[4,384,384]{2,1,0:T(8,128)(2,1)} collective-permute-done((bf16[4,384,384]{2,1,0:T(8,128)(2,1)}, bf16[4,384,384]{2,1,0:T(8,128)(2,1)}, u32[]{:S(2)}, u32[]{:S(2)}) %collective-permute-start.27) | collective-permute-done | bytes 1179680 | tf_op jit(solution)/shard_map/ppermute | solution.py:1016
  154.4 3.0 collective-permute-done.29.refs_10_
  157.4 25.1 %shard_map.306 = (bf16[2,128,768]{2,1,0:T(8,128)(2,1)S(1)}, bf16[2,128,768]{2,1,0:T(8,128)(2,1)}, bf16[2,128,768]{2,1,0:T(8,128)(2,1)}, bf16[2,128,768]{2,1,0:T(...) custom-call(s32[5]{0:T(128)S(1)} %stack.79.refs_0_, ...), custom_call_target="tpu_custom_call" | custom-call | flops 99999997952 | bytes 1024 | tf_op jit(solution)/shard_map/pallas_call | solution.py:167
  183.3 1.4 copy-done.32
  184.7 8.8 %shard_map.307 = (bf16[768,1536]{1,0:T(8,128)(2,1)S(1)}, bf16[768,1536]{1,0:T(8,128)(2,1)}, f32[8,128]{1,0:T(8,128)S(1)}) custom-call(s32[5]{0:T(128)S(1)} %stack.79.refs_0_, bf16[1024,3072]{1,0:T(8,128)(2,1)} %get-tuple-element.169.refs_1_, bf16[1024,768]{1,0:T(8,128)(2,1)S(1)} %bitcast.156), custom_call_target="tpu_custom_call" | custom-call | flops 99999997952 | bytes 1024 | tf_op jit(solution)/shard_map/pallas_call | solution.py:167
  193.6 1.5 copy-done.30
  196.2 1.3 collective-permute-start.32
  197.9 1.4 copy-done.41
  199.4 9.1 %shard_map.308 = (bf16[768,1536]{1,0:T(8,128)(2,1)S(1)}, bf16[768,1536]{1,0:T(8,128)(2,1)}, f32[8,128]{1,0:T(8,128)S(1)}) custom-call(s32[5]{0:T(128)S(1)} %stack.79.refs_0_, bf16[1024,768]{1,0:T(8,128)(2,1)S(1)} %copy-done.41, bf16[1024,3072]{1,0:T(8,128)(2,1)} %bitcast.208, bf16[1024,3072]{1,0:T(8,128)(2,1)} %bitcast.209, ...), custom_call_target="tpu_custom_call" | custom-call | flops 99999997952 | bytes 1024 | tf_op jit(solution)/shard_map/pallas_call | solution.py:167
  208.6 1.4 copy-done.49
  210.0 3.3 shard_map.309
  214.7 1.5 copy-done.48
  216.2 3.3 shard_map.310
  220.5 1.5 collective-permute-start.35
  222.0 16.7 %shard_map.311 = (f32[1024,768]{1,0:T(8,128)}, bf16[1024,768]{1,0:T(8,128)(2,1)}, bf16[2,1024,384]{2,1,0:T(8,128)(2,1)}, f32[8,768]{1,0:T(8,128)S(1)}, f32[8,128]{1,0:T(8,128)S(1)}) custom-call(s32[5]{0:T(128)S(1)} %stack.79.refs_0_, bf16[1024,3072]{1,0:T(8,128)(2,1)} %bitcast.210, f32[1024,768]{1,0:T(8,128)} %bitcast.215, ...), custom_call_target="tpu_custom_call" | custom-call | flops 99999997952 | bytes 1024 | tf_op jit(solution)/shard_map/pallas_call | solution.py:167
  241.4 1.4 copy-done.37
  242.8 1.4 copy-done.39
  245.4 15.1 %shard_map.313 = (bf16[1,1024,1152]{2,1,0:T(8,128)(2,1)}, f32[1,3,8,384]{3,2,1,0:T(8,128)S(1)}, f32[8,128]{1,0:T(8,128)S(1)}) custom-call(s32[5]{0:T(128)S(1)} %stack.79.refs_0_, bf16[2,1024,1152]{2,1,0:T(8,128)(2,1)} %get-tuple-element.195.refs_1_, bf16[2,1024,384]{2,1,0:T(8,128)(2,1)S(1)} %copy-done.39, bf16[2,1024,384]{2,1,0:T(8,128)(2,1)S(1)} %copy-done.37, ...), custom_call_target="tpu_custom_call" | custom-call | flops 99999997952 | bytes 1024 | tf_op jit(solution)/shard_map/pallas_call | solution.py:167
  260.6 2.0 shard_map.314
  262.7 2.3 shard_map.315
  265.0 1.5 collective-permute-start.37
  267.2 15.0 %shard_map.316 = (bf16[1,1024,1152]{2,1,0:T(8,128)(2,1)}, f32[1,3,8,384]{3,2,1,0:T(8,128)S(1)}, f32[8,128]{1,0:T(8,128)S(1)}) custom-call(s32[5]{0:T(128)S(1)} %stack.79.refs_0_, bf16[2,1024,1152]{2,1,0:T(8,128)(2,1)} %get-tuple-element.195.refs_1_, bf16[2,1024,384]{2,1,0:T(8,128)(2,1)S(1)} %copy-done.40, bf16[2,1024,384]{2,1,0:T(8,128)(2,1)S(1)} %copy-done.38, ...), custom_call_target="tpu_custom_call" | custom-call | flops 99999997952 | bytes 1024 | tf_op jit(solution)/shard_map/pallas_call | solution.py:167
  282.1 1.6 shard_map.317
  283.7 9.8 %shard_map.318 = (bf16[768,896]{1,0:T(8,128)(2,1)S(1)}, bf16[768,896]{1,0:T(8,128)(2,1)S(1)}, bf16[768,768]{1,0:T(8,128)(2,1)S(1)}, bf16[768,768]{1,0:T(8,128)(2,1)S(1)}, f32[8,128]{1,0:T(8,128)S(1)}) custom-call(s32[5]{0:T(128)S(1)} %stack.79.refs_0_, bf16[1024,768]{1,0:T(8,128)(2,1)} %bitcast.220, bf16[1,1024,1152]{2,1,0:T(8,128)(2,1)} %get-tuple-element.206.refs_2_, ...), custom_call_target="tpu_custom_call" | custom-call | flops 99999997952 | bytes 1024 | tf_op jit(solution)/shard_map/pallas_call | solution.py:167
  293.9 2.8 collective-permute-start.52
  296.7 1.3 collective-permute-start.53
  299.3 1.6 collective-permute-done.39
  300.9 1.8 shard_map.320
  302.7 1.3 collective-permute-start.41
  304.6 10.2 %shard_map.321 = (bf16[2,128,768]{2,1,0:T(8,128)(2,1)S(1)}, bf16[2,128,768]{2,1,0:T(8,128)(2,1)}, bf16[2,128,768]{2,1,0:T(8,128)(2,1)}, bf16[2,128,768]{2,1,0:T(8,128)(2,1)S(1)}, f32[8,128]{1,0:T(8,128)S(1)}) custom-call(s32[5]{0:T(128)S(1)} %stack.79.refs_0_, bf16[2,512,1152]{2,1,0:T(8,128)(2,1)} %bitcast.218, bf16[2,512,1152]{2,1,0:T(8,128)(2,1)} %bitcast.217, ...), custom_call_target="tpu_custom_call" | custom-call | flops 99999997952 | bytes 1024 | tf_op jit(solution)/shard_map/pallas_call | solution.py:167
  314.8 6.4 %collective-permute-done.42 = bf16[8,48,896]{2,1,0:T(8,128)(2,1)S(1)} collective-permute-done((bf16[8,48,896]{2,1,0:T(8,128)(2,1)S(1)}, bf16[8,48,896]{2,1,0:T(8,128)(2,1)S(1)}, u32[]{:S(2)}, u32[]{:S(2)}) %collective-permute-start.42) | collective-permute-done | bytes 688160 | tf_op jit(solution)/shard_map/ppermute | solution.py:1016
  322.2 1.8 shard_map.323
  325.2 2.9 shard_map.324
  328.2 3.8 %collective-permute-done.47 = bf16[4,48,768]{2,1,0:T(8,128)(2,1)S(1)} collective-permute-done((bf16[4,48,768]{2,1,0:T(8,128)(2,1)S(1)}, bf16[4,48,768]{2,1,0:T(8,128)(2,1)S(1)}, u32[]{:S(2)}, u32[]{:S(2)}) %collective-permute-start.47) | collective-permute-done | bytes 294944 | tf_op jit(solution)/shard_map/ppermute | solution.py:1016
  332.0 1.4 collective-permute-done.46
  333.4 1.4 collective-permute-start.44
  335.5 2.0 shard_map.326
  337.6 2.9 collective-permute-start.49
  340.5 1.5 collective-permute-start.50
  343.8 3.3 collective-permute-done.48
  347.1 5.3 %collective-permute-done.49 = bf16[1,48,1664]{2,1,0:T(8,128)(2,1)S(1)} collective-permute-done((bf16[1,48,1664]{2,1,0:T(8,128)(2,1)S(1)}, bf16[1,48,1664]{2,1,0:T(8,128)(2,1)S(1)}, u32[]{:S(2)}, u32[]{:S(2)}) %collective-permute-start.49) | collective-permute-done | bytes 159776 | tf_op jit(solution)/shard_map/ppermute | solution.py:1016
  353.8 4.5 %collective-permute-done.45.refs_4_ = bf16[2,128,768]{2,1,0:T(8,128)(2,1)S(1)} collective-permute-done((bf16[2,128,768]{2,1,0:T(8,128)(2,1)S(1)}, bf16[2,128,768]{2,1,0:T(8,128)(2,1)S(1)}, u32[]{:S(2)}, u32[]{:S(2)}) %collective-permute-start.45) | collective-permute-done | bytes 393248 | tf_op jit(solution)/shard_map/ppermute | solution.py:1020
  358.3 3.5 shard_map.328
  (234 shorter events, 50.7 us)
Async XLA Ops:
  0.6 153.7 %copy-start = (s32[8,128]{1,0:T(8,128)S(1)}, s32[8,128]{1,0:T(8,128)}, u32[]{:S(2)}) copy-start(s32[8,128]{1,0:T(8,128)} %param.33) | copy-start | bytes 12292
  7.2 2.0 collective-permute-start.11
  7.6 1.6 collective-permute-start.12
  7.7 1.5 collective-permute-start
  9.3 7.3 %collective-permute-start.1 = (bf16[48,1664]{1,0:T(8,128)(2,1)S(1)}, bf16[48,1664]{1,0:T(8,128)(2,1)S(1)}, u32[]{:S(2)}, u32[]{:S(2)}) collective-permute-start(bf16[48,1664]{1,0:T(8,128)(2,1)S(1)} %bitcast.119), channel_id=1, source_target_pairs={{0,2},{1,3},{2,0},{3,1},{4,6},{5,7},{6,4},{7,5},{8,10},{9,11},{10,... | collective-permute-start | bytes 479240 | tf_op jit(solution)/shard_map/ppermute | solution.py:1016
  18.5 17.6 %collective-permute-start.10 = (bf16[96,1664]{1,0:T(8,128)(2,1)}, bf16[96,1664]{1,0:T(8,128)(2,1)}, u32[]{:S(2)}, u32[]{:S(2)}) collective-permute-start(bf16[96,1664]{1,0:T(8,128)(2,1)} %bitcast.25.refs_1_), channel_id=1, source_target_pairs={{0,24},{1,25},{2,26},{3,27},{4,28},{5,29},{6,30},{7,31},{8,16},{9,... | collective-permute-start | bytes 958472 | tf_op jit(solution)/shard_map/ppermute | solution.py:1016
  22.4 27.2 %collective-permute-start.9 = (bf16[96,1664]{1,0:T(8,128)(2,1)}, bf16[96,1664]{1,0:T(8,128)(2,1)}, u32[]{:S(2)}, u32[]{:S(2)}) collective-permute-start(bf16[96,1664]{1,0:T(8,128)(2,1)} %bitcast.25.refs_1_), channel_id=1, source_target_pairs={{0,16},{1,17},{2,18},{3,19},{4,20},{5,21},{6,22},{7,23},{8,24},{9,... | collective-permute-start | bytes 958472 | tf_op jit(solution)/shard_map/ppermute | solution.py:1016
  22.4 27.2 %collective-permute-start.8 = (bf16[96,1664]{1,0:T(8,128)(2,1)}, bf16[96,1664]{1,0:T(8,128)(2,1)}, u32[]{:S(2)}, u32[]{:S(2)}) collective-permute-start(bf16[96,1664]{1,0:T(8,128)(2,1)} %bitcast.25.refs_1_), channel_id=1, source_target_pairs={{0,8},{1,9},{2,10},{3,11},{4,12},{5,13},{6,14},{7,15},{8,0},{9,1},... | collective-permute-start | bytes 958472 | tf_op jit(solution)/shard_map/ppermute | solution.py:1016
  23.5 6.6 %collective-permute-start.13 = (bf16[48,1536]{1,0:T(8,128)(2,1)}, bf16[48,1536]{1,0:T(8,128)(2,1)S(1)}, u32[]{:S(2)}, u32[]{:S(2)}) collective-permute-start(bf16[48,1536]{1,0:T(8,128)(2,1)} %get-tuple-element.149.refs_1_), channel_id=1, source_target_pairs={{0,2},{1,3},{2,0},{3,1},{4,6},{5,7},{6,4},{7,5},{8,10},{9,11},{10,... | collective-permute-start | bytes 442376 | tf_op jit(solution)/shard_map/ppermute | solution.py:1016
  25.3 6.6 %copy-start.2 = (bf16[48,1536]{1,0:T(8,128)(2,1)S(1)}, bf16[48,1536]{1,0:T(8,128)(2,1)}, u32[]{:S(2)}) copy-start(bf16[48,1536]{1,0:T(8,128)(2,1)} %get-tuple-element.149.refs_1_) | copy-start | bytes 442372
  25.3 8.3 %collective-permute-start.14 = (bf16[192,384]{1,0:T(8,128)(2,1)}, bf16[192,384]{1,0:T(8,128)(2,1)}, u32[]{:S(2)}, u32[]{:S(2)}) collective-permute-start(bf16[192,384]{1,0:T(8,128)(2,1)} %get-tuple-element.151.refs_1_), channel_id=1, source_target_pairs={{0,2},{1,3},{2,0},{3,1},{4,6},{5,7},{6,4},{7,5},{8,10},{9,11},{10,... | collective-permute-start | bytes 442376 | tf_op jit(solution)/shard_map/ppermute | solution.py:1016
  29.5 54.3 %copy-start.18 = (bf16[12,128,512]{2,1,0:T(8,128)(2,1)}, bf16[12,128,512]{2,1,0:T(8,128)(2,1)S(1)}, u32[]{:S(2)}) copy-start(bf16[12,128,512]{2,1,0:T(8,128)(2,1)S(1)} %get-tuple-element.141.refs_1_.refs_5_) | copy-start | bytes 4718596
  30.2 19.5 %collective-permute-start.6 = (bf16[2,128,768]{2,1,0:T(8,128)(2,1)}, bf16[2,128,768]{2,1,0:T(8,128)(2,1)}, u32[]{:S(2)}, u32[]{:S(2)}) collective-permute-start(bf16[2,128,768]{2,1,0:T(8,128)(2,1)} %get-tuple-element.142), channel_id=1, source_target_pairs={{0,2},{1,3},{2,0},{3,1},{4,6},{5,7},{6,4},{7,5},{8,10},{9,11},{10,... | collective-permute-start | bytes 1179656 | tf_op jit(solution)/shard_map/ppermute | solution.py:1020
  33.6 16.5 %collective-permute-start.7 = (bf16[2,128,768]{2,1,0:T(8,128)(2,1)S(1)}, bf16[2,128,768]{2,1,0:T(8,128)(2,1)S(1)}, u32[]{:S(2)}, u32[]{:S(2)}) collective-permute-start(bf16[2,128,768]{2,1,0:T(8,128)(2,1)S(1)} %copy-done.46), channel_id=1, source_target_pairs={{0,3},{1,2},{2,1},{3,0},{4,7},{5,6},{6,5},{7,4},{8,11},{9,10},{10,... | collective-permute-start | bytes 1179656 | tf_op jit(solution)/shard_map/ppermute | solution.py:1020
  36.1 48.2 %collective-permute-start.3 = (bf16[12,128,512]{2,1,0:T(8,128)(2,1)S(1)}, bf16[12,128,512]{2,1,0:T(8,128)(2,1)}, u32[]{:S(2)}, u32[]{:S(2)}) collective-permute-start(bf16[12,128,512]{2,1,0:T(8,128)(2,1)S(1)} %get-tuple-element.141.refs_1_.refs_5_), channel_id=1, source_target_pairs={{0,2},{1,3},{2,0},{3,1},{4,6},{5,7},{6,4},{7,5},{8,10},{9,11},{10,... | collective-permute-start | bytes 4718600 | tf_op jit(solution)/shard_map/ppermute | solution.py:1016
  52.3 32.1 %collective-permute-start.15 = (bf16[4,96,1664]{2,1,0:T(8,128)(2,1)S(1)}, bf16[4,96,1664]{2,1,0:T(8,128)(2,1)}, u32[]{:S(2)}, u32[]{:S(2)}) collective-permute-start(bf16[4,96,1664]{2,1,0:T(8,128)(2,1)S(1)} %get-tuple-element.153.refs_9_.refs_4_), channel_id=1, source_target_pairs={{0,4},{1,5},{2,6},{3,7},{4,0},{5,1},{6,2},{7,3},{8,12},{9,13},{10,... | collective-permute-start | bytes 3833864 | tf_op jit(solution)/shard_map/ppermute | solution.py:1016
  54.5 11.9 %collective-permute-start.20 = (bf16[96,1536]{1,0:T(8,128)(2,1)}, bf16[96,1536]{1,0:T(8,128)(2,1)S(1)}, u32[]{:S(2)}, u32[]{:S(2)}) collective-permute-start(bf16[96,1536]{1,0:T(8,128)(2,1)} %get-tuple-element.157.refs_1_), channel_id=1, source_target_pairs={{0,24},{1,25},{2,26},{3,27},{4,28},{5,29},{6,30},{7,31},{8,16},{9,... | collective-permute-start | bytes 884744 | tf_op jit(solution)/shard_map/ppermute | solution.py:1016
  58.1 25.7 %collective-permute-start.19 = (bf16[96,1536]{1,0:T(8,128)(2,1)}, bf16[96,1536]{1,0:T(8,128)(2,1)S(1)}, u32[]{:S(2)}, u32[]{:S(2)}) collective-permute-start(bf16[96,1536]{1,0:T(8,128)(2,1)} %get-tuple-element.157.refs_1_), channel_id=1, source_target_pairs={{0,16},{1,17},{2,18},{3,19},{4,20},{5,21},{6,22},{7,23},{8,24},{9,... | collective-permute-start | bytes 884744 | tf_op jit(solution)/shard_map/ppermute | solution.py:1016
  58.1 25.7 %collective-permute-start.18 = (bf16[96,1536]{1,0:T(8,128)(2,1)}, bf16[96,1536]{1,0:T(8,128)(2,1)S(1)}, u32[]{:S(2)}, u32[]{:S(2)}) collective-permute-start(bf16[96,1536]{1,0:T(8,128)(2,1)} %get-tuple-element.157.refs_1_), channel_id=1, source_target_pairs={{0,8},{1,9},{2,10},{3,11},{4,12},{5,13},{6,14},{7,15},{8,0},{9,1},... | collective-permute-start | bytes 884744 | tf_op jit(solution)/shard_map/ppermute | solution.py:1016
  66.4 22.4 %collective-permute-start.5 = (bf16[2,128,768]{2,1,0:T(8,128)(2,1)}, bf16[2,128,768]{2,1,0:T(8,128)(2,1)}, u32[]{:S(2)}, u32[]{:S(2)}) collective-permute-start(bf16[2,128,768]{2,1,0:T(8,128)(2,1)} %get-tuple-element.271), channel_id=1, source_target_pairs={{0,1},{1,0},{2,3},{3,2},{4,5},{5,4},{6,7},{7,6},{8,9},{9,8},{10,11... | collective-permute-start | bytes 1179656 | tf_op jit(solution)/shard_map/ppermute | solution.py:1020
  83.8 7.4 %collective-permute-start.2 = (bf16[12,128,512]{2,1,0:T(8,128)(2,1)S(1)}, bf16[12,128,512]{2,1,0:T(8,128)(2,1)}, u32[]{:S(2)}, u32[]{:S(2)}) collective-permute-start(bf16[12,128,512]{2,1,0:T(8,128)(2,1)S(1)} %get-tuple-element.141.refs_1_.refs_5_), channel_id=1, source_target_pairs={{0,1},{1,0},{2,3},{3,2},{4,5},{5,4},{6,7},{7,6},{8,9},{9,8},{10,11... | collective-permute-start | bytes 4718600 | tf_op jit(solution)/shard_map/ppermute | solution.py:1016
  83.8 7.4 %collective-permute-start.16 = (bf16[4,96,1664]{2,1,0:T(8,128)(2,1)S(1)}, bf16[4,96,1664]{2,1,0:T(8,128)(2,1)}, u32[]{:S(2)}, u32[]{:S(2)}) collective-permute-start(bf16[4,96,1664]{2,1,0:T(8,128)(2,1)S(1)} %get-tuple-element.153.refs_9_.refs_4_), channel_id=1, source_target_pairs={{0,1},{1,0},{2,3},{3,2},{4,5},{5,4},{6,7},{7,6},{8,9},{9,8},{10,11... | collective-permute-start | bytes 3833864 | tf_op jit(solution)/shard_map/ppermute | solution.py:1016
  84.3 9.3 %collective-permute-start.4 = (bf16[12,128,512]{2,1,0:T(8,128)(2,1)}, bf16[12,128,512]{2,1,0:T(8,128)(2,1)}, u32[]{:S(2)}, u32[]{:S(2)}) collective-permute-start(bf16[12,128,512]{2,1,0:T(8,128)(2,1)} %collective-permute-done.3.refs_5_.refs_3_.refs_7_), channel_id=1, source_target_pairs={{0,1},{1,0},{2,3},{3,2},{4,5},{5,4},{6,7},{7,6},{8,9},{9,8},{10,11... | collective-permute-start | bytes 4718600 | tf_op jit(solution)/shard_map/ppermute | solution.py:1016
  84.4 9.1 %collective-permute-start.17 = (bf16[4,96,1664]{2,1,0:T(8,128)(2,1)}, bf16[4,96,1664]{2,1,0:T(8,128)(2,1)}, u32[]{:S(2)}, u32[]{:S(2)}) collective-permute-start(bf16[4,96,1664]{2,1,0:T(8,128)(2,1)} %collective-permute-done.15.refs_10_.refs_5_), channel_id=1, source_target_pairs={{0,1},{1,0},{2,3},{3,2},{4,5},{5,4},{6,7},{7,6},{8,9},{9,8},{10,11... | collective-permute-start | bytes 3833864 | tf_op jit(solution)/shard_map/ppermute | solution.py:1016
  88.8 33.8 %collective-permute-start.24 = (bf16[384,384]{1,0:T(8,128)(2,1)}, bf16[384,384]{1,0:T(8,128)(2,1)S(1)}, u32[]{:S(2)}, u32[]{:S(2)}) collective-permute-start(bf16[384,384]{1,0:T(8,128)(2,1)} %get-tuple-element.165.refs_1_), channel_id=1, source_target_pairs={{0,24},{1,25},{2,26},{3,27},{4,28},{5,29},{6,30},{7,31},{8,16},{9,... | collective-permute-start | bytes 884744 | tf_op jit(solution)/shard_map/ppermute | solution.py:1016
  91.2 31.5 %collective-permute-start.23 = (bf16[384,384]{1,0:T(8,128)(2,1)}, bf16[384,384]{1,0:T(8,128)(2,1)S(1)}, u32[]{:S(2)}, u32[]{:S(2)}) collective-permute-start(bf16[384,384]{1,0:T(8,128)(2,1)} %get-tuple-element.165.refs_1_), channel_id=1, source_target_pairs={{0,16},{1,17},{2,18},{3,19},{4,20},{5,21},{6,22},{7,23},{8,24},{9,... | collective-permute-start | bytes 884744 | tf_op jit(solution)/shard_map/ppermute | solution.py:1016
  91.2 31.5 %collective-permute-start.22 = (bf16[384,384]{1,0:T(8,128)(2,1)}, bf16[384,384]{1,0:T(8,128)(2,1)S(1)}, u32[]{:S(2)}, u32[]{:S(2)}) collective-permute-start(bf16[384,384]{1,0:T(8,128)(2,1)} %get-tuple-element.165.refs_1_), channel_id=1, source_target_pairs={{0,8},{1,9},{2,10},{3,11},{4,12},{5,13},{6,14},{7,15},{8,0},{9,1},... | collective-permute-start | bytes 884744 | tf_op jit(solution)/shard_map/ppermute | solution.py:1016
  93.5 41.5 %collective-permute-start.25 = (bf16[4,96,1536]{2,1,0:T(8,128)(2,1)}, bf16[4,96,1536]{2,1,0:T(8,128)(2,1)}, u32[]{:S(2)}, u32[]{:S(2)}) collective-permute-start(bf16[4,96,1536]{2,1,0:T(8,128)(2,1)} %copy-done.20), channel_id=1, source_target_pairs={{0,1},{1,0},{2,3},{3,2},{4,5},{5,4},{6,7},{7,6},{8,9},{9,8},{10,11... | collective-permute-start | bytes 3538952 | tf_op jit(solution)/shard_map/ppermute | solution.py:1016
  93.6 32.6 %collective-permute-start.21 = (bf16[4,96,1536]{2,1,0:T(8,128)(2,1)}, bf16[4,96,1536]{2,1,0:T(8,128)(2,1)}, u32[]{:S(2)}, u32[]{:S(2)}) collective-permute-start(bf16[4,96,1536]{2,1,0:T(8,128)(2,1)} %copy-done.20), channel_id=1, source_target_pairs={{0,4},{1,5},{2,6},{3,7},{4,0},{5,1},{6,2},{7,3},{8,12},{9,13},{10,... | collective-permute-start | bytes 3538952 | tf_op jit(solution)/shard_map/ppermute | solution.py:1016
  96.1 26.6 %copy-start.7 = (bf16[384,384]{1,0:T(8,128)(2,1)S(1)}, bf16[384,384]{1,0:T(8,128)(2,1)}, u32[]{:S(2)}) copy-start(bf16[384,384]{1,0:T(8,128)(2,1)} %get-tuple-element.165.refs_1_) | copy-start | bytes 884740
  124.9 29.5 %collective-permute-start.28 = (bf16[4,384,384]{2,1,0:T(8,128)(2,1)}, bf16[4,384,384]{2,1,0:T(8,128)(2,1)}, u32[]{:S(2)}, u32[]{:S(2)}) collective-permute-start(bf16[4,384,384]{2,1,0:T(8,128)(2,1)} %get-tuple-element.172.refs_7_), channel_id=1, source_target_pairs={{0,1},{1,0},{2,3},{3,2},{4,5},{5,4},{6,7},{7,6},{8,9},{9,8},{10,11... | collective-permute-start | bytes 3538952 | tf_op jit(solution)/shard_map/ppermute | solution.py:1016
  125.0 28.6 %collective-permute-start.27 = (bf16[4,384,384]{2,1,0:T(8,128)(2,1)}, bf16[4,384,384]{2,1,0:T(8,128)(2,1)}, u32[]{:S(2)}, u32[]{:S(2)}) collective-permute-start(bf16[4,384,384]{2,1,0:T(8,128)(2,1)} %get-tuple-element.172.refs_7_), channel_id=1, source_target_pairs={{0,4},{1,5},{2,6},{3,7},{4,0},{5,1},{6,2},{7,3},{8,12},{9,13},{10,... | collective-permute-start | bytes 3538952 | tf_op jit(solution)/shard_map/ppermute | solution.py:1016
  126.8 8.1 %collective-permute-start.26 = (bf16[4,96,1536]{2,1,0:T(8,128)(2,1)}, bf16[4,96,1536]{2,1,0:T(8,128)(2,1)}, u32[]{:S(2)}, u32[]{:S(2)}) collective-permute-start(bf16[4,96,1536]{2,1,0:T(8,128)(2,1)} %get-tuple-element.168.refs_4_.refs_6_), channel_id=1, source_target_pairs={{0,1},{1,0},{2,3},{3,2},{4,5},{5,4},{6,7},{7,6},{8,9},{9,8},{10,11... | collective-permute-start | bytes 3538952 | tf_op jit(solution)/shard_map/ppermute | solution.py:1016
  127.0 8.0 %copy-start.21 = (bf16[4,96,1536]{2,1,0:T(8,128)(2,1)S(1)}, bf16[4,96,1536]{2,1,0:T(8,128)(2,1)}, u32[]{:S(2)}) copy-start(bf16[4,96,1536]{2,1,0:T(8,128)(2,1)} %copy-done.20) | copy-start | bytes 3538948
  135.0 19.3 %copy-start.47 = (s32[8]{0:T(128)S(1)}, s32[8]{0:T(128)}, u32[]{:S(2)}) copy-start(s32[8]{0:T(128)} %param.34) | copy-start | bytes 100
  154.2 3.2 collective-permute-start.29
  195.6 43.7 %collective-permute-start.30 = (bf16[2,128,768]{2,1,0:T(8,128)(2,1)}, bf16[2,128,768]{2,1,0:T(8,128)(2,1)}, u32[]{:S(2)}, u32[]{:S(2)}) collective-permute-start(bf16[2,128,768]{2,1,0:T(8,128)(2,1)} %get-tuple-element.176), channel_id=1, source_target_pairs={{0,1},{1,0},{2,3},{3,2},{4,5},{5,4},{6,7},{7,6},{8,9},{9,8},{10,11... | collective-permute-start | bytes 1179656 | tf_op jit(solution)/shard_map/ppermute | solution.py:1020
  195.8 43.5 %collective-permute-start.31 = (bf16[2,128,768]{2,1,0:T(8,128)(2,1)}, bf16[2,128,768]{2,1,0:T(8,128)(2,1)}, u32[]{:S(2)}, u32[]{:S(2)}) collective-permute-start(bf16[2,128,768]{2,1,0:T(8,128)(2,1)} %get-tuple-element.177), channel_id=1, source_target_pairs={{0,2},{1,3},{2,0},{3,1},{4,6},{5,7},{6,4},{7,5},{8,10},{9,11},{10,... | collective-permute-start | bytes 1179656 | tf_op jit(solution)/shard_map/ppermute | solution.py:1020
  196.2 43.1 %collective-permute-start.32 = (bf16[2,128,768]{2,1,0:T(8,128)(2,1)}, bf16[2,128,768]{2,1,0:T(8,128)(2,1)}, u32[]{:S(2)}, u32[]{:S(2)}) collective-permute-start(bf16[2,128,768]{2,1,0:T(8,128)(2,1)} %get-tuple-element.178), channel_id=1, source_target_pairs={{0,3},{1,2},{2,1},{3,0},{4,7},{5,6},{6,5},{7,4},{8,11},{9,10},{10,... | collective-permute-start | bytes 1179656 | tf_op jit(solution)/shard_map/ppermute | solution.py:1020
  197.5 11.1 %collective-permute-start.34 = (bf16[768,1536]{1,0:T(8,128)(2,1)}, bf16[768,1536]{1,0:T(8,128)(2,1)S(1)}, u32[]{:S(2)}, u32[]{:S(2)}) collective-permute-start(bf16[768,1536]{1,0:T(8,128)(2,1)} %get-tuple-element.186), channel_id=1, source_target_pairs={{0,1},{1,0},{2,3},{3,2},{4,5},{5,4},{6,7},{7,6},{8,9},{9,8},{10,11... | collective-permute-start | bytes 7077896 | tf_op jit(solution)/shard_map/ppermute | solution.py:1016
  199.4 10.7 %copy-start.31 = (bf16[768,1536]{1,0:T(8,128)(2,1)S(1)}, bf16[768,1536]{1,0:T(8,128)(2,1)}, u32[]{:S(2)}) copy-start(bf16[768,1536]{1,0:T(8,128)(2,1)} %copy-done.30) | copy-start | bytes 7077892
  208.5 6.2 %collective-permute-start.33 = (bf16[768,1536]{1,0:T(8,128)(2,1)}, bf16[768,1536]{1,0:T(8,128)(2,1)S(1)}, u32[]{:S(2)}, u32[]{:S(2)}) collective-permute-start(bf16[768,1536]{1,0:T(8,128)(2,1)} %get-tuple-element.184), channel_id=1, source_target_pairs={{0,1},{1,0},{2,3},{3,2},{4,5},{5,4},{6,7},{7,6},{8,9},{9,8},{10,11... | collective-permute-start | bytes 7077896 | tf_op jit(solution)/shard_map/ppermute | solution.py:1016
  214.3 46.2 %collective-permute-start.36 = (bf16[8,48,1536]{2,1,0:T(8,128)(2,1)}, bf16[8,48,1536]{2,1,0:T(8,128)(2,1)}, u32[]{:S(2)}, u32[]{:S(2)}) collective-permute-start(bf16[8,48,1536]{2,1,0:T(8,128)(2,1)} %get-tuple-element.201), channel_id=1, source_target_pairs={{0,2},{1,3},{2,0},{3,1},{4,6},{5,7},{6,4},{7,5},{8,10},{9,11},{10,... | collective-permute-start | bytes 3538952 | tf_op jit(solution)/shard_map/ppermute | solution.py:1016
  220.5 42.1 %collective-permute-start.35 = (bf16[4,96,1536]{2,1,0:T(8,128)(2,1)}, bf16[4,96,1536]{2,1,0:T(8,128)(2,1)}, u32[]{:S(2)}, u32[]{:S(2)}) collective-permute-start(bf16[4,96,1536]{2,1,0:T(8,128)(2,1)} %get-tuple-element.199), channel_id=1, source_target_pairs={{0,4},{1,5},{2,6},{3,7},{4,0},{5,1},{6,2},{7,3},{8,12},{9,13},{10,... | collective-permute-start | bytes 3538952 | tf_op jit(solution)/shard_map/ppermute | solution.py:1016
  245.4 15.1 %copy-start.34 = (bf16[8,48,1536]{2,1,0:T(8,128)(2,1)S(1)}, bf16[8,48,1536]{2,1,0:T(8,128)(2,1)}, u32[]{:S(2)}) copy-start(bf16[8,48,1536]{2,1,0:T(8,128)(2,1)} %copy-done.33) | copy-start | bytes 3538948
  265.0 17.2 %collective-permute-start.37 = (bf16[4,48,1536]{2,1,0:T(8,128)(2,1)S(1)}, bf16[4,48,1536]{2,1,0:T(8,128)(2,1)S(1)}, u32[]{:S(2)}, u32[]{:S(2)}) collective-permute-start(bf16[4,48,1536]{2,1,0:T(8,128)(2,1)S(1)} %get-tuple-element.215), channel_id=1, source_target_pairs={{0,2},{1,3},{2,0},{3,1},{4,6},{5,7},{6,4},{7,5},{8,10},{9,11},{10,... | collective-permute-start | bytes 1769480 | tf_op jit(solution)/shard_map/ppermute | solution.py:1016
  266.4 15.7 %collective-permute-start.38 = (bf16[4,48,1536]{2,1,0:T(8,128)(2,1)S(1)}, bf16[4,48,1536]{2,1,0:T(8,128)(2,1)S(1)}, u32[]{:S(2)}, u32[]{:S(2)}) collective-permute-start(bf16[4,48,1536]{2,1,0:T(8,128)(2,1)S(1)} %get-tuple-element.217), channel_id=1, source_target_pairs={{0,4},{1,5},{2,6},{3,7},{4,0},{5,1},{6,2},{7,3},{8,12},{9,13},{10,... | collective-permute-start | bytes 1769480 | tf_op jit(solution)/shard_map/ppermute | solution.py:1016
  293.5 4.5 %collective-permute-start.40 = (bf16[768,896]{1,0:T(8,128)(2,1)S(1)}, bf16[768,896]{1,0:T(8,128)(2,1)S(1)}, u32[]{:S(2)}, u32[]{:S(2)}) collective-permute-start(bf16[768,896]{1,0:T(8,128)(2,1)S(1)} %get-tuple-element.223), channel_id=1, source_target_pairs={{0,1},{1,0},{2,3},{3,2},{4,5},{5,4},{6,7},{7,6},{8,9},{9,8},{10,11... | collective-permute-start | bytes 4128776 | tf_op jit(solution)/shard_map/ppermute | solution.py:1016
  293.6 41.9 %collective-permute-start.51 = (bf16[1,48,3072]{2,1,0:T(8,128)(2,1)}, bf16[1,48,3072]{2,1,0:T(8,128)(2,1)}, u32[]{:S(2)}, u32[]{:S(2)}) collective-permute-start(bf16[1,48,3072]{2,1,0:T(8,128)(2,1)} %get-tuple-element.250), channel_id=1, source_target_pairs={{0,8},{1,9},{2,10},{3,11},{4,12},{5,13},{6,14},{7,15},{8,0},{9,1},... | collective-permute-start | bytes 884744 | tf_op jit(solution)/shard_map/ppermute | solution.py:1016
  293.9 41.6 %collective-permute-start.52 = (bf16[1,48,3072]{2,1,0:T(8,128)(2,1)}, bf16[1,48,3072]{2,1,0:T(8,128)(2,1)}, u32[]{:S(2)}, u32[]{:S(2)}) collective-permute-start(bf16[1,48,3072]{2,1,0:T(8,128)(2,1)} %get-tuple-element.251), channel_id=1, source_target_pairs={{0,16},{1,17},{2,18},{3,19},{4,20},{5,21},{6,22},{7,23},{8,24},{9,... | collective-permute-start | bytes 884744 | tf_op jit(solution)/shard_map/ppermute | solution.py:1016
  296.7 38.8 %collective-permute-start.53 = (bf16[1,48,3072]{2,1,0:T(8,128)(2,1)}, bf16[1,48,3072]{2,1,0:T(8,128)(2,1)}, u32[]{:S(2)}, u32[]{:S(2)}) collective-permute-start(bf16[1,48,3072]{2,1,0:T(8,128)(2,1)} %get-tuple-element.252), channel_id=1, source_target_pairs={{0,24},{1,25},{2,26},{3,27},{4,28},{5,29},{6,30},{7,31},{8,16},{9,... | collective-permute-start | bytes 884744 | tf_op jit(solution)/shard_map/ppermute | solution.py:1016
  298.1 2.8 collective-permute-start.39
  302.7 19.5 %collective-permute-start.41 = (bf16[4,96,768]{2,1,0:T(8,128)(2,1)}, bf16[4,96,768]{2,1,0:T(8,128)(2,1)}, u32[]{:S(2)}, u32[]{:S(2)}) collective-permute-start(bf16[4,96,768]{2,1,0:T(8,128)(2,1)} %get-tuple-element.227), channel_id=1, source_target_pairs={{0,4},{1,5},{2,6},{3,7},{4,0},{5,1},{6,2},{7,3},{8,12},{9,13},{10,... | collective-permute-start | bytes 1769480 | tf_op jit(solution)/shard_map/ppermute | solution.py:1016
  304.0 17.2 %collective-permute-start.42 = (bf16[8,48,896]{2,1,0:T(8,128)(2,1)S(1)}, bf16[8,48,896]{2,1,0:T(8,128)(2,1)S(1)}, u32[]{:S(2)}, u32[]{:S(2)}) collective-permute-start(bf16[8,48,896]{2,1,0:T(8,128)(2,1)S(1)} %get-tuple-element.229), channel_id=1, source_target_pairs={{0,2},{1,3},{2,0},{3,1},{4,6},{5,7},{6,4},{7,5},{8,10},{9,11},{10,... | collective-permute-start | bytes 2064392 | tf_op jit(solution)/shard_map/ppermute | solution.py:1016
  324.0 8.0 %collective-permute-start.47 = (bf16[4,48,768]{2,1,0:T(8,128)(2,1)S(1)}, bf16[4,48,768]{2,1,0:T(8,128)(2,1)S(1)}, u32[]{:S(2)}, u32[]{:S(2)}) collective-permute-start(bf16[4,48,768]{2,1,0:T(8,128)(2,1)S(1)} %get-tuple-element.243), channel_id=1, source_target_pairs={{0,2},{1,3},{2,0},{3,1},{4,6},{5,7},{6,4},{7,5},{8,10},{9,11},{10,... | collective-permute-start | bytes 884744 | tf_op jit(solution)/shard_map/ppermute | solution.py:1016
  324.7 8.7 %collective-permute-start.46 = (bf16[4,48,896]{2,1,0:T(8,128)(2,1)S(1)}, bf16[4,48,896]{2,1,0:T(8,128)(2,1)S(1)}, u32[]{:S(2)}, u32[]{:S(2)}) collective-permute-start(bf16[4,48,896]{2,1,0:T(8,128)(2,1)S(1)} %get-tuple-element.241), channel_id=1, source_target_pairs={{0,4},{1,5},{2,6},{3,7},{4,0},{5,1},{6,2},{7,3},{8,12},{9,13},{10,... | collective-permute-start | bytes 1032200 | tf_op jit(solution)/shard_map/ppermute | solution.py:1016
  332.0 21.9 %collective-permute-start.43 = (bf16[2,128,768]{2,1,0:T(8,128)(2,1)}, bf16[2,128,768]{2,1,0:T(8,128)(2,1)}, u32[]{:S(2)}, u32[]{:S(2)}) collective-permute-start(bf16[2,128,768]{2,1,0:T(8,128)(2,1)} %get-tuple-element.237), channel_id=1, source_target_pairs={{0,1},{1,0},{2,3},{3,2},{4,5},{5,4},{6,7},{7,6},{8,9},{9,8},{10,11... | collective-permute-start | bytes 1179656 | tf_op jit(solution)/shard_map/ppermute | solution.py:1020
  333.4 20.5 %collective-permute-start.44 = (bf16[2,128,768]{2,1,0:T(8,128)(2,1)}, bf16[2,128,768]{2,1,0:T(8,128)(2,1)}, u32[]{:S(2)}, u32[]{:S(2)}) collective-permute-start(bf16[2,128,768]{2,1,0:T(8,128)(2,1)} %get-tuple-element.238), channel_id=1, source_target_pairs={{0,2},{1,3},{2,0},{3,1},{4,6},{5,7},{6,4},{7,5},{8,10},{9,11},{10,... | collective-permute-start | bytes 1179656 | tf_op jit(solution)/shard_map/ppermute | solution.py:1020
  337.4 3.1 collective-permute-start.55
  337.5 9.6 %collective-permute-start.48 = (bf16[1,48,1664]{2,1,0:T(8,128)(2,1)S(1)}, bf16[1,48,1664]{2,1,0:T(8,128)(2,1)S(1)}, u32[]{:S(2)}, u32[]{:S(2)}) collective-permute-start(bf16[1,48,1664]{2,1,0:T(8,128)(2,1)S(1)} %get-tuple-element.246), channel_id=1, source_target_pairs={{0,8},{1,9},{2,10},{3,11},{4,12},{5,13},{6,14},{7,15},{8,0},{9,1},... | collective-permute-start | bytes 479240 | tf_op jit(solution)/shard_map/ppermute | solution.py:1016
  337.6 14.8 %collective-permute-start.49 = (bf16[1,48,1664]{2,1,0:T(8,128)(2,1)S(1)}, bf16[1,48,1664]{2,1,0:T(8,128)(2,1)S(1)}, u32[]{:S(2)}, u32[]{:S(2)}) collective-permute-start(bf16[1,48,1664]{2,1,0:T(8,128)(2,1)S(1)} %get-tuple-element.247), channel_id=1, source_target_pairs={{0,16},{1,17},{2,18},{3,19},{4,20},{5,21},{6,22},{7,23},{8,24},{9,... | collective-permute-start | bytes 479240 | tf_op jit(solution)/shard_map/ppermute | solution.py:1016
  340.5 11.9 %collective-permute-start.50 = (bf16[1,48,1664]{2,1,0:T(8,128)(2,1)S(1)}, bf16[1,48,1664]{2,1,0:T(8,128)(2,1)S(1)}, u32[]{:S(2)}, u32[]{:S(2)}) collective-permute-start(bf16[1,48,1664]{2,1,0:T(8,128)(2,1)S(1)} %get-tuple-element.248), channel_id=1, source_target_pairs={{0,24},{1,25},{2,26},{3,27},{4,28},{5,29},{6,30},{7,31},{8,16},{9,... | collective-permute-start | bytes 479240 | tf_op jit(solution)/shard_map/ppermute | solution.py:1016
  347.1 11.3 %collective-permute-start.45 = (bf16[2,128,768]{2,1,0:T(8,128)(2,1)S(1)}, bf16[2,128,768]{2,1,0:T(8,128)(2,1)S(1)}, u32[]{:S(2)}, u32[]{:S(2)}) collective-permute-start(bf16[2,128,768]{2,1,0:T(8,128)(2,1)S(1)} %get-tuple-element.239), channel_id=1, source_target_pairs={{0,3},{1,2},{2,1},{3,0},{4,7},{5,6},{6,5},{7,4},{8,11},{9,10},{10,... | collective-permute-start | bytes 1179656 | tf_op jit(solution)/shard_map/ppermute | solution.py:1020
  353.0 9.7 %collective-permute-start.54 = (bf16[24,1664]{1,0:T(8,128)(2,1)S(1)}, bf16[24,1664]{1,0:T(8,128)(2,1)S(1)}, u32[]{:S(2)}, u32[]{:S(2)}) collective-permute-start(bf16[24,1664]{1,0:T(8,128)(2,1)S(1)} %bitcast.151), channel_id=1, source_target_pairs={{0,1},{1,0},{2,3},{3,2},{4,5},{5,4},{6,7},{7,6},{8,9},{9,8},{10,11... | collective-permute-start | bytes 239624 | tf_op jit(solution)/shard_map/ppermute | solution.py:1016
  (42 other events, 65.3 us)
